TPU v7x, 128 devices: a whole 4x4x4 slice. The times are simulated.
128 devices in a mesh: dp: 8 (over z_hi, y), ctx: 4 (over z_lo, core), tensor: 4 (over x).
Axes of the slice: x: 4, y: 4, z: 4 (z_hi: 2, z_lo: 2; z = z_hi * 2 + z_lo), core: 2. Of those that a mesh axis runs over, the one named last changes fastest.
Arguments:
- stream: bfloat16 [16, 1152, 1024], P('dp', ('ctx', 'tensor')), may hold values from -6 to 6
- segments: int32 [16, 1152], P('dp'), may hold values from 0 to 2, as said below
- w_qkv: bfloat16 [2, 1024, 3, 1024], P(None, ('dp', 'ctx'), None, 'tensor'), may hold values from -0.1875 to 0.1875
- qv_bias: bfloat16 [2, 2, 16, 64], P(None, None, 'tensor', ('dp', 'ctx')), may hold values from -3 to 3
- w_out: bfloat16 [2, 1024, 1024], P(None, 'tensor', ('dp', 'ctx')), may hold values from -2 to 2
- norm_gains: bfloat16 [2, 2, 1024], P(None, None, ('dp', 'ctx')), may hold values from 0.5 to 1.5
- shifts: bfloat16 [2, 4, 1024], P(None, None, ('dp', 'ctx')), may hold values from -2 to 2
- w_in: bfloat16 [2, 1024, 4096], P(None, ('dp', 'ctx'), 'tensor'), may hold values from -0.1875 to 0.1875
- in_bias: bfloat16 [2, 16, 256], P(None, 'tensor', ('dp', 'ctx')), may hold values from -2 to 2
- w_back: bfloat16 [2, 4096, 1024], P(None, 'tensor', ('dp', 'ctx')), may hold values from -0.09375 to 0.09375
- cotangent: bfloat16 [16, 1152, 1024], P('dp', ('ctx', 'tensor')), may hold values from -6 to 6
Outputs:
- result: float32 [16, 1152, 1024], P('dp', ('ctx', 'tensor'))
- grad_stream: float32 [16, 1152, 1024], P('dp', ('ctx', 'tensor'))
- grad_qkv: float32 [2, 1024, 3, 1024], P(None, ('dp', 'ctx'), None, 'tensor')
- grad_qvbias: float32 [2, 2, 16, 64], P(None, None, 'tensor', ('dp', 'ctx'))
- grad_wout: float32 [2, 1024, 1024], P(None, 'tensor', ('dp', 'ctx'))
- grad_gains: float32 [2, 2, 1024], P(None, None, ('dp', 'ctx'))
- grad_shifts: float32 [2, 4, 1024], P(None, None, ('dp', 'ctx'))
- grad_win: float32 [2, 1024, 4096], P(None, ('dp', 'ctx'), 'tensor')
- grad_inbias: float32 [2, 16, 256], P(None, 'tensor', ('dp', 'ctx'))
- grad_wback: float32 [2, 4096, 1024], P(None, 'tensor', ('dp', 'ctx'))
Inputs may be any that keep to these rules, and one draw needn't show every extreme that they name: `segments`: each packed row holds three documents numbered 0, 1 and 2 in order, each of one token or more.
All inputs are finite; a program needn't handle non-finite values.
Results may differ from a plain program's by a relative error of at most 0.035.
Values may be sent and summed in bfloat16 or wider, within the bound.
No kernel may reach another device: no remote copies, remote signals or barrier semaphores. Data moves between devices by JAX's collectives and lax.ppermute only.
A program may use at most 192 MiB of HBM per device.

v0:
```python
import jax
import jax.numpy as jnp
from jax import lax
from jax.sharding import PartitionSpec as P

EPSILON = 1e-12
MASKED = -1000000000.0
ROOT_HALF = 0.7071067811865476
ROOT_TWOPI = 2.5066282746310002


def paired(tensor):
    return tensor.reshape((tensor.shape[0] // 2, 2) + tensor.shape[1:])


def unpaired(tensor):
    return tensor.reshape((tensor.shape[0] * tensor.shape[1],) + tensor.shape[2:])


def normalize(values, gain, shift):
    mean = jnp.mean(values, axis=-1, keepdims=True)
    centred = values - mean
    inverse = lax.rsqrt(jnp.mean(centred * centred, axis=-1, keepdims=True) + EPSILON)
    unit = centred * inverse
    return (unit * gain + shift, unit, inverse)


def normalize_back(incoming, unit, inverse, gain):
    scaled = incoming * gain
    inner = (
        scaled
        - jnp.mean(scaled, axis=-1, keepdims=True)
        - unit * jnp.mean(scaled * unit, axis=-1, keepdims=True)
    )
    return (inverse * inner, jnp.sum(incoming * unit, axis=(0, 1)), jnp.sum(incoming, axis=(0, 1)))


def gelu_slope(value):
    cdf = 0.5 * (1.0 + lax.erf(value * ROOT_HALF))
    return cdf + value * jnp.exp(-0.5 * value * value) / ROOT_TWOPI


def masked_scores(query, keys, marks, scale):
    scores = jnp.einsum("sqhe,skhe->shqk", query, keys, preferred_element_type=jnp.float32) * scale
    return jnp.where(marks[:, None], scores, MASKED)


def attend(items, scale):
    query, keys, values, marks = items
    scores = masked_scores(query, keys, marks, scale)
    top = jnp.max(scores, axis=-1, keepdims=True)
    weights = jnp.exp(scores - top)
    total = jnp.sum(weights, axis=-1, keepdims=True)
    probs = (weights / total).astype(jnp.bfloat16)
    mixed = jnp.einsum("shqk,skhe->sqhe", probs, values, preferred_element_type=jnp.float32)
    return (mixed.astype(jnp.bfloat16), top + jnp.log(total))


def attend_back(items, scale):
    query, keys, values, marks, summary, grad_mixed = items
    probs = jnp.exp(masked_scores(query, keys, marks, scale) - summary)
    low_probs = probs.astype(jnp.bfloat16)
    grad_probs = jnp.einsum(
        "sqhe,skhe->shqk", grad_mixed, values, preferred_element_type=jnp.float32
    )
    inner = jnp.sum(probs * grad_probs, axis=-1, keepdims=True)
    grad_scores = (probs * (grad_probs - inner)).astype(jnp.bfloat16)
    grad_query = (
        jnp.einsum("shqk,skhe->sqhe", grad_scores, keys, preferred_element_type=jnp.float32) * scale
    )
    grad_keys = (
        jnp.einsum("shqk,sqhe->skhe", grad_scores, query, preferred_element_type=jnp.float32)
        * scale
    )
    grad_values = jnp.einsum(
        "shqk,sqhe->skhe", low_probs, grad_mixed, preferred_element_type=jnp.float32
    )
    return (grad_query, grad_keys, grad_values)


def rows_in(values):
    return lax.all_gather(values, "tensor", axis=1, tiled=True)


def row_sums(values):
    return lax.psum_scatter(
        values.astype(jnp.bfloat16), "tensor", scatter_dimension=1, tiled=True
    ).astype(jnp.float32)


def attention_weights(w_qkv, qv_bias, w_out, norm_gains, shifts, layer):
    return (
        lax.all_gather(w_qkv[layer], ("dp", "ctx"), axis=0, tiled=True),
        lax.all_gather(qv_bias[layer], ("dp", "ctx"), axis=2, tiled=True),
        lax.all_gather(w_out[layer], ("dp", "ctx"), axis=1, tiled=True),
        lax.all_gather(norm_gains[layer], ("dp", "ctx"), axis=1, tiled=True),
        lax.all_gather(shifts[layer], ("dp", "ctx"), axis=1, tiled=True),
    )


def feed_weights(w_in, in_bias, w_back, layer):
    return (
        lax.all_gather(w_in[layer], ("dp", "ctx"), axis=0, tiled=True),
        lax.all_gather(in_bias[layer], ("dp", "ctx"), axis=1, tiled=True),
        lax.all_gather(w_back[layer], ("dp", "ctx"), axis=1, tiled=True),
    )


def stack_member(grad_layers, index):
    return jnp.stack([terms[index] for terms in grad_layers])


def local(
    stream, segments, w_qkv, qv_bias, w_out, norm_gains, shifts, w_in, in_bias, w_back, cotangent
):
    layers = w_qkv.shape[0]
    rows = stream.shape[1]
    block = rows * lax.axis_size("tensor")
    seg_query = lax.dynamic_slice_in_dim(segments, lax.axis_index("ctx") * block, block, 1)
    marks = paired(seg_query[:, :, None] == segments[:, None, :])
    state = stream.astype(jnp.float32)
    saved = []
    kept_weights = []
    for layer in range(layers):
        fetched = attention_weights(w_qkv, qv_bias, w_out, norm_gains, shifts, layer)
        fed = feed_weights(w_in, in_bias, w_back, layer)
        kept_weights.append(None)
        w_proj, pair_bias, w_mix, gains, shift = fetched
        heads, head_size = (pair_bias.shape[1], pair_bias.shape[2])
        scale = head_size ** (-0.5)
        gains = gains.astype(jnp.float32)
        shift = shift.astype(jnp.float32)
        bias_rows = pair_bias.astype(jnp.float32).reshape(2, heads * head_size)
        gathered = rows_in(state.astype(jnp.bfloat16))
        packed = jnp.einsum("scd,dke->scke", gathered, w_proj, preferred_element_type=jnp.float32)
        query = (packed[:, :, 0] + bias_rows[0]).astype(jnp.bfloat16)
        keys = packed[:, :, 1].astype(jnp.bfloat16)
        values = (packed[:, :, 2] + bias_rows[1]).astype(jnp.bfloat16)
        all_keys, all_values = (
            lax.all_gather(keys, "ctx", axis=1, tiled=True),
            lax.all_gather(values, "ctx", axis=1, tiled=True),
        )
        query_heads = paired(query.reshape(query.shape[0], query.shape[1], heads, head_size))
        key_heads = paired(all_keys.reshape(all_keys.shape[0], all_keys.shape[1], heads, head_size))
        value_heads = paired(
            all_values.reshape(all_values.shape[0], all_values.shape[1], heads, head_size)
        )
        mixed, summary = lax.map(
            lambda items: attend(items, scale), (query_heads, key_heads, value_heads, marks)
        )
        mixed = unpaired(mixed).reshape(query.shape)
        attended = (
            row_sums(jnp.einsum("sce,ed->scd", mixed, w_mix, preferred_element_type=jnp.float32))
            + shift[2]
        )
        first, unit_one, inv_one = normalize(state + attended, gains[0], shift[0])
        gathered_two = rows_in(first.astype(jnp.bfloat16))
        w_up, up_bias, w_down = fed
        hidden = jnp.einsum(
            "scd,df->scf", gathered_two, w_up, preferred_element_type=jnp.float32
        ) + up_bias.astype(jnp.float32).reshape(-1)
        active = jax.nn.gelu(hidden, approximate=False).astype(jnp.bfloat16)
        down = (
            row_sums(jnp.einsum("scf,fd->scd", active, w_down, preferred_element_type=jnp.float32))
            + shift[3]
        )
        state, unit_two, inv_two = normalize(first + down, gains[1], shift[1])
        saved.append(
            (
                gathered,
                query_heads,
                key_heads,
                value_heads,
                summary,
                mixed,
                unit_one,
                inv_one,
                gathered_two,
                hidden,
                active,
                unit_two,
                inv_two,
            )
        )
    incoming = cotangent.astype(jnp.float32)
    grad_layers = [None] * layers
    for layer in reversed(range(layers)):
        (
            gathered,
            query_heads,
            key_heads,
            value_heads,
            summary,
            mixed,
            unit_one,
            inv_one,
            gathered_two,
            hidden,
            active,
            unit_two,
            inv_two,
        ) = saved[layer]
        fetched = attention_weights(w_qkv, qv_bias, w_out, norm_gains, shifts, layer)
        fed = feed_weights(w_in, in_bias, w_back, layer)
        w_proj, pair_bias, w_mix, gains, shift = fetched
        w_up, up_bias, w_down = fed
        heads, head_size = (pair_bias.shape[1], pair_bias.shape[2])
        scale = head_size ** (-0.5)
        gains = gains.astype(jnp.float32)
        grad_two, gain_two, shift_two = normalize_back(incoming, unit_two, inv_two, gains[1])
        down_bias = jnp.sum(grad_two, axis=(0, 1))
        spread_two = rows_in(grad_two.astype(jnp.bfloat16))
        grad_down = jnp.einsum(
            "scf,scd->fd", active, spread_two, preferred_element_type=jnp.float32
        )
        grad_hidden = jnp.einsum(
            "scd,fd->scf", spread_two, w_down, preferred_element_type=jnp.float32
        ) * gelu_slope(hidden)
        grad_upbias = jnp.sum(grad_hidden, axis=(0, 1)).reshape(up_bias.shape)
        low_hidden = grad_hidden.astype(jnp.bfloat16)
        grad_up = jnp.einsum(
            "scd,scf->df", gathered_two, low_hidden, preferred_element_type=jnp.float32
        )
        grad_first = grad_two + row_sums(
            jnp.einsum("scf,df->scd", low_hidden, w_up, preferred_element_type=jnp.float32)
        )
        grad_one, gain_one, shift_one = normalize_back(grad_first, unit_one, inv_one, gains[0])
        out_bias = jnp.sum(grad_one, axis=(0, 1))
        spread_one = rows_in(grad_one.astype(jnp.bfloat16))
        grad_mix = jnp.einsum("sce,scd->ed", mixed, spread_one, preferred_element_type=jnp.float32)
        grad_mixed = jnp.einsum(
            "scd,ed->sce", spread_one, w_mix, preferred_element_type=jnp.float32
        ).astype(jnp.bfloat16)
        grad_mixed_heads = paired(
            grad_mixed.reshape(grad_mixed.shape[0], grad_mixed.shape[1], heads, head_size)
        )
        grad_q, grad_k, grad_v = lax.map(
            lambda items: attend_back(items, scale),
            (query_heads, key_heads, value_heads, marks, summary, grad_mixed_heads),
        )
        grad_query = unpaired(grad_q).reshape(mixed.shape)
        full_shape = (mixed.shape[0], grad_k.shape[2], mixed.shape[2])
        grad_keys, grad_values = (
            lax.psum_scatter(
                unpaired(grad_k).reshape(full_shape).astype(jnp.bfloat16),
                "ctx",
                scatter_dimension=1,
                tiled=True,
            ).astype(jnp.float32),
            lax.psum_scatter(
                unpaired(grad_v).reshape(full_shape).astype(jnp.bfloat16),
                "ctx",
                scatter_dimension=1,
                tiled=True,
            ).astype(jnp.float32),
        )
        grad_pair = jnp.stack(
            [jnp.sum(grad_query, axis=(0, 1)), jnp.sum(grad_values, axis=(0, 1))]
        ).reshape(pair_bias.shape)
        low_packed = jnp.stack([grad_query, grad_keys, grad_values], axis=2).astype(jnp.bfloat16)
        grad_proj = jnp.einsum(
            "scd,scke->dke", gathered, low_packed, preferred_element_type=jnp.float32
        )
        incoming = grad_one + row_sums(
            jnp.einsum("scke,dke->scd", low_packed, w_proj, preferred_element_type=jnp.float32)
        )
        gain_grad = jnp.stack([gain_one, gain_two])
        shift_grad = jnp.stack([shift_one, shift_two, out_bias, down_bias])
        grad_layers[layer] = (
            grad_proj,
            grad_pair,
            grad_mix,
            gain_grad,
            shift_grad,
            grad_up,
            grad_upbias,
            grad_down,
        )
    stacked_proj = stack_member(grad_layers, 0)
    stacked_pair = stack_member(grad_layers, 1)
    stacked_mix = stack_member(grad_layers, 2)
    stacked_gain = stack_member(grad_layers, 3)
    stacked_shift = stack_member(grad_layers, 4)
    stacked_up = stack_member(grad_layers, 5)
    stacked_upbias = stack_member(grad_layers, 6)
    stacked_down = stack_member(grad_layers, 7)
    (
        stacked_proj,
        stacked_pair,
        stacked_mix,
        stacked_gain,
        stacked_shift,
        stacked_up,
        stacked_upbias,
        stacked_down,
    ) = (
        lax.psum_scatter(
            stacked_proj.astype(jnp.bfloat16), ("dp", "ctx"), scatter_dimension=1, tiled=True
        ).astype(jnp.float32),
        lax.psum_scatter(
            stacked_pair.astype(jnp.bfloat16), ("dp", "ctx"), scatter_dimension=3, tiled=True
        ).astype(jnp.float32),
        lax.psum_scatter(
            stacked_mix.astype(jnp.bfloat16), ("dp", "ctx"), scatter_dimension=2, tiled=True
        ).astype(jnp.float32),
        lax.psum_scatter(
            stacked_gain.astype(jnp.bfloat16), ("dp", "ctx"), scatter_dimension=2, tiled=True
        ).astype(jnp.float32),
        lax.psum_scatter(
            stacked_shift.astype(jnp.bfloat16), ("dp", "ctx"), scatter_dimension=2, tiled=True
        ).astype(jnp.float32),
        lax.psum_scatter(
            stacked_up.astype(jnp.bfloat16), ("dp", "ctx"), scatter_dimension=1, tiled=True
        ).astype(jnp.float32),
        lax.psum_scatter(
            stacked_upbias.astype(jnp.bfloat16), ("dp", "ctx"), scatter_dimension=2, tiled=True
        ).astype(jnp.float32),
        lax.psum_scatter(
            stacked_down.astype(jnp.bfloat16), ("dp", "ctx"), scatter_dimension=2, tiled=True
        ).astype(jnp.float32),
    )
    gain_total, shift_total = lax.psum((stacked_gain, stacked_shift), "tensor")
    return (
        state,
        incoming,
        stacked_proj,
        stacked_pair,
        stacked_mix,
        gain_total,
        shift_total,
        stacked_up,
        stacked_upbias,
        stacked_down,
    )


def solution(mesh):
    return jax.shard_map(
        local,
        mesh=mesh,
        in_specs=(
            P("dp", ("ctx", "tensor"), None),
            P("dp", None),
            P(None, ("dp", "ctx"), None, "tensor"),
            P(None, None, "tensor", ("dp", "ctx")),
            P(None, "tensor", ("dp", "ctx")),
            P(None, None, ("dp", "ctx")),
            P(None, None, ("dp", "ctx")),
            P(None, ("dp", "ctx"), "tensor"),
            P(None, "tensor", ("dp", "ctx")),
            P(None, "tensor", ("dp", "ctx")),
            P("dp", ("ctx", "tensor"), None),
        ),
        out_specs=(
            P("dp", ("ctx", "tensor"), None),
            P("dp", ("ctx", "tensor"), None),
            P(None, ("dp", "ctx"), None, "tensor"),
            P(None, None, "tensor", ("dp", "ctx")),
            P(None, "tensor", ("dp", "ctx")),
            P(None, None, ("dp", "ctx")),
            P(None, None, ("dp", "ctx")),
            P(None, ("dp", "ctx"), "tensor"),
            P(None, "tensor", ("dp", "ctx")),
            P(None, "tensor", ("dp", "ctx")),
        ),
        check_vma=False,
    )
```

profile of v0, /device:TPU:1, one launch (start us, length us, event | category | flops | bytes accessed | tf_op | source)
XLA Modules:
  0.0 1740.3 jit_solution(3008308890084779487)
XLA Ops:
  9.5 26.8 %all-gather.37.cloned.1.call-done = bf16[2,288,1024]{2,1,0:T(8,128)(2,1)} async-done(((bf16[2,72,1024]{2,1,0:T(8,128)(2,1)}), bf16[2,288,1024]{2,1,0:T(8,128)(2,1)}) %all-gather.37.cloned.1.call-update) | async-done | bytes 1179664 | tf_op jit(solution)/shard_map/all_gather | solution.py:82
  36.3 61.1 %all-gather.57.cloned.1.call-done = bf16[1,1024,3,256]{3,1,2,0:T(8,128)(2,1)} async-done(((bf16[1,32,3,256]{3,1,2,0:T(8,128)(2,1)}), bf16[1,1024,3,256]{3,1,2,0:T(8,128)(2,1)}) %all-gather.57.cloned.1.call-update) | async-done | bytes 1572880 | tf_op jit(solution)/shard_map/all_gather | solution.py:93
  101.8 37.9 %all-gather.1 = bf16[1,2,4,64]{2,1,0,3:T(2,128)(2,1)S(1)} all-gather(bf16[1,2,4,2]{2,1,0,3:T(2,128)(2,1)S(1)} %copy.258), channel_id=3, replica_groups=mesh['dp'=8,'ctx'=4,'tensor'=4] {'dp','ctx'}, dimensions={3}, use_global_device_ids=true | all-gather | bytes 1056 | tf_op jit(solution)/shard_map/all_gather | solution.py:94
  141.4 39.6 %all-gather.3 = bf16[1,256,1024]{1,2,0:T(8,128)(2,1)} all-gather(bf16[1,256,32]{1,2,0:T(8,128)(2,1)S(1)} %get-tuple-element.233), channel_id=5, replica_groups=mesh['dp'=8,'ctx'=4,'tensor'=4] {'dp','ctx'}, dimensions={2}, use_global_device_ids=true | all-gather | bytes 540672 | tf_op jit(solution)/shard_map/all_gather | solution.py:95
  206.7 38.6 %all-gather.5 = bf16[1,2,1024]{1,0,2:T(2,128)(2,1)S(1)} all-gather(bf16[1,2,32]{1,0,2:T(2,128)(2,1)S(1)} %copy.260), channel_id=7, replica_groups=mesh['dp'=8,'ctx'=4,'tensor'=4] {'dp','ctx'}, dimensions={2}, use_global_device_ids=true | all-gather | bytes 4224 | tf_op jit(solution)/shard_map/all_gather | solution.py:96
  245.9 37.0 %all-gather.4 = bf16[1,4,1024]{1,0,2:T(2,128)(2,1)S(1)} all-gather(bf16[1,4,32]{1,0,2:T(2,128)(2,1)S(1)} %copy.259), channel_id=6, replica_groups=mesh['dp'=8,'ctx'=4,'tensor'=4] {'dp','ctx'}, dimensions={2}, use_global_device_ids=true | all-gather | bytes 8448 | tf_op jit(solution)/shard_map/all_gather | solution.py:97
  283.4 6.2 slice_reduce_fusion.7
  289.7 22.6 %slice_reduce_fusion.6 = (f32[1024]{0:T(1024)S(1)}, f32[1024]{0:T(1024)}, f32[1024]{0:T(1024)S(1)}, f32[1024]{0:T(1024)S(1)}) fusion(f32[1,4,1024]{1,0,2:T(1,128)S(1)} %convert_element_type.330), kind=kLoop, calls=%fused_computation.212 | loop fusion | bytes 32768 | tf_op jit(solution)/shard_map/slice | solution.py:167
  316.4 37.4 %all-gather.7 = bf16[1,4,256]{1,0,2:T(2,128)(2,1)S(1)} all-gather(bf16[1,4,8]{1,0,2:T(2,128)(2,1)S(1)} %copy.261), channel_id=9, replica_groups=mesh['dp'=8,'ctx'=4,'tensor'=4] {'dp','ctx'}, dimensions={2}, use_global_device_ids=true | all-gather | bytes 2112 | tf_op jit(solution)/shard_map/all_gather | solution.py:104
  359.5 6.7 fusion.22
  366.2 31.0 %all-gather.63.cloned.1.call-done = bf16[1,1024,1024]{1,2,0:T(8,128)(2,1)} async-done(((bf16[1,1024,32]{1,2,0:T(8,128)(2,1)}), bf16[1,1024,1024]{1,2,0:T(8,128)(2,1)}) %all-gather.63.cloned.1.call-update) | async-done | bytes 2097168 | tf_op jit(solution)/shard_map/all_gather | solution.py:105
  403.4 21.2 %reduce-scatter.49.cloned.1.call-done = bf16[72,2048]{1,0:T(8,128)(2,1)} async-done(((bf16[288,2048]{1,0:T(8,128)(2,1)}), bf16[72,2048]{1,0:T(8,128)(2,1)}) %reduce-scatter.49.cloned.1.call-update) | async-done | bytes 294928
  427.5 56.9 %all-gather.65.cloned.1.call-done = bf16[1,1024,3,256]{3,1,2,0:T(8,128)(2,1)} async-done(((bf16[1,32,3,256]{3,1,2,0:T(8,128)(2,1)}), bf16[1,1024,3,256]{3,1,2,0:T(8,128)(2,1)}) %all-gather.65.cloned.1.call-update) | async-done | bytes 1572880 | tf_op jit(solution)/shard_map/all_gather | solution.py:93
  484.3 24.5 %all-gather.43.cloned.1.call-done = bf16[2,288,1024]{2,1,0:T(8,128)(2,1)} async-done(((bf16[2,72,1024]{2,1,0:T(8,128)(2,1)}), bf16[2,288,1024]{2,1,0:T(8,128)(2,1)}) %all-gather.43.cloned.1.call-update) | async-done | bytes 1179664 | tf_op jit(solution)/shard_map/all_gather | solution.py:82
  513.8 41.9 %all-gather.10 = bf16[1,2,4,64]{2,1,0,3:T(2,128)(2,1)S(1)} all-gather(bf16[1,2,4,2]{2,1,0,3:T(2,128)(2,1)S(1)} %copy.262), channel_id=12, replica_groups=mesh['dp'=8,'ctx'=4,'tensor'=4] {'dp','ctx'}, dimensions={3}, use_global_device_ids=true | all-gather | bytes 1056 | tf_op jit(solution)/shard_map/all_gather | solution.py:94
  558.5 39.6 %all-gather.12 = bf16[1,256,1024]{1,2,0:T(8,128)(2,1)} all-gather(bf16[1,256,32]{1,2,0:T(8,128)(2,1)S(1)} %copy-done.53), channel_id=14, replica_groups=mesh['dp'=8,'ctx'=4,'tensor'=4] {'dp','ctx'}, dimensions={2}, use_global_device_ids=true | all-gather | bytes 540672 | tf_op jit(solution)/shard_map/all_gather | solution.py:95
  613.6 5.7 fusion.96
  623.5 38.4 %all-gather.13 = bf16[1,4,1024]{1,0,2:T(2,128)(2,1)S(1)} all-gather(bf16[1,4,32]{1,0,2:T(2,128)(2,1)S(1)} %copy.263), channel_id=15, replica_groups=mesh['dp'=8,'ctx'=4,'tensor'=4] {'dp','ctx'}, dimensions={2}, use_global_device_ids=true | all-gather | bytes 8448 | tf_op jit(solution)/shard_map/all_gather | solution.py:97
  662.4 37.2 %all-gather.14 = bf16[1,2,1024]{1,0,2:T(2,128)(2,1)S(1)} all-gather(bf16[1,2,32]{1,0,2:T(2,128)(2,1)S(1)} %copy.264), channel_id=16, replica_groups=mesh['dp'=8,'ctx'=4,'tensor'=4] {'dp','ctx'}, dimensions={2}, use_global_device_ids=true | all-gather | bytes 4224 | tf_op jit(solution)/shard_map/all_gather | solution.py:96
  700.2 6.2 slice_reduce_fusion.1
  706.4 22.6 %slice_reduce_fusion = (f32[1024]{0:T(1024)}, f32[1024]{0:T(1024)}, f32[1024]{0:T(1024)S(1)}, f32[1024]{0:T(1024)S(1)}) fusion(f32[1,4,1024]{1,0,2:T(1,128)S(1)} %convert_element_type.333), kind=kLoop, calls=%fused_computation.206 | loop fusion | bytes 32768 | tf_op jit(solution)/shard_map/slice | solution.py:167
  732.4 37.2 %all-gather.16 = bf16[1,4,256]{1,0,2:T(2,128)(2,1)S(1)} all-gather(bf16[1,4,8]{1,0,2:T(2,128)(2,1)S(1)} %copy.265), channel_id=18, replica_groups=mesh['dp'=8,'ctx'=4,'tensor'=4] {'dp','ctx'}, dimensions={2}, use_global_device_ids=true | all-gather | bytes 2112 | tf_op jit(solution)/shard_map/all_gather | solution.py:104
  775.8 6.7 fusion.25
  782.5 30.4 %all-gather.71.cloned.1.call-done = bf16[1,1024,1024]{1,2,0:T(8,128)(2,1)} async-done(((bf16[1,1024,32]{1,2,0:T(8,128)(2,1)}), bf16[1,1024,1024]{1,2,0:T(8,128)(2,1)}) %all-gather.71.cloned.1.call-update) | async-done | bytes 2097168 | tf_op jit(solution)/shard_map/all_gather | solution.py:105
  818.9 21.8 %reduce-scatter.53.cloned.1.call-done = bf16[72,2048]{1,0:T(8,128)(2,1)} async-done(((bf16[288,2048]{1,0:T(8,128)(2,1)}), bf16[72,2048]{1,0:T(8,128)(2,1)}) %reduce-scatter.53.cloned.1.call-update) | async-done | bytes 294928
  847.9 24.5 %all-gather.49.cloned.1.call-done = bf16[2,288,1024]{2,1,0:T(8,128)(2,1)} async-done(((bf16[2,72,1024]{2,1,0:T(8,128)(2,1)}), bf16[2,288,1024]{2,1,0:T(8,128)(2,1)}) %all-gather.49.cloned.1.call-update) | async-done | bytes 1179664 | tf_op jit(solution)/shard_map/all_gather | solution.py:82
  882.1 24.5 %reduce-scatter.55.cloned.1.call-done = bf16[72,2048]{1,0:T(8,128)(2,1)} async-done(((bf16[288,2048]{1,0:T(8,128)(2,1)}), bf16[72,2048]{1,0:T(8,128)(2,1)}) %reduce-scatter.55.cloned.1.call-update) | async-done | bytes 294928
  913.8 24.2 %all-gather.51.cloned.1.call-done = bf16[2,288,1024]{2,1,0:T(8,128)(2,1)} async-done(((bf16[2,72,1024]{2,1,0:T(8,128)(2,1)}), bf16[2,288,1024]{2,1,0:T(8,128)(2,1)}) %all-gather.51.cloned.1.call-update) | async-done | bytes 1179664 | tf_op jit(solution)/shard_map/all_gather | solution.py:82
  942.4 6.7 fusion.12
  951.7 7.0 multiply_reduce_fusion.1
  958.7 5.9 multiply_convert_fusion.1
  977.4 21.4 %reduce-scatter.37.cloned.1.call-done = bf16[2,288,256]{2,1,0:T(8,128)(2,1)} async-done(((bf16[2,1152,256]{2,1,0:T(8,128)(2,1)}), bf16[2,288,256]{2,1,0:T(8,128)(2,1)}) %reduce-scatter.37.cloned.1.call-update) | async-done | bytes 294928 | tf_op jit(solution)/shard_map/reduce_scatter | solution.py:244
  1004.3 23.4 %reduce-scatter.57.cloned.1.call-done = bf16[72,2048]{1,0:T(8,128)(2,1)} async-done(((bf16[288,2048]{1,0:T(8,128)(2,1)}), bf16[72,2048]{1,0:T(8,128)(2,1)}) %reduce-scatter.57.cloned.1.call-update) | async-done | bytes 294928
  1032.1 24.2 %all-gather.53.cloned.1.call-done = bf16[2,288,1024]{2,1,0:T(8,128)(2,1)} async-done(((bf16[2,72,1024]{2,1,0:T(8,128)(2,1)}), bf16[2,288,1024]{2,1,0:T(8,128)(2,1)}) %all-gather.53.cloned.1.call-update) | async-done | bytes 1179664 | tf_op jit(solution)/shard_map/all_gather | solution.py:82
  1065.9 24.5 %reduce-scatter.59.cloned.1.call-done = bf16[72,2048]{1,0:T(8,128)(2,1)} async-done(((bf16[288,2048]{1,0:T(8,128)(2,1)}), bf16[72,2048]{1,0:T(8,128)(2,1)}) %reduce-scatter.59.cloned.1.call-update) | async-done | bytes 294928
  1095.2 24.4 %all-gather.55.cloned.1.call-done = bf16[2,288,1024]{2,1,0:T(8,128)(2,1)} async-done(((bf16[2,72,1024]{2,1,0:T(8,128)(2,1)}), bf16[2,288,1024]{2,1,0:T(8,128)(2,1)}) %all-gather.55.cloned.1.call-update) | async-done | bytes 1179664 | tf_op jit(solution)/shard_map/all_gather | solution.py:82
  1122.4 5.7 fusion.15
  1130.0 7.0 multiply_reduce_fusion
  1137.0 5.8 multiply_convert_fusion
  1168.3 8.4 reduce-scatter.41.cloned.1.call-done
  1193.1 11.4 copy.221
  1211.7 5.8 copy.216
  1220.9 85.8 %reduce-scatter.63.cloned.1.call-done = bf16[32,4]{1,0:T(8,128)(2,1)} async-done(((bf16[1024,4]{1,0:T(8,128)(2,1)}), bf16[32,4]{1,0:T(8,128)(2,1)}) %reduce-scatter.63.cloned.1.call-update) | async-done | bytes 272
  1307.6 130.5 %reduce-scatter.65.cloned.1.call-done = bf16[32,8]{1,0:T(8,128)(2,1)} async-done(((bf16[1024,8]{1,0:T(8,128)(2,1)}), bf16[32,8]{1,0:T(8,128)(2,1)}) %reduce-scatter.65.cloned.1.call-update) | async-done | bytes 528
  1439.0 9.5 all-reduce.5
  1448.8 125.9 %all-reduce.6 = (bf16[2,2,4,64]{2,1,0,3:T(2,128)(2,1)S(1)}, bf16[2,4,256]{2,1,0:T(4,128)(2,1)S(1)}) all-reduce(bf16[2,2,4,64]{2,1,0,3:T(2,128)(2,1)S(1)} %copy.217, bf16[2,4,256]{2,1,0:T(4,128)(2,1)S(1)} %pad_maximum_fusion.12), channel_id=33, replica_groups=mesh['dp'=8,'ctx'=4,'tensor'=4] {'dp','ctx'}, use_global_device_ids=true, to_apply=%region_39.40.clone | all-reduce | flops 3072 | bytes 12288
  1577.6 24.8 %reduce-scatter.61.cloned.1.call-done = bf16[72,2048]{1,0:T(8,128)(2,1)} async-done(((bf16[288,2048]{1,0:T(8,128)(2,1)}), bf16[72,2048]{1,0:T(8,128)(2,1)}) %reduce-scatter.61.cloned.1.call-update) | async-done | bytes 294928
  1604.5 123.9 %all-reduce.10.cloned.1.call-done = (bf16[2,1024,3,256]{3,0,2,1:T(2,128)(2,1)}, bf16[2,256,1024]{1,0,2:T(2,128)(2,1)}, bf16[2,1024,1024]{1,0,2:T(2,128)(2,1)}) async-done(((bf16[2,1024,3,256]{3,0,2,1:T(2,128)(2,1)}, bf16[2,256,1024]{1,0,2:T(2,128)(2,1)}, bf16[2,1024,1024]{1,0,2:T(2,128)(2,1)}), (bf16[2,1024,3,256]{3,0,2,1:T(2,128)(2,1)}, bf16[2,256,1024]{1,0,2:T(2,128)(2,1)}, ...) | async-done | bytes 8388624
  (529 shorter events, 231.1 us)
Async XLA Ops:
  7.2 29.1 %all-gather.37.cloned.1.call-start = ((), (), s32[]{:S(2)}) async-start(), calls=%async_computation.15 | async-start | bytes 1474560 | tf_op jit(solution)/shard_map/all_gather | solution.py:82
  7.9 89.5 %all-gather.57.cloned.1.call-start = ((), (), s32[]{:S(2)}) async-start(), calls=%async_computation.30 | async-start | bytes 1622016 | tf_op jit(solution)/shard_map/all_gather | solution.py:93
  9.4 91.8 %copy-start.102 = (bf16[2,2,4,2]{2,3,1,0:T(2,128)(2,1)S(1)}, bf16[2,2,4,2]{2,3,1,0:T(2,128)(2,1)}, u32[]{:S(2)}) copy-start(bf16[2,2,4,2]{2,3,1,0:T(2,128)(2,1)} %param.14) | copy-start | bytes 196
  9.5 130.5 %copy-start.72 = (bf16[2,256,32]{1,2,0:T(8,128)(2,1)S(1)}, bf16[2,256,32]{1,2,0:T(8,128)(2,1)}, u32[]{:S(2)}) copy-start(bf16[2,256,32]{1,2,0:T(8,128)(2,1)} %param.15) | copy-start | bytes 98308
  9.5 173.8 %all-gather.59.cloned.1.call-start = ((), (), s32[]{:S(2)}) async-start(), calls=%async_computation.31 | async-start | bytes 1474560 | tf_op jit(solution)/shard_map/all_gather | solution.py:140
  100.3 80.8 %copy-start.30 = (f32[2,288,3,256]{3,1,2,0:T(8,128)}, f32[2,288,3,256]{3,1,2,0:T(8,128)S(1)}, u32[]{:S(2)}) copy-start(f32[2,288,3,256]{3,1,2,0:T(8,128)S(1)} %fusion.72) | copy-start | bytes 5308420
  101.2 92.7 %all-gather.39.cloned.1.call-start = ((), (), s32[]{:S(2)}) async-start(), calls=%async_computation.16 | async-start | bytes 1474560 | tf_op jit(solution)/shard_map/all_gather | solution.py:141
  141.3 170.9 %reduce-scatter.47.cloned.1.call-start = ((), (), s32[]{:S(2)}) async-start(), calls=%async_computation.38 | async-start | bytes 1474560
  204.6 149.3 %all-gather.61.cloned.1.call-start = ((), (), s32[]{:S(2)}) async-start(), calls=%async_computation.32 | async-start | bytes 2162688 | tf_op jit(solution)/shard_map/all_gather | solution.py:103
  205.3 148.6 %all-gather.41.cloned.1.call-start = ((), (), s32[]{:S(2)}) async-start(), calls=%async_computation.17 | async-start | bytes 1474560 | tf_op jit(solution)/shard_map/all_gather | solution.py:82
  289.6 136.2 %copy-start.48 = (f32[1024]{0:T(1024)}, f32[1024]{0:T(1024)S(1)}, u32[]{:S(2)}) copy-start(f32[1024]{0:T(1024)S(1)} %get-tuple-element.189) | copy-start | bytes 12292
  289.6 136.8 %copy-start.50 = (f32[1024]{0:T(1024)}, f32[1024]{0:T(1024)S(1)}, u32[]{:S(2)}) copy-start(f32[1024]{0:T(1024)S(1)} %get-tuple-element.188) | copy-start | bytes 12292
  312.3 114.2 %copy-start.60 = (f32[1024]{0:T(1024)}, f32[1024]{0:T(1024)S(1)}, u32[]{:S(2)}) copy-start(f32[1024]{0:T(1024)S(1)} %get-tuple-element.190) | copy-start | bytes 12292
  314.9 82.3 %all-gather.63.cloned.1.call-start = ((), (), s32[]{:S(2)}) async-start(), calls=%async_computation.33 | async-start | bytes 2162688 | tf_op jit(solution)/shard_map/all_gather | solution.py:105
  315.6 109.0 %reduce-scatter.49.cloned.1.call-start = ((), (), s32[]{:S(2)}) async-start(), calls=%async_computation.39 | async-start | bytes 1474560
  402.8 81.5 %all-gather.65.cloned.1.call-start = ((), (), s32[]{:S(2)}) async-start(), calls=%async_computation.34 | async-start | bytes 1622016 | tf_op jit(solution)/shard_map/all_gather | solution.py:93
  403.4 105.4 %all-gather.43.cloned.1.call-start = ((), (), s32[]{:S(2)}) async-start(), calls=%async_computation.18 | async-start | bytes 1474560 | tf_op jit(solution)/shard_map/all_gather | solution.py:82
  426.2 85.5 %copy-start.69 = (f32[2,72]{1,0:T(2,128)}, f32[2,72]{1,0:T(2,128)S(1)}, u32[]{:S(2)}) copy-start(f32[2,72]{1,0:T(2,128)S(1)} %broadcast_multiply_fusion.10) | copy-start | bytes 1732
  426.5 85.2 %copy-start.78 = (f32[2,72]{1,0:T(2,128)}, f32[2,72]{1,0:T(2,128)S(1)}, u32[]{:S(2)}) copy-start(f32[2,72]{1,0:T(2,128)S(1)} %add_rsqrt_fusion.2) | copy-start | bytes 1732
  427.4 86.4 %copy-start.101 = (bf16[1,2,4,2]{2,3,1,0:T(2,128)(2,1)S(1)}, bf16[1,2,4,2]{2,3,1,0:T(2,128)(2,1)}, u32[]{:S(2)}) copy-start(bf16[1,2,4,2]{2,3,1,0:T(2,128)(2,1)} %get-tuple-element.240) | copy-start | bytes 100
  427.4 131.1 %copy-start.53 = (bf16[1,256,32]{1,2,0:T(8,128)(2,1)S(1)}, bf16[1,256,32]{1,2,0:T(8,128)(2,1)}, u32[]{:S(2)}) copy-start(bf16[1,256,32]{1,2,0:T(8,128)(2,1)} %get-tuple-element.232) | copy-start | bytes 49156
  427.4 171.9 %all-gather.67.cloned.1.call-start = ((), (), s32[]{:S(2)}) async-start(), calls=%async_computation.35 | async-start | bytes 1474560 | tf_op jit(solution)/shard_map/all_gather | solution.py:140
  513.7 84.4 %slice-start = ((f32[2,288,3,256]{3,1,2,0:T(8,128)}), f32[2,288,1,256]{3,1,2,0:T(8,128)S(1)}, s32[]{:S(2)}) async-start(f32[2,288,3,256]{3,1,2,0:T(8,128)} %copy-done.24), calls=%async_computation.49 | async-start | bytes 1179648 | tf_op jit(solution)/shard_map/slice | solution.py:136
  513.8 98.1 %all-gather.45.cloned.1.call-start = ((), (), s32[]{:S(2)}) async-start(), calls=%async_computation.19 | async-start | bytes 1474560 | tf_op jit(solution)/shard_map/all_gather | solution.py:141
  557.8 171.1 %reduce-scatter.51.cloned.1.call-start = ((), (), s32[]{:S(2)}) async-start(), calls=%async_computation.40 | async-start | bytes 1474560
  622.6 147.7 %all-gather.69.cloned.1.call-start = ((), (), s32[]{:S(2)}) async-start(), calls=%async_computation.36 | async-start | bytes 2162688 | tf_op jit(solution)/shard_map/all_gather | solution.py:103
  623.2 147.1 %all-gather.47.cloned.1.call-start = ((), (), s32[]{:S(2)}) async-start(), calls=%async_computation.20 | async-start | bytes 1474560 | tf_op jit(solution)/shard_map/all_gather | solution.py:82
  731.6 81.2 %all-gather.71.cloned.1.call-start = ((), (), s32[]{:S(2)}) async-start(), calls=%async_computation.37 | async-start | bytes 2162688 | tf_op jit(solution)/shard_map/all_gather | solution.py:105
  732.2 108.5 %reduce-scatter.53.cloned.1.call-start = ((), (), s32[]{:S(2)}) async-start(), calls=%async_computation.41 | async-start | bytes 1474560
  818.8 53.6 %all-gather.49.cloned.1.call-start = ((), (), s32[]{:S(2)}) async-start(), calls=%async_computation.21 | async-start | bytes 1474560 | tf_op jit(solution)/shard_map/all_gather | solution.py:82
  847.9 58.7 %reduce-scatter.55.cloned.1.call-start = ((), (), s32[]{:S(2)}) async-start(), calls=%async_computation.42 | async-start | bytes 1474560
  882.0 56.0 %all-gather.51.cloned.1.call-start = ((), (), s32[]{:S(2)}) async-start(), calls=%async_computation.22 | async-start | bytes 1474560 | tf_op jit(solution)/shard_map/all_gather | solution.py:82
  913.5 63.9 %reduce-scatter.39.cloned.1.call-start = ((), (), s32[]{:S(2)}) async-start(), calls=%async_computation.24 | async-start | bytes 1474560 | tf_op jit(solution)/shard_map/reduce_scatter | solution.py:250
  951.6 47.2 %reduce-scatter.37.cloned.1.call-start = ((), (), s32[]{:S(2)}) async-start(), calls=%async_computation.23 | async-start | bytes 1474560 | tf_op jit(solution)/shard_map/reduce_scatter | solution.py:244
  969.9 57.9 %reduce-scatter.57.cloned.1.call-start = ((), (), s32[]{:S(2)}) async-start(), calls=%async_computation.43 | async-start | bytes 1474560
  1004.3 52.1 %all-gather.53.cloned.1.call-start = ((), (), s32[]{:S(2)}) async-start(), calls=%async_computation.25 | async-start | bytes 1474560 | tf_op jit(solution)/shard_map/all_gather | solution.py:82
  1031.9 58.5 %reduce-scatter.59.cloned.1.call-start = ((), (), s32[]{:S(2)}) async-start(), calls=%async_computation.44 | async-start | bytes 1474560
  1065.9 53.8 %all-gather.55.cloned.1.call-start = ((), (), s32[]{:S(2)}) async-start(), calls=%async_computation.26 | async-start | bytes 1474560 | tf_op jit(solution)/shard_map/all_gather | solution.py:82
  1095.1 73.1 %reduce-scatter.43.cloned.1.call-start = ((), (), s32[]{:S(2)}) async-start(), calls=%async_computation.28 | async-start | bytes 1474560 | tf_op jit(solution)/shard_map/reduce_scatter | solution.py:250
  1129.5 47.2 %reduce-scatter.41.cloned.1.call-start = ((), (), s32[]{:S(2)}) async-start(), calls=%async_computation.27 | async-start | bytes 1474560 | tf_op jit(solution)/shard_map/reduce_scatter | solution.py:244
  1146.6 160.1 %reduce-scatter.63.cloned.1.call-start = ((), (), s32[]{:S(2)}) async-start(), calls=%async_computation.46 | async-start | bytes 270336
  1156.9 281.3 %reduce-scatter.65.cloned.1.call-start = ((), (), s32[]{:S(2)}) async-start(), calls=%async_computation.47 | async-start | bytes 270336
  1158.4 417.5 %reduce-scatter.45.cloned.1.call-start = ((), (), s32[]{:S(2)}) async-start(), calls=%async_computation.29 | async-start | bytes 4325376 | tf_op jit(solution)/shard_map/reduce_scatter | solution.py:312
  1163.1 439.2 %reduce-scatter.61.cloned.1.call-start = ((), (), s32[]{:S(2)}) async-start(), calls=%async_computation.45 | async-start | bytes 1474560
  1181.4 546.9 %all-reduce.10.cloned.1.call-start = ((), (), s32[]{:S(2)}) async-start(), calls=%async_computation.48 | async-start | bytes 16777216
  1217.5 230.9 %copy-start.40 = (bf16[2,288,256]{2,1,0:T(8,128)(2,1)S(1)}, bf16[2,288,256]{2,1,0:T(8,128)(2,1)}, u32[]{:S(2)}) copy-start(bf16[2,288,256]{2,1,0:T(8,128)(2,1)} %reduce-scatter.43.cloned.1.call-done) | copy-start | bytes 884740
  1217.5 231.1 %copy-start.98 = (bf16[4,64]{1,0:T(4,128)(2,1)S(1)}, bf16[4,64]{1,0:T(4,128)(2,1)}, u32[]{:S(2)}) copy-start(bf16[4,64]{1,0:T(4,128)(2,1)} %get-tuple-element.223) | copy-start | bytes 1540
  1217.6 386.0 %copy-start.12 = (f32[2,72,1024]{2,1,0:T(8,128)S(1)}, f32[2,72,1024]{2,1,0:T(8,128)}, u32[]{:S(2)}) copy-start(f32[2,72,1024]{2,1,0:T(8,128)} %copy-done.11) | copy-start | bytes 1769476
  (109 other events, 1109.7 us)
Sparse Core Ops, SparseCore 0:
  9.7 26.5 all-gather.36
  38.6 58.7 all-gather.56
  101.3 20.8 all-gather.58
  141.5 18.7 all-gather.38
  204.7 19.8 reduce-scatter.46
  226.7 59.0 all-gather.60
  315.0 20.4 all-gather.40
  337.8 59.3 all-gather.62
  402.9 21.6 reduce-scatter.48
  426.2 58.1 all-gather.64
  486.6 22.2 all-gather.42
  513.9 23.8 all-gather.66
  557.9 17.8 all-gather.44
  622.7 19.1 reduce-scatter.50
  644.0 59.1 all-gather.68
  731.8 19.5 all-gather.46
  753.5 59.3 all-gather.70
  819.0 21.6 reduce-scatter.52
  848.0 24.3 all-gather.48
  882.1 24.3 reduce-scatter.54
  913.7 24.3 all-gather.50
  951.7 22.8 reduce-scatter.38
  977.0 21.7 reduce-scatter.36
  1004.4 23.2 reduce-scatter.56
  1032.0 24.3 all-gather.52
  1066.0 24.3 reduce-scatter.58
  1095.2 24.3 all-gather.54
  1129.6 22.7 reduce-scatter.42
  1154.8 21.8 reduce-scatter.40
  1179.4 127.2 reduce-scatter.62
  1309.8 128.3 reduce-scatter.64
  1440.5 135.3 reduce-scatter.44
  1578.2 24.1 reduce-scatter.60
  1606.1 122.2 all-reduce.9
where the time goes:
time: 1750 us; the launch traced here: 1740 us
  waiting for transfers between devices  841 us (48%)
  blocking collectives  520 us (30%)
  local copies, waits for them, and re-layouts  166 us (9%)
  matrix products  124 us (7%)
  other arithmetic  68.2 us (4%)
  between operations  18.8 us (1%)
    unnamed x45, waiting for transfers between devices  483 us
    all_gather x8, waiting for transfers between devices, rows_in(): return lax.all_gather(values, 'tensor', axis=1, tiled=True)  149 us
    unnamed x1, blocking collectives  126 us
    all_gather x2, waiting for transfers between devices, attention_weights(): lax.all_gather(w_qkv[layer], ('dp', 'ctx'), axis=0, tiled=True)  118 us
    all_gather x2, blocking collectives, attention_weights(): lax.all_gather(qv_bias[layer], ('dp', 'ctx'), axis=2, tiled=True)  79.9 us
    all_gather x2, blocking collectives, attention_weights(): lax.all_gather(w_out[layer], ('dp', 'ctx'), axis=1, tiled=True)  79.2 us
    all_gather x2, blocking collectives, attention_weights(): lax.all_gather(norm_gains[layer], ('dp', 'ctx'), axis=1, tiled=True)  75.8 us
    all_gather x2, blocking collectives, attention_weights(): lax.all_gather(shifts[layer], ('dp', 'ctx'), axis=1, tiled=True)  75.4 us
  transfers between devices with their start and end apart: 34, of which 21 were waited for; matrix products, arithmetic and copies ran while one was open for 13% of the time, Pallas kernels for 0%

commit v1 on v0

v1 whole, which is shorter than its diff:
```python
import jax
import jax.numpy as jnp
from jax import lax
from jax.sharding import PartitionSpec as P

EPSILON = 1e-12
MASKED = -1000000000.0
ROOT_HALF = 0.7071067811865476
ROOT_TWOPI = 2.5066282746310002
ALL = ("dp", "ctx", "tensor")
LOW = jnp.bfloat16
FULL = jnp.float32

DIMS = (("x", 1), ("y", 1), ("z", 1), ("x", 3), ("y", 3), ("z", 3))
CANON = (("z", 3), ("z", 1), ("y", 3), ("y", 1), ("x", 3), ("x", 1))
GROUPS = [[(zl * 2 + c) * 4 + x for zl in range(2) for x in range(4)] for c in range(2)]


def exchange_perm(axis, mask):
    pairs = []
    for device in range(128):
        dp, ctx, x = device // 16, (device // 4) % 4, device % 4
        at = {"x": x, "y": dp % 4, "z": (dp // 4) * 2 + ctx // 2, "core": ctx % 2}
        at[axis] ^= mask
        other = ((at["z"] // 2) * 4 + at["y"]) * 16
        other += ((at["z"] % 2) * 2 + at["core"]) * 4 + at["x"]
        pairs.append((device, other))
    return pairs


def swap(value, axis="core", mask=1):
    return lax.ppermute(value, ALL, exchange_perm(axis, mask))


def dim_at(part, phase):
    return DIMS[(part + phase) % 6]


def gather_phases(parts, first, last):
    for phase in range(first, last):
        got = [swap(value, *dim_at(q, phase)) for q, value in enumerate(parts)]
        parts = [jnp.concatenate([value, new], 0) for value, new in zip(parts, got)]
    return parts


def canonical(part, value):
    rows, cols = value.shape[1:]
    value = value.reshape((2,) * 6 + (rows, cols))
    place = [5 - [dim_at(part, phase) for phase in range(6)].index(dim) for dim in CANON]
    value = value.transpose(place[:4] + [6] + place[4:] + [7])
    return value.reshape(16 * rows, 4 * cols)


def by_phase(part, value):
    rows, cols = value.shape[0] // 16, value.shape[1] // 4
    value = value.reshape((2,) * 4 + (rows, 2, 2, cols))
    axis_of = dict(zip(CANON, (0, 1, 2, 3, 5, 6)))
    order = [axis_of[dim_at(part, phase)] for phase in range(6)]
    return value.transpose(order + [4, 7]).reshape(64, rows, cols)


def reduce_phases(parts, first, last):
    for phase in range(first, last):
        half = parts[0].shape[0] // 2
        got = [swap(value[half:], *dim_at(q, phase)) for q, value in enumerate(parts)]
        parts = [
            (value[:half].astype(FULL) + new.astype(FULL)).astype(LOW)
            for value, new in zip(parts, got)
        ]
    return parts


def relative_x(me_x, r):
    return me_x ^ (0, 1, 3, 2)[r]


def take_relative(value, me_x, axis):
    return jnp.concatenate(
        [lax.dynamic_slice_in_dim(value, relative_x(me_x, r), 1, axis) for r in range(4)], axis
    )


def take_absolute(value, me_x, axis):
    parts = []
    for x in range(4):
        off = me_x ^ x
        parts.append(lax.dynamic_slice_in_dim(value, off ^ (off >> 1), 1, axis))
    return jnp.concatenate(parts, axis)


def both(value):
    return jnp.concatenate([value, swap(value)], 0)


def own_sum(value):
    half = value.shape[0] // 2
    value = value.astype(FULL)
    return value[:half] + swap(value[half:].astype(LOW)).astype(FULL)


def normalize(values, gain, shift):
    mean = jnp.mean(values, axis=-1, keepdims=True)
    centred = values - mean
    inverse = lax.rsqrt(jnp.mean(centred * centred, axis=-1, keepdims=True) + EPSILON)
    unit = centred * inverse
    return (unit * gain + shift, unit, inverse)


def normalize_back(incoming, unit, inverse, gain):
    scaled = incoming * gain
    inner = (
        scaled
        - jnp.mean(scaled, axis=-1, keepdims=True)
        - unit * jnp.mean(scaled * unit, axis=-1, keepdims=True)
    )
    return (inverse * inner, jnp.sum(incoming * unit, axis=0), jnp.sum(incoming, axis=0))


def gelu_slope(value):
    cdf = 0.5 * (1.0 + lax.erf(value * ROOT_HALF))
    return cdf + value * jnp.exp(-0.5 * value * value) / ROOT_TWOPI


def dot(left, right, dims):
    return lax.dot_general(left, right, (dims, ((), ())), preferred_element_type=FULL)


def times(left, right):
    return dot(left, right, ((1,), (0,)))


def times_t(left, right):
    return dot(left, right, ((1,), (1,)))


def t_times(left, right):
    return dot(left, right, ((0,), (0,)))


def masked_scores(query, keys, marks, scale):
    scores = jnp.einsum("qse,kse->sqk", query, keys, preferred_element_type=FULL) * scale
    return jnp.where(marks, scores, MASKED)


def attend(qkv, marks, scale):
    scores = masked_scores(qkv[:, 0], qkv[:, 1], marks, scale)
    top = jnp.max(scores, axis=-1, keepdims=True)
    weights = jnp.exp(scores - top)
    total = jnp.sum(weights, axis=-1, keepdims=True)
    probs = (weights / total).astype(LOW)
    mixed = jnp.einsum("sqk,kse->qse", probs, qkv[:, 2], preferred_element_type=FULL)
    return mixed.astype(LOW), top + jnp.log(total)


def attend_back(qkv, marks, summary, grad_mixed, scale):
    probs = jnp.exp(masked_scores(qkv[:, 0], qkv[:, 1], marks, scale) - summary)
    low_probs = probs.astype(LOW)
    grad_probs = jnp.einsum("qse,kse->sqk", grad_mixed, qkv[:, 2], preferred_element_type=FULL)
    inner = jnp.sum(probs * grad_probs, axis=-1, keepdims=True)
    grad_scores = (probs * (grad_probs - inner)).astype(LOW)
    grad_q = jnp.einsum("sqk,kse->qse", grad_scores, qkv[:, 1], preferred_element_type=FULL)
    grad_k = jnp.einsum("sqk,qse->kse", grad_scores, qkv[:, 0], preferred_element_type=FULL)
    grad_v = jnp.einsum("sqk,qse->kse", low_probs, grad_mixed, preferred_element_type=FULL)
    return grad_q * scale, grad_k * scale, grad_v


def trade(value):
    return lax.all_to_all(
        value, ("ctx", "tensor"), 0, 0, axis_index_groups=GROUPS, tiled=True
    )


def to_heads(value, me_x):
    rows = value.shape[0] // 4
    kinds = value.shape[3]
    value = take_absolute(value, me_x, 1).reshape(2, 2, rows, 4, 2, kinds, 64)
    value = value.transpose(4, 3, 0, 2, 5, 1, 6).reshape(8, 2 * rows, kinds * 128)
    return trade(value).reshape(16 * rows, kinds, 2, 64)


def to_tokens(value, me_x):
    rows = value.shape[0] // 16
    kinds = value.shape[1]
    value = trade(value.reshape(8, 2 * rows, kinds * 128))
    value = value.reshape(2, 4, 2, rows, kinds, 2, 64).transpose(2, 5, 3, 1, 0, 4, 6)
    return take_relative(value.reshape(4 * rows, 4, 2, kinds, 64), me_x, 1)


def local(
    stream, segments, w_qkv, qv_bias, w_out, norm_gains, shifts, w_in, in_bias, w_back, cotangent
):
    layers = w_qkv.shape[0]
    dp, ctx, me_x = lax.axis_index("dp"), lax.axis_index("ctx"), lax.axis_index("tensor")
    core, z_lo = ctx & 1, ctx >> 1
    me_y, me_z = dp & 3, (dp >> 2) * 2 + z_lo
    rows = stream.shape[1]
    width = stream.shape[2]
    scale = 64 ** (-0.5)

    vectors = jnp.concatenate(
        [norm_gains.reshape(-1), shifts.reshape(-1), qv_bias.reshape(-1), in_bias.reshape(-1)]
    )
    vectors = jnp.pad(vectors, (0, 512 - vectors.shape[0]))
    spread = lax.all_to_all(jnp.broadcast_to(vectors, (128, 512)), ALL, 0, 0, tiled=True)
    spread = spread.reshape(32, 4, 512)
    gains_abs = spread[:, 0, 0:128].reshape(32, 4, 32).transpose(1, 0, 2).reshape(4, width)
    shifts_abs = spread[:, 0, 128:384].reshape(32, 8, 32).transpose(1, 0, 2).reshape(8, width)
    pair = spread[:, :, 384:416].reshape(32, 4, layers, 2, 2, 2, 2).transpose(2, 3, 1, 4, 5, 0, 6)
    pair = lax.dynamic_index_in_dim(pair.reshape(layers, 2, 4, 2, 2, 64), core, 3, False)
    pair = take_relative(pair, me_x, 2).astype(FULL)
    up = spread[:, :, 416:480].reshape(32, 4, layers, 2, 2, 8).transpose(2, 1, 3, 4, 0, 5)
    up = lax.dynamic_index_in_dim(up.reshape(layers, 4, 2, 2, 256), core, 2, False)
    up = take_relative(up, me_x, 1).astype(FULL)

    place = lax.broadcasted_iota(jnp.int32, (width, width), 1)
    block = place >> 6
    far_z = me_z ^ (((block >> 2) & 1) ^ ((block >> 3) * 3))
    far_y = me_y ^ ((block & 1) ^ (((block >> 1) & 1) * 3))
    source = (((far_z >> 1) * 4 + far_y) * 2 + (far_z & 1)) * 64 + (place & 63)
    reorder = source == lax.broadcasted_iota(jnp.int32, (width, width), 0)
    reorder_low = reorder.astype(LOW)
    reorder_full = reorder.astype(FULL)

    def absolute(value):
        return lax.dot_general(
            value, reorder_full, (((1,), (1,)), ((), ())), precision=lax.Precision.HIGHEST,
            preferred_element_type=FULL,
        )

    tokens = 2 * rows
    inputs = times(
        jnp.concatenate(
            [
                stream.reshape(tokens, width), cotangent.reshape(tokens, width),
                gains_abs, shifts_abs,
            ]
        ),
        reorder_low,
    )
    state = inputs[:tokens]
    incoming = inputs[tokens : 2 * tokens]
    gains = inputs[2 * tokens : 2 * tokens + 4].reshape(layers, 2, width)
    shift = inputs[2 * tokens + 4 :].reshape(layers, 4, width)

    columns = jnp.concatenate(
        [
            w_qkv.reshape(layers, 32, 3, 2, 128).transpose(0, 1, 3, 2, 4).reshape(
                layers, 32, 2, 384
            ),
            w_out.transpose(0, 2, 1).reshape(layers, 32, 2, 128),
            w_in.reshape(layers, 32, 2, 512),
            w_back.transpose(0, 2, 1).reshape(layers, 32, 2, 512),
        ],
        3,
    )
    keep = lax.dynamic_index_in_dim(columns, core, 2, False)
    new = swap(lax.dynamic_index_in_dim(columns, 1 - core, 2, False))
    rows_two = jnp.where(
        core == 0, jnp.concatenate([keep, new], 1), jnp.concatenate([new, keep], 1)
    )
    parts = [rows_two[None, :, :, q * 256 : (q + 1) * 256] for q in range(6)]
    parts = gather_phases(parts, 0, 4)
    weights = []
    for layer in range(layers):
        mine = [value[:, layer] for value in parts]
        if layer:
            mine, weights[-1] = lax.optimization_barrier((mine, weights[-1]))
        mine = gather_phases(mine, 4, 6)
        weights.append([canonical(q, value) for q, value in enumerate(mine)])

    marks = segments.reshape(2, 2, 2, 4, rows)
    marks = jnp.where(core == 0, marks, marks[:, :, ::-1])
    marks = marks.transpose(0, 1, 3, 2, 4).reshape(2, 16 * rows)
    marks = marks[:, :, None] == marks[:, None, :]

    saved = []
    for layer in range(layers):
        w_qk, w_vo, w_up0, w_up1, w_down0, w_down1 = weights[layer]
        w_vo = w_vo.reshape(width, 4, 256)
        w_v = w_vo[:, :, :128].reshape(width, 512)
        w_o = w_vo[:, :, 128:].reshape(width, 512)
        gathered = both(state.astype(LOW))
        qk = times(gathered, w_qk).reshape(2 * tokens, 4, 2, 2, 64).transpose(0, 1, 3, 2, 4)
        v = times(gathered, w_v).reshape(2 * tokens, 4, 2, 1, 64)
        bias = jnp.stack([pair[layer, 0], jnp.zeros_like(pair[layer, 0])], 2)
        packed = jnp.concatenate([qk + bias, v + pair[layer, 1][:, :, None]], 3).astype(LOW)
        qkv = to_heads(packed, me_x)
        mixed, summary = attend(qkv, marks, scale)
        mixed = to_tokens(mixed[:, None], me_x).reshape(2 * tokens, 512)
        attended = own_sum(times_t(mixed, w_o)) + shift[layer, 2]
        first, unit_one, inv_one = normalize(state + attended, gains[layer, 0], shift[layer, 0])
        gathered_two = both(first.astype(LOW))
        hidden = [
            times(gathered_two, w) + up[layer, :, j].reshape(1024)
            for j, w in enumerate((w_up0, w_up1))
        ]
        active = [jax.nn.gelu(value, approximate=False).astype(LOW) for value in hidden]
        down = own_sum(times_t(active[0], w_down0) + times_t(active[1], w_down1))
        state, unit_two, inv_two = normalize(
            first + down + shift[layer, 3], gains[layer, 1], shift[layer, 1]
        )
        saved.append(
            (gathered, qkv, summary, mixed, unit_one, inv_one, gathered_two, hidden, active,
             unit_two, inv_two, w_v, w_o)
        )
    result = absolute(state)

    grads = [None] * layers
    small = [None] * layers
    for layer in reversed(range(layers)):
        w_qk, _, w_up0, w_up1, w_down0, w_down1 = weights[layer]
        (gathered, qkv, summary, mixed, unit_one, inv_one, gathered_two, hidden, active,
         unit_two, inv_two, w_v, w_o) = saved[layer]
        grad_two, gain_two, shift_two = normalize_back(
            incoming, unit_two, inv_two, gains[layer, 1]
        )
        spread_two = both(grad_two.astype(LOW))
        grad_down = [t_times(spread_two, value).astype(LOW) for value in active]
        grad_hidden = [
            times(spread_two, w) * gelu_slope(value)
            for w, value in zip((w_down0, w_down1), hidden)
        ]
        grad_upbias = jnp.stack(
            [jnp.sum(value, axis=0).reshape(4, 256) for value in grad_hidden], 1
        )
        low_hidden = [value.astype(LOW) for value in grad_hidden]
        grad_up = [t_times(gathered_two, value).astype(LOW) for value in low_hidden]
        grad_first = grad_two + own_sum(
            times_t(low_hidden[0], w_up0) + times_t(low_hidden[1], w_up1)
        )
        grad_one, gain_one, shift_one = normalize_back(
            grad_first, unit_one, inv_one, gains[layer, 0]
        )
        spread_one = both(grad_one.astype(LOW))
        grad_o = t_times(spread_one, mixed).astype(LOW)
        grad_mixed = times(spread_one, w_o).astype(LOW).reshape(2 * tokens, 4, 2, 1, 64)
        grad_mixed = to_heads(grad_mixed, me_x)[:, 0]
        grad_q, grad_k, grad_v = attend_back(qkv, marks, summary, grad_mixed, scale)
        grad_pair = jnp.stack([jnp.sum(grad_q, axis=(0, 1)), jnp.sum(grad_v, axis=(0, 1))])
        low_packed = to_tokens(jnp.stack([grad_q, grad_k, grad_v], 1).astype(LOW), me_x)
        low_qk = low_packed[:, :, :, :2].transpose(0, 1, 3, 2, 4).reshape(2 * tokens, 1024)
        low_v = low_packed[:, :, :, 2].reshape(2 * tokens, 512)
        grad_qk = t_times(gathered, low_qk).astype(LOW)
        grad_v = t_times(gathered, low_v).astype(LOW)
        incoming = grad_one + own_sum(times_t(low_qk, w_qk) + times_t(low_v, w_v))
        grad_vo = jnp.concatenate(
            [grad_v.reshape(width, 4, 128), grad_o.reshape(width, 4, 128)], 2
        ).reshape(width, 1024)
        grads[layer] = reduce_phases(
            [by_phase(q, value) for q, value in enumerate([grad_qk, grad_vo] + grad_up + grad_down)],
            0,
            2,
        )
        small[layer] = (
            jnp.stack([gain_one, gain_two]),
            jnp.stack(
                [shift_one, shift_two, jnp.sum(grad_one, axis=0), jnp.sum(grad_two, axis=0)]
            ),
            grad_pair,
            grad_upbias,
        )
    grad_stream = absolute(incoming)

    parts = [jnp.stack([grads[layer][q] for layer in range(layers)], 1) for q in range(6)]
    parts = reduce_phases(parts, 2, 6)
    total = jnp.concatenate([value[0] for value in parts], 2).reshape(layers, 2, 32, 1536)
    keep = lax.dynamic_index_in_dim(total, core, 1, False)
    new = swap(lax.dynamic_index_in_dim(total, 1 - core, 1, False))
    total = jnp.stack(
        [jnp.where(core == 0, keep, new), jnp.where(core == 0, new, keep)], 2
    ).astype(FULL)
    out_qkv = total[..., :384].reshape(layers, 32, 2, 3, 128).transpose(0, 1, 3, 2, 4)
    out_qkv = out_qkv.reshape(layers, 32, 3, 256)
    out_o = total[..., 384:512].reshape(layers, 32, 256).transpose(0, 2, 1)
    out_up = total[..., 512:1024].reshape(layers, 32, 1024)
    out_down = total[..., 1024:].reshape(layers, 32, 1024).transpose(0, 2, 1)

    vec = absolute(
        jnp.concatenate([small[layer][0] for layer in range(layers)]
                        + [small[layer][1] for layer in range(layers)])
    )
    vec = vec.reshape(12, 32, 32).transpose(1, 0, 2).reshape(32, 1, 384)
    vec = jnp.broadcast_to(vec, (32, 4, 384))
    pair = jnp.stack([small[layer][2] for layer in range(layers)])
    head = me_x * 4 + core * 2 + z_lo
    pair = jnp.where((jnp.arange(16) == head)[:, None], pair[:, :, None], 0.0)
    pair = pair.reshape(layers, 2, 4, 4, 32, 2).transpose(4, 2, 0, 1, 3, 5).reshape(32, 4, 32)
    up = take_absolute(jnp.stack([small[layer][3] for layer in range(layers)]), me_x, 1)
    up = jnp.where((jnp.arange(2) == core)[:, None, None], up[:, :, None], 0.0)
    up = up.reshape(layers, 4, 4, 32, 8).transpose(3, 1, 0, 2, 4).reshape(32, 4, 64)
    vec = jnp.concatenate([vec, pair, up, jnp.zeros((32, 4, 32), FULL)], 2).reshape(128, 512)
    vec = jnp.sum(lax.all_to_all(vec, ALL, 0, 0, tiled=True), axis=0)

    return (
        result.reshape(stream.shape),
        grad_stream.reshape(stream.shape),
        out_qkv,
        vec[384:416].reshape(qv_bias.shape),
        out_o,
        vec[:128].reshape(norm_gains.shape),
        vec[128:384].reshape(shifts.shape),
        out_up,
        vec[416:480].reshape(in_bias.shape),
        out_down,
    )


def solution(mesh):
    return jax.shard_map(
        local,
        mesh=mesh,
        in_specs=(
            P("dp", ("ctx", "tensor"), None),
            P("dp", None),
            P(None, ("dp", "ctx"), None, "tensor"),
            P(None, None, "tensor", ("dp", "ctx")),
            P(None, "tensor", ("dp", "ctx")),
            P(None, None, ("dp", "ctx")),
            P(None, None, ("dp", "ctx")),
            P(None, ("dp", "ctx"), "tensor"),
            P(None, "tensor", ("dp", "ctx")),
            P(None, "tensor", ("dp", "ctx")),
            P("dp", ("ctx", "tensor"), None),
        ),
        out_specs=(
            P("dp", ("ctx", "tensor"), None),
            P("dp", ("ctx", "tensor"), None),
            P(None, ("dp", "ctx"), None, "tensor"),
            P(None, None, "tensor", ("dp", "ctx")),
            P(None, "tensor", ("dp", "ctx")),
            P(None, None, ("dp", "ctx")),
            P(None, None, ("dp", "ctx")),
            P(None, ("dp", "ctx"), "tensor"),
            P(None, "tensor", ("dp", "ctx")),
            P(None, "tensor", ("dp", "ctx")),
        ),
        check_vma=False,
    )
```

time: 1750 us -> 969 us (0.55)
  waiting for transfers between devices: 841 us -> 195 us
  blocking collectives: 520 us -> 0 us
  starting transfers between devices: 2.37 us -> 192 us
  local copies, waits for them, and re-layouts: 166 us -> 332 us
  other arithmetic: 68.2 us -> 102 us
    unnamed x45 -> x0, waiting for transfers between devices: 483 us -> none
    all_gather x10 -> x0, blocking collectives: 385 us -> none  [the longest x2 79.9 us: attention_weights(): lax.all_gather(qv_bias[layer], ('dp', 'ctx'), axis=2, tiled=True)]
    all_gather x18 -> x0, waiting for transfers between devices: 328 us -> none  [the longest x8 149 us: rows_in(): return lax.all_gather(values, 'tensor', axis=1, tiled=True)]
    reshape x0 -> x90, local copies, waits for them, and re-layouts: none -> 190 us  [the longest x20 49.4 us: by_phase(): value = value.reshape((2,) * 4 + (rows, 2, 2, cols))]
    ppermute x0 -> x114, waiting for transfers between devices: none -> 152 us  [swap(): return lax.ppermute(value, ALL, exchange_perm(axis, mask))]
    ppermute x0 -> x114, starting transfers between devices: none -> 140 us  [swap(): return lax.ppermute(value, ALL, exchange_perm(axis, mask))]
    unnamed x1 -> x0, blocking collectives: 126 us -> none
    all_to_all x0 -> x10, starting transfers between devices: none -> 51.5 us  [the longest x8 33.8 us: trade(): lax.all_to_all(value, ('ctx', 'tensor'), 0, 0, axis_index_groups=GROUPS,...]
  transfers between devices with their start and end apart: 34 -> 124, of which waited for: 21 -> 33; matrix products, arithmetic and copies ran while one was open for 13% -> 46% of each run, Pallas kernels for 0% -> 0%
where the time goes in v1:
time: 969 us; the launch traced here: 955 us
  local copies, waits for them, and re-layouts  332 us (34%)
  waiting for transfers between devices  195 us (20%)
  starting transfers between devices  192 us (20%)
  matrix products  128 us (13%)
  other arithmetic  102 us (11%)
    ppermute x114, waiting for transfers between devices, swap(): return lax.ppermute(value, ALL, exchange_perm(axis, mask))  152 us
    ppermute x114, starting transfers between devices, swap(): return lax.ppermute(value, ALL, exchange_perm(axis, mask))  140 us
    dot_general x43, matrix products, dot(): lax.dot_general(left, right, (dims, ((), ())), preferred_element_type=FULL)  80.3 us
    reshape x20, local copies, waits for them, and re-layouts, by_phase(): value = value.reshape((2,) * 4 + (rows, 2, 2, cols))  49.4 us
    reshape x11, local copies, waits for them, and re-layouts, canonical(): return value.reshape(16 * rows, 4 * cols)  43 us
    unnamed x394, local copies, waits for them, and re-layouts  41.5 us
    all_to_all x8, waiting for transfers between devices, trade(): lax.all_to_all(value, ('ctx', 'tensor'), 0, 0, axis_index_groups=GROUPS,...  35.7 us
    concatenate x42, other arithmetic, gather_phases(): parts = [jnp.concatenate([value, new], 0) for value, new in zip(parts, got)]  35.1 us
  transfers between devices with their start and end apart: 124, of which 33 were waited for; matrix products, arithmetic and copies ran while one was open for 46% of the time, Pallas kernels for 0%

profile of v1, /device:TPU:1, one launch (start us, length us, event | category | flops | bytes accessed | tf_op | source)
XLA Modules:
  0.0 954.9 jit_solution(16782725376835943788)
XLA Ops:
  6.8 11.5 %all-to-all-start = ((bf16[128,2,256]{2,1,0:T(2,128)(2,1)}), bf16[128,2,256]{2,1,0:T(2,128)(2,1)S(1)}, u32[]{:S(2)}, u32[]{:S(2)}) async-start(bf16[128,2,256]{2,1,0:T(2,128)(2,1)} %reshape.745), calls=%async_computation | async-start | bytes 262144 | tf_op jit(solution)/shard_map/all_to_all | solution.py:204
  21.2 7.0 all-to-all-done
  60.5 5.0 collective-permute-done.25
  76.4 9.5 collective-permute-done.36
  98.3 18.8 %collective-permute-done.26 = bf16[16,64,256]{2,1,0:T(8,128)(2,1)S(1)} collective-permute-done((bf16[16,64,256]{2,1,0:T(8,128)(2,1)S(1)}, bf16[16,64,256]{2,1,0:T(8,128)(2,1)S(1)}, u32[]{:S(2)}, u32[]{:S(2)}) %collective-permute-start.26) | collective-permute-done | bytes 524320 | tf_op jit(solution)/shard_map/ppermute | solution.py:32
  128.0 7.6 collective-permute-start
  140.7 4.5 reshape.646
  150.3 4.5 reshape.644
  159.9 4.5 reshape.642
  169.5 4.5 reshape.640
  179.1 4.5 reshape.638
  183.6 4.7 reshape.652
  201.8 5.7 reshape.654
  207.5 8.3 copy.215
  215.9 4.4 reshape.655
  220.3 4.9 all-to-all-start.1
  226.1 13.3 %all-to-all-done.1 = bf16[8,144,384]{2,1,0:T(8,128)(2,1)} async-done(((bf16[8,144,384]{2,1,0:T(8,128)(2,1)}), bf16[8,144,384]{2,1,0:T(8,128)(2,1)}, u32[]{:S(2)}, u32[]{:S(2)}) %all-to-all-start.1) | async-done | bytes 884768 | tf_op jit(solution)/shard_map/all_to_all | solution.py:168
  239.4 4.4 reshape.734
  269.3 6.0 all-to-all-done.2
  288.3 10.3 %collective-permute-done.42 = bf16[16,64,256]{2,1,0:T(8,128)(2,1)S(1)} collective-permute-done((bf16[16,64,256]{2,1,0:T(8,128)(2,1)}, bf16[16,64,256]{2,1,0:T(8,128)(2,1)S(1)}, u32[]{:S(2)}, u32[]{:S(2)}) %collective-permute-start.42) | collective-permute-done | bytes 524320 | tf_op jit(solution)/shard_map/ppermute | solution.py:32
  304.0 4.6 fusion.52
  308.7 4.5 fusion.49
  317.0 8.0 collective-permute-done.43
  352.4 7.2 copy.228
  361.5 4.4 all-to-all-start.3
  375.2 13.9 %collective-permute-done.50 = bf16[16,64,256]{2,1,0:T(8,128)(2,1)S(1)} collective-permute-done((bf16[16,64,256]{2,1,0:T(8,128)(2,1)S(1)}, bf16[16,64,256]{2,1,0:T(8,128)(2,1)S(1)}, u32[]{:S(2)}, u32[]{:S(2)}) %collective-permute-start.50) | collective-permute-done | bytes 524320 | tf_op jit(solution)/shard_map/ppermute | solution.py:32
  451.5 4.5 reshape.682
  461.0 4.4 reshape.684
  465.5 4.8 fusion.58
  493.2 4.5 reshape.702
  503.8 4.5 reshape.704
  517.5 4.5 reshape.706
  528.0 4.5 reshape.708
  558.7 6.6 multiply_reduce_fusion.1
  579.7 4.4 all-to-all-start.6
  599.9 8.5 collective-permute-done.84
  614.8 5.6 copy.245
  718.8 14.2 %all-to-all-done.7 = bf16[8,144,128]{2,1,0:T(8,128)(2,1)S(1)} async-done(((bf16[8,144,128]{2,1,0:T(8,128)(2,1)}), bf16[8,144,128]{2,1,0:T(8,128)(2,1)S(1)}, u32[]{:S(2)}, u32[]{:S(2)}) %all-to-all-start.7) | async-done | bytes 294944 | tf_op jit(solution)/shard_map/all_to_all | solution.py:168
  734.0 5.9 fusion.6
  740.0 5.4 multiply_reduce_fusion
  751.8 6.3 all-to-all-start.9
  784.8 6.6 collective-permute-done.89
  796.5 4.8 all-to-all-start.8
  854.7 4.5 collective-permute-done.110
  859.2 20.2 %collective-permute-done.102 = bf16[4,2,64,256]{3,2,0,1:T(8,128)(2,1)S(1)} collective-permute-done((bf16[4,2,64,256]{3,2,0,1:T(8,128)(2,1)S(1)}, bf16[4,2,64,256]{3,2,0,1:T(8,128)(2,1)S(1)}, u32[]{:S(2)}, u32[]{:S(2)}) %collective-permute-start.102) | collective-permute-done | bytes 262176 | tf_op jit(solution)/shard_map/ppermute | solution.py:32
  898.4 8.8 collective-permute-done.66
  911.4 9.0 collective-permute-done.69
  939.1 8.0 collective-permute-start.113
  (1095 shorter events, 612.6 us)
Async XLA Ops:
  86.1 33.0 %collective-permute-start.37 = (bf16[32,64,256]{2,1,0:T(8,128)(2,1)S(1)}, bf16[32,64,256]{2,1,0:T(8,128)(2,1)S(1)}, u32[]{:S(2)}, u32[]{:S(2)}) collective-permute-start(bf16[32,64,256]{2,1,0:T(8,128)(2,1)S(1)} %pad_maximum_fusion.21), channel_id=1, source_target_pairs={{0,48},{1,49},{2,50},{3,51},{4,52},{5,53},{6,54},{7,55},{8,56},{9,... | collective-permute-start | bytes 3145736 | tf_op jit(solution)/shard_map/ppermute | solution.py:32
  88.8 28.3 %collective-permute-start.26 = (bf16[16,64,256]{2,1,0:T(8,128)(2,1)S(1)}, bf16[16,64,256]{2,1,0:T(8,128)(2,1)S(1)}, u32[]{:S(2)}, u32[]{:S(2)}) collective-permute-start(bf16[16,64,256]{2,1,0:T(8,128)(2,1)S(1)} %get-tuple-element.173), channel_id=1, source_target_pairs={{0,48},{1,49},{2,50},{3,51},{4,52},{5,53},{6,54},{7,55},{8,56},{9,... | collective-permute-start | bytes 1572872 | tf_op jit(solution)/shard_map/ppermute | solution.py:32
  90.8 37.2 %collective-permute-start.35 = (bf16[32,64,256]{2,1,0:T(8,128)(2,1)}, bf16[32,64,256]{2,1,0:T(8,128)(2,1)}, u32[]{:S(2)}, u32[]{:S(2)}) collective-permute-start(bf16[32,64,256]{2,1,0:T(8,128)(2,1)} %pad_maximum_fusion.20), channel_id=1, source_target_pairs={{0,3},{1,2},{2,1},{3,0},{4,7},{5,6},{6,5},{7,4},{8,11},{9,10},{10,... | collective-permute-start | bytes 3145736 | tf_op jit(solution)/shard_map/ppermute | solution.py:32
  94.2 51.0 %collective-permute-start.33 = (bf16[32,64,256]{2,1,0:T(8,128)(2,1)}, bf16[32,64,256]{2,1,0:T(8,128)(2,1)}, u32[]{:S(2)}, u32[]{:S(2)}) collective-permute-start(bf16[32,64,256]{2,1,0:T(8,128)(2,1)} %pad_maximum_fusion.19), channel_id=1, source_target_pairs={{0,8},{1,9},{2,10},{3,11},{4,12},{5,13},{6,14},{7,15},{8,0},{9,1},... | collective-permute-start | bytes 3145736 | tf_op jit(solution)/shard_map/ppermute | solution.py:32
  96.6 58.2 %collective-permute-start.31 = (bf16[32,64,256]{2,1,0:T(8,128)(2,1)}, bf16[32,64,256]{2,1,0:T(8,128)(2,1)}, u32[]{:S(2)}, u32[]{:S(2)}) collective-permute-start(bf16[32,64,256]{2,1,0:T(8,128)(2,1)} %pad_maximum_fusion.18), channel_id=1, source_target_pairs={{0,16},{1,17},{2,18},{3,19},{4,20},{5,21},{6,22},{7,23},{8,24},{9,... | collective-permute-start | bytes 3145736 | tf_op jit(solution)/shard_map/ppermute | solution.py:32
  117.1 47.3 %collective-permute-start.29 = (bf16[32,64,256]{2,1,0:T(8,128)(2,1)}, bf16[32,64,256]{2,1,0:T(8,128)(2,1)}, u32[]{:S(2)}, u32[]{:S(2)}) collective-permute-start(bf16[32,64,256]{2,1,0:T(8,128)(2,1)} %pad_maximum_fusion.17), channel_id=1, source_target_pairs={{0,1},{1,0},{2,3},{3,2},{4,5},{5,4},{6,7},{7,6},{8,9},{9,8},{10,11... | collective-permute-start | bytes 3145736 | tf_op jit(solution)/shard_map/ppermute | solution.py:32
  119.1 54.9 %collective-permute-start.27 = (bf16[32,64,256]{2,1,0:T(8,128)(2,1)}, bf16[32,64,256]{2,1,0:T(8,128)(2,1)}, u32[]{:S(2)}, u32[]{:S(2)}) collective-permute-start(bf16[32,64,256]{2,1,0:T(8,128)(2,1)} %pad_maximum_fusion.16), channel_id=1, source_target_pairs={{0,72},{1,73},{2,74},{3,75},{4,76},{5,77},{6,78},{7,79},{8,64},{9,... | collective-permute-start | bytes 3145736 | tf_op jit(solution)/shard_map/ppermute | solution.py:32
  128.0 66.3 %collective-permute-start = (bf16[144,1024]{1,0:T(8,128)(2,1)}, bf16[144,1024]{1,0:T(8,128)(2,1)}, u32[]{:S(2)}, u32[]{:S(2)}) collective-permute-start(bf16[144,1024]{1,0:T(8,128)(2,1)} %slice.1185), channel_id=1, source_target_pairs={{0,4},{1,5},{2,6},{3,7},{4,0},{5,1},{6,2},{7,3},{8,12},{9,13},{10,... | collective-permute-start | bytes 884744 | tf_op jit(solution)/shard_map/ppermute | solution.py:32
  287.7 83.8 %collective-permute-start.48 = (bf16[16,64,256]{2,1,0:T(8,128)(2,1)}, bf16[16,64,256]{2,1,0:T(8,128)(2,1)}, u32[]{:S(2)}, u32[]{:S(2)}) collective-permute-start(bf16[16,64,256]{2,1,0:T(8,128)(2,1)} %get-tuple-element.30), channel_id=1, source_target_pairs={{0,1},{1,0},{2,3},{3,2},{4,5},{5,4},{6,7},{7,6},{8,9},{9,8},{10,11... | collective-permute-start | bytes 1572872 | tf_op jit(solution)/shard_map/ppermute | solution.py:32
  299.8 25.2 %collective-permute-start.43 = (bf16[32,64,256]{2,1,0:T(8,128)(2,1)S(1)}, bf16[32,64,256]{2,1,0:T(8,128)(2,1)S(1)}, u32[]{:S(2)}, u32[]{:S(2)}) collective-permute-start(bf16[32,64,256]{2,1,0:T(8,128)(2,1)S(1)} %pad_maximum_fusion.22), channel_id=1, source_target_pairs={{0,72},{1,73},{2,74},{3,75},{4,76},{5,77},{6,78},{7,79},{8,64},{9,... | collective-permute-start | bytes 3145736 | tf_op jit(solution)/shard_map/ppermute | solution.py:32
  303.4 27.7 %collective-permute-start.45 = (bf16[32,64,256]{2,1,0:T(8,128)(2,1)}, bf16[32,64,256]{2,1,0:T(8,128)(2,1)}, u32[]{:S(2)}, u32[]{:S(2)}) collective-permute-start(bf16[32,64,256]{2,1,0:T(8,128)(2,1)} %pad_maximum_fusion.23), channel_id=1, source_target_pairs={{0,1},{1,0},{2,3},{3,2},{4,5},{5,4},{6,7},{7,6},{8,9},{9,8},{10,11... | collective-permute-start | bytes 3145736 | tf_op jit(solution)/shard_map/ppermute | solution.py:32
  361.5 31.5 %all-to-all-start.3 = ((bf16[8,144,384]{2,1,0:T(8,128)(2,1)}), bf16[8,144,384]{2,1,0:T(8,128)(2,1)}, u32[]{:S(2)}, u32[]{:S(2)}) async-start(bf16[8,144,384]{2,1,0:T(8,128)(2,1)} %reshape.671), calls=%async_computation.3 | async-start | bytes 1769472 | tf_op jit(solution)/shard_map/all_to_all | solution.py:168
  365.9 23.2 %collective-permute-start.50 = (bf16[16,64,256]{2,1,0:T(8,128)(2,1)S(1)}, bf16[16,64,256]{2,1,0:T(8,128)(2,1)S(1)}, u32[]{:S(2)}, u32[]{:S(2)}) collective-permute-start(bf16[16,64,256]{2,1,0:T(8,128)(2,1)S(1)} %copy-done.32), channel_id=1, source_target_pairs={{0,8},{1,9},{2,10},{3,11},{4,12},{5,13},{6,14},{7,15},{8,0},{9,1},... | collective-permute-start | bytes 1572872 | tf_op jit(solution)/shard_map/ppermute | solution.py:32
  369.1 47.4 %collective-permute-start.52 = (bf16[16,64,256]{2,1,0:T(8,128)(2,1)}, bf16[16,64,256]{2,1,0:T(8,128)(2,1)}, u32[]{:S(2)}, u32[]{:S(2)}) collective-permute-start(bf16[16,64,256]{2,1,0:T(8,128)(2,1)} %get-tuple-element.32), channel_id=1, source_target_pairs={{0,16},{1,17},{2,18},{3,19},{4,20},{5,21},{6,22},{7,23},{8,24},{9,... | collective-permute-start | bytes 1572872 | tf_op jit(solution)/shard_map/ppermute | solution.py:32
  369.1 51.1 %collective-permute-start.54 = (bf16[16,64,256]{2,1,0:T(8,128)(2,1)S(1)}, bf16[16,64,256]{2,1,0:T(8,128)(2,1)}, u32[]{:S(2)}, u32[]{:S(2)}) collective-permute-start(bf16[16,64,256]{2,1,0:T(8,128)(2,1)S(1)} %get-tuple-element.33), channel_id=1, source_target_pairs={{0,3},{1,2},{2,1},{3,0},{4,7},{5,6},{6,5},{7,4},{8,11},{9,10},{10,... | collective-permute-start | bytes 1572872 | tf_op jit(solution)/shard_map/ppermute | solution.py:32
  373.8 57.1 %collective-permute-start.49 = (bf16[32,64,256]{2,1,0:T(8,128)(2,1)}, bf16[32,64,256]{2,1,0:T(8,128)(2,1)}, u32[]{:S(2)}, u32[]{:S(2)}) collective-permute-start(bf16[32,64,256]{2,1,0:T(8,128)(2,1)} %pad_maximum_fusion.24), channel_id=1, source_target_pairs={{0,16},{1,17},{2,18},{3,19},{4,20},{5,21},{6,22},{7,23},{8,24},{9,... | collective-permute-start | bytes 3145736 | tf_op jit(solution)/shard_map/ppermute | solution.py:32
  390.3 47.2 %collective-permute-start.51 = (bf16[32,64,256]{2,1,0:T(8,128)(2,1)}, bf16[32,64,256]{2,1,0:T(8,128)(2,1)}, u32[]{:S(2)}, u32[]{:S(2)}) collective-permute-start(bf16[32,64,256]{2,1,0:T(8,128)(2,1)} %pad_maximum_fusion.25), channel_id=1, source_target_pairs={{0,3},{1,2},{2,1},{3,0},{4,7},{5,6},{6,5},{7,4},{8,11},{9,10},{10,... | collective-permute-start | bytes 3145736 | tf_op jit(solution)/shard_map/ppermute | solution.py:32
  418.9 27.4 %collective-permute-start.53 = (bf16[32,64,256]{2,1,0:T(8,128)(2,1)}, bf16[32,64,256]{2,1,0:T(8,128)(2,1)}, u32[]{:S(2)}, u32[]{:S(2)}) collective-permute-start(bf16[32,64,256]{2,1,0:T(8,128)(2,1)} %pad_maximum_fusion.26), channel_id=1, source_target_pairs={{0,8},{1,9},{2,10},{3,11},{4,12},{5,13},{6,14},{7,15},{8,0},{9,1},... | collective-permute-start | bytes 3145736 | tf_op jit(solution)/shard_map/ppermute | solution.py:32
  422.3 33.6 %collective-permute-start.55 = (bf16[32,64,256]{2,1,0:T(8,128)(2,1)}, bf16[32,64,256]{2,1,0:T(8,128)(2,1)}, u32[]{:S(2)}, u32[]{:S(2)}) collective-permute-start(bf16[32,64,256]{2,1,0:T(8,128)(2,1)} %pad_maximum_fusion.27), channel_id=1, source_target_pairs={{0,48},{1,49},{2,50},{3,51},{4,52},{5,53},{6,54},{7,55},{8,56},{9,... | collective-permute-start | bytes 3145736 | tf_op jit(solution)/shard_map/ppermute | solution.py:32
  490.4 46.0 %collective-permute-start.58 = (bf16[144,1024]{1,0:T(8,128)(2,1)}, bf16[144,1024]{1,0:T(8,128)(2,1)}, u32[]{:S(2)}, u32[]{:S(2)}) collective-permute-start(bf16[144,1024]{1,0:T(8,128)(2,1)} %slice.1180), channel_id=1, source_target_pairs={{0,4},{1,5},{2,6},{3,7},{4,0},{5,1},{6,2},{7,3},{8,12},{9,13},{10,... | collective-permute-start | bytes 884744 | tf_op jit(solution)/shard_map/ppermute | solution.py:32
  511.8 72.3 %collective-permute-start.91 = (bf16[32,64,256]{2,1,0:T(8,128)(2,1)}, bf16[32,64,256]{2,1,0:T(8,128)(2,1)}, u32[]{:S(2)}, u32[]{:S(2)}) collective-permute-start(bf16[32,64,256]{2,1,0:T(8,128)(2,1)} %bitcast.174), channel_id=1, source_target_pairs={{0,3},{1,2},{2,1},{3,0},{4,7},{5,6},{6,5},{7,4},{8,11},{9,10},{10,... | collective-permute-start | bytes 3145736 | tf_op jit(solution)/shard_map/ppermute | solution.py:32
  514.2 73.1 %collective-permute-start.83 = (bf16[32,64,256]{2,1,0:T(8,128)(2,1)}, bf16[32,64,256]{2,1,0:T(8,128)(2,1)}, u32[]{:S(2)}, u32[]{:S(2)}) collective-permute-start(bf16[32,64,256]{2,1,0:T(8,128)(2,1)} %bitcast.165), channel_id=1, source_target_pairs={{0,8},{1,9},{2,10},{3,11},{4,12},{5,13},{6,14},{7,15},{8,0},{9,1},... | collective-permute-start | bytes 3145736 | tf_op jit(solution)/shard_map/ppermute | solution.py:32
  535.9 55.7 %collective-permute-start.107 = (bf16[32,64,256]{2,1,0:T(8,128)(2,1)}, bf16[32,64,256]{2,1,0:T(8,128)(2,1)}, u32[]{:S(2)}, u32[]{:S(2)}) collective-permute-start(bf16[32,64,256]{2,1,0:T(8,128)(2,1)} %bitcast.192), channel_id=1, source_target_pairs={{0,72},{1,73},{2,74},{3,75},{4,76},{5,77},{6,78},{7,79},{8,64},{9,... | collective-permute-start | bytes 3145736 | tf_op jit(solution)/shard_map/ppermute | solution.py:32
  540.9 52.5 %collective-permute-start.99 = (bf16[32,64,256]{2,1,0:T(8,128)(2,1)}, bf16[32,64,256]{2,1,0:T(8,128)(2,1)}, u32[]{:S(2)}, u32[]{:S(2)}) collective-permute-start(bf16[32,64,256]{2,1,0:T(8,128)(2,1)} %bitcast.183), channel_id=1, source_target_pairs={{0,48},{1,49},{2,50},{3,51},{4,52},{5,53},{6,54},{7,55},{8,56},{9,... | collective-permute-start | bytes 3145736 | tf_op jit(solution)/shard_map/ppermute | solution.py:32
  579.7 31.5 %all-to-all-start.6 = ((bf16[8,144,384]{2,1,0:T(8,128)(2,1)}), bf16[8,144,384]{2,1,0:T(8,128)(2,1)}, u32[]{:S(2)}, u32[]{:S(2)}) async-start(bf16[8,144,384]{2,1,0:T(8,128)(2,1)} %copy.244), calls=%async_computation.6 | async-start | bytes 1769472 | tf_op jit(solution)/shard_map/all_to_all | solution.py:168
  642.9 56.5 %collective-permute-start.67 = (bf16[32,64,256]{2,1,0:T(8,128)(2,1)}, bf16[32,64,256]{2,1,0:T(8,128)(2,1)}, u32[]{:S(2)}, u32[]{:S(2)}) collective-permute-start(bf16[32,64,256]{2,1,0:T(8,128)(2,1)} %bitcast.147), channel_id=1, source_target_pairs={{0,1},{1,0},{2,3},{3,2},{4,5},{5,4},{6,7},{7,6},{8,9},{9,8},{10,11... | collective-permute-start | bytes 3145736 | tf_op jit(solution)/shard_map/ppermute | solution.py:32
  647.8 54.9 %collective-permute-start.75 = (bf16[32,64,256]{2,1,0:T(8,128)(2,1)}, bf16[32,64,256]{2,1,0:T(8,128)(2,1)}, u32[]{:S(2)}, u32[]{:S(2)}) collective-permute-start(bf16[32,64,256]{2,1,0:T(8,128)(2,1)} %bitcast.156), channel_id=1, source_target_pairs={{0,16},{1,17},{2,18},{3,19},{4,20},{5,21},{6,22},{7,23},{8,24},{9,... | collective-permute-start | bytes 3145736 | tf_op jit(solution)/shard_map/ppermute | solution.py:32
  656.5 37.9 %collective-permute-start.62 = (bf16[144,1024]{1,0:T(8,128)(2,1)}, bf16[144,1024]{1,0:T(8,128)(2,1)}, u32[]{:S(2)}, u32[]{:S(2)}) collective-permute-start(bf16[144,1024]{1,0:T(8,128)(2,1)} %slice.1178), channel_id=1, source_target_pairs={{0,4},{1,5},{2,6},{3,7},{4,0},{5,1},{6,2},{7,3},{8,12},{9,13},{10,... | collective-permute-start | bytes 884744 | tf_op jit(solution)/shard_map/ppermute | solution.py:32
  674.9 98.1 %collective-permute-start.105 = (bf16[32,64,256]{2,1,0:T(8,128)(2,1)}, bf16[32,64,256]{2,1,0:T(8,128)(2,1)}, u32[]{:S(2)}, u32[]{:S(2)}) collective-permute-start(bf16[32,64,256]{2,1,0:T(8,128)(2,1)} %bitcast.188), channel_id=1, source_target_pairs={{0,72},{1,73},{2,74},{3,75},{4,76},{5,77},{6,78},{7,79},{8,64},{9,... | collective-permute-start | bytes 3145736 | tf_op jit(solution)/shard_map/ppermute | solution.py:32
  677.4 98.0 %collective-permute-start.97 = (bf16[32,64,256]{2,1,0:T(8,128)(2,1)}, bf16[32,64,256]{2,1,0:T(8,128)(2,1)}, u32[]{:S(2)}, u32[]{:S(2)}) collective-permute-start(bf16[32,64,256]{2,1,0:T(8,128)(2,1)} %bitcast.179), channel_id=1, source_target_pairs={{0,48},{1,49},{2,50},{3,51},{4,52},{5,53},{6,54},{7,55},{8,56},{9,... | collective-permute-start | bytes 3145736 | tf_op jit(solution)/shard_map/ppermute | solution.py:32
  694.4 87.2 %collective-permute-start.81 = (bf16[32,64,256]{2,1,0:T(8,128)(2,1)}, bf16[32,64,256]{2,1,0:T(8,128)(2,1)}, u32[]{:S(2)}, u32[]{:S(2)}) collective-permute-start(bf16[32,64,256]{2,1,0:T(8,128)(2,1)} %bitcast.161), channel_id=1, source_target_pairs={{0,8},{1,9},{2,10},{3,11},{4,12},{5,13},{6,14},{7,15},{8,0},{9,1},... | collective-permute-start | bytes 3145736 | tf_op jit(solution)/shard_map/ppermute | solution.py:32
  702.8 63.5 %collective-permute-start.68 = (bf16[16,64,256]{2,1,0:T(8,128)(2,1)}, bf16[16,64,256]{2,1,0:T(8,128)(2,1)}, u32[]{:S(2)}, u32[]{:S(2)}) collective-permute-start(bf16[16,64,256]{2,1,0:T(8,128)(2,1)} %slice.915), channel_id=1, source_target_pairs={{0,16},{1,17},{2,18},{3,19},{4,20},{5,21},{6,22},{7,23},{8,24},{9,... | collective-permute-start | bytes 1572872 | tf_op jit(solution)/shard_map/ppermute | solution.py:32
  706.9 64.0 %collective-permute-start.76 = (bf16[16,64,256]{2,1,0:T(8,128)(2,1)}, bf16[16,64,256]{2,1,0:T(8,128)(2,1)}, u32[]{:S(2)}, u32[]{:S(2)}) collective-permute-start(bf16[16,64,256]{2,1,0:T(8,128)(2,1)} %slice.931), channel_id=1, source_target_pairs={{0,8},{1,9},{2,10},{3,11},{4,12},{5,13},{6,14},{7,15},{8,0},{9,1},... | collective-permute-start | bytes 1572872 | tf_op jit(solution)/shard_map/ppermute | solution.py:32
  710.8 22.3 %all-to-all-start.7 = ((bf16[8,144,128]{2,1,0:T(8,128)(2,1)}), bf16[8,144,128]{2,1,0:T(8,128)(2,1)S(1)}, u32[]{:S(2)}, u32[]{:S(2)}) async-start(bf16[8,144,128]{2,1,0:T(8,128)(2,1)} %reshape.694), calls=%async_computation.7 | async-start | bytes 589824 | tf_op jit(solution)/shard_map/all_to_all | solution.py:168
  751.8 44.7 %all-to-all-start.9 = ((f32[128,1,512]{2,1,0:T(1,128)}), f32[128,1,512]{2,1,0:T(1,128)}, u32[]{:S(2)}, u32[]{:S(2)}) async-start(f32[128,1,512]{2,1,0:T(1,128)} %all_to_all.43), calls=%async_computation.9 | async-start | bytes 524288 | tf_op jit(solution)/shard_map/all_to_all | solution.py:392
  766.3 25.1 %collective-permute-start.89 = (bf16[32,64,256]{2,1,0:T(8,128)(2,1)}, bf16[32,64,256]{2,1,0:T(8,128)(2,1)S(1)}, u32[]{:S(2)}, u32[]{:S(2)}) collective-permute-start(bf16[32,64,256]{2,1,0:T(8,128)(2,1)} %bitcast.660), channel_id=1, source_target_pairs={{0,3},{1,2},{2,1},{3,0},{4,7},{5,6},{6,5},{7,4},{8,11},{9,10},{10,... | collective-permute-start | bytes 3145736 | tf_op jit(solution)/shard_map/ppermute | solution.py:32
  775.5 30.0 %collective-permute-start.106 = (bf16[16,64,256]{2,1,0:T(8,128)(2,1)}, bf16[16,64,256]{2,1,0:T(8,128)(2,1)}, u32[]{:S(2)}, u32[]{:S(2)}) collective-permute-start(bf16[16,64,256]{2,1,0:T(8,128)(2,1)} %slice.991), channel_id=1, source_target_pairs={{0,1},{1,0},{2,3},{3,2},{4,5},{5,4},{6,7},{7,6},{8,9},{9,8},{10,11... | collective-permute-start | bytes 1572872 | tf_op jit(solution)/shard_map/ppermute | solution.py:32
  778.5 29.8 %collective-permute-start.98 = (bf16[16,64,256]{2,1,0:T(8,128)(2,1)}, bf16[16,64,256]{2,1,0:T(8,128)(2,1)}, u32[]{:S(2)}, u32[]{:S(2)}) collective-permute-start(bf16[16,64,256]{2,1,0:T(8,128)(2,1)} %slice.975), channel_id=1, source_target_pairs={{0,72},{1,73},{2,74},{3,75},{4,76},{5,77},{6,78},{7,79},{8,64},{9,... | collective-permute-start | bytes 1572872 | tf_op jit(solution)/shard_map/ppermute | solution.py:32
  784.1 27.8 %collective-permute-start.82 = (bf16[16,64,256]{2,1,0:T(8,128)(2,1)}, bf16[16,64,256]{2,1,0:T(8,128)(2,1)}, u32[]{:S(2)}, u32[]{:S(2)}) collective-permute-start(bf16[16,64,256]{2,1,0:T(8,128)(2,1)} %slice.943), channel_id=1, source_target_pairs={{0,3},{1,2},{2,1},{3,0},{4,7},{5,6},{6,5},{7,4},{8,11},{9,10},{10,... | collective-permute-start | bytes 1572872 | tf_op jit(solution)/shard_map/ppermute | solution.py:32
  796.5 23.4 %all-to-all-start.8 = ((bf16[8,144,384]{2,1,0:T(8,128)(2,1)}), bf16[8,144,384]{2,1,0:T(8,128)(2,1)S(1)}, u32[]{:S(2)}, u32[]{:S(2)}) async-start(bf16[8,144,384]{2,1,0:T(8,128)(2,1)} %copy.253), calls=%async_computation.8 | async-start | bytes 1769472 | tf_op jit(solution)/shard_map/all_to_all | solution.py:168
  808.3 38.5 %collective-permute-start.109 = (bf16[8,2,64,256]{3,2,0,1:T(8,128)(2,1)}, bf16[8,2,64,256]{3,2,0,1:T(8,128)(2,1)}, u32[]{:S(2)}, u32[]{:S(2)}) collective-permute-start(bf16[8,2,64,256]{3,2,0,1:T(8,128)(2,1)} %pad_maximum_fusion.38), channel_id=1, source_target_pairs={{0,16},{1,17},{2,18},{3,19},{4,20},{5,21},{6,22},{7,23},{8,24},{9,... | collective-permute-start | bytes 1572872 | tf_op jit(solution)/shard_map/ppermute | solution.py:32
  810.4 38.5 %collective-permute-start.101 = (bf16[8,2,64,256]{3,2,0,1:T(8,128)(2,1)}, bf16[8,2,64,256]{3,2,0,1:T(8,128)(2,1)}, u32[]{:S(2)}, u32[]{:S(2)}) collective-permute-start(bf16[8,2,64,256]{3,2,0,1:T(8,128)(2,1)} %pad_maximum_fusion.39), channel_id=1, source_target_pairs={{0,1},{1,0},{2,3},{3,2},{4,5},{5,4},{6,7},{7,6},{8,9},{9,8},{10,11... | collective-permute-start | bytes 1572872 | tf_op jit(solution)/shard_map/ppermute | solution.py:32
  814.0 37.4 %collective-permute-start.85 = (bf16[8,2,64,256]{3,2,0,1:T(8,128)(2,1)}, bf16[8,2,64,256]{3,2,0,1:T(8,128)(2,1)}, u32[]{:S(2)}, u32[]{:S(2)}) collective-permute-start(bf16[8,2,64,256]{3,2,0,1:T(8,128)(2,1)} %pad_maximum_fusion.41), channel_id=1, source_target_pairs={{0,48},{1,49},{2,50},{3,51},{4,52},{5,53},{6,54},{7,55},{8,56},{9,... | collective-permute-start | bytes 1572872 | tf_op jit(solution)/shard_map/ppermute | solution.py:32
  817.0 35.9 %collective-permute-start.93 = (bf16[8,2,64,256]{3,2,0,1:T(8,128)(2,1)}, bf16[8,2,64,256]{3,2,0,1:T(8,128)(2,1)}, u32[]{:S(2)}, u32[]{:S(2)}) collective-permute-start(bf16[8,2,64,256]{3,2,0,1:T(8,128)(2,1)} %pad_maximum_fusion.40), channel_id=1, source_target_pairs={{0,72},{1,73},{2,74},{3,75},{4,76},{5,77},{6,78},{7,79},{8,64},{9,... | collective-permute-start | bytes 1572872 | tf_op jit(solution)/shard_map/ppermute | solution.py:32
  830.7 116.4 %collective-permute-start.64 = (bf16[144,1024]{1,0:T(8,128)(2,1)}, bf16[144,1024]{1,0:T(8,128)(2,1)}, u32[]{:S(2)}, u32[]{:S(2)}) collective-permute-start(bf16[144,1024]{1,0:T(8,128)(2,1)} %slice.1177), channel_id=1, source_target_pairs={{0,4},{1,5},{2,6},{3,7},{4,0},{5,1},{6,2},{7,3},{8,12},{9,13},{10,... | collective-permute-start | bytes 884744 | tf_op jit(solution)/shard_map/ppermute | solution.py:32
  846.8 48.6 %collective-permute-start.65 = (bf16[32,64,256]{2,1,0:T(8,128)(2,1)S(1)}, bf16[32,64,256]{2,1,0:T(8,128)(2,1)S(1)}, u32[]{:S(2)}, u32[]{:S(2)}) collective-permute-start(bf16[32,64,256]{2,1,0:T(8,128)(2,1)S(1)} %bitcast.662), channel_id=1, source_target_pairs={{0,1},{1,0},{2,3},{3,2},{4,5},{5,4},{6,7},{7,6},{8,9},{9,8},{10,11... | collective-permute-start | bytes 3145736 | tf_op jit(solution)/shard_map/ppermute | solution.py:32
  848.9 48.2 %collective-permute-start.73 = (bf16[32,64,256]{2,1,0:T(8,128)(2,1)S(1)}, bf16[32,64,256]{2,1,0:T(8,128)(2,1)S(1)}, u32[]{:S(2)}, u32[]{:S(2)}) collective-permute-start(bf16[32,64,256]{2,1,0:T(8,128)(2,1)S(1)} %bitcast.661), channel_id=1, source_target_pairs={{0,16},{1,17},{2,18},{3,19},{4,20},{5,21},{6,22},{7,23},{8,24},{9,... | collective-permute-start | bytes 3145736 | tf_op jit(solution)/shard_map/ppermute | solution.py:32
  852.9 26.6 %collective-permute-start.102 = (bf16[4,2,64,256]{3,2,0,1:T(8,128)(2,1)S(1)}, bf16[4,2,64,256]{3,2,0,1:T(8,128)(2,1)S(1)}, u32[]{:S(2)}, u32[]{:S(2)}) collective-permute-start(bf16[4,2,64,256]{3,2,0,1:T(8,128)(2,1)S(1)} %slice.983), channel_id=1, source_target_pairs={{0,16},{1,17},{2,18},{3,19},{4,20},{5,21},{6,22},{7,23},{8,24},{9,... | collective-permute-start | bytes 786440 | tf_op jit(solution)/shard_map/ppermute | solution.py:32
  (254 other events, 2054.1 us)

commit v2 on v1

--- a/solution.py
+++ b/solution.py
@@ -1,6 +1,8 @@
 import jax
 import jax.numpy as jnp
 from jax import lax
+from jax.experimental import pallas as pl
+from jax.experimental.pallas import tpu as pltpu
 from jax.sharding import PartitionSpec as P
 
 EPSILON = 1e-12
@@ -43,22 +45,6 @@
     return parts
 
 
-def canonical(part, value):
-    rows, cols = value.shape[1:]
-    value = value.reshape((2,) * 6 + (rows, cols))
-    place = [5 - [dim_at(part, phase) for phase in range(6)].index(dim) for dim in CANON]
-    value = value.transpose(place[:4] + [6] + place[4:] + [7])
-    return value.reshape(16 * rows, 4 * cols)
-
-
-def by_phase(part, value):
-    rows, cols = value.shape[0] // 16, value.shape[1] // 4
-    value = value.reshape((2,) * 4 + (rows, 2, 2, cols))
-    axis_of = dict(zip(CANON, (0, 1, 2, 3, 5, 6)))
-    order = [axis_of[dim_at(part, phase)] for phase in range(6)]
-    return value.transpose(order + [4, 7]).reshape(64, rows, cols)
-
-
 def reduce_phases(parts, first, last):
     for phase in range(first, last):
         half = parts[0].shape[0] // 2
@@ -116,11 +102,6 @@
     return (inverse * inner, jnp.sum(incoming * unit, axis=0), jnp.sum(incoming, axis=0))
 
 
-def gelu_slope(value):
-    cdf = 0.5 * (1.0 + lax.erf(value * ROOT_HALF))
-    return cdf + value * jnp.exp(-0.5 * value * value) / ROOT_TWOPI
-
-
 def dot(left, right, dims):
     return lax.dot_general(left, right, (dims, ((), ())), preferred_element_type=FULL)
 
@@ -137,53 +118,353 @@
     return dot(left, right, ((0,), (0,)))
 
 
-def masked_scores(query, keys, marks, scale):
-    scores = jnp.einsum("qse,kse->sqk", query, keys, preferred_element_type=FULL) * scale
-    return jnp.where(marks, scores, MASKED)
-
-
-def attend(qkv, marks, scale):
-    scores = masked_scores(qkv[:, 0], qkv[:, 1], marks, scale)
-    top = jnp.max(scores, axis=-1, keepdims=True)
-    weights = jnp.exp(scores - top)
-    total = jnp.sum(weights, axis=-1, keepdims=True)
-    probs = (weights / total).astype(LOW)
-    mixed = jnp.einsum("sqk,kse->qse", probs, qkv[:, 2], preferred_element_type=FULL)
-    return mixed.astype(LOW), top + jnp.log(total)
-
-
-def attend_back(qkv, marks, summary, grad_mixed, scale):
-    probs = jnp.exp(masked_scores(qkv[:, 0], qkv[:, 1], marks, scale) - summary)
-    low_probs = probs.astype(LOW)
-    grad_probs = jnp.einsum("qse,kse->sqk", grad_mixed, qkv[:, 2], preferred_element_type=FULL)
-    inner = jnp.sum(probs * grad_probs, axis=-1, keepdims=True)
-    grad_scores = (probs * (grad_probs - inner)).astype(LOW)
-    grad_q = jnp.einsum("sqk,kse->qse", grad_scores, qkv[:, 1], preferred_element_type=FULL)
-    grad_k = jnp.einsum("sqk,qse->kse", grad_scores, qkv[:, 0], preferred_element_type=FULL)
-    grad_v = jnp.einsum("sqk,qse->kse", low_probs, grad_mixed, preferred_element_type=FULL)
-    return grad_q * scale, grad_k * scale, grad_v
+VMEM_BYTES = 56 * 1024 * 1024
+
+
+def part_axes(part, gathered):
+    return [dim_at(part, 5 - a if gathered else a) for a in range(6)]
+
+
+def part_spec(part, gathered):
+    axes = part_axes(part, gathered)
+
+    def index(r, *_):
+        at = {("x", 3): r // 2, ("x", 1): r % 2}
+        return tuple(at.get(dim, 0) for dim in axes) + (0, 0)
+
+    return pl.BlockSpec(tuple(1 if dim[0] == "x" else 2 for dim in axes) + (64, 256), index)
+
+
+def part_places(part, gathered):
+    axes = part_axes(part, gathered)
+    places = []
+    for i in range(16):
+        bits = {("z", 3): i >> 3, ("z", 1): (i >> 2) & 1, ("y", 3): (i >> 1) & 1, ("y", 1): i & 1}
+        places.append(tuple(bits.get(dim, 0) for dim in axes))
+    return places
+
+
+def load_part(ref, part):
+    return jnp.concatenate([ref[place] for place in part_places(part, True)], 0)
+
+
+def store_part(ref, part, value):
+    for i, place in enumerate(part_places(part, False)):
+        ref[place] = value[i * 64 : (i + 1) * 64]
+
+
+def part_view(value):
+    return value.reshape((2,) * 6 + value.shape[-2:])
+
+
+PART_OUT = jax.ShapeDtypeStruct((2,) * 6 + (64, 256), LOW)
+
+
+def call(body, grid, in_specs, out_specs, out_shape, scratch, args, flops, scalars=()):
+    size = sum(value.size * value.dtype.itemsize for value in args)
+    size += sum(value.size * value.dtype.itemsize for value in out_shape)
+    return pl.pallas_call(
+        body,
+        grid_spec=pltpu.PrefetchScalarGridSpec(
+            num_scalar_prefetch=len(scalars),
+            grid=grid,
+            in_specs=in_specs,
+            out_specs=out_specs,
+            scratch_shapes=scratch,
+        ),
+        out_shape=out_shape,
+        compiler_params=pltpu.CompilerParams(vmem_limit_bytes=VMEM_BYTES),
+        cost_estimate=pl.CostEstimate(flops=flops, bytes_accessed=size, transcendentals=0),
+    )(*scalars, *args)
+
+
+def whole(shape):
+    return pl.BlockSpec(shape, lambda *_: (0,) * len(shape))
+
+
+def pick(value):
+    return pl.BlockSpec(
+        (1,) + value.shape[1:], lambda r, *_: (r,) + (0,) * (len(value.shape) - 1)
+    )
+
+
+def cross(left, right):
+    lane = lax.broadcasted_iota(jnp.int32, left.shape, 1) < 64
+    turned_left, turned_right = pltpu.roll(left, 64, 1), pltpu.roll(right, 64, 1)
+    return jnp.where(lane, left, turned_right), jnp.where(lane, turned_left, right)
+
+
+def split_rows(value):
+    n = value.shape[0] // 4
+    return (
+        jnp.concatenate([value[:n], value[2 * n : 3 * n]], 0),
+        jnp.concatenate([value[n : 2 * n], value[3 * n :]], 0),
+    )
+
+
+def join_rows(left, right):
+    n = left.shape[0] // 2
+    return jnp.concatenate([left[:n], right[:n], left[n:], right[n:]], 0)
+
+
+def accumulate(ref, r, value):
+    @pl.when(r == 0)
+    def _():
+        ref[...] = value
+
+    @pl.when(r > 0)
+    def _():
+        ref[...] += value
+
+
+def project_body(order, x, w_qk, w_vo, bias_q, bias_v, out):
+    qk = times(x[...], load_part(w_qk, 0))
+    v = times(x[...], load_part(w_vo, 1)[:, :128]) + bias_v[0]
+    kinds = (qk[:, :128] + bias_q[0], qk[:, 128:], v)
+    for i, value in enumerate(kinds):
+        for j, head in enumerate(cross(*split_rows(value))):
+            out[j, 0, :, i * 128 : (i + 1) * 128] = head.astype(LOW)
+
+
+def heads_spec(rows, lanes):
+    return pl.BlockSpec((2, 1, rows, lanes), lambda r, order: (0, order[r], 0, 0))
+
+
+def project(order, x, w_qk, w_vo, bias_q, bias_v):
+    m = x.shape[0]
+    (out,) = call(
+        project_body, (4,),
+        [whole(x.shape), part_spec(0, True), part_spec(1, True), pick(bias_q), pick(bias_v)],
+        [heads_spec(m // 2, 384)],
+        [jax.ShapeDtypeStruct((2, 4, m // 2, 384), LOW)], [],
+        (x, part_view(w_qk), part_view(w_vo), bias_q, bias_v), 2 * m * 1024 * 1536, (order,),
+    )
+    return out
+
+
+def tokens_of(ref, lanes):
+    left, right = cross(ref[0, 0, :, lanes].astype(FULL), ref[1, 0, :, lanes].astype(FULL))
+    return join_rows(left, right).astype(LOW)
+
+
+def mix_body(order, heads, w_vo, mixed_out, out):
+    r = pl.program_id(0)
+    mixed = tokens_of(heads, slice(0, 128))
+    mixed_out[0] = mixed
+    accumulate(out, r, times_t(mixed, load_part(w_vo, 1)[:, 128:]))
+
+
+def mix(order, heads, w_vo):
+    m = heads.shape[2] * 2
+    return call(
+        mix_body, (4,),
+        [heads_spec(m // 2, 128), part_spec(1, True)],
+        [pl.BlockSpec((1, m, 128), lambda r, *_: (r, 0, 0)), whole((m, 1024))],
+        [jax.ShapeDtypeStruct((4, m, 128), LOW), jax.ShapeDtypeStruct((m, 1024), FULL)], [],
+        (heads, part_view(w_vo)), 2 * m * 1024 * 512, (order,),
+    )
+
+
+def mix_back_body(order, x, w_vo, out):
+    value = times(x[...], load_part(w_vo, 1)[:, 128:])
+    for j, head in enumerate(cross(*split_rows(value))):
+        out[j, 0] = head.astype(LOW)
+
+
+def mix_back(order, x, w_vo):
+    m = x.shape[0]
+    (out,) = call(
+        mix_back_body, (4,),
+        [whole(x.shape), part_spec(1, True)],
+        [heads_spec(m // 2, 128)],
+        [jax.ShapeDtypeStruct((2, 4, m // 2, 128), LOW)], [],
+        (x, part_view(w_vo)), 2 * m * 1024 * 512, (order,),
+    )
+    return out
+
+
+def project_back_body(order, heads, x, spread, mixed, w_qk, w_vo, grad_qk, grad_vo, out):
+    r = pl.program_id(0)
+    q, k, v = [tokens_of(heads, slice(i * 128, (i + 1) * 128)) for i in range(3)]
+    qk = jnp.concatenate([q, k], 1)
+    store_part(grad_qk, 0, t_times(x[...], qk).astype(LOW))
+    grad_v = t_times(x[...], v).astype(LOW)
+    grad_o = t_times(spread[...], mixed[0]).astype(LOW)
+    store_part(grad_vo, 1, jnp.concatenate([grad_v, grad_o], 1))
+    terms = times_t(qk, load_part(w_qk, 0)) + times_t(v, load_part(w_vo, 1)[:, :128])
+    accumulate(out, r, terms)
+
+
+def project_back(order, heads, x, spread, mixed, w_qk, w_vo):
+    m = x.shape[0]
+    return call(
+        project_back_body, (4,),
+        [
+            heads_spec(m // 2, 384), whole(x.shape), whole(x.shape), pick(mixed),
+            part_spec(0, True), part_spec(1, True),
+        ],
+        [part_spec(0, False), part_spec(1, False), whole((m, 1024))],
+        [PART_OUT, PART_OUT, jax.ShapeDtypeStruct((m, 1024), FULL)], [],
+        (heads, x, spread, mixed, part_view(w_qk), part_view(w_vo)),
+        2 * m * 1024 * 3584, (order,),
+    )
+
+
+def feed_body(x, bias, u0, u1, d0, d1, hidden_out, active_out, out):
+    total = None
+    for j, (up, down) in enumerate(((u0, d0), (u1, d1))):
+        hidden = times(x[...], load_part(up, 2 + j)) + bias[0, j : j + 1]
+        hidden_out[0, j] = hidden
+        active = (hidden * (0.5 * (1.0 + lax.erf(hidden * ROOT_HALF)))).astype(LOW)
+        active_out[0, j] = active
+        term = times_t(active, load_part(down, 4 + j))
+        total = term if total is None else total + term
+    accumulate(out, pl.program_id(0), total)
+
+
+def feed(x, bias, weights):
+    m = x.shape[0]
+    block = pl.BlockSpec((1, 2, m, 256), lambda r: (r, 0, 0, 0))
+    return call(
+        feed_body, (4,),
+        [whole(x.shape), pick(bias)] + [part_spec(q, True) for q in range(2, 6)],
+        [block, block, whole((m, 1024))],
+        [
+            jax.ShapeDtypeStruct((4, 2, m, 256), FULL), jax.ShapeDtypeStruct((4, 2, m, 256), LOW),
+            jax.ShapeDtypeStruct((m, 1024), FULL),
+        ], [],
+        (x, bias) + tuple(part_view(w) for w in weights), 4 * m * 1024 * 2048,
+    )
+
+
+def feed_back_body(
+    spread, x, hidden, active, u0, u1, d0, d1, g_u0, g_u1, g_d0, g_d1, grad_bias, out
+):
+    total = None
+    for j, (up, down, g_up, g_down) in enumerate(((u0, d0, g_u0, g_d0), (u1, d1, g_u1, g_d1))):
+        value = hidden[0, j]
+        slope = 0.5 * (1.0 + lax.erf(value * ROOT_HALF))
+        slope += value * jnp.exp(-0.5 * value * value) * (1.0 / ROOT_TWOPI)
+        grad = times(spread[...], load_part(down, 4 + j)) * slope
+        grad_bias[0, j : j + 1] = jnp.sum(grad, axis=0, keepdims=True)
+        low = grad.astype(LOW)
+        store_part(g_down, 4 + j, t_times(spread[...], active[0, j]).astype(LOW))
+        store_part(g_up, 2 + j, t_times(x[...], low).astype(LOW))
+        term = times_t(low, load_part(up, 2 + j))
+        total = term if total is None else total + term
+    accumulate(out, pl.program_id(0), total)
+
+
+def feed_back(spread, x, hidden, active, weights):
+    m = x.shape[0]
+    return call(
+        feed_back_body, (4,),
+        [whole(x.shape), whole(x.shape), pick(hidden), pick(active)]
+        + [part_spec(q, True) for q in range(2, 6)],
+        [part_spec(q, False) for q in range(2, 6)]
+        + [pl.BlockSpec((1, 2, 256), lambda r: (r, 0, 0)), whole((m, 1024))],
+        [PART_OUT] * 4
+        + [jax.ShapeDtypeStruct((4, 2, 256), FULL), jax.ShapeDtypeStruct((m, 1024), FULL)], [],
+        (spread, x, hidden, active) + tuple(part_view(w) for w in weights), 8 * m * 1024 * 2048,
+    )
+
+
+def one_row(value, s):
+    lane = lax.broadcasted_iota(jnp.int32, value.shape, 1) // 64 == s
+    return jnp.where(lane, value, jnp.zeros_like(value))
+
+
+def scores_of(keys, query, mark_keys, mark_query, s):
+    scores = times_t(keys, one_row(query, s) * LOW(0.125))
+    same = mark_keys[:, s : s + 1] == mark_query[s : s + 1, :]
+    return jnp.where(same, scores, MASKED)
+
+
+def attend_body(query, keys, values, mark_keys, mark_query, out, summary):
+    turned = values[...].astype(FULL).T.astype(LOW)
+    results = []
+    for s in range(2):
+        scores = scores_of(keys[...], query[...], mark_keys, mark_query, s)
+        top = jnp.max(scores, axis=0, keepdims=True)
+        weights = jnp.exp(scores - top)
+        total = jnp.sum(weights, axis=0, keepdims=True)
+        probs = (weights * (1.0 / total)).astype(LOW)
+        results.append(times(turned[s * 64 : (s + 1) * 64], probs))
+        summary[s : s + 1] = top + jnp.log(total)
+    out[...] = jnp.concatenate(results, 0).T.astype(LOW)
+
+
+def attend(qkv, mark_keys, mark_query):
+    n = qkv.shape[0]
+    q = 384
+
+    return call(
+        attend_body, (n // q,),
+        [
+            pl.BlockSpec((q, 128), lambda i: (i, 0)), pl.BlockSpec((n, 128), lambda i: (0, 1)),
+            pl.BlockSpec((n, 128), lambda i: (0, 2)), whole((n, 2)),
+            pl.BlockSpec((2, q), lambda i: (0, i)),
+        ],
+        [pl.BlockSpec((q, 128), lambda i: (i, 0)), pl.BlockSpec((2, q), lambda i: (0, i))],
+        [jax.ShapeDtypeStruct((n, 128), LOW), jax.ShapeDtypeStruct((2, n), FULL)], [],
+        (qkv, qkv, qkv, mark_keys, mark_query), 8 * n * n * 128,
+    )
+
+
+def attend_back_body(
+    query, keys, values, grad_mixed, mark_keys, mark_query, summary, out, sums, sum_k, sum_v, sum_q
+):
+    i = pl.program_id(0)
+    n, q = keys.shape[0], query.shape[0]
+    turned = keys[...].astype(FULL).T.astype(LOW)
+    lane = lax.broadcasted_iota(jnp.int32, (n, 128), 1) < 64
+    grads_q, grads_k, grads_v = [], [], []
+    for s in range(2):
+        scores = scores_of(keys[...], query[...], mark_keys, mark_query, s)
+        probs = jnp.exp(scores - summary[s : s + 1])
+        grad_probs = times_t(values[...], one_row(grad_mixed[...], s))
+        inner = jnp.sum(probs * grad_probs, axis=0, keepdims=True)
+        low_probs = probs.astype(LOW)
+        grad_scores = (probs * (grad_probs - inner)).astype(LOW)
+        grads_v.append(times(low_probs, grad_mixed[...]))
+        grads_k.append(times(grad_scores, query[...]))
+        grads_q.append(times(turned[s * 64 : (s + 1) * 64], grad_scores))
+    accumulate(sum_k, i, jnp.where(lane, grads_k[0], grads_k[1]) * 0.125)
+    accumulate(sum_v, i, jnp.where(lane, grads_v[0], grads_v[1]))
+    grad_q = jnp.concatenate(grads_q, 0).T * 0.125
+    accumulate(sum_q, i, jnp.sum(grad_q, axis=0, keepdims=True))
+    out[pl.ds(pl.multiple_of(i * q, q), q), :128] = grad_q.astype(LOW)
+
+    @pl.when(i == pl.num_programs(0) - 1)
+    def _():
+        out[:, 128:256] = sum_k[...].astype(LOW)
+        out[:, 256:] = sum_v[...].astype(LOW)
+        sums[0:1] = sum_q[...]
+        sums[1:2] = jnp.sum(sum_v[...], axis=0, keepdims=True)
+
+
+def attend_back(qkv, grad_mixed, mark_keys, mark_query, summary):
+    n = qkv.shape[0]
+    q = 384
+    return call(
+        attend_back_body, (n // q,),
+        [
+            pl.BlockSpec((q, 128), lambda i: (i, 0)), pl.BlockSpec((n, 128), lambda i: (0, 1)),
+            pl.BlockSpec((n, 128), lambda i: (0, 2)), pl.BlockSpec((q, 128), lambda i: (i, 0)),
+            whole((n, 2)), pl.BlockSpec((2, q), lambda i: (0, i)),
+            pl.BlockSpec((2, q), lambda i: (0, i)),
+        ],
+        [whole((n, 384)), whole((2, 128))],
+        [jax.ShapeDtypeStruct((n, 384), LOW), jax.ShapeDtypeStruct((2, 128), FULL)],
+        [pltpu.VMEM((n, 128), FULL), pltpu.VMEM((n, 128), FULL), pltpu.VMEM((1, 128), FULL)],
+        (qkv, qkv, qkv, grad_mixed, mark_keys, mark_query, summary), 20 * n * n * 128,
+    )
 
 
 def trade(value):
     return lax.all_to_all(
         value, ("ctx", "tensor"), 0, 0, axis_index_groups=GROUPS, tiled=True
     )
-
-
-def to_heads(value, me_x):
-    rows = value.shape[0] // 4
-    kinds = value.shape[3]
-    value = take_absolute(value, me_x, 1).reshape(2, 2, rows, 4, 2, kinds, 64)
-    value = value.transpose(4, 3, 0, 2, 5, 1, 6).reshape(8, 2 * rows, kinds * 128)
-    return trade(value).reshape(16 * rows, kinds, 2, 64)
-
-
-def to_tokens(value, me_x):
-    rows = value.shape[0] // 16
-    kinds = value.shape[1]
-    value = trade(value.reshape(8, 2 * rows, kinds * 128))
-    value = value.reshape(2, 4, 2, rows, kinds, 2, 64).transpose(2, 5, 3, 1, 0, 4, 6)
-    return take_relative(value.reshape(4 * rows, 4, 2, kinds, 64), me_x, 1)
 
 
 def local(
@@ -195,7 +476,6 @@
     me_y, me_z = dp & 3, (dp >> 2) * 2 + z_lo
     rows = stream.shape[1]
     width = stream.shape[2]
-    scale = 64 ** (-0.5)
 
     vectors = jnp.concatenate(
         [norm_gains.reshape(-1), shifts.reshape(-1), qv_bias.reshape(-1), in_bias.reshape(-1)]
@@ -265,91 +545,67 @@
         mine = [value[:, layer] for value in parts]
         if layer:
             mine, weights[-1] = lax.optimization_barrier((mine, weights[-1]))
-        mine = gather_phases(mine, 4, 6)
-        weights.append([canonical(q, value) for q, value in enumerate(mine)])
+        weights.append(gather_phases(mine, 4, 6))
 
     marks = segments.reshape(2, 2, 2, 4, rows)
     marks = jnp.where(core == 0, marks, marks[:, :, ::-1])
     marks = marks.transpose(0, 1, 3, 2, 4).reshape(2, 16 * rows)
-    marks = marks[:, :, None] == marks[:, None, :]
+    marks_t = marks.T
+    order = jnp.stack([relative_x(me_x, r) for r in range(4)]).astype(jnp.int32)
 
     saved = []
     for layer in range(layers):
-        w_qk, w_vo, w_up0, w_up1, w_down0, w_down1 = weights[layer]
-        w_vo = w_vo.reshape(width, 4, 256)
-        w_v = w_vo[:, :, :128].reshape(width, 512)
-        w_o = w_vo[:, :, 128:].reshape(width, 512)
+        w_qk, w_vo = weights[layer][:2]
+        bias = pair[layer].reshape(2, 4, 1, 128)
         gathered = both(state.astype(LOW))
-        qk = times(gathered, w_qk).reshape(2 * tokens, 4, 2, 2, 64).transpose(0, 1, 3, 2, 4)
-        v = times(gathered, w_v).reshape(2 * tokens, 4, 2, 1, 64)
-        bias = jnp.stack([pair[layer, 0], jnp.zeros_like(pair[layer, 0])], 2)
-        packed = jnp.concatenate([qk + bias, v + pair[layer, 1][:, :, None]], 3).astype(LOW)
-        qkv = to_heads(packed, me_x)
-        mixed, summary = attend(qkv, marks, scale)
-        mixed = to_tokens(mixed[:, None], me_x).reshape(2 * tokens, 512)
-        attended = own_sum(times_t(mixed, w_o)) + shift[layer, 2]
+        qkv = trade(project(order, gathered, w_qk, w_vo, bias[0], bias[1]).reshape(8, 2 * rows, 384))
+        qkv = qkv.reshape(16 * rows, 384)
+        mixed, summary = attend(qkv, marks_t, marks)
+        mixed = trade(mixed.reshape(8, 2 * rows, 128)).reshape(2, 4, 2 * rows, 128)
+        mixed, attended = mix(order, mixed, w_vo)
+        attended = own_sum(attended) + shift[layer, 2]
         first, unit_one, inv_one = normalize(state + attended, gains[layer, 0], shift[layer, 0])
         gathered_two = both(first.astype(LOW))
-        hidden = [
-            times(gathered_two, w) + up[layer, :, j].reshape(1024)
-            for j, w in enumerate((w_up0, w_up1))
-        ]
-        active = [jax.nn.gelu(value, approximate=False).astype(LOW) for value in hidden]
-        down = own_sum(times_t(active[0], w_down0) + times_t(active[1], w_down1))
+        hidden, active, down = feed(gathered_two, up[layer], weights[layer][2:])
+        down = own_sum(down)
         state, unit_two, inv_two = normalize(
             first + down + shift[layer, 3], gains[layer, 1], shift[layer, 1]
         )
         saved.append(
             (gathered, qkv, summary, mixed, unit_one, inv_one, gathered_two, hidden, active,
-             unit_two, inv_two, w_v, w_o)
+             unit_two, inv_two)
         )
     result = absolute(state)
 
     grads = [None] * layers
     small = [None] * layers
     for layer in reversed(range(layers)):
-        w_qk, _, w_up0, w_up1, w_down0, w_down1 = weights[layer]
+        w_qk, w_vo = weights[layer][:2]
         (gathered, qkv, summary, mixed, unit_one, inv_one, gathered_two, hidden, active,
-         unit_two, inv_two, w_v, w_o) = saved[layer]
+         unit_two, inv_two) = saved[layer]
         grad_two, gain_two, shift_two = normalize_back(
             incoming, unit_two, inv_two, gains[layer, 1]
         )
         spread_two = both(grad_two.astype(LOW))
-        grad_down = [t_times(spread_two, value).astype(LOW) for value in active]
-        grad_hidden = [
-            times(spread_two, w) * gelu_slope(value)
-            for w, value in zip((w_down0, w_down1), hidden)
-        ]
-        grad_upbias = jnp.stack(
-            [jnp.sum(value, axis=0).reshape(4, 256) for value in grad_hidden], 1
-        )
-        low_hidden = [value.astype(LOW) for value in grad_hidden]
-        grad_up = [t_times(gathered_two, value).astype(LOW) for value in low_hidden]
-        grad_first = grad_two + own_sum(
-            times_t(low_hidden[0], w_up0) + times_t(low_hidden[1], w_up1)
-        )
+        *grad_feed, grad_upbias, grad_first = feed_back(
+            spread_two, gathered_two, hidden, active, weights[layer][2:]
+        )
+        grad_first = grad_two + own_sum(grad_first)
         grad_one, gain_one, shift_one = normalize_back(
             grad_first, unit_one, inv_one, gains[layer, 0]
         )
         spread_one = both(grad_one.astype(LOW))
-        grad_o = t_times(spread_one, mixed).astype(LOW)
-        grad_mixed = times(spread_one, w_o).astype(LOW).reshape(2 * tokens, 4, 2, 1, 64)
-        grad_mixed = to_heads(grad_mixed, me_x)[:, 0]
-        grad_q, grad_k, grad_v = attend_back(qkv, marks, summary, grad_mixed, scale)
-        grad_pair = jnp.stack([jnp.sum(grad_q, axis=(0, 1)), jnp.sum(grad_v, axis=(0, 1))])
-        low_packed = to_tokens(jnp.stack([grad_q, grad_k, grad_v], 1).astype(LOW), me_x)
-        low_qk = low_packed[:, :, :, :2].transpose(0, 1, 3, 2, 4).reshape(2 * tokens, 1024)
-        low_v = low_packed[:, :, :, 2].reshape(2 * tokens, 512)
-        grad_qk = t_times(gathered, low_qk).astype(LOW)
-        grad_v = t_times(gathered, low_v).astype(LOW)
-        incoming = grad_one + own_sum(times_t(low_qk, w_qk) + times_t(low_v, w_v))
-        grad_vo = jnp.concatenate(
-            [grad_v.reshape(width, 4, 128), grad_o.reshape(width, 4, 128)], 2
-        ).reshape(width, 1024)
+        grad_mixed = trade(mix_back(order, spread_one, w_vo).reshape(8, 2 * rows, 128))
+        grad_mixed = grad_mixed.reshape(16 * rows, 128)
+        low_packed, grad_pair = attend_back(qkv, grad_mixed, marks_t, marks, summary)
+        grad_pair = grad_pair.reshape(2, 2, 64).sum(1)
+        low_packed = trade(low_packed.reshape(8, 2 * rows, 384)).reshape(2, 4, 2 * rows, 384)
+        grad_qk, grad_vo, grad_x = project_back(
+            order, low_packed, gathered, spread_one, mixed, w_qk, w_vo
+        )
+        incoming = grad_one + own_sum(grad_x)
         grads[layer] = reduce_phases(
-            [by_phase(q, value) for q, value in enumerate([grad_qk, grad_vo] + grad_up + grad_down)],
-            0,
-            2,
+            [value.reshape(64, 64, 256) for value in [grad_qk, grad_vo] + grad_feed], 0, 2
         )
         small[layer] = (
             jnp.stack([gain_one, gain_two]),

time: 969 us -> 742 us (0.77)
  local copies, waits for them, and re-layouts: 332 us -> 76.1 us
  Pallas kernels: 0 us -> 135 us
  matrix products: 128 us -> 9.57 us
  other arithmetic: 102 us -> 113 us
    reshape x63 -> x3, local copies, waits for them, and re-layouts: 182 us -> 1.62 us  [the longest x2 1.52 us: local(): grad_pair = grad_pair.reshape(2, 2, 64).sum(1)]
    pallas_call x0 -> x16, Pallas kernels: none -> 135 us  [call(): pl.pallas_call(body, grid_spec=pltpu.PrefetchScalarGridSpec(num_scalar_pr...]
    dot_general x43 -> x1, matrix products: 80.3 us -> 0.98 us  [dot(): lax.dot_general(left, right, (dims, ((), ())), preferred_element_type=FULL)]
    dot_general x12 -> x0, matrix products: 38.6 us -> none  [the longest x2 12 us: attend_back(): jnp.einsum('qse,kse->sqk', grad_mixed, qkv[:, 2], preferred_element_type=...]
    unnamed x394 -> x186, local copies, waits for them, and re-layouts: 41.5 us -> 9.63 us
    ppermute x114, waiting for transfers between devices: 152 us -> 168 us  [swap(): return lax.ppermute(value, ALL, exchange_perm(axis, mask))]
    concatenate x42, other arithmetic: 35.1 us -> 51.3 us  [gather_phases(): parts = [jnp.concatenate([value, new], 0) for value, new in zip(parts, got)]]
    transpose x12 -> x1, local copies, waits for them, and re-layouts: 17.2 us -> 1.08 us  [local(): marks_t = marks.T]
  transfers between devices with their start and end apart: 124 -> 124, of which waited for: 33 -> 46; matrix products, arithmetic and copies ran while one was open for 46% -> 23% of each run, Pallas kernels for 0% -> 12%
where the time goes in v2:
time: 742 us; the launch traced here: 730 us
  waiting for transfers between devices  203 us (27%)
  starting transfers between devices  190 us (26%)
  Pallas kernels  135 us (18%)
  other arithmetic  113 us (15%)
  local copies, waits for them, and re-layouts  76.1 us (10%)
  matrix products  9.57 us (1%)
    ppermute x114, waiting for transfers between devices, swap(): return lax.ppermute(value, ALL, exchange_perm(axis, mask))  168 us
    ppermute x114, starting transfers between devices, swap(): return lax.ppermute(value, ALL, exchange_perm(axis, mask))  139 us
    pallas_call x16, Pallas kernels, call(): pl.pallas_call(body, grid_spec=pltpu.PrefetchScalarGridSpec(num_scalar_pr...  135 us
    concatenate x42, other arithmetic, gather_phases(): parts = [jnp.concatenate([value, new], 0) for value, new in zip(parts, got)]  51.3 us
    all_to_all x8, starting transfers between devices, trade(): lax.all_to_all(value, ('ctx', 'tensor'), 0, 0, axis_index_groups=GROUPS,...  33.8 us
    all_to_all x8, waiting for transfers between devices, trade(): lax.all_to_all(value, ('ctx', 'tensor'), 0, 0, axis_index_groups=GROUPS,...  29.6 us
    slice x12, local copies, waits for them, and re-layouts, reduce_phases(): value[:half].astype(FULL) + new.astype(FULL)  25.5 us
    convert_element_type x36, other arithmetic, reduce_phases(): (value[:half].astype(FULL) + new.astype(FULL)).astype(LOW)  22.7 us
  transfers between devices with their start and end apart: 124, of which 46 were waited for; matrix products, arithmetic and copies ran while one was open for 23% of the time, Pallas kernels for 12%

profile of v2, /device:TPU:1, one launch (start us, length us, event | category | flops | bytes accessed | tf_op | source)
XLA Modules:
  0.0 729.7 jit_solution(13964389820106367764)
XLA Ops:
  6.7 11.5 %all-to-all-start = ((bf16[128,2,256]{2,1,0:T(2,128)(2,1)}), bf16[128,2,256]{2,1,0:T(2,128)(2,1)S(1)}, u32[]{:S(2)}, u32[]{:S(2)}) async-start(bf16[128,2,256]{2,1,0:T(2,128)(2,1)} %reshape.560), calls=%async_computation | async-start | bytes 262144 | tf_op jit(solution)/shard_map/all_to_all | solution.py:484
  23.5 4.7 all-to-all-done
  61.6 6.1 collective-permute-done.5
  80.8 4.7 collective-permute-done.28
  91.3 3.7 collective-permute-done.36
  97.2 9.4 %collective-permute-done.27 = bf16[32,64,256]{2,1,0:T(8,128)(2,1)S(1)} collective-permute-done((bf16[32,64,256]{2,1,0:T(8,128)(2,1)S(1)}, bf16[32,64,256]{2,1,0:T(8,128)(2,1)S(1)}, u32[]{:S(2)}, u32[]{:S(2)}) %collective-permute-start.27) | collective-permute-done | bytes 1048608 | tf_op jit(solution)/shard_map/ppermute | solution.py:34
  128.4 6.1 shard_map.186
  134.5 4.6 all-to-all-start.1
  140.5 8.1 %all-to-all-done.1 = bf16[8,144,384]{2,1,0:T(8,128)(2,1)} async-done(((bf16[8,144,384]{2,1,0:T(8,128)(2,1)}), bf16[8,144,384]{2,1,0:T(8,128)(2,1)}, u32[]{:S(2)}, u32[]{:S(2)}) %all-to-all-start.1) | async-done | bytes 884768 | tf_op jit(solution)/shard_map/all_to_all | solution.py:465
  148.6 7.9 %shard_map.187 = (bf16[1152,128]{1,0:T(8,128)(2,1)}, f32[2,1152]{1,0:T(2,128)}) custom-call(bf16[1152,384]{1,0:T(8,128)(2,1)} %bitcast.35.query.keys.values, bf16[1152,384]{1,0:T(8,128)(2,1)} %bitcast.35.query.keys.values, bf16[1152,384]{1,0:T(8,128)(2,1)} %bitcast.35.query.keys.values, s32[1152,2]{1,0:T(8,128)} %copy.98.mark_keys, s32[2,1152]{1,0:T(2,128)} %copy-done.70), custom_call_target="tpu_custom_call" | custom-call | flops 1358954496 | bytes 2976768 | tf_op jit(solution)/shard_map/pallas_call | solution.py:166
  161.5 4.7 all-to-all-done.2
  166.9 5.4 shard_map.188
  173.5 13.4 %collective-permute-start.38 = (bf16[144,1024]{1,0:T(8,128)(2,1)S(1)}, bf16[144,1024]{1,0:T(8,128)(2,1)S(1)}, u32[]{:S(2)}, u32[]{:S(2)}) collective-permute-start(bf16[144,1024]{1,0:T(8,128)(2,1)S(1)} %slice.1048), channel_id=1, source_target_pairs={{0,4},{1,5},{2,6},{3,7},{4,0},{5,1},{6,2},{7,3},{8,12},{9,13},{10,... | collective-permute-start | bytes 884744 | tf_op jit(solution)/shard_map/ppermute | solution.py:34
  192.8 8.2 %shard_map.189 = (f32[4,2,288,256]{3,2,1,0:T(8,128)}, bf16[4,2,288,256]{3,2,1,0:T(8,128)(2,1)}, f32[288,1024]{1,0:T(8,128)}) custom-call(bf16[288,1024]{1,0:T(8,128)(2,1)} %pad_maximum_fusion.25.x, f32[4,2,256]{2,1,0:T(2,128)} %get-tuple-element.256.bias, bf16[2,2,2,2,2,2,64,256]{7,6,5,4,3,2,1,0:T(8,128)(2,1)} %bitcast.302, ...), custom_call_target="tpu_custom_call" | custom-call | flops 2415919104 | bytes 13705216 | tf_op jit(solution)/shard_map/pallas_call | solution.py:166
  214.3 17.9 %collective-permute-done.43 = bf16[32,64,256]{2,1,0:T(8,128)(2,1)S(1)} collective-permute-done((bf16[32,64,256]{2,1,0:T(8,128)(2,1)S(1)}, bf16[32,64,256]{2,1,0:T(8,128)(2,1)S(1)}, u32[]{:S(2)}, u32[]{:S(2)}) %collective-permute-start.43) | collective-permute-done | bytes 1048608 | tf_op jit(solution)/shard_map/ppermute | solution.py:34
  234.7 5.8 collective-permute-done.45
  244.2 5.9 shard_map.190
  250.1 4.2 all-to-all-start.3
  262.7 5.7 all-to-all-done.3
  268.4 7.9 %shard_map.191 = (bf16[1152,128]{1,0:T(8,128)(2,1)}, f32[2,1152]{1,0:T(2,128)}) custom-call(bf16[1152,384]{1,0:T(8,128)(2,1)} %bitcast.60.query.keys.values, bf16[1152,384]{1,0:T(8,128)(2,1)} %bitcast.60.query.keys.values, bf16[1152,384]{1,0:T(8,128)(2,1)} %bitcast.60.query.keys.values, s32[1152,2]{1,0:T(8,128)} %copy.98.mark_keys, s32[2,1152]{1,0:T(2,128)} %copy-done.70), custom_call_target="tpu_custom_call" | custom-call | flops 1358954496 | bytes 2976768 | tf_op jit(solution)/shard_map/pallas_call | solution.py:166
  276.3 4.1 all-to-all-start.4
  280.4 22.7 %collective-permute-done.52 = bf16[16,64,256]{2,1,0:T(8,128)(2,1)} collective-permute-done((bf16[16,64,256]{2,1,0:T(8,128)(2,1)S(1)}, bf16[16,64,256]{2,1,0:T(8,128)(2,1)}, u32[]{:S(2)}, u32[]{:S(2)}) %collective-permute-start.52) | collective-permute-done | bytes 524320 | tf_op jit(solution)/shard_map/ppermute | solution.py:34
  311.1 5.5 shard_map.192
  325.8 4.9 collective-permute-done.53
  338.2 8.2 %shard_map.193 = (f32[4,2,288,256]{3,2,1,0:T(8,128)}, bf16[4,2,288,256]{3,2,1,0:T(8,128)(2,1)}, f32[288,1024]{1,0:T(8,128)}) custom-call(bf16[288,1024]{1,0:T(8,128)(2,1)} %pad_maximum_fusion.27.x, f32[4,2,256]{2,1,0:T(2,128)} %get-tuple-element.255.bias, bf16[2,2,2,2,2,2,64,256]{7,6,5,4,3,2,1,0:T(8,128)(2,1)} %bitcast.310, ...), custom_call_target="tpu_custom_call" | custom-call | flops 2415919104 | bytes 13705216 | tf_op jit(solution)/shard_map/pallas_call | solution.py:166
  361.2 13.1 %shard_map.194 = (bf16[2,2,2,2,2,2,64,256]{7,6,5,4,3,2,1,0:T(8,128)(2,1)}, bf16[2,2,2,2,2,2,64,256]{7,6,5,4,3,2,1,0:T(8,128)(2,1)}, bf16[2,2,2,2,2,2,64,256]{7,6...) custom-call(bf16[288,1024]{1,0:T(8,128)(2,1)} %pad_maximum_fusion.28, ...), custom_call_target="tpu_custom_call" | custom-call | flops 4831838208 | bytes 22683648 | tf_op jit(solution)/shard_map/pallas_call | solution.py:166
  387.6 5.1 shard_map.195
  392.6 4.0 all-to-all-start.5
  401.9 8.2 %all-to-all-done.5 = bf16[8,144,128]{2,1,0:T(8,128)(2,1)S(1)} async-done(((bf16[8,144,128]{2,1,0:T(8,128)(2,1)}), bf16[8,144,128]{2,1,0:T(8,128)(2,1)S(1)}, u32[]{:S(2)}, u32[]{:S(2)}) %all-to-all-start.5) | async-done | bytes 294944 | tf_op jit(solution)/shard_map/all_to_all | solution.py:465
  410.8 11.8 %shard_map.196 = (bf16[1152,384]{1,0:T(8,128)(2,1)}, f32[2,128]{1,0:T(2,128)}) custom-call(bf16[1152,384]{1,0:T(8,128)(2,1)} %bitcast.60.query.keys.values, bf16[1152,384]{1,0:T(8,128)(2,1)} %bitcast.60.query.keys.values, bf16[1152,384]{1,0:T(8,128)(2,1)} %bitcast.60.query.keys.values, bf16[1152,128]{1,0:T(8,128)(2,1)} %bitcast.339, ...), custom_call_target="tpu_custom_call" | custom-call | flops 3397386240 | bytes 3862528 | tf_op jit(solution)/shard_map/pallas_call | solution.py:166
  422.6 4.2 all-to-all-start.6
  442.1 9.0 %collective-permute-done.84 = bf16[16,64,256]{2,1,0:T(8,128)(2,1)S(1)} collective-permute-done((bf16[16,64,256]{2,1,0:T(8,128)(2,1)S(1)}, bf16[16,64,256]{2,1,0:T(8,128)(2,1)S(1)}, u32[]{:S(2)}, u32[]{:S(2)}) %collective-permute-start.84) | collective-permute-done | bytes 524320 | tf_op jit(solution)/shard_map/ppermute | solution.py:34
  453.4 9.8 %shard_map.197 = (bf16[2,2,2,2,2,2,64,256]{7,6,5,4,3,2,1,0:T(8,128)(2,1)}, bf16[2,2,2,2,2,2,64,256]{7,6,5,4,3,2,1,0:T(8,128)(2,1)}, f32[288,1024]{1,0:T(8,128)}) custom-call(s32[4]{0:T(128)} %pad_add_fusion.order, bf16[2,4,144,384]{3,2,1,0:T(8,128)(2,1)} %bitcast.78.heads, bf16[288,1024]{1,0:T(8,128)(2,1)} %pad_maximum_fusion.26.x, ...), custom_call_target="tpu_custom_call" | custom-call | flops 2113929216 | bytes 11927552 | tf_op jit(solution)/shard_map/pallas_call | solution.py:166
  474.7 13.0 %shard_map.198 = (bf16[2,2,2,2,2,2,64,256]{7,6,5,4,3,2,1,0:T(8,128)(2,1)}, bf16[2,2,2,2,2,2,64,256]{7,6,5,4,3,2,1,0:T(8,128)(2,1)}, bf16[2,2,2,2,2,2,64,256]{7,6...) custom-call(bf16[288,1024]{1,0:T(8,128)(2,1)} %pad_maximum_fusion.30, ...), custom_call_target="tpu_custom_call" | custom-call | flops 4831838208 | bytes 22683648 | tf_op jit(solution)/shard_map/pallas_call | solution.py:166
  512.4 5.0 shard_map.199
  517.5 4.9 all-to-all-start.7
  530.2 11.8 %shard_map.200 = (bf16[1152,384]{1,0:T(8,128)(2,1)}, f32[2,128]{1,0:T(2,128)}) custom-call(bf16[1152,384]{1,0:T(8,128)(2,1)} %bitcast.35.query.keys.values, bf16[1152,384]{1,0:T(8,128)(2,1)} %bitcast.35.query.keys.values, bf16[1152,384]{1,0:T(8,128)(2,1)} %bitcast.35.query.keys.values, bf16[1152,128]{1,0:T(8,128)(2,1)} %bitcast.80.grad_mixed, ...), custom_call_target="tpu_custom_call" | custom-call | flops 3397386240 | bytes 3862528 | tf_op jit(solution)/shard_map/pallas_call | solution.py:166
  544.5 5.5 all-to-all-start.9
  569.3 10.0 %collective-permute-done.105 = bf16[32,64,256]{2,1,0:T(8,128)(2,1)S(1)} collective-permute-done((bf16[32,64,256]{2,1,0:T(8,128)(2,1)}, bf16[32,64,256]{2,1,0:T(8,128)(2,1)S(1)}, u32[]{:S(2)}, u32[]{:S(2)}) %collective-permute-start.105) | collective-permute-done | bytes 1048608 | tf_op jit(solution)/shard_map/ppermute | solution.py:34
  582.3 4.2 all-to-all-start.8
  603.4 9.8 %shard_map.201 = (bf16[2,2,2,2,2,2,64,256]{7,6,5,4,3,2,1,0:T(8,128)(2,1)}, bf16[2,2,2,2,2,2,64,256]{7,6,5,4,3,2,1,0:T(8,128)(2,1)}, f32[288,1024]{1,0:T(8,128)}) custom-call(s32[4]{0:T(128)} %pad_add_fusion.order, bf16[2,4,144,384]{3,2,1,0:T(8,128)(2,1)} %bitcast.82.heads, bf16[288,1024]{1,0:T(8,128)(2,1)} %pad_maximum_fusion.24.x, ...), custom_call_target="tpu_custom_call" | custom-call | flops 2113929216 | bytes 11927552 | tf_op jit(solution)/shard_map/pallas_call | solution.py:166
  629.5 4.7 collective-permute-done.86
  634.6 16.4 %collective-permute-done.94 = bf16[4,2,64,256]{3,2,0,1:T(8,128)(2,1)S(1)} collective-permute-done((bf16[4,2,64,256]{3,2,0,1:T(8,128)(2,1)S(1)}, bf16[4,2,64,256]{3,2,0,1:T(8,128)(2,1)S(1)}, u32[]{:S(2)}, u32[]{:S(2)}) %collective-permute-start.94) | collective-permute-done | bytes 262176 | tf_op jit(solution)/shard_map/ppermute | solution.py:34
  654.3 4.3 collective-permute-done.110
  673.3 6.5 collective-permute-done.66
  684.3 7.6 %collective-permute-done.69 = bf16[8,2,64,256]{3,2,0,1:T(8,128)(2,1)S(1)} collective-permute-done((bf16[8,2,64,256]{3,2,0,1:T(8,128)(2,1)S(1)}, bf16[8,2,64,256]{3,2,0,1:T(8,128)(2,1)S(1)}, u32[]{:S(2)}, u32[]{:S(2)}) %collective-permute-start.69) | collective-permute-done | bytes 524320 | tf_op jit(solution)/shard_map/ppermute | solution.py:34
  696.6 5.2 collective-permute-done.70
  712.8 9.8 %collective-permute-start.113 = (bf16[2,32,1536]{2,1,0:T(8,128)(2,1)S(1)}, bf16[2,32,1536]{2,1,0:T(8,128)(2,1)S(1)}, u32[]{:S(2)}, u32[]{:S(2)}) collective-permute-start(bf16[2,32,1536]{2,1,0:T(8,128)(2,1)S(1)} %dynamic-slice_bitcast_fusion), channel_id=1, source_target_pairs={{0,4},{1,5},{2,6},{3,7},{4,0},{5,1},{6,2},{7,3},{8,12},{9,13},{10,... | collective-permute-start | bytes 589832 | tf_op jit(solution)/shard_map/ppermute | solution.py:34
  (725 shorter events, 350.8 us)
Async XLA Ops:
  6.7 21.5 %all-to-all-start = ((bf16[128,2,256]{2,1,0:T(2,128)(2,1)}), bf16[128,2,256]{2,1,0:T(2,128)(2,1)S(1)}, u32[]{:S(2)}, u32[]{:S(2)}) async-start(bf16[128,2,256]{2,1,0:T(2,128)(2,1)} %reshape.560), calls=%async_computation | async-start | bytes 262144 | tf_op jit(solution)/shard_map/all_to_all | solution.py:484
  32.5 48.0 %collective-permute-start = (bf16[144,1024]{1,0:T(8,128)(2,1)}, bf16[144,1024]{1,0:T(8,128)(2,1)}, u32[]{:S(2)}, u32[]{:S(2)}) collective-permute-start(bf16[144,1024]{1,0:T(8,128)(2,1)} %slice.1049), channel_id=1, source_target_pairs={{0,4},{1,5},{2,6},{3,7},{4,0},{5,1},{6,2},{7,3},{8,12},{9,13},{10,... | collective-permute-start | bytes 884744 | tf_op jit(solution)/shard_map/ppermute | solution.py:34
  79.5 27.1 %collective-permute-start.27 = (bf16[32,64,256]{2,1,0:T(8,128)(2,1)S(1)}, bf16[32,64,256]{2,1,0:T(8,128)(2,1)S(1)}, u32[]{:S(2)}, u32[]{:S(2)}) collective-permute-start(bf16[32,64,256]{2,1,0:T(8,128)(2,1)S(1)} %pad_maximum_fusion.12), channel_id=1, source_target_pairs={{0,72},{1,73},{2,74},{3,75},{4,76},{5,77},{6,78},{7,79},{8,64},{9,... | collective-permute-start | bytes 3145736 | tf_op jit(solution)/shard_map/ppermute | solution.py:34
  87.7 26.5 %collective-permute-start.29 = (bf16[32,64,256]{2,1,0:T(8,128)(2,1)}, bf16[32,64,256]{2,1,0:T(8,128)(2,1)}, u32[]{:S(2)}, u32[]{:S(2)}) collective-permute-start(bf16[32,64,256]{2,1,0:T(8,128)(2,1)} %pad_maximum_fusion.13), channel_id=1, source_target_pairs={{0,1},{1,0},{2,3},{3,2},{4,5},{5,4},{6,7},{7,6},{8,9},{9,8},{10,11... | collective-permute-start | bytes 3145736 | tf_op jit(solution)/shard_map/ppermute | solution.py:34
  88.9 28.1 %collective-permute-start.31 = (bf16[32,64,256]{2,1,0:T(8,128)(2,1)}, bf16[32,64,256]{2,1,0:T(8,128)(2,1)}, u32[]{:S(2)}, u32[]{:S(2)}) collective-permute-start(bf16[32,64,256]{2,1,0:T(8,128)(2,1)} %pad_maximum_fusion.14), channel_id=1, source_target_pairs={{0,16},{1,17},{2,18},{3,19},{4,20},{5,21},{6,22},{7,23},{8,24},{9,... | collective-permute-start | bytes 3145736 | tf_op jit(solution)/shard_map/ppermute | solution.py:34
  90.1 29.9 %collective-permute-start.33 = (bf16[32,64,256]{2,1,0:T(8,128)(2,1)}, bf16[32,64,256]{2,1,0:T(8,128)(2,1)}, u32[]{:S(2)}, u32[]{:S(2)}) collective-permute-start(bf16[32,64,256]{2,1,0:T(8,128)(2,1)} %pad_maximum_fusion.15), channel_id=1, source_target_pairs={{0,8},{1,9},{2,10},{3,11},{4,12},{5,13},{6,14},{7,15},{8,0},{9,1},... | collective-permute-start | bytes 3145736 | tf_op jit(solution)/shard_map/ppermute | solution.py:34
  95.0 27.8 %collective-permute-start.35 = (bf16[32,64,256]{2,1,0:T(8,128)(2,1)}, bf16[32,64,256]{2,1,0:T(8,128)(2,1)}, u32[]{:S(2)}, u32[]{:S(2)}) collective-permute-start(bf16[32,64,256]{2,1,0:T(8,128)(2,1)} %pad_maximum_fusion.16), channel_id=1, source_target_pairs={{0,3},{1,2},{2,1},{3,0},{4,7},{5,6},{6,5},{7,4},{8,11},{9,10},{10,... | collective-permute-start | bytes 3145736 | tf_op jit(solution)/shard_map/ppermute | solution.py:34
  204.6 49.8 %collective-permute-start.48 = (bf16[16,64,256]{2,1,0:T(8,128)(2,1)S(1)}, bf16[16,64,256]{2,1,0:T(8,128)(2,1)}, u32[]{:S(2)}, u32[]{:S(2)}) collective-permute-start(bf16[16,64,256]{2,1,0:T(8,128)(2,1)S(1)} %get-tuple-element.71), channel_id=1, source_target_pairs={{0,1},{1,0},{2,3},{3,2},{4,5},{5,4},{6,7},{7,6},{8,9},{9,8},{10,11... | collective-permute-start | bytes 1572872 | tf_op jit(solution)/shard_map/ppermute | solution.py:34
  205.2 51.3 %collective-permute-start.50 = (bf16[16,64,256]{2,1,0:T(8,128)(2,1)S(1)}, bf16[16,64,256]{2,1,0:T(8,128)(2,1)}, u32[]{:S(2)}, u32[]{:S(2)}) collective-permute-start(bf16[16,64,256]{2,1,0:T(8,128)(2,1)S(1)} %get-tuple-element.72), channel_id=1, source_target_pairs={{0,16},{1,17},{2,18},{3,19},{4,20},{5,21},{6,22},{7,23},{8,24},{9,... | collective-permute-start | bytes 1572872 | tf_op jit(solution)/shard_map/ppermute | solution.py:34
  206.3 25.8 %collective-permute-start.43 = (bf16[32,64,256]{2,1,0:T(8,128)(2,1)S(1)}, bf16[32,64,256]{2,1,0:T(8,128)(2,1)S(1)}, u32[]{:S(2)}, u32[]{:S(2)}) collective-permute-start(bf16[32,64,256]{2,1,0:T(8,128)(2,1)S(1)} %pad_maximum_fusion.18), channel_id=1, source_target_pairs={{0,72},{1,73},{2,74},{3,75},{4,76},{5,77},{6,78},{7,79},{8,64},{9,... | collective-permute-start | bytes 3145736 | tf_op jit(solution)/shard_map/ppermute | solution.py:34
  210.6 29.9 %collective-permute-start.45 = (bf16[32,64,256]{2,1,0:T(8,128)(2,1)S(1)}, bf16[32,64,256]{2,1,0:T(8,128)(2,1)S(1)}, u32[]{:S(2)}, u32[]{:S(2)}) collective-permute-start(bf16[32,64,256]{2,1,0:T(8,128)(2,1)S(1)} %pad_maximum_fusion.19), channel_id=1, source_target_pairs={{0,1},{1,0},{2,3},{3,2},{4,5},{5,4},{6,7},{7,6},{8,9},{9,8},{10,11... | collective-permute-start | bytes 3145736 | tf_op jit(solution)/shard_map/ppermute | solution.py:34
  213.3 30.0 %collective-permute-start.41 = (bf16[144,1024]{1,0:T(8,128)(2,1)S(1)}, bf16[144,1024]{1,0:T(8,128)(2,1)S(1)}, u32[]{:S(2)}, u32[]{:S(2)}) collective-permute-start(bf16[144,1024]{1,0:T(8,128)(2,1)S(1)} %fusion.52), channel_id=1, source_target_pairs={{0,4},{1,5},{2,6},{3,7},{4,0},{5,1},{6,2},{7,3},{8,12},{9,13},{10,... | collective-permute-start | bytes 884744 | tf_op jit(solution)/shard_map/ppermute | solution.py:34
  256.4 62.6 %collective-permute-start.49 = (bf16[32,64,256]{2,1,0:T(8,128)(2,1)}, bf16[32,64,256]{2,1,0:T(8,128)(2,1)}, u32[]{:S(2)}, u32[]{:S(2)}) collective-permute-start(bf16[32,64,256]{2,1,0:T(8,128)(2,1)} %pad_maximum_fusion.20), channel_id=1, source_target_pairs={{0,16},{1,17},{2,18},{3,19},{4,20},{5,21},{6,22},{7,23},{8,24},{9,... | collective-permute-start | bytes 3145736 | tf_op jit(solution)/shard_map/ppermute | solution.py:34
  258.5 63.4 %collective-permute-start.51 = (bf16[32,64,256]{2,1,0:T(8,128)(2,1)}, bf16[32,64,256]{2,1,0:T(8,128)(2,1)}, u32[]{:S(2)}, u32[]{:S(2)}) collective-permute-start(bf16[32,64,256]{2,1,0:T(8,128)(2,1)} %pad_maximum_fusion.21), channel_id=1, source_target_pairs={{0,8},{1,9},{2,10},{3,11},{4,12},{5,13},{6,14},{7,15},{8,0},{9,1},... | collective-permute-start | bytes 3145736 | tf_op jit(solution)/shard_map/ppermute | solution.py:34
  259.9 43.2 %collective-permute-start.52 = (bf16[16,64,256]{2,1,0:T(8,128)(2,1)S(1)}, bf16[16,64,256]{2,1,0:T(8,128)(2,1)}, u32[]{:S(2)}, u32[]{:S(2)}) collective-permute-start(bf16[16,64,256]{2,1,0:T(8,128)(2,1)S(1)} %get-tuple-element.73), channel_id=1, source_target_pairs={{0,8},{1,9},{2,10},{3,11},{4,12},{5,13},{6,14},{7,15},{8,0},{9,1},... | collective-permute-start | bytes 1572872 | tf_op jit(solution)/shard_map/ppermute | solution.py:34
  260.0 47.1 %collective-permute-start.54 = (bf16[16,64,256]{2,1,0:T(8,128)(2,1)S(1)}, bf16[16,64,256]{2,1,0:T(8,128)(2,1)}, u32[]{:S(2)}, u32[]{:S(2)}) collective-permute-start(bf16[16,64,256]{2,1,0:T(8,128)(2,1)S(1)} %get-tuple-element.74), channel_id=1, source_target_pairs={{0,3},{1,2},{2,1},{3,0},{4,7},{5,6},{6,5},{7,4},{8,11},{9,10},{10,... | collective-permute-start | bytes 1572872 | tf_op jit(solution)/shard_map/ppermute | solution.py:34
  276.3 34.8 %all-to-all-start.4 = ((bf16[8,144,128]{2,1,0:T(8,128)(2,1)}), bf16[8,144,128]{2,1,0:T(8,128)(2,1)}, u32[]{:S(2)}, u32[]{:S(2)}) async-start(bf16[8,144,128]{2,1,0:T(8,128)(2,1)} %bitcast.338), calls=%async_computation.4 | async-start | bytes 589824 | tf_op jit(solution)/shard_map/all_to_all | solution.py:465
  305.2 25.5 %collective-permute-start.53 = (bf16[32,64,256]{2,1,0:T(8,128)(2,1)}, bf16[32,64,256]{2,1,0:T(8,128)(2,1)}, u32[]{:S(2)}, u32[]{:S(2)}) collective-permute-start(bf16[32,64,256]{2,1,0:T(8,128)(2,1)} %pad_maximum_fusion.22), channel_id=1, source_target_pairs={{0,3},{1,2},{2,1},{3,0},{4,7},{5,6},{6,5},{7,4},{8,11},{9,10},{10,... | collective-permute-start | bytes 3145736 | tf_op jit(solution)/shard_map/ppermute | solution.py:34
  309.3 25.2 %collective-permute-start.55 = (bf16[32,64,256]{2,1,0:T(8,128)(2,1)}, bf16[32,64,256]{2,1,0:T(8,128)(2,1)}, u32[]{:S(2)}, u32[]{:S(2)}) collective-permute-start(bf16[32,64,256]{2,1,0:T(8,128)(2,1)} %pad_maximum_fusion.23), channel_id=1, source_target_pairs={{0,48},{1,49},{2,50},{3,51},{4,52},{5,53},{6,54},{7,55},{8,56},{9,... | collective-permute-start | bytes 3145736 | tf_op jit(solution)/shard_map/ppermute | solution.py:34
  379.0 48.8 %collective-permute-start.83 = (bf16[32,64,256]{2,1,0:T(8,128)(2,1)}, bf16[32,64,256]{2,1,0:T(8,128)(2,1)}, u32[]{:S(2)}, u32[]{:S(2)}) collective-permute-start(bf16[32,64,256]{2,1,0:T(8,128)(2,1)} %bitcast.102), channel_id=1, source_target_pairs={{0,8},{1,9},{2,10},{3,11},{4,12},{5,13},{6,14},{7,15},{8,0},{9,1},... | collective-permute-start | bytes 3145736 | tf_op jit(solution)/shard_map/ppermute | solution.py:34
  380.6 52.3 %collective-permute-start.91 = (bf16[32,64,256]{2,1,0:T(8,128)(2,1)}, bf16[32,64,256]{2,1,0:T(8,128)(2,1)}, u32[]{:S(2)}, u32[]{:S(2)}) collective-permute-start(bf16[32,64,256]{2,1,0:T(8,128)(2,1)} %bitcast.109), channel_id=1, source_target_pairs={{0,3},{1,2},{2,1},{3,0},{4,7},{5,6},{6,5},{7,4},{8,11},{9,10},{10,... | collective-permute-start | bytes 3145736 | tf_op jit(solution)/shard_map/ppermute | solution.py:34
  384.8 51.8 %collective-permute-start.99 = (bf16[32,64,256]{2,1,0:T(8,128)(2,1)}, bf16[32,64,256]{2,1,0:T(8,128)(2,1)}, u32[]{:S(2)}, u32[]{:S(2)}) collective-permute-start(bf16[32,64,256]{2,1,0:T(8,128)(2,1)} %bitcast.116), channel_id=1, source_target_pairs={{0,48},{1,49},{2,50},{3,51},{4,52},{5,53},{6,54},{7,55},{8,56},{9,... | collective-permute-start | bytes 3145736 | tf_op jit(solution)/shard_map/ppermute | solution.py:34
  399.7 40.6 %collective-permute-start.107 = (bf16[32,64,256]{2,1,0:T(8,128)(2,1)}, bf16[32,64,256]{2,1,0:T(8,128)(2,1)}, u32[]{:S(2)}, u32[]{:S(2)}) collective-permute-start(bf16[32,64,256]{2,1,0:T(8,128)(2,1)} %bitcast.123), channel_id=1, source_target_pairs={{0,72},{1,73},{2,74},{3,75},{4,76},{5,77},{6,78},{7,79},{8,64},{9,... | collective-permute-start | bytes 3145736 | tf_op jit(solution)/shard_map/ppermute | solution.py:34
  422.6 30.8 %all-to-all-start.6 = ((bf16[8,144,384]{2,1,0:T(8,128)(2,1)}), bf16[8,144,384]{2,1,0:T(8,128)(2,1)}, u32[]{:S(2)}, u32[]{:S(2)}) async-start(bf16[8,144,384]{2,1,0:T(8,128)(2,1)} %bitcast.334), calls=%async_computation.6 | async-start | bytes 1769472 | tf_op jit(solution)/shard_map/all_to_all | solution.py:465
  429.9 21.2 %collective-permute-start.84 = (bf16[16,64,256]{2,1,0:T(8,128)(2,1)S(1)}, bf16[16,64,256]{2,1,0:T(8,128)(2,1)S(1)}, u32[]{:S(2)}, u32[]{:S(2)}) collective-permute-start(bf16[16,64,256]{2,1,0:T(8,128)(2,1)S(1)} %slice.849), channel_id=1, source_target_pairs={{0,3},{1,2},{2,1},{3,0},{4,7},{5,6},{6,5},{7,4},{8,11},{9,10},{10,... | collective-permute-start | bytes 1572872 | tf_op jit(solution)/shard_map/ppermute | solution.py:34
  470.8 35.6 %collective-permute-start.67 = (bf16[32,64,256]{2,1,0:T(8,128)(2,1)}, bf16[32,64,256]{2,1,0:T(8,128)(2,1)}, u32[]{:S(2)}, u32[]{:S(2)}) collective-permute-start(bf16[32,64,256]{2,1,0:T(8,128)(2,1)} %bitcast.88), channel_id=1, source_target_pairs={{0,1},{1,0},{2,3},{3,2},{4,5},{5,4},{6,7},{7,6},{8,9},{9,8},{10,11... | collective-permute-start | bytes 3145736 | tf_op jit(solution)/shard_map/ppermute | solution.py:34
  473.8 48.6 %collective-permute-start.75 = (bf16[32,64,256]{2,1,0:T(8,128)(2,1)}, bf16[32,64,256]{2,1,0:T(8,128)(2,1)}, u32[]{:S(2)}, u32[]{:S(2)}) collective-permute-start(bf16[32,64,256]{2,1,0:T(8,128)(2,1)} %bitcast.95), channel_id=1, source_target_pairs={{0,16},{1,17},{2,18},{3,19},{4,20},{5,21},{6,22},{7,23},{8,24},{9,... | collective-permute-start | bytes 3145736 | tf_op jit(solution)/shard_map/ppermute | solution.py:34
  492.2 63.7 %collective-permute-start.81 = (bf16[32,64,256]{2,1,0:T(8,128)(2,1)}, bf16[32,64,256]{2,1,0:T(8,128)(2,1)}, u32[]{:S(2)}, u32[]{:S(2)}) collective-permute-start(bf16[32,64,256]{2,1,0:T(8,128)(2,1)} %bitcast.99), channel_id=1, source_target_pairs={{0,8},{1,9},{2,10},{3,11},{4,12},{5,13},{6,14},{7,15},{8,0},{9,1},... | collective-permute-start | bytes 3145736 | tf_op jit(solution)/shard_map/ppermute | solution.py:34
  493.7 67.6 %collective-permute-start.89 = (bf16[32,64,256]{2,1,0:T(8,128)(2,1)}, bf16[32,64,256]{2,1,0:T(8,128)(2,1)}, u32[]{:S(2)}, u32[]{:S(2)}) collective-permute-start(bf16[32,64,256]{2,1,0:T(8,128)(2,1)} %bitcast.106), channel_id=1, source_target_pairs={{0,3},{1,2},{2,1},{3,0},{4,7},{5,6},{6,5},{7,4},{8,11},{9,10},{10,... | collective-permute-start | bytes 3145736 | tf_op jit(solution)/shard_map/ppermute | solution.py:34
  500.5 66.2 %collective-permute-start.97 = (bf16[32,64,256]{2,1,0:T(8,128)(2,1)}, bf16[32,64,256]{2,1,0:T(8,128)(2,1)}, u32[]{:S(2)}, u32[]{:S(2)}) collective-permute-start(bf16[32,64,256]{2,1,0:T(8,128)(2,1)} %bitcast.113), channel_id=1, source_target_pairs={{0,48},{1,49},{2,50},{3,51},{4,52},{5,53},{6,54},{7,55},{8,56},{9,... | collective-permute-start | bytes 3145736 | tf_op jit(solution)/shard_map/ppermute | solution.py:34
  509.7 40.2 %collective-permute-start.68 = (bf16[16,64,256]{2,1,0:T(8,128)(2,1)}, bf16[16,64,256]{2,1,0:T(8,128)(2,1)}, u32[]{:S(2)}, u32[]{:S(2)}) collective-permute-start(bf16[16,64,256]{2,1,0:T(8,128)(2,1)} %slice.825), channel_id=1, source_target_pairs={{0,16},{1,17},{2,18},{3,19},{4,20},{5,21},{6,22},{7,23},{8,24},{9,... | collective-permute-start | bytes 1572872 | tf_op jit(solution)/shard_map/ppermute | solution.py:34
  525.9 28.6 %collective-permute-start.76 = (bf16[16,64,256]{2,1,0:T(8,128)(2,1)}, bf16[16,64,256]{2,1,0:T(8,128)(2,1)}, u32[]{:S(2)}, u32[]{:S(2)}) collective-permute-start(bf16[16,64,256]{2,1,0:T(8,128)(2,1)} %slice.837), channel_id=1, source_target_pairs={{0,8},{1,9},{2,10},{3,11},{4,12},{5,13},{6,14},{7,15},{8,0},{9,1},... | collective-permute-start | bytes 1572872 | tf_op jit(solution)/shard_map/ppermute | solution.py:34
  544.5 37.8 %all-to-all-start.9 = ((f32[128,1,512]{2,1,0:T(1,128)}), f32[128,1,512]{2,1,0:T(1,128)S(1)}, u32[]{:S(2)}, u32[]{:S(2)}) async-start(f32[128,1,512]{2,1,0:T(1,128)} %all_to_all.43), calls=%async_computation.9 | async-start | bytes 524288 | tf_op jit(solution)/shard_map/all_to_all | solution.py:648
  550.0 29.3 %collective-permute-start.105 = (bf16[32,64,256]{2,1,0:T(8,128)(2,1)}, bf16[32,64,256]{2,1,0:T(8,128)(2,1)S(1)}, u32[]{:S(2)}, u32[]{:S(2)}) collective-permute-start(bf16[32,64,256]{2,1,0:T(8,128)(2,1)} %bitcast.330), channel_id=1, source_target_pairs={{0,72},{1,73},{2,74},{3,75},{4,76},{5,77},{6,78},{7,79},{8,64},{9,... | collective-permute-start | bytes 3145736 | tf_op jit(solution)/shard_map/ppermute | solution.py:34
  558.8 30.9 %collective-permute-start.82 = (bf16[16,64,256]{2,1,0:T(8,128)(2,1)}, bf16[16,64,256]{2,1,0:T(8,128)(2,1)}, u32[]{:S(2)}, u32[]{:S(2)}) collective-permute-start(bf16[16,64,256]{2,1,0:T(8,128)(2,1)} %slice.847), channel_id=1, source_target_pairs={{0,3},{1,2},{2,1},{3,0},{4,7},{5,6},{6,5},{7,4},{8,11},{9,10},{10,... | collective-permute-start | bytes 1572872 | tf_op jit(solution)/shard_map/ppermute | solution.py:34
  563.8 30.8 %collective-permute-start.90 = (bf16[16,64,256]{2,1,0:T(8,128)(2,1)}, bf16[16,64,256]{2,1,0:T(8,128)(2,1)}, u32[]{:S(2)}, u32[]{:S(2)}) collective-permute-start(bf16[16,64,256]{2,1,0:T(8,128)(2,1)} %slice.859), channel_id=1, source_target_pairs={{0,48},{1,49},{2,50},{3,51},{4,52},{5,53},{6,54},{7,55},{8,56},{9,... | collective-permute-start | bytes 1572872 | tf_op jit(solution)/shard_map/ppermute | solution.py:34
  569.2 28.0 %collective-permute-start.98 = (bf16[16,64,256]{2,1,0:T(8,128)(2,1)}, bf16[16,64,256]{2,1,0:T(8,128)(2,1)}, u32[]{:S(2)}, u32[]{:S(2)}) collective-permute-start(bf16[16,64,256]{2,1,0:T(8,128)(2,1)} %slice.871), channel_id=1, source_target_pairs={{0,72},{1,73},{2,74},{3,75},{4,76},{5,77},{6,78},{7,79},{8,64},{9,... | collective-permute-start | bytes 1572872 | tf_op jit(solution)/shard_map/ppermute | solution.py:34
  580.8 19.7 %collective-permute-start.106 = (bf16[16,64,256]{2,1,0:T(8,128)(2,1)}, bf16[16,64,256]{2,1,0:T(8,128)(2,1)}, u32[]{:S(2)}, u32[]{:S(2)}) collective-permute-start(bf16[16,64,256]{2,1,0:T(8,128)(2,1)} %slice.883), channel_id=1, source_target_pairs={{0,1},{1,0},{2,3},{3,2},{4,5},{5,4},{6,7},{7,6},{8,9},{9,8},{10,11... | collective-permute-start | bytes 1572872 | tf_op jit(solution)/shard_map/ppermute | solution.py:34
  582.3 21.1 %all-to-all-start.8 = ((bf16[8,144,384]{2,1,0:T(8,128)(2,1)}), bf16[8,144,384]{2,1,0:T(8,128)(2,1)}, u32[]{:S(2)}, u32[]{:S(2)}) async-start(bf16[8,144,384]{2,1,0:T(8,128)(2,1)} %bitcast.333), calls=%async_computation.8 | async-start | bytes 1769472 | tf_op jit(solution)/shard_map/all_to_all | solution.py:465
  592.0 28.5 %collective-permute-start.85 = (bf16[8,2,64,256]{3,2,0,1:T(8,128)(2,1)}, bf16[8,2,64,256]{3,2,0,1:T(8,128)(2,1)}, u32[]{:S(2)}, u32[]{:S(2)}) collective-permute-start(bf16[8,2,64,256]{3,2,0,1:T(8,128)(2,1)} %pad_maximum_fusion.35), channel_id=1, source_target_pairs={{0,48},{1,49},{2,50},{3,51},{4,52},{5,53},{6,54},{7,55},{8,56},{9,... | collective-permute-start | bytes 1572872 | tf_op jit(solution)/shard_map/ppermute | solution.py:34
  596.7 26.1 %collective-permute-start.93 = (bf16[8,2,64,256]{3,2,0,1:T(8,128)(2,1)}, bf16[8,2,64,256]{3,2,0,1:T(8,128)(2,1)}, u32[]{:S(2)}, u32[]{:S(2)}) collective-permute-start(bf16[8,2,64,256]{3,2,0,1:T(8,128)(2,1)} %pad_maximum_fusion.34), channel_id=1, source_target_pairs={{0,72},{1,73},{2,74},{3,75},{4,76},{5,77},{6,78},{7,79},{8,64},{9,... | collective-permute-start | bytes 1572872 | tf_op jit(solution)/shard_map/ppermute | solution.py:34
  599.4 26.3 %collective-permute-start.101 = (bf16[8,2,64,256]{3,2,0,1:T(8,128)(2,1)}, bf16[8,2,64,256]{3,2,0,1:T(8,128)(2,1)}, u32[]{:S(2)}, u32[]{:S(2)}) collective-permute-start(bf16[8,2,64,256]{3,2,0,1:T(8,128)(2,1)} %pad_maximum_fusion.33), channel_id=1, source_target_pairs={{0,1},{1,0},{2,3},{3,2},{4,5},{5,4},{6,7},{7,6},{8,9},{9,8},{10,11... | collective-permute-start | bytes 1572872 | tf_op jit(solution)/shard_map/ppermute | solution.py:34
  603.4 24.1 %collective-permute-start.109 = (bf16[8,2,64,256]{3,2,0,1:T(8,128)(2,1)}, bf16[8,2,64,256]{3,2,0,1:T(8,128)(2,1)}, u32[]{:S(2)}, u32[]{:S(2)}) collective-permute-start(bf16[8,2,64,256]{3,2,0,1:T(8,128)(2,1)} %pad_maximum_fusion.32), channel_id=1, source_target_pairs={{0,16},{1,17},{2,18},{3,19},{4,20},{5,21},{6,22},{7,23},{8,24},{9,... | collective-permute-start | bytes 1572872 | tf_op jit(solution)/shard_map/ppermute | solution.py:34
  614.4 108.3 %collective-permute-start.64 = (bf16[144,1024]{1,0:T(8,128)(2,1)S(1)}, bf16[144,1024]{1,0:T(8,128)(2,1)S(1)}, u32[]{:S(2)}, u32[]{:S(2)}) collective-permute-start(bf16[144,1024]{1,0:T(8,128)(2,1)S(1)} %slice.1041), channel_id=1, source_target_pairs={{0,4},{1,5},{2,6},{3,7},{4,0},{5,1},{6,2},{7,3},{8,12},{9,13},{10,... | collective-permute-start | bytes 884744 | tf_op jit(solution)/shard_map/ppermute | solution.py:34
  620.6 48.3 %collective-permute-start.65 = (bf16[32,64,256]{2,1,0:T(8,128)(2,1)S(1)}, bf16[32,64,256]{2,1,0:T(8,128)(2,1)S(1)}, u32[]{:S(2)}, u32[]{:S(2)}) collective-permute-start(bf16[32,64,256]{2,1,0:T(8,128)(2,1)S(1)} %bitcast.332), channel_id=1, source_target_pairs={{0,1},{1,0},{2,3},{3,2},{4,5},{5,4},{6,7},{7,6},{8,9},{9,8},{10,11... | collective-permute-start | bytes 3145736 | tf_op jit(solution)/shard_map/ppermute | solution.py:34
  622.8 47.5 %collective-permute-start.73 = (bf16[32,64,256]{2,1,0:T(8,128)(2,1)S(1)}, bf16[32,64,256]{2,1,0:T(8,128)(2,1)S(1)}, u32[]{:S(2)}, u32[]{:S(2)}) collective-permute-start(bf16[32,64,256]{2,1,0:T(8,128)(2,1)S(1)} %bitcast.331), channel_id=1, source_target_pairs={{0,16},{1,17},{2,18},{3,19},{4,20},{5,21},{6,22},{7,23},{8,24},{9,... | collective-permute-start | bytes 3145736 | tf_op jit(solution)/shard_map/ppermute | solution.py:34
  627.5 23.5 %collective-permute-start.94 = (bf16[4,2,64,256]{3,2,0,1:T(8,128)(2,1)S(1)}, bf16[4,2,64,256]{3,2,0,1:T(8,128)(2,1)S(1)}, u32[]{:S(2)}, u32[]{:S(2)}) collective-permute-start(bf16[4,2,64,256]{3,2,0,1:T(8,128)(2,1)S(1)} %slice.865), channel_id=1, source_target_pairs={{0,1},{1,0},{2,3},{3,2},{4,5},{5,4},{6,7},{7,6},{8,9},{9,8},{10,11... | collective-permute-start | bytes 786440 | tf_op jit(solution)/shard_map/ppermute | solution.py:34
  634.3 19.0 %collective-permute-start.102 = (bf16[4,2,64,256]{3,2,0,1:T(8,128)(2,1)S(1)}, bf16[4,2,64,256]{3,2,0,1:T(8,128)(2,1)S(1)}, u32[]{:S(2)}, u32[]{:S(2)}) collective-permute-start(bf16[4,2,64,256]{3,2,0,1:T(8,128)(2,1)S(1)} %slice.877), channel_id=1, source_target_pairs={{0,16},{1,17},{2,18},{3,19},{4,20},{5,21},{6,22},{7,23},{8,24},{9,... | collective-permute-start | bytes 786440 | tf_op jit(solution)/shard_map/ppermute | solution.py:34
  (153 other events, 1294.2 us)

commit v3 on v2

--- a/solution.py
+++ b/solution.py
@@ -1,3 +1,5 @@
+import functools
+
 import jax
 import jax.numpy as jnp
 from jax import lax
@@ -13,8 +15,13 @@
 LOW = jnp.bfloat16
 FULL = jnp.float32
 
-DIMS = (("x", 1), ("y", 1), ("z", 1), ("x", 3), ("y", 3), ("z", 3))
-CANON = (("z", 3), ("z", 1), ("y", 3), ("y", 1), ("x", 3), ("x", 1))
+X1, X3, Y1, Y3, Z1, Z3 = ("x", 1), ("x", 3), ("y", 1), ("y", 3), ("z", 1), ("z", 3)
+ORDERS = (
+    (X1, Y3, X3, Z3, Y1, Z1),
+    (Y1, X1, Z3, X3, Z1, Y3),
+    (X3, Z1, X1, Y1, Y3, Z3),
+    (Z1, X3, Y3, X1, Z3, Y1),
+)
 GROUPS = [[(zl * 2 + c) * 4 + x for zl in range(2) for x in range(4)] for c in range(2)]
 
 
@@ -34,26 +41,39 @@
     return lax.ppermute(value, ALL, exchange_perm(axis, mask))
 
 
-def dim_at(part, phase):
-    return DIMS[(part + phase) % 6]
-
-
-def gather_phases(parts, first, last):
-    for phase in range(first, last):
-        got = [swap(value, *dim_at(q, phase)) for q, value in enumerate(parts)]
+def gather_early(parts):
+    for phase in range(4):
+        got = [swap(value, *ORDERS[k][phase]) for k, value in enumerate(parts)]
         parts = [jnp.concatenate([value, new], 0) for value, new in zip(parts, got)]
     return parts
 
 
-def reduce_phases(parts, first, last):
-    for phase in range(first, last):
-        half = parts[0].shape[0] // 2
-        got = [swap(value[half:], *dim_at(q, phase)) for q, value in enumerate(parts)]
-        parts = [
-            (value[:half].astype(FULL) + new.astype(FULL)).astype(LOW)
-            for value, new in zip(parts, got)
-        ]
-    return parts
+def gather_late(parts):
+    near = [swap(value, *ORDERS[k][4]) for k, value in enumerate(parts)]
+    far = [swap(value, *ORDERS[k][5]) for k, value in enumerate(parts)]
+    both_far = [swap(value, *ORDERS[k][5]) for k, value in enumerate(near)]
+    return [list(four) for four in zip(parts, near, far, both_far)]
+
+
+def add_low(left, right):
+    return (left.astype(FULL) + right.astype(FULL)).astype(LOW)
+
+
+def reduce_first(pairs, orders):
+    parts = [add_low(kept, swap(sent, *ORDERS[k][5])) for k, (kept, sent) in zip(orders, pairs)]
+    return reduce_phase(parts, orders, 1)
+
+
+def reduce_phase(parts, orders, phase):
+    half = parts[0].shape[0] // 2
+    got = [swap(value[half:], *ORDERS[k][5 - phase]) for k, value in zip(orders, parts)]
+    return [add_low(value[:half], new) for value, new in zip(parts, got)]
+
+
+def reduce_rest(parts, orders):
+    for phase in range(2, 6):
+        parts = reduce_phase(parts, orders, phase)
+    return [value[0] for value in parts]
 
 
 def relative_x(me_x, r):
@@ -121,43 +141,108 @@
 VMEM_BYTES = 56 * 1024 * 1024
 
 
-def part_axes(part, gathered):
-    return [dim_at(part, 5 - a if gathered else a) for a in range(6)]
-
-
-def part_spec(part, gathered):
-    axes = part_axes(part, gathered)
+ZY = (Z3, Z1, Y3, Y1)
+
+
+class Exchanged:
+    def __init__(self, k, pieces, columns):
+        self.k = k
+        self.arrays = [value.reshape((2,) * 4 + value.shape[1:]) for value in pieces]
+        axes = ORDERS[k][3::-1]
+
+        def index(r, *_):
+            at = {X3: r // 2, X1: r % 2}
+            return tuple(at.get(dim, 0) for dim in axes) + (0, 0)
+
+        shape = tuple(1 if dim[0] == "x" else 2 for dim in axes) + (64, columns)
+        self.specs = [pl.BlockSpec(shape, index)] * 4
+
+    def load(self, info, refs):
+        rows = []
+        for i in range(16):
+            bits = dict(zip(ZY, (i >> 3, (i >> 2) & 1, (i >> 1) & 1, i & 1)))
+            piece = 2 * bits[ORDERS[self.k][5]] + bits[ORDERS[self.k][4]]
+            at = tuple(bits.get(dim, 0) for dim in ORDERS[self.k][3::-1])
+            rows.append(refs[piece][at])
+        return jnp.concatenate(rows, 0)
+
+
+class Gathered:
+    def __init__(self, array, base, columns, step):
+        self.arrays = [array]
+
+        def index(r, info):
+            return (0, 0, info[r], 0, base + info[4] * step)
+
+        self.specs = [pl.BlockSpec((16, 2, 1, 32, columns), index)]
+
+    def load(self, info, refs):
+        (ref,) = refs
+        return jnp.concatenate(
+            [ref[info[5 + i], half, 0] for i in range(16) for half in range(2)], 0
+        )
+
+
+class Grads:
+    def __init__(self, k, width, at):
+        self.k, self.width, self.at = k, width, at
+
+    def store(self, refs, value):
+        for i in range(16):
+            bits = dict(zip(ZY, (i >> 3, (i >> 2) & 1, (i >> 1) & 1, i & 1)))
+            place = tuple(bits.get(dim, 0) for dim in ORDERS[self.k][4::-1])
+            place += (slice(None), slice(self.at, self.at + value.shape[1]))
+            refs[bits[ORDERS[self.k][5]]][place] = value[i * 64 : (i + 1) * 64]
+
+
+def grad_spec(sink):
+    axes = ORDERS[sink.k][4::-1]
 
     def index(r, *_):
-        at = {("x", 3): r // 2, ("x", 1): r % 2}
+        at = {X3: r // 2, X1: r % 2}
         return tuple(at.get(dim, 0) for dim in axes) + (0, 0)
 
-    return pl.BlockSpec(tuple(1 if dim[0] == "x" else 2 for dim in axes) + (64, 256), index)
-
-
-def part_places(part, gathered):
-    axes = part_axes(part, gathered)
-    places = []
-    for i in range(16):
-        bits = {("z", 3): i >> 3, ("z", 1): (i >> 2) & 1, ("y", 3): (i >> 1) & 1, ("y", 1): i & 1}
-        places.append(tuple(bits.get(dim, 0) for dim in axes))
-    return places
-
-
-def load_part(ref, part):
-    return jnp.concatenate([ref[place] for place in part_places(part, True)], 0)
-
-
-def store_part(ref, part, value):
-    for i, place in enumerate(part_places(part, False)):
-        ref[place] = value[i * 64 : (i + 1) * 64]
-
-
-def part_view(value):
-    return value.reshape((2,) * 6 + value.shape[-2:])
-
-
-PART_OUT = jax.ShapeDtypeStruct((2,) * 6 + (64, 256), LOW)
+    shape = tuple(1 if dim[0] == "x" else 2 for dim in axes) + (64, sink.width)
+    return [pl.BlockSpec(shape, index)] * 2
+
+
+def grad_outs(sinks):
+    first = [sink for sink in sinks if sink.at == 0]
+    specs = [spec for sink in first for spec in grad_spec(sink)]
+    shapes = [
+        jax.ShapeDtypeStruct((2,) * 5 + (64, sink.width), LOW) for sink in first for _ in range(2)
+    ]
+    return specs, shapes
+
+
+def grad_refs(sinks, refs):
+    pairs, at = [], -2
+    for sink in sinks:
+        at += 2 if sink.at == 0 else 0
+        pairs.append(refs[at : at + 2])
+    return pairs
+
+
+def take_refs(weights, refs):
+    groups = []
+    for weight in weights:
+        groups.append(refs[: len(weight.arrays)])
+        refs = refs[len(weight.arrays) :]
+    return groups, refs
+
+
+APART = [Grads(k, 128, 0) for k in range(4)]
+PAIRED = [Grads(k, 256, at) for k in (0, 2) for at in (0, 128)]
+FEED = [Grads(k, 512, at) for k in (0, 2) for at in (0, 256)]
+
+
+def halves(refs):
+    pairs = zip(refs[::2], refs[1::2])
+    return [tuple(v.reshape((32,) + v.shape[-2:]) for v in pair) for pair in pairs]
+
+
+def joined(weights, field):
+    return [entry for weight in weights for entry in getattr(weight, field)]
 
 
 def call(body, grid, in_specs, out_specs, out_shape, scratch, args, flops, scalars=()):
@@ -217,11 +302,10 @@
         ref[...] += value
 
 
-def project_body(order, x, w_qk, w_vo, bias_q, bias_v, out):
-    qk = times(x[...], load_part(w_qk, 0))
-    v = times(x[...], load_part(w_vo, 1)[:, :128]) + bias_v[0]
-    kinds = (qk[:, :128] + bias_q[0], qk[:, 128:], v)
-    for i, value in enumerate(kinds):
+def project_body(weights, info, x, *refs):
+    groups, (bias_q, bias_v, out) = take_refs(weights, refs)
+    q, k, v = [times(x[...], w.load(info, group)) for w, group in zip(weights, groups)]
+    for i, value in enumerate((q + bias_q[0], k, v + bias_v[0])):
         for j, head in enumerate(cross(*split_rows(value))):
             out[j, 0, :, i * 128 : (i + 1) * 128] = head.astype(LOW)
 
@@ -230,14 +314,15 @@
     return pl.BlockSpec((2, 1, rows, lanes), lambda r, order: (0, order[r], 0, 0))
 
 
-def project(order, x, w_qk, w_vo, bias_q, bias_v):
+def project(order, x, weights, bias_q, bias_v):
     m = x.shape[0]
+    weights = weights[:3]
     (out,) = call(
-        project_body, (4,),
-        [whole(x.shape), part_spec(0, True), part_spec(1, True), pick(bias_q), pick(bias_v)],
+        functools.partial(project_body, weights), (4,),
+        [whole(x.shape)] + joined(weights, "specs") + [pick(bias_q), pick(bias_v)],
         [heads_spec(m // 2, 384)],
         [jax.ShapeDtypeStruct((2, 4, m // 2, 384), LOW)], [],
-        (x, part_view(w_qk), part_view(w_vo), bias_q, bias_v), 2 * m * 1024 * 1536, (order,),
+        [x] + joined(weights, "arrays") + [bias_q, bias_v], 2 * m * 1024 * 1536, (order,),
     )
     return out
 
@@ -247,126 +332,129 @@
     return join_rows(left, right).astype(LOW)
 
 
-def mix_body(order, heads, w_vo, mixed_out, out):
-    r = pl.program_id(0)
+def mix_body(weight, info, heads, *refs):
+    (group,), (mixed_out, out) = take_refs([weight], refs)
     mixed = tokens_of(heads, slice(0, 128))
     mixed_out[0] = mixed
-    accumulate(out, r, times_t(mixed, load_part(w_vo, 1)[:, 128:]))
-
-
-def mix(order, heads, w_vo):
+    accumulate(out, pl.program_id(0), times_t(mixed, weight.load(info, group)))
+
+
+def mix(order, heads, weight):
     m = heads.shape[2] * 2
     return call(
-        mix_body, (4,),
-        [heads_spec(m // 2, 128), part_spec(1, True)],
+        functools.partial(mix_body, weight), (4,),
+        [heads_spec(m // 2, 128)] + weight.specs,
         [pl.BlockSpec((1, m, 128), lambda r, *_: (r, 0, 0)), whole((m, 1024))],
         [jax.ShapeDtypeStruct((4, m, 128), LOW), jax.ShapeDtypeStruct((m, 1024), FULL)], [],
-        (heads, part_view(w_vo)), 2 * m * 1024 * 512, (order,),
-    )
-
-
-def mix_back_body(order, x, w_vo, out):
-    value = times(x[...], load_part(w_vo, 1)[:, 128:])
+        [heads] + weight.arrays, 2 * m * 1024 * 512, (order,),
+    )
+
+
+def mix_back_body(weight, info, x, *refs):
+    (group,), (out,) = take_refs([weight], refs)
+    value = times(x[...], weight.load(info, group))
     for j, head in enumerate(cross(*split_rows(value))):
         out[j, 0] = head.astype(LOW)
 
 
-def mix_back(order, x, w_vo):
+def mix_back(order, x, weight):
     m = x.shape[0]
     (out,) = call(
-        mix_back_body, (4,),
-        [whole(x.shape), part_spec(1, True)],
+        functools.partial(mix_back_body, weight), (4,),
+        [whole(x.shape)] + weight.specs,
         [heads_spec(m // 2, 128)],
         [jax.ShapeDtypeStruct((2, 4, m // 2, 128), LOW)], [],
-        (x, part_view(w_vo)), 2 * m * 1024 * 512, (order,),
+        [x] + weight.arrays, 2 * m * 1024 * 512, (order,),
     )
     return out
 
 
-def project_back_body(order, heads, x, spread, mixed, w_qk, w_vo, grad_qk, grad_vo, out):
-    r = pl.program_id(0)
-    q, k, v = [tokens_of(heads, slice(i * 128, (i + 1) * 128)) for i in range(3)]
-    qk = jnp.concatenate([q, k], 1)
-    store_part(grad_qk, 0, t_times(x[...], qk).astype(LOW))
-    grad_v = t_times(x[...], v).astype(LOW)
-    grad_o = t_times(spread[...], mixed[0]).astype(LOW)
-    store_part(grad_vo, 1, jnp.concatenate([grad_v, grad_o], 1))
-    terms = times_t(qk, load_part(w_qk, 0)) + times_t(v, load_part(w_vo, 1)[:, :128])
-    accumulate(out, r, terms)
-
-
-def project_back(order, heads, x, spread, mixed, w_qk, w_vo):
+def project_back_body(weights, sinks, info, heads, x, spread, mixed, *refs):
+    groups, refs = take_refs(weights, refs)
+    pairs, out = grad_refs(sinks, refs[:-1]), refs[-1]
+    terms = None
+    for i in range(3):
+        low = tokens_of(heads, slice(i * 128, (i + 1) * 128))
+        sinks[i].store(pairs[i], t_times(x[...], low).astype(LOW))
+        term = times_t(low, weights[i].load(info, groups[i]))
+        terms = term if terms is None else terms + term
+    sinks[3].store(pairs[3], t_times(spread[...], mixed[0]).astype(LOW))
+    accumulate(out, pl.program_id(0), terms)
+
+
+def project_back(order, heads, x, spread, mixed, weights, sinks):
     m = x.shape[0]
-    return call(
-        project_back_body, (4,),
-        [
-            heads_spec(m // 2, 384), whole(x.shape), whole(x.shape), pick(mixed),
-            part_spec(0, True), part_spec(1, True),
-        ],
-        [part_spec(0, False), part_spec(1, False), whole((m, 1024))],
-        [PART_OUT, PART_OUT, jax.ShapeDtypeStruct((m, 1024), FULL)], [],
-        (heads, x, spread, mixed, part_view(w_qk), part_view(w_vo)),
-        2 * m * 1024 * 3584, (order,),
-    )
-
-
-def feed_body(x, bias, u0, u1, d0, d1, hidden_out, active_out, out):
+    weights = weights[:3]
+    specs, shapes = grad_outs(sinks)
+    *grads, out = call(
+        functools.partial(project_back_body, weights, sinks), (4,),
+        [heads_spec(m // 2, 384), whole(x.shape), whole(x.shape), pick(mixed)]
+        + joined(weights, "specs"),
+        specs + [whole((m, 1024))],
+        shapes + [jax.ShapeDtypeStruct((m, 1024), FULL)], [],
+        [heads, x, spread, mixed] + joined(weights, "arrays"), 2 * m * 1024 * 3584, (order,),
+    )
+    return halves(grads), out
+
+
+def feed_body(weights, info, x, bias, *refs):
+    groups, (hidden_out, active_out, out) = take_refs(weights, refs)
     total = None
-    for j, (up, down) in enumerate(((u0, d0), (u1, d1))):
-        hidden = times(x[...], load_part(up, 2 + j)) + bias[0, j : j + 1]
+    for j in range(2):
+        hidden = times(x[...], weights[j].load(info, groups[j])) + bias[0, j : j + 1]
         hidden_out[0, j] = hidden
         active = (hidden * (0.5 * (1.0 + lax.erf(hidden * ROOT_HALF)))).astype(LOW)
         active_out[0, j] = active
-        term = times_t(active, load_part(down, 4 + j))
+        term = times_t(active, weights[2 + j].load(info, groups[2 + j]))
         total = term if total is None else total + term
     accumulate(out, pl.program_id(0), total)
 
 
-def feed(x, bias, weights):
+def feed(order, x, bias, weights):
     m = x.shape[0]
-    block = pl.BlockSpec((1, 2, m, 256), lambda r: (r, 0, 0, 0))
+    block = pl.BlockSpec((1, 2, m, 256), lambda r, *_: (r, 0, 0, 0))
     return call(
-        feed_body, (4,),
-        [whole(x.shape), pick(bias)] + [part_spec(q, True) for q in range(2, 6)],
+        functools.partial(feed_body, weights), (4,),
+        [whole(x.shape), pick(bias)] + joined(weights, "specs"),
         [block, block, whole((m, 1024))],
         [
             jax.ShapeDtypeStruct((4, 2, m, 256), FULL), jax.ShapeDtypeStruct((4, 2, m, 256), LOW),
             jax.ShapeDtypeStruct((m, 1024), FULL),
         ], [],
-        (x, bias) + tuple(part_view(w) for w in weights), 4 * m * 1024 * 2048,
-    )
-
-
-def feed_back_body(
-    spread, x, hidden, active, u0, u1, d0, d1, g_u0, g_u1, g_d0, g_d1, grad_bias, out
-):
+        [x, bias] + joined(weights, "arrays"), 4 * m * 1024 * 2048, (order,),
+    )
+
+
+def feed_back_body(weights, info, spread, x, hidden, active, *refs):
+    groups, refs = take_refs(weights, refs)
+    pairs, (grad_bias, out) = grad_refs(FEED, refs[:-2]), refs[-2:]
     total = None
-    for j, (up, down, g_up, g_down) in enumerate(((u0, d0, g_u0, g_d0), (u1, d1, g_u1, g_d1))):
+    for j in range(2):
         value = hidden[0, j]
         slope = 0.5 * (1.0 + lax.erf(value * ROOT_HALF))
         slope += value * jnp.exp(-0.5 * value * value) * (1.0 / ROOT_TWOPI)
-        grad = times(spread[...], load_part(down, 4 + j)) * slope
+        grad = times(spread[...], weights[2 + j].load(info, groups[2 + j])) * slope
         grad_bias[0, j : j + 1] = jnp.sum(grad, axis=0, keepdims=True)
         low = grad.astype(LOW)
-        store_part(g_down, 4 + j, t_times(spread[...], active[0, j]).astype(LOW))
-        store_part(g_up, 2 + j, t_times(x[...], low).astype(LOW))
-        term = times_t(low, load_part(up, 2 + j))
+        FEED[2 + j].store(pairs[2 + j], t_times(spread[...], active[0, j]).astype(LOW))
+        FEED[j].store(pairs[j], t_times(x[...], low).astype(LOW))
+        term = times_t(low, weights[j].load(info, groups[j]))
         total = term if total is None else total + term
     accumulate(out, pl.program_id(0), total)
 
 
-def feed_back(spread, x, hidden, active, weights):
+def feed_back(order, spread, x, hidden, active, weights):
     m = x.shape[0]
-    return call(
-        feed_back_body, (4,),
-        [whole(x.shape), whole(x.shape), pick(hidden), pick(active)]
-        + [part_spec(q, True) for q in range(2, 6)],
-        [part_spec(q, False) for q in range(2, 6)]
-        + [pl.BlockSpec((1, 2, 256), lambda r: (r, 0, 0)), whole((m, 1024))],
-        [PART_OUT] * 4
+    specs, shapes = grad_outs(FEED)
+    *grads, grad_bias, out = call(
+        functools.partial(feed_back_body, weights), (4,),
+        [whole(x.shape), whole(x.shape), pick(hidden), pick(active)] + joined(weights, "specs"),
+        specs + [pl.BlockSpec((1, 2, 256), lambda r, *_: (r, 0, 0)), whole((m, 1024))],
+        shapes
         + [jax.ShapeDtypeStruct((4, 2, 256), FULL), jax.ShapeDtypeStruct((m, 1024), FULL)], [],
-        (spread, x, hidden, active) + tuple(part_view(w) for w in weights), 8 * m * 1024 * 2048,
-    )
+        [spread, x, hidden, active] + joined(weights, "arrays"), 8 * m * 1024 * 2048, (order,),
+    )
+    return halves(grads), grad_bias, out
 
 
 def one_row(value, s):
@@ -477,6 +565,47 @@
     rows = stream.shape[1]
     width = stream.shape[2]
 
+    def both_rows(columns):
+        axis = columns.ndim - 2
+        keep = lax.dynamic_index_in_dim(columns, core, axis, False)
+        new = swap(lax.dynamic_index_in_dim(columns, 1 - core, axis, False))
+        return jnp.where(
+            core == 0, jnp.concatenate([keep, new], -2), jnp.concatenate([new, keep], -2)
+        )
+
+    lead = both_rows(
+        jnp.concatenate(
+            [
+                w_qkv[0].reshape(32, 3, 2, 128).transpose(0, 2, 1, 3).reshape(32, 2, 384),
+                w_out[0].T.reshape(32, 2, 128),
+            ],
+            2,
+        )
+    )
+    lead = gather_early([lead[None, :, k * 128 : (k + 1) * 128] for k in range(4)])
+    lead, norm_gains = lax.optimization_barrier((lead, norm_gains))
+    lead = gather_late(lead)
+
+    later = jnp.concatenate(
+        [w_in[0], w_back[0].T, w_qkv[1].reshape(32, 768), w_out[1].T, w_in[1], w_back[1].T], 1
+    )
+    later = lax.all_gather(later, "tensor", axis=0, tiled=True)
+
+    def everywhere(value):
+        value = lax.all_gather(value, ("dp", "ctx"), axis=0, tiled=True)
+        return value.reshape(16, 2, 4, 32, value.shape[1])
+
+    feed_zero = everywhere(later[:, :2048])
+    attention_one = everywhere(later[:, 2048:3072])
+    feed_one = everywhere(later[:, 3072:])
+    attention_w = [
+        [Exchanged(k, lead[k], 128) for k in range(4)],
+        [Gathered(attention_one, 2 * k, 128, 1) for k in range(4)],
+    ]
+    feed_w = [
+        [Gathered(value, base, 256, 2) for base in (0, 1, 4, 5)] for value in (feed_zero, feed_one)
+    ]
+
     vectors = jnp.concatenate(
         [norm_gains.reshape(-1), shifts.reshape(-1), qv_bias.reshape(-1), in_bias.reshape(-1)]
     )
@@ -522,51 +651,31 @@
     gains = inputs[2 * tokens : 2 * tokens + 4].reshape(layers, 2, width)
     shift = inputs[2 * tokens + 4 :].reshape(layers, 4, width)
 
-    columns = jnp.concatenate(
-        [
-            w_qkv.reshape(layers, 32, 3, 2, 128).transpose(0, 1, 3, 2, 4).reshape(
-                layers, 32, 2, 384
-            ),
-            w_out.transpose(0, 2, 1).reshape(layers, 32, 2, 128),
-            w_in.reshape(layers, 32, 2, 512),
-            w_back.transpose(0, 2, 1).reshape(layers, 32, 2, 512),
-        ],
-        3,
-    )
-    keep = lax.dynamic_index_in_dim(columns, core, 2, False)
-    new = swap(lax.dynamic_index_in_dim(columns, 1 - core, 2, False))
-    rows_two = jnp.where(
-        core == 0, jnp.concatenate([keep, new], 1), jnp.concatenate([new, keep], 1)
-    )
-    parts = [rows_two[None, :, :, q * 256 : (q + 1) * 256] for q in range(6)]
-    parts = gather_phases(parts, 0, 4)
-    weights = []
-    for layer in range(layers):
-        mine = [value[:, layer] for value in parts]
-        if layer:
-            mine, weights[-1] = lax.optimization_barrier((mine, weights[-1]))
-        weights.append(gather_phases(mine, 4, 6))
-
     marks = segments.reshape(2, 2, 2, 4, rows)
     marks = jnp.where(core == 0, marks, marks[:, :, ::-1])
     marks = marks.transpose(0, 1, 3, 2, 4).reshape(2, 16 * rows)
     marks_t = marks.T
-    order = jnp.stack([relative_x(me_x, r) for r in range(4)]).astype(jnp.int32)
+    chips = []
+    for i in range(16):
+        far_z = me_z ^ (((i >> 2) & 1) ^ ((i >> 3) * 3))
+        far_y = me_y ^ ((i & 1) ^ (((i >> 1) & 1) * 3))
+        chips.append(((far_z >> 1) * 4 + far_y) * 2 + (far_z & 1))
+    order = [relative_x(me_x, r) for r in range(4)] + [core] + chips
+    order = jnp.stack(order).astype(jnp.int32)
 
     saved = []
     for layer in range(layers):
-        w_qk, w_vo = weights[layer][:2]
         bias = pair[layer].reshape(2, 4, 1, 128)
         gathered = both(state.astype(LOW))
-        qkv = trade(project(order, gathered, w_qk, w_vo, bias[0], bias[1]).reshape(8, 2 * rows, 384))
-        qkv = qkv.reshape(16 * rows, 384)
+        qkv = project(order, gathered, attention_w[layer], bias[0], bias[1])
+        qkv = trade(qkv.reshape(8, 2 * rows, 384)).reshape(16 * rows, 384)
         mixed, summary = attend(qkv, marks_t, marks)
         mixed = trade(mixed.reshape(8, 2 * rows, 128)).reshape(2, 4, 2 * rows, 128)
-        mixed, attended = mix(order, mixed, w_vo)
+        mixed, attended = mix(order, mixed, attention_w[layer][3])
         attended = own_sum(attended) + shift[layer, 2]
         first, unit_one, inv_one = normalize(state + attended, gains[layer, 0], shift[layer, 0])
         gathered_two = both(first.astype(LOW))
-        hidden, active, down = feed(gathered_two, up[layer], weights[layer][2:])
+        hidden, active, down = feed(order, gathered_two, up[layer], feed_w[layer])
         down = own_sum(down)
         state, unit_two, inv_two = normalize(
             first + down + shift[layer, 3], gains[layer, 1], shift[layer, 1]
@@ -577,36 +686,42 @@
         )
     result = absolute(state)
 
-    grads = [None] * layers
     small = [None] * layers
     for layer in reversed(range(layers)):
-        w_qk, w_vo = weights[layer][:2]
         (gathered, qkv, summary, mixed, unit_one, inv_one, gathered_two, hidden, active,
          unit_two, inv_two) = saved[layer]
         grad_two, gain_two, shift_two = normalize_back(
             incoming, unit_two, inv_two, gains[layer, 1]
         )
         spread_two = both(grad_two.astype(LOW))
-        *grad_feed, grad_upbias, grad_first = feed_back(
-            spread_two, gathered_two, hidden, active, weights[layer][2:]
-        )
+        grad_feed, grad_upbias, grad_first = feed_back(
+            order, spread_two, gathered_two, hidden, active, feed_w[layer]
+        )
+        grad_feed = reduce_first(grad_feed, (0, 2))
         grad_first = grad_two + own_sum(grad_first)
         grad_one, gain_one, shift_one = normalize_back(
             grad_first, unit_one, inv_one, gains[layer, 0]
         )
         spread_one = both(grad_one.astype(LOW))
-        grad_mixed = trade(mix_back(order, spread_one, w_vo).reshape(8, 2 * rows, 128))
+        grad_mixed = trade(mix_back(order, spread_one, attention_w[layer][3]).reshape(8, 2 * rows, 128))
         grad_mixed = grad_mixed.reshape(16 * rows, 128)
         low_packed, grad_pair = attend_back(qkv, grad_mixed, marks_t, marks, summary)
         grad_pair = grad_pair.reshape(2, 2, 64).sum(1)
         low_packed = trade(low_packed.reshape(8, 2 * rows, 384)).reshape(2, 4, 2 * rows, 384)
-        grad_qk, grad_vo, grad_x = project_back(
-            order, low_packed, gathered, spread_one, mixed, w_qk, w_vo
+        grad_attention, grad_x = project_back(
+            order, low_packed, gathered, spread_one, mixed, attention_w[layer],
+            PAIRED if layer else APART,
         )
         incoming = grad_one + own_sum(grad_x)
-        grads[layer] = reduce_phases(
-            [value.reshape(64, 64, 256) for value in [grad_qk, grad_vo] + grad_feed], 0, 2
-        )
+        if layer:
+            grad_attention = reduce_first(grad_attention, (0, 2))
+            later = reduce_rest(
+                [jnp.concatenate(pair, 2) for pair in zip(grad_feed, grad_attention)], (0, 2)
+            )
+        else:
+            tail = reduce_rest(grad_feed, (0, 2))
+            grad_attention, later, tail = lax.optimization_barrier((grad_attention, later, tail))
+            lead = reduce_rest(reduce_first(grad_attention, range(4)), range(4))
         small[layer] = (
             jnp.stack([gain_one, gain_two]),
             jnp.stack(
@@ -617,19 +732,25 @@
         )
     grad_stream = absolute(incoming)
 
-    parts = [jnp.stack([grads[layer][q] for layer in range(layers)], 1) for q in range(6)]
-    parts = reduce_phases(parts, 2, 6)
-    total = jnp.concatenate([value[0] for value in parts], 2).reshape(layers, 2, 32, 1536)
-    keep = lax.dynamic_index_in_dim(total, core, 1, False)
-    new = swap(lax.dynamic_index_in_dim(total, 1 - core, 1, False))
-    total = jnp.stack(
-        [jnp.where(core == 0, keep, new), jnp.where(core == 0, new, keep)], 2
-    ).astype(FULL)
-    out_qkv = total[..., :384].reshape(layers, 32, 2, 3, 128).transpose(0, 1, 3, 2, 4)
-    out_qkv = out_qkv.reshape(layers, 32, 3, 256)
-    out_o = total[..., 384:512].reshape(layers, 32, 256).transpose(0, 2, 1)
-    out_up = total[..., 512:1024].reshape(layers, 32, 1024)
-    out_down = total[..., 1024:].reshape(layers, 32, 1024).transpose(0, 2, 1)
+    def own_rows(parts):
+        total = jnp.stack(parts, 1)
+        total = total.reshape((2, 32) + total.shape[1:])
+        keep = lax.dynamic_index_in_dim(total, core, 0, False)
+        new = swap(lax.dynamic_index_in_dim(total, 1 - core, 0, False))
+        return jnp.stack(
+            [jnp.where(core == 0, keep, new), jnp.where(core == 0, new, keep)], 1
+        ).astype(FULL)
+
+    tail = own_rows([jnp.concatenate([a, b], 1) for a, b in zip(tail, later)])
+    lead = own_rows(lead)
+    attention = [lead, tail[..., 1024:].reshape(32, 2, 4, 128)]
+    feeds = [tail[..., i * 512 : (i + 1) * 512].reshape(32, 2, 4, 256) for i in range(2)]
+    out_qkv = jnp.stack(
+        [value[:, :, :3].transpose(0, 2, 1, 3).reshape(32, 3, 256) for value in attention]
+    )
+    out_o = jnp.stack([value[:, :, 3].reshape(32, 256).T for value in attention])
+    out_up = jnp.stack([value[:, :, :2].reshape(32, 1024) for value in feeds])
+    out_down = jnp.stack([value[:, :, 2:].reshape(32, 1024).T for value in feeds])
 
     vec = absolute(
         jnp.concatenate([small[layer][0] for layer in range(layers)]

time: 742 us -> 779 us (1.050)
  waiting for transfers between devices: 203 us -> 297 us
  other arithmetic: 113 us -> 54.1 us
  blocking collectives: 0 us -> 42.7 us
  starting transfers between devices: 190 us -> 148 us
  local copies, waits for them, and re-layouts: 76.1 us -> 57.4 us
  between operations: 3.57 us -> 16.6 us
    all_gather x0 -> x4, waiting for transfers between devices: none -> 103 us  [the longest x3 76 us: everywhere(): value = lax.all_gather(value, ('dp', 'ctx'), axis=0, tiled=True)]
    concatenate x42 -> x16, other arithmetic: 51.3 us -> 2.07 us  [the longest x2 1.93 us: local(): jnp.concatenate(pair, 2)]
    all_to_all x0 -> x3, blocking collectives: none -> 42.7 us  [trade(): lax.all_to_all(value, ('ctx', 'tensor'), 0, 0, axis_index_groups=GROUPS,...]
    ppermute x114 -> x99, waiting for transfers between devices: 168 us -> 132 us  [swap(): return lax.ppermute(value, ALL, exchange_perm(axis, mask))]
    ppermute x114 -> x99, starting transfers between devices: 139 us -> 111 us  [swap(): return lax.ppermute(value, ALL, exchange_perm(axis, mask))]
    slice x45 -> x52, local copies, waits for them, and re-layouts: 31.2 us -> 11.6 us  [the longest x40 4.56 us: reduce_phase(): value[half:]]
    all_to_all x8 -> x5, waiting for transfers between devices: 29.6 us -> 49.1 us  [trade(): lax.all_to_all(value, ('ctx', 'tensor'), 0, 0, axis_index_groups=GROUPS,...]
    all_to_all x8 -> x5, starting transfers between devices: 33.8 us -> 20.2 us  [trade(): lax.all_to_all(value, ('ctx', 'tensor'), 0, 0, axis_index_groups=GROUPS,...]
  transfers between devices with their start and end apart: 124 -> 110, of which waited for: 46 -> 49; matrix products, arithmetic and copies ran while one was open for 23% -> 12% of each run, Pallas kernels for 12% -> 13%
where the time goes in v3:
time: 779 us; the launch traced here: 768 us
  waiting for transfers between devices  297 us (38%)
  starting transfers between devices  148 us (19%)
  Pallas kernels  141 us (18%)
  local copies, waits for them, and re-layouts  57.4 us (7%)
  other arithmetic  54.1 us (7%)
  blocking collectives  42.7 us (5%)
  between operations  16.6 us (2%)
  matrix products  10.5 us (1%)
    pallas_call x16, Pallas kernels, call(): pl.pallas_call(body, grid_spec=pltpu.PrefetchScalarGridSpec(num_scalar_pr...  141 us
    ppermute x99, waiting for transfers between devices, swap(): return lax.ppermute(value, ALL, exchange_perm(axis, mask))  132 us
    ppermute x99, starting transfers between devices, swap(): return lax.ppermute(value, ALL, exchange_perm(axis, mask))  111 us
    all_gather x3, waiting for transfers between devices, everywhere(): value = lax.all_gather(value, ('dp', 'ctx'), axis=0, tiled=True)  76 us
    all_to_all x5, waiting for transfers between devices, trade(): lax.all_to_all(value, ('ctx', 'tensor'), 0, 0, axis_index_groups=GROUPS,...  49.1 us
    all_to_all x3, blocking collectives, trade(): lax.all_to_all(value, ('ctx', 'tensor'), 0, 0, axis_index_groups=GROUPS,...  42.7 us
    all_gather x1, waiting for transfers between devices, local(): later = lax.all_gather(later, 'tensor', axis=0, tiled=True)  27 us
    convert_element_type x48, other arithmetic, add_low(): return (left.astype(FULL) + right.astype(FULL)).astype(LOW)  24.1 us
  transfers between devices with their start and end apart: 110, of which 49 were waited for; matrix products, arithmetic and copies ran while one was open for 12% of the time, Pallas kernels for 13%

profile of v3, /device:TPU:1, one launch (start us, length us, event | category | flops | bytes accessed | tf_op | source)
XLA Modules:
  0.0 767.6 jit_solution(16880264521264889776)
XLA Ops:
  13.0 27.0 %all-gather.5.cloned.1.call-done = bf16[128,5120]{1,0:T(8,128)(2,1)} async-done(((bf16[32,5120]{1,0:T(8,128)(2,1)}), bf16[128,5120]{1,0:T(8,128)(2,1)}) %all-gather.5.cloned.1.call-update) | async-done | bytes 1310736 | tf_op jit(solution)/shard_map/all_gather | solution.py:592
  75.3 10.4 %all-to-all-start = ((bf16[128,2,256]{2,1,0:T(2,128)(2,1)}), bf16[128,2,256]{2,1,0:T(2,128)(2,1)S(1)}, u32[]{:S(2)}, u32[]{:S(2)}) async-start(bf16[128,2,256]{2,1,0:T(2,128)(2,1)} %reshape.576), calls=%async_computation | async-start | bytes 262144 | tf_op jit(solution)/shard_map/all_to_all | solution.py:613
  85.7 9.9 %all-to-all-done = bf16[128,2,256]{2,1,0:T(2,128)(2,1)S(1)} async-done(((bf16[128,2,256]{2,1,0:T(2,128)(2,1)}), bf16[128,2,256]{2,1,0:T(2,128)(2,1)S(1)}, u32[]{:S(2)}, u32[]{:S(2)}) %all-to-all-start) | async-done | bytes 131104 | tf_op jit(solution)/shard_map/all_to_all | solution.py:613
  104.6 8.9 %collective-permute-done.18 = bf16[16,64,128]{2,1,0:T(8,128)(2,1)} collective-permute-done((bf16[16,64,128]{2,1,0:T(8,128)(2,1)S(1)}, bf16[16,64,128]{2,1,0:T(8,128)(2,1)}, u32[]{:S(2)}, u32[]{:S(2)}) %collective-permute-start.18) | collective-permute-done | bytes 262176 | tf_op jit(solution)/shard_map/ppermute | solution.py:41
  114.7 10.3 %collective-permute-done.21 = bf16[16,64,128]{2,1,0:T(8,128)(2,1)} collective-permute-done((bf16[16,64,128]{2,1,0:T(8,128)(2,1)S(1)}, bf16[16,64,128]{2,1,0:T(8,128)(2,1)}, u32[]{:S(2)}, u32[]{:S(2)}) %collective-permute-start.21) | collective-permute-done | bytes 262176 | tf_op jit(solution)/shard_map/ppermute | solution.py:41
  129.5 9.2 %collective-permute-done.20 = bf16[16,64,128]{2,1,0:T(8,128)(2,1)} collective-permute-done((bf16[16,64,128]{2,1,0:T(8,128)(2,1)}, bf16[16,64,128]{2,1,0:T(8,128)(2,1)}, u32[]{:S(2)}, u32[]{:S(2)}) %collective-permute-start.20) | collective-permute-done | bytes 262176 | tf_op jit(solution)/shard_map/ppermute | solution.py:41
  138.7 6.4 shard_map.186
  145.1 4.5 all-to-all-start.1
  156.5 7.3 all-to-all-done.1
  163.8 7.9 %shard_map.187 = (bf16[1152,128]{1,0:T(8,128)(2,1)}, f32[2,1152]{1,0:T(2,128)}) custom-call(bf16[1152,384]{1,0:T(8,128)(2,1)} %bitcast.50.query.keys.values, bf16[1152,384]{1,0:T(8,128)(2,1)} %bitcast.50.query.keys.values, bf16[1152,384]{1,0:T(8,128)(2,1)} %bitcast.50.query.keys.values, s32[1152,2]{1,0:T(8,128)} %copy.97.mark_keys, s32[2,1152]{1,0:T(2,128)} %copy-done.39), custom_call_target="tpu_custom_call" | custom-call | flops 1358954496 | bytes 2976768 | tf_op jit(solution)/shard_map/pallas_call | solution.py:251
  171.7 4.5 all-to-all-start.2
  177.0 5.6 all-to-all-done.2
  183.3 5.2 shard_map.188
  189.7 3.8 collective-permute-start.30
  198.9 9.2 %shard_map.189 = (f32[4,2,288,256]{3,2,1,0:T(8,128)}, bf16[4,2,288,256]{3,2,1,0:T(8,128)(2,1)}, f32[288,1024]{1,0:T(8,128)}) custom-call(s32[21]{0:T(128)} %stack.203.info, bf16[288,1024]{1,0:T(8,128)(2,1)} %pad_maximum_fusion.3.x, f32[4,2,256]{2,1,0:T(2,128)} %get-tuple-element.252.bias, bf16[16,2,4,32,2048]{4,3,2,1,0:T(8,128)(2,1)} %bitcast.305, ...), custom_call_target="tpu_custom_call" | custom-call | flops 2415919104 | bytes 72425472 | tf_op jit(solution)/shard_map/pallas_call | solution.py:251
  215.3 24.1 %all-gather.9.cloned.1.call-done = bf16[4096,1024]{1,0:T(8,128)(2,1)} async-done(((bf16[128,1024]{1,0:T(8,128)(2,1)}), bf16[4096,1024]{1,0:T(8,128)(2,1)}) %all-gather.9.cloned.1.call-update) | async-done | bytes 8388624 | tf_op jit(solution)/shard_map/all_gather | solution.py:595
  239.4 6.3 shard_map.190
  245.7 19.7 %all_to_all.55 = bf16[8,144,384]{2,1,0:T(8,128)(2,1)} all-to-all(bf16[8,144,384]{2,1,0:T(8,128)(2,1)} %bitcast.331), channel_id=1, replica_groups={{0,1,2,3,8,9,10,11},{4,5,6,7,12,13,14,15},{16,17,18,19,24,25,26,27},{20..., dimensions={0} | all-to-all | bytes 1769472 | tf_op jit(solution)/shard_map/all_to_all | solution.py:553
  265.4 7.9 %shard_map.191 = (bf16[1152,128]{1,0:T(8,128)(2,1)}, f32[2,1152]{1,0:T(2,128)}) custom-call(bf16[1152,384]{1,0:T(8,128)(2,1)} %bitcast.350, bf16[1152,384]{1,0:T(8,128)(2,1)} %bitcast.351, bf16[1152,384]{1,0:T(8,128)(2,1)} %bitcast.352, s32[1152,2]{1,0:T(8,128)} %copy.97.mark_keys, s32[2,1152]{1,0:T(2,128)} %copy-done.39), custom_call_target="tpu_custom_call" | custom-call | flops 1358954496 | bytes 2976768 | tf_op jit(solution)/shard_map/pallas_call | solution.py:251
  273.2 11.0 %all_to_all.56 = bf16[8,144,128]{2,1,0:T(8,128)(2,1)} all-to-all(bf16[8,144,128]{2,1,0:T(8,128)(2,1)} %bitcast.373), channel_id=1, replica_groups={{0,1,2,3,8,9,10,11},{4,5,6,7,12,13,14,15},{16,17,18,19,24,25,26,27},{20..., dimensions={0} | all-to-all | bytes 589824 | tf_op jit(solution)/shard_map/all_to_all | solution.py:553
  284.2 5.3 shard_map.192
  298.5 51.9 %all-gather.11.cloned.1.call-done = bf16[4096,2048]{1,0:T(8,128)(2,1)} async-done(((bf16[128,2048]{1,0:T(8,128)(2,1)}), bf16[4096,2048]{1,0:T(8,128)(2,1)}) %all-gather.11.cloned.1.call-update) | async-done | bytes 16777232 | tf_op jit(solution)/shard_map/all_gather | solution.py:595
  350.4 9.1 %shard_map.193 = (f32[4,2,288,256]{3,2,1,0:T(8,128)}, bf16[4,2,288,256]{3,2,1,0:T(8,128)(2,1)}, f32[288,1024]{1,0:T(8,128)}) custom-call(s32[21]{0:T(128)} %stack.203.info, bf16[288,1024]{1,0:T(8,128)(2,1)} %pad_maximum_fusion.5.x, f32[4,2,256]{2,1,0:T(2,128)} %get-tuple-element.251.bias, bf16[16,2,4,32,2048]{4,3,2,1,0:T(8,128)(2,1)} %bitcast.313, ...), custom_call_target="tpu_custom_call" | custom-call | flops 2415919104 | bytes 72425472 | tf_op jit(solution)/shard_map/pallas_call | solution.py:251
  367.2 13.8 %shard_map.194 = (bf16[2,2,2,2,2,64,512]{6,5,4,3,2,1,0:T(8,128)(2,1)}, bf16[2,2,2,2,2,64,512]{6,5,4,3,2,1,0:T(8,128)(2,1)}, bf16[2,2,2,2,2,64,512]{6,5,4,3,2,1,0...) custom-call(s32[21]{0:T(128)} %stack.203.info, ...), custom_call_target="tpu_custom_call" | custom-call | flops 4831838208 | bytes 81403904 | tf_op jit(solution)/shard_map/pallas_call | solution.py:251
  388.2 4.9 shard_map.195
  393.0 12.1 %all_to_all.57 = bf16[8,144,128]{2,1,0:T(8,128)(2,1)} all-to-all(bf16[8,144,128]{2,1,0:T(8,128)(2,1)} %bitcast.338), channel_id=1, replica_groups={{0,1,2,3,8,9,10,11},{4,5,6,7,12,13,14,15},{16,17,18,19,24,25,26,27},{20..., dimensions={0} | all-to-all | bytes 589824 | tf_op jit(solution)/shard_map/all_to_all | solution.py:553
  405.1 11.8 %shard_map.196 = (bf16[1152,384]{1,0:T(8,128)(2,1)}, f32[2,128]{1,0:T(2,128)}) custom-call(bf16[1152,384]{1,0:T(8,128)(2,1)} %bitcast.353, bf16[1152,384]{1,0:T(8,128)(2,1)} %bitcast.354, bf16[1152,384]{1,0:T(8,128)(2,1)} %bitcast.355, bf16[1152,128]{1,0:T(8,128)(2,1)} %bitcast.372, s32[1152,2]{1,0:T(8,128)} %copy.97.mark_keys, s32[2,1152]{1,0:T(2,128)} %copy-done.39, ...), custom_call_target="tpu_custom_call" | custom-call | flops 3397386240 | bytes 3862528 | tf_op jit(solution)/shard_map/pallas_call | solution.py:251
  416.9 3.6 all-to-all-start.6
  423.5 11.0 %all-to-all-done.6 = bf16[8,144,384]{2,1,0:T(8,128)(2,1)S(1)} async-done(((bf16[8,144,384]{2,1,0:T(8,128)(2,1)}), bf16[8,144,384]{2,1,0:T(8,128)(2,1)S(1)}, u32[]{:S(2)}, u32[]{:S(2)}) %all-to-all-start.6) | async-done | bytes 884768 | tf_op jit(solution)/shard_map/all_to_all | solution.py:553
  435.4 11.1 %shard_map.197 = (bf16[2,2,2,2,2,64,256]{6,5,4,3,2,1,0:T(8,128)(2,1)}, bf16[2,2,2,2,2,64,256]{6,5,4,3,2,1,0:T(8,128)(2,1)}, bf16[2,2,2,2,2,64,256]{6,5,4,3,2,1,0...) custom-call(s32[21]{0:T(128)} %stack.203.info, bf16[2,4,144,384]{3,2,1,0:T(8,128)(2,1)} %bitcast.330, ...), custom_call_target="tpu_custom_call" | custom-call | flops 2113929216 | bytes 32899072 | tf_op jit(solution)/shard_map/pallas_call | solution.py:251
  455.1 21.2 %collective-permute-done.45 = bf16[32,64,512]{2,1,0:T(8,128)(2,1)} collective-permute-done((bf16[32,64,512]{2,1,0:T(8,128)(2,1)}, bf16[32,64,512]{2,1,0:T(8,128)(2,1)}, u32[]{:S(2)}, u32[]{:S(2)}) %collective-permute-start.45) | collective-permute-done | bytes 2097184 | tf_op jit(solution)/shard_map/ppermute | solution.py:41
  488.6 14.0 %shard_map.198 = (bf16[2,2,2,2,2,64,512]{6,5,4,3,2,1,0:T(8,128)(2,1)}, bf16[2,2,2,2,2,64,512]{6,5,4,3,2,1,0:T(8,128)(2,1)}, bf16[2,2,2,2,2,64,512]{6,5,4,3,2,1,0...) custom-call(s32[21]{0:T(128)} %stack.203.info, ...), custom_call_target="tpu_custom_call" | custom-call | flops 4831838208 | bytes 81403904 | tf_op jit(solution)/shard_map/pallas_call | solution.py:251
  504.4 3.8 collective-permute-start.42
  524.6 4.9 shard_map.199
  529.6 3.4 all-to-all-start.7
  536.7 24.3 %all-to-all-done.7 = bf16[8,144,128]{2,1,0:T(8,128)(2,1)S(1)} async-done(((bf16[8,144,128]{2,1,0:T(8,128)(2,1)}), bf16[8,144,128]{2,1,0:T(8,128)(2,1)S(1)}, u32[]{:S(2)}, u32[]{:S(2)}) %all-to-all-start.7) | async-done | bytes 294944 | tf_op jit(solution)/shard_map/all_to_all | solution.py:553
  561.7 11.8 %shard_map.200 = (bf16[1152,384]{1,0:T(8,128)(2,1)}, f32[2,128]{1,0:T(2,128)}) custom-call(bf16[1152,384]{1,0:T(8,128)(2,1)} %bitcast.50.query.keys.values, bf16[1152,384]{1,0:T(8,128)(2,1)} %bitcast.50.query.keys.values, bf16[1152,384]{1,0:T(8,128)(2,1)} %bitcast.50.query.keys.values, bf16[1152,128]{1,0:T(8,128)(2,1)} %bitcast.371, ...), custom_call_target="tpu_custom_call" | custom-call | flops 3397386240 | bytes 3862528 | tf_op jit(solution)/shard_map/pallas_call | solution.py:251
  576.0 6.0 all-to-all-start.9
  592.9 4.2 all-to-all-start.8
  611.3 11.3 %shard_map.201 = (bf16[2,2,2,2,2,64,128]{6,5,4,3,2,1,0:T(8,128)(2,1)}, bf16[2,2,2,2,2,64,128]{6,5,4,3,2,1,0:T(8,128)(2,1)}, bf16[2,2,2,2,2,64,128]{6,5,4,3,2,1,0...) custom-call(s32[21]{0:T(128)} %stack.203.info, ...), custom_call_target="tpu_custom_call" | custom-call | flops 2113929216 | bytes 10878976 | tf_op jit(solution)/shard_map/pallas_call | solution.py:251
  640.6 25.3 %collective-permute-done.51 = bf16[2,64,768]{2,1,0:T(8,128)(2,1)S(1)} collective-permute-done((bf16[2,64,768]{2,1,0:T(8,128)(2,1)S(1)}, bf16[2,64,768]{2,1,0:T(8,128)(2,1)S(1)}, u32[]{:S(2)}, u32[]{:S(2)}) %collective-permute-start.51) | collective-permute-done | bytes 196640 | tf_op jit(solution)/shard_map/ppermute | solution.py:41
  671.9 8.6 %collective-permute-done.63 = bf16[8,64,512]{2,1,0:T(8,128)(2,1)S(1)} collective-permute-done((bf16[8,64,512]{2,1,0:T(8,128)(2,1)S(1)}, bf16[8,64,512]{2,1,0:T(8,128)(2,1)S(1)}, u32[]{:S(2)}, u32[]{:S(2)}) %collective-permute-start.63) | collective-permute-done | bytes 524320 | tf_op jit(solution)/shard_map/ppermute | solution.py:41
  682.1 5.1 collective-permute-done.64
  688.8 3.5 collective-permute-done.65
  697.3 6.3 collective-permute-start.98
  716.8 3.9 collective-permute-done.91
  725.6 3.7 collective-permute-done.92
  750.9 7.2 collective-permute-start.97
  (636 shorter events, 248.9 us)
Async XLA Ops:
  7.2 32.9 %all-gather.5.cloned.1.call-start = ((), (), s32[]{:S(2)}) async-start(), calls=%async_computation.10 | async-start | bytes 1638400 | tf_op jit(solution)/shard_map/all_gather | solution.py:592
  13.0 185.9 %all-gather.7.cloned.1.call-start = ((), (), s32[]{:S(2)}) async-start(), calls=%async_computation.11 | async-start | bytes 17301504 | tf_op jit(solution)/shard_map/all_gather | solution.py:595
  42.4 197.0 %all-gather.9.cloned.1.call-start = ((), (), s32[]{:S(2)}) async-start(), calls=%async_computation.12 | async-start | bytes 8650752 | tf_op jit(solution)/shard_map/all_gather | solution.py:595
  44.1 306.3 %all-gather.11.cloned.1.call-start = ((), (), s32[]{:S(2)}) async-start(), calls=%async_computation.13 | async-start | bytes 17301504 | tf_op jit(solution)/shard_map/all_gather | solution.py:595
  75.3 20.3 %all-to-all-start = ((bf16[128,2,256]{2,1,0:T(2,128)(2,1)}), bf16[128,2,256]{2,1,0:T(2,128)(2,1)S(1)}, u32[]{:S(2)}, u32[]{:S(2)}) async-start(bf16[128,2,256]{2,1,0:T(2,128)(2,1)} %reshape.576), calls=%async_computation | async-start | bytes 262144 | tf_op jit(solution)/shard_map/all_to_all | solution.py:613
  99.2 26.8 %collective-permute-start.17 = (bf16[144,1024]{1,0:T(8,128)(2,1)S(1)}, bf16[144,1024]{1,0:T(8,128)(2,1)S(1)}, u32[]{:S(2)}, u32[]{:S(2)}) collective-permute-start(bf16[144,1024]{1,0:T(8,128)(2,1)S(1)} %slice.929), channel_id=1, source_target_pairs={{0,4},{1,5},{2,6},{3,7},{4,0},{5,1},{6,2},{7,3},{8,12},{9,13},{10,... | collective-permute-start | bytes 884744 | tf_op jit(solution)/shard_map/ppermute | solution.py:41
  99.6 13.9 %collective-permute-start.18 = (bf16[16,64,128]{2,1,0:T(8,128)(2,1)S(1)}, bf16[16,64,128]{2,1,0:T(8,128)(2,1)}, u32[]{:S(2)}, u32[]{:S(2)}) collective-permute-start(bf16[16,64,128]{2,1,0:T(8,128)(2,1)S(1)} %constant_dynamic-update-slice_fusion.2), channel_id=1, source_target_pairs={{0,16},{1,17},{2,18},{3,19},{4,20},{5,21},{6,22},{7,23},{8,24},{9,... | collective-permute-start | bytes 786440 | tf_op jit(solution)/shard_map/ppermute | solution.py:41
  100.0 14.2 %collective-permute-start.19 = (bf16[16,64,128]{2,1,0:T(8,128)(2,1)S(1)}, bf16[16,64,128]{2,1,0:T(8,128)(2,1)}, u32[]{:S(2)}, u32[]{:S(2)}) collective-permute-start(bf16[16,64,128]{2,1,0:T(8,128)(2,1)S(1)} %constant_dynamic-update-slice_fusion.2), channel_id=1, source_target_pairs={{0,8},{1,9},{2,10},{3,11},{4,12},{5,13},{6,14},{7,15},{8,0},{9,1},... | collective-permute-start | bytes 786440 | tf_op jit(solution)/shard_map/ppermute | solution.py:41
  100.6 24.4 %collective-permute-start.21 = (bf16[16,64,128]{2,1,0:T(8,128)(2,1)S(1)}, bf16[16,64,128]{2,1,0:T(8,128)(2,1)}, u32[]{:S(2)}, u32[]{:S(2)}) collective-permute-start(bf16[16,64,128]{2,1,0:T(8,128)(2,1)S(1)} %constant_dynamic-update-slice_fusion.7), channel_id=1, source_target_pairs={{0,8},{1,9},{2,10},{3,11},{4,12},{5,13},{6,14},{7,15},{8,0},{9,1},... | collective-permute-start | bytes 786440 | tf_op jit(solution)/shard_map/ppermute | solution.py:41
  101.5 23.9 %collective-permute-start.24 = (bf16[16,64,128]{2,1,0:T(8,128)(2,1)S(1)}, bf16[16,64,128]{2,1,0:T(8,128)(2,1)}, u32[]{:S(2)}, u32[]{:S(2)}) collective-permute-start(bf16[16,64,128]{2,1,0:T(8,128)(2,1)S(1)} %constant_dynamic-update-slice_fusion.12), channel_id=1, source_target_pairs={{0,48},{1,49},{2,50},{3,51},{4,52},{5,53},{6,54},{7,55},{8,56},{9,... | collective-permute-start | bytes 786440 | tf_op jit(solution)/shard_map/ppermute | solution.py:41
  113.5 16.0 %collective-permute-start.22 = (bf16[16,64,128]{2,1,0:T(8,128)(2,1)S(1)}, bf16[16,64,128]{2,1,0:T(8,128)(2,1)S(1)}, u32[]{:S(2)}, u32[]{:S(2)}) collective-permute-start(bf16[16,64,128]{2,1,0:T(8,128)(2,1)S(1)} %constant_dynamic-update-slice_fusion.7), channel_id=1, source_target_pairs={{0,48},{1,49},{2,50},{3,51},{4,52},{5,53},{6,54},{7,55},{8,56},{9,... | collective-permute-start | bytes 786440 | tf_op jit(solution)/shard_map/ppermute | solution.py:41
  114.3 15.2 %collective-permute-start.25 = (bf16[16,64,128]{2,1,0:T(8,128)(2,1)S(1)}, bf16[16,64,128]{2,1,0:T(8,128)(2,1)S(1)}, u32[]{:S(2)}, u32[]{:S(2)}) collective-permute-start(bf16[16,64,128]{2,1,0:T(8,128)(2,1)S(1)} %constant_dynamic-update-slice_fusion.12), channel_id=1, source_target_pairs={{0,72},{1,73},{2,74},{3,75},{4,76},{5,77},{6,78},{7,79},{8,64},{9,... | collective-permute-start | bytes 786440 | tf_op jit(solution)/shard_map/ppermute | solution.py:41
  125.0 13.8 %collective-permute-start.20 = (bf16[16,64,128]{2,1,0:T(8,128)(2,1)}, bf16[16,64,128]{2,1,0:T(8,128)(2,1)}, u32[]{:S(2)}, u32[]{:S(2)}) collective-permute-start(bf16[16,64,128]{2,1,0:T(8,128)(2,1)} %collective-permute-done.18), channel_id=1, source_target_pairs={{0,8},{1,9},{2,10},{3,11},{4,12},{5,13},{6,14},{7,15},{8,0},{9,1},... | collective-permute-start | bytes 786440 | tf_op jit(solution)/shard_map/ppermute | solution.py:41
  125.4 13.3 %collective-permute-start.23 = (bf16[16,64,128]{2,1,0:T(8,128)(2,1)}, bf16[16,64,128]{2,1,0:T(8,128)(2,1)}, u32[]{:S(2)}, u32[]{:S(2)}) collective-permute-start(bf16[16,64,128]{2,1,0:T(8,128)(2,1)} %collective-permute-done.21), channel_id=1, source_target_pairs={{0,48},{1,49},{2,50},{3,51},{4,52},{5,53},{6,54},{7,55},{8,56},{9,... | collective-permute-start | bytes 786440 | tf_op jit(solution)/shard_map/ppermute | solution.py:41
  126.0 12.8 %collective-permute-start.26 = (bf16[16,64,128]{2,1,0:T(8,128)(2,1)}, bf16[16,64,128]{2,1,0:T(8,128)(2,1)}, u32[]{:S(2)}, u32[]{:S(2)}) collective-permute-start(bf16[16,64,128]{2,1,0:T(8,128)(2,1)} %collective-permute-done.24), channel_id=1, source_target_pairs={{0,72},{1,73},{2,74},{3,75},{4,76},{5,77},{6,78},{7,79},{8,64},{9,... | collective-permute-start | bytes 786440 | tf_op jit(solution)/shard_map/ppermute | solution.py:41
  145.1 18.7 %all-to-all-start.1 = ((bf16[8,144,384]{2,1,0:T(8,128)(2,1)}), bf16[8,144,384]{2,1,0:T(8,128)(2,1)}, u32[]{:S(2)}, u32[]{:S(2)}) async-start(bf16[8,144,384]{2,1,0:T(8,128)(2,1)} %bitcast.329), calls=%async_computation.1 | async-start | bytes 1769472 | tf_op jit(solution)/shard_map/all_to_all | solution.py:553
  153.3 23.7 %collective-permute-start.28 = (bf16[16,64,128]{2,1,0:T(8,128)(2,1)S(1)}, bf16[16,64,128]{2,1,0:T(8,128)(2,1)S(1)}, u32[]{:S(2)}, u32[]{:S(2)}) collective-permute-start(bf16[16,64,128]{2,1,0:T(8,128)(2,1)S(1)} %constant_dynamic-update-slice_fusion.17), channel_id=1, source_target_pairs={{0,16},{1,17},{2,18},{3,19},{4,20},{5,21},{6,22},{7,23},{8,24},{9,... | collective-permute-start | bytes 786440 | tf_op jit(solution)/shard_map/ppermute | solution.py:41
  156.5 20.5 %collective-permute-start.29 = (bf16[16,64,128]{2,1,0:T(8,128)(2,1)S(1)}, bf16[16,64,128]{2,1,0:T(8,128)(2,1)S(1)}, u32[]{:S(2)}, u32[]{:S(2)}) collective-permute-start(bf16[16,64,128]{2,1,0:T(8,128)(2,1)S(1)} %collective-permute-done.27), channel_id=1, source_target_pairs={{0,16},{1,17},{2,18},{3,19},{4,20},{5,21},{6,22},{7,23},{8,24},{9,... | collective-permute-start | bytes 786440 | tf_op jit(solution)/shard_map/ppermute | solution.py:41
  416.9 17.5 %all-to-all-start.6 = ((bf16[8,144,384]{2,1,0:T(8,128)(2,1)}), bf16[8,144,384]{2,1,0:T(8,128)(2,1)S(1)}, u32[]{:S(2)}, u32[]{:S(2)}) async-start(bf16[8,144,384]{2,1,0:T(8,128)(2,1)} %bitcast.357), calls=%async_computation.6 | async-start | bytes 1769472 | tf_op jit(solution)/shard_map/all_to_all | solution.py:553
  420.5 55.8 %collective-permute-start.45 = (bf16[32,64,512]{2,1,0:T(8,128)(2,1)}, bf16[32,64,512]{2,1,0:T(8,128)(2,1)}, u32[]{:S(2)}, u32[]{:S(2)}) collective-permute-start(bf16[32,64,512]{2,1,0:T(8,128)(2,1)} %bitcast.440), channel_id=1, source_target_pairs={{0,8},{1,9},{2,10},{3,11},{4,12},{5,13},{6,14},{7,15},{8,0},{9,1},... | collective-permute-start | bytes 6291464 | tf_op jit(solution)/shard_map/ppermute | solution.py:41
  421.9 57.9 %collective-permute-start.53 = (bf16[32,64,512]{2,1,0:T(8,128)(2,1)}, bf16[32,64,512]{2,1,0:T(8,128)(2,1)}, u32[]{:S(2)}, u32[]{:S(2)}) collective-permute-start(bf16[32,64,512]{2,1,0:T(8,128)(2,1)} %bitcast.439), channel_id=1, source_target_pairs={{0,72},{1,73},{2,74},{3,75},{4,76},{5,77},{6,78},{7,79},{8,64},{9,... | collective-permute-start | bytes 6291464 | tf_op jit(solution)/shard_map/ppermute | solution.py:41
  449.7 67.4 %collective-permute-start.47 = (bf16[32,64,256]{2,1,0:T(8,128)(2,1)}, bf16[32,64,256]{2,1,0:T(8,128)(2,1)}, u32[]{:S(2)}, u32[]{:S(2)}) collective-permute-start(bf16[32,64,256]{2,1,0:T(8,128)(2,1)} %bitcast.442), channel_id=1, source_target_pairs={{0,8},{1,9},{2,10},{3,11},{4,12},{5,13},{6,14},{7,15},{8,0},{9,1},... | collective-permute-start | bytes 3145736 | tf_op jit(solution)/shard_map/ppermute | solution.py:41
  449.9 83.1 %collective-permute-start.55 = (bf16[32,64,256]{2,1,0:T(8,128)(2,1)}, bf16[32,64,256]{2,1,0:T(8,128)(2,1)}, u32[]{:S(2)}, u32[]{:S(2)}) collective-permute-start(bf16[32,64,256]{2,1,0:T(8,128)(2,1)} %bitcast.441), channel_id=1, source_target_pairs={{0,72},{1,73},{2,74},{3,75},{4,76},{5,77},{6,78},{7,79},{8,64},{9,... | collective-permute-start | bytes 3145736 | tf_op jit(solution)/shard_map/ppermute | solution.py:41
  454.4 33.4 %collective-permute-start.41 = (bf16[144,1024]{1,0:T(8,128)(2,1)S(1)}, bf16[144,1024]{1,0:T(8,128)(2,1)S(1)}, u32[]{:S(2)}, u32[]{:S(2)}) collective-permute-start(bf16[144,1024]{1,0:T(8,128)(2,1)S(1)} %convert_element_type.572), channel_id=1, source_target_pairs={{0,4},{1,5},{2,6},{3,7},{4,0},{5,1},{6,2},{7,3},{8,12},{9,13},{10,... | collective-permute-start | bytes 884744 | tf_op jit(solution)/shard_map/ppermute | solution.py:41
  479.8 102.3 %collective-permute-start.46 = (bf16[16,64,512]{2,1,0:T(8,128)(2,1)}, bf16[16,64,512]{2,1,0:T(8,128)(2,1)S(1)}, u32[]{:S(2)}, u32[]{:S(2)}) collective-permute-start(bf16[16,64,512]{2,1,0:T(8,128)(2,1)} %slice.720), channel_id=1, source_target_pairs={{0,16},{1,17},{2,18},{3,19},{4,20},{5,21},{6,22},{7,23},{8,24},{9,... | collective-permute-start | bytes 3145736 | tf_op jit(solution)/shard_map/ppermute | solution.py:41
  485.0 102.5 %collective-permute-start.54 = (bf16[16,64,512]{2,1,0:T(8,128)(2,1)}, bf16[16,64,512]{2,1,0:T(8,128)(2,1)}, u32[]{:S(2)}, u32[]{:S(2)}) collective-permute-start(bf16[16,64,512]{2,1,0:T(8,128)(2,1)} %slice.732), channel_id=1, source_target_pairs={{0,48},{1,49},{2,50},{3,51},{4,52},{5,53},{6,54},{7,55},{8,56},{9,... | collective-permute-start | bytes 3145736 | tf_op jit(solution)/shard_map/ppermute | solution.py:41
  510.2 119.7 %collective-permute-start.61 = (bf16[32,64,512]{2,1,0:T(8,128)(2,1)}, bf16[32,64,512]{2,1,0:T(8,128)(2,1)}, u32[]{:S(2)}, u32[]{:S(2)}) collective-permute-start(bf16[32,64,512]{2,1,0:T(8,128)(2,1)} %bitcast.438), channel_id=1, source_target_pairs={{0,8},{1,9},{2,10},{3,11},{4,12},{5,13},{6,14},{7,15},{8,0},{9,1},... | collective-permute-start | bytes 6291464 | tf_op jit(solution)/shard_map/ppermute | solution.py:41
  520.7 113.3 %collective-permute-start.67 = (bf16[32,64,512]{2,1,0:T(8,128)(2,1)}, bf16[32,64,512]{2,1,0:T(8,128)(2,1)}, u32[]{:S(2)}, u32[]{:S(2)}) collective-permute-start(bf16[32,64,512]{2,1,0:T(8,128)(2,1)} %bitcast.126), channel_id=1, source_target_pairs={{0,72},{1,73},{2,74},{3,75},{4,76},{5,77},{6,78},{7,79},{8,64},{9,... | collective-permute-start | bytes 6291464 | tf_op jit(solution)/shard_map/ppermute | solution.py:41
  529.6 31.4 %all-to-all-start.7 = ((bf16[8,144,128]{2,1,0:T(8,128)(2,1)}), bf16[8,144,128]{2,1,0:T(8,128)(2,1)S(1)}, u32[]{:S(2)}, u32[]{:S(2)}) async-start(bf16[8,144,128]{2,1,0:T(8,128)(2,1)} %bitcast.340), calls=%async_computation.7 | async-start | bytes 589824 | tf_op jit(solution)/shard_map/all_to_all | solution.py:553
  533.0 56.2 %collective-permute-start.48 = (bf16[16,64,256]{2,1,0:T(8,128)(2,1)}, bf16[16,64,256]{2,1,0:T(8,128)(2,1)}, u32[]{:S(2)}, u32[]{:S(2)}) collective-permute-start(bf16[16,64,256]{2,1,0:T(8,128)(2,1)} %slice.722), channel_id=1, source_target_pairs={{0,16},{1,17},{2,18},{3,19},{4,20},{5,21},{6,22},{7,23},{8,24},{9,... | collective-permute-start | bytes 1572872 | tf_op jit(solution)/shard_map/ppermute | solution.py:41
  576.0 16.9 %all-to-all-start.9 = ((f32[128,1,512]{2,1,0:T(1,128)}), f32[128,1,512]{2,1,0:T(1,128)}, u32[]{:S(2)}, u32[]{:S(2)}) async-start(f32[128,1,512]{2,1,0:T(1,128)} %all_to_all.43), calls=%async_computation.9 | async-start | bytes 524288 | tf_op jit(solution)/shard_map/all_to_all | solution.py:769
  583.0 16.8 %collective-permute-start.56 = (bf16[16,64,256]{2,1,0:T(8,128)(2,1)}, bf16[16,64,256]{2,1,0:T(8,128)(2,1)}, u32[]{:S(2)}, u32[]{:S(2)}) collective-permute-start(bf16[16,64,256]{2,1,0:T(8,128)(2,1)} %slice.734), channel_id=1, source_target_pairs={{0,48},{1,49},{2,50},{3,51},{4,52},{5,53},{6,54},{7,55},{8,56},{9,... | collective-permute-start | bytes 1572872 | tf_op jit(solution)/shard_map/ppermute | solution.py:41
  592.9 18.4 %all-to-all-start.8 = ((bf16[8,144,384]{2,1,0:T(8,128)(2,1)}), bf16[8,144,384]{2,1,0:T(8,128)(2,1)}, u32[]{:S(2)}, u32[]{:S(2)}) async-start(bf16[8,144,384]{2,1,0:T(8,128)(2,1)} %bitcast.356), calls=%async_computation.8 | async-start | bytes 1769472 | tf_op jit(solution)/shard_map/all_to_all | solution.py:553
  598.1 26.6 %collective-permute-start.49 = (bf16[8,64,768]{2,1,0:T(8,128)(2,1)}, bf16[8,64,768]{2,1,0:T(8,128)(2,1)}, u32[]{:S(2)}, u32[]{:S(2)}) collective-permute-start(bf16[8,64,768]{2,1,0:T(8,128)(2,1)} %pad_maximum_fusion.1), channel_id=1, source_target_pairs={{0,72},{1,73},{2,74},{3,75},{4,76},{5,77},{6,78},{7,79},{8,64},{9,... | collective-permute-start | bytes 2359304 | tf_op jit(solution)/shard_map/ppermute | solution.py:41
  602.8 25.6 %collective-permute-start.57 = (bf16[8,64,768]{2,1,0:T(8,128)(2,1)}, bf16[8,64,768]{2,1,0:T(8,128)(2,1)}, u32[]{:S(2)}, u32[]{:S(2)}) collective-permute-start(bf16[8,64,768]{2,1,0:T(8,128)(2,1)} %pad_maximum_fusion), channel_id=1, source_target_pairs={{0,16},{1,17},{2,18},{3,19},{4,20},{5,21},{6,22},{7,23},{8,24},{9,... | collective-permute-start | bytes 2359304 | tf_op jit(solution)/shard_map/ppermute | solution.py:41
  623.6 80.0 %collective-permute-start.44 = (bf16[144,1024]{1,0:T(8,128)(2,1)S(1)}, bf16[144,1024]{1,0:T(8,128)(2,1)S(1)}, u32[]{:S(2)}, u32[]{:S(2)}) collective-permute-start(bf16[144,1024]{1,0:T(8,128)(2,1)S(1)} %slice.921), channel_id=1, source_target_pairs={{0,4},{1,5},{2,6},{3,7},{4,0},{5,1},{6,2},{7,3},{8,12},{9,13},{10,... | collective-permute-start | bytes 884744 | tf_op jit(solution)/shard_map/ppermute | solution.py:41
  626.1 12.0 %collective-permute-start.50 = (bf16[4,64,768]{2,1,0:T(8,128)(2,1)S(1)}, bf16[4,64,768]{2,1,0:T(8,128)(2,1)S(1)}, u32[]{:S(2)}, u32[]{:S(2)}) collective-permute-start(bf16[4,64,768]{2,1,0:T(8,128)(2,1)S(1)} %slice.726), channel_id=1, source_target_pairs={{0,3},{1,2},{2,1},{3,0},{4,7},{5,6},{6,5},{7,4},{8,11},{9,10},{10,... | collective-permute-start | bytes 1179656 | tf_op jit(solution)/shard_map/ppermute | solution.py:41
  632.4 35.1 %collective-permute-start.62 = (bf16[16,64,512]{2,1,0:T(8,128)(2,1)S(1)}, bf16[16,64,512]{2,1,0:T(8,128)(2,1)S(1)}, u32[]{:S(2)}, u32[]{:S(2)}) collective-permute-start(bf16[16,64,512]{2,1,0:T(8,128)(2,1)S(1)} %slice.744), channel_id=1, source_target_pairs={{0,16},{1,17},{2,18},{3,19},{4,20},{5,21},{6,22},{7,23},{8,24},{9,... | collective-permute-start | bytes 3145736 | tf_op jit(solution)/shard_map/ppermute | solution.py:41
  636.5 33.3 %collective-permute-start.68 = (bf16[16,64,512]{2,1,0:T(8,128)(2,1)S(1)}, bf16[16,64,512]{2,1,0:T(8,128)(2,1)S(1)}, u32[]{:S(2)}, u32[]{:S(2)}) collective-permute-start(bf16[16,64,512]{2,1,0:T(8,128)(2,1)S(1)} %slice.754), channel_id=1, source_target_pairs={{0,48},{1,49},{2,50},{3,51},{4,52},{5,53},{6,54},{7,55},{8,56},{9,... | collective-permute-start | bytes 3145736 | tf_op jit(solution)/shard_map/ppermute | solution.py:41
  638.2 27.7 %collective-permute-start.51 = (bf16[2,64,768]{2,1,0:T(8,128)(2,1)S(1)}, bf16[2,64,768]{2,1,0:T(8,128)(2,1)S(1)}, u32[]{:S(2)}, u32[]{:S(2)}) collective-permute-start(bf16[2,64,768]{2,1,0:T(8,128)(2,1)S(1)} %slice.728), channel_id=1, source_target_pairs={{0,48},{1,49},{2,50},{3,51},{4,52},{5,53},{6,54},{7,55},{8,56},{9,... | collective-permute-start | bytes 589832 | tf_op jit(solution)/shard_map/ppermute | solution.py:41
  640.4 30.0 %collective-permute-start.59 = (bf16[2,64,768]{2,1,0:T(8,128)(2,1)S(1)}, bf16[2,64,768]{2,1,0:T(8,128)(2,1)S(1)}, u32[]{:S(2)}, u32[]{:S(2)}) collective-permute-start(bf16[2,64,768]{2,1,0:T(8,128)(2,1)S(1)} %slice.740), channel_id=1, source_target_pairs={{0,8},{1,9},{2,10},{3,11},{4,12},{5,13},{6,14},{7,15},{8,0},{9,1},... | collective-permute-start | bytes 589832 | tf_op jit(solution)/shard_map/ppermute | solution.py:41
  667.8 12.7 %collective-permute-start.63 = (bf16[8,64,512]{2,1,0:T(8,128)(2,1)S(1)}, bf16[8,64,512]{2,1,0:T(8,128)(2,1)S(1)}, u32[]{:S(2)}, u32[]{:S(2)}) collective-permute-start(bf16[8,64,512]{2,1,0:T(8,128)(2,1)S(1)} %slice.746), channel_id=1, source_target_pairs={{0,72},{1,73},{2,74},{3,75},{4,76},{5,77},{6,78},{7,79},{8,64},{9,... | collective-permute-start | bytes 1572872 | tf_op jit(solution)/shard_map/ppermute | solution.py:41
  670.2 11.6 %collective-permute-start.69 = (bf16[8,64,512]{2,1,0:T(8,128)(2,1)S(1)}, bf16[8,64,512]{2,1,0:T(8,128)(2,1)S(1)}, u32[]{:S(2)}, u32[]{:S(2)}) collective-permute-start(bf16[8,64,512]{2,1,0:T(8,128)(2,1)S(1)} %slice.756), channel_id=1, source_target_pairs={{0,16},{1,17},{2,18},{3,19},{4,20},{5,21},{6,22},{7,23},{8,24},{9,... | collective-permute-start | bytes 1572872 | tf_op jit(solution)/shard_map/ppermute | solution.py:41
  697.3 13.5 %collective-permute-start.98 = (bf16[32,2,1280]{2,0,1:T(8,128)(2,1)S(1)}, bf16[32,2,1280]{2,0,1:T(8,128)(2,1)S(1)}, u32[]{:S(2)}, u32[]{:S(2)}) collective-permute-start(bf16[32,2,1280]{2,0,1:T(8,128)(2,1)S(1)} %fusion.38), channel_id=1, source_target_pairs={{0,4},{1,5},{2,6},{3,7},{4,0},{5,1},{6,2},{7,3},{8,12},{9,13},{10,... | collective-permute-start | bytes 491528 | tf_op jit(solution)/shard_map/ppermute | solution.py:41
  707.0 13.7 %collective-permute-start.91 = (bf16[32,64,128]{2,1,0:T(8,128)(2,1)}, bf16[32,64,128]{2,1,0:T(8,128)(2,1)S(1)}, u32[]{:S(2)}, u32[]{:S(2)}) collective-permute-start(bf16[32,64,128]{2,1,0:T(8,128)(2,1)} %bitcast.111), channel_id=1, source_target_pairs={{0,16},{1,17},{2,18},{3,19},{4,20},{5,21},{6,22},{7,23},{8,24},{9,... | collective-permute-start | bytes 1572872 | tf_op jit(solution)/shard_map/ppermute | solution.py:41
  707.0 16.6 %collective-permute-start.85 = (bf16[32,64,128]{2,1,0:T(8,128)(2,1)}, bf16[32,64,128]{2,1,0:T(8,128)(2,1)S(1)}, u32[]{:S(2)}, u32[]{:S(2)}) collective-permute-start(bf16[32,64,128]{2,1,0:T(8,128)(2,1)} %bitcast.109), channel_id=1, source_target_pairs={{0,72},{1,73},{2,74},{3,75},{4,76},{5,77},{6,78},{7,79},{8,64},{9,... | collective-permute-start | bytes 1572872 | tf_op jit(solution)/shard_map/ppermute | solution.py:41
  709.5 15.4 %collective-permute-start.79 = (bf16[32,64,128]{2,1,0:T(8,128)(2,1)}, bf16[32,64,128]{2,1,0:T(8,128)(2,1)S(1)}, u32[]{:S(2)}, u32[]{:S(2)}) collective-permute-start(bf16[32,64,128]{2,1,0:T(8,128)(2,1)} %bitcast.107), channel_id=1, source_target_pairs={{0,48},{1,49},{2,50},{3,51},{4,52},{5,53},{6,54},{7,55},{8,56},{9,... | collective-permute-start | bytes 1572872 | tf_op jit(solution)/shard_map/ppermute | solution.py:41
  710.6 14.7 %collective-permute-start.73 = (bf16[32,64,128]{2,1,0:T(8,128)(2,1)}, bf16[32,64,128]{2,1,0:T(8,128)(2,1)S(1)}, u32[]{:S(2)}, u32[]{:S(2)}) collective-permute-start(bf16[32,64,128]{2,1,0:T(8,128)(2,1)} %bitcast.105), channel_id=1, source_target_pairs={{0,8},{1,9},{2,10},{3,11},{4,12},{5,13},{6,14},{7,15},{8,0},{9,1},... | collective-permute-start | bytes 1572872 | tf_op jit(solution)/shard_map/ppermute | solution.py:41
  (116 other events, 942.6 us)
Sparse Core Ops, SparseCore 0:
  13.1 26.8 all-gather.4
  42.5 130.0 all-gather.6
  174.4 64.9 all-gather.8
  240.9 109.4 all-gather.10

commit v4 on v3

--- a/solution.py
+++ b/solution.py
@@ -70,8 +70,8 @@
     return [add_low(value[:half], new) for value, new in zip(parts, got)]
 
 
-def reduce_rest(parts, orders):
-    for phase in range(2, 6):
+def reduce_phases(parts, orders, first):
+    for phase in range(first, 6):
         parts = reduce_phase(parts, orders, phase)
     return [value[0] for value in parts]
 
@@ -232,8 +232,7 @@
 
 
 APART = [Grads(k, 128, 0) for k in range(4)]
-PAIRED = [Grads(k, 256, at) for k in (0, 2) for at in (0, 128)]
-FEED = [Grads(k, 512, at) for k in (0, 2) for at in (0, 256)]
+FEED = [Grads(k, 256, 0) for k in range(4)]
 
 
 def halves(refs):
@@ -576,32 +575,37 @@
     lead = both_rows(
         jnp.concatenate(
             [
-                w_qkv[0].reshape(32, 3, 2, 128).transpose(0, 2, 1, 3).reshape(32, 2, 384),
-                w_out[0].T.reshape(32, 2, 128),
+                jnp.concatenate(
+                    [
+                        w_qkv[layer].reshape(32, 3, 2, 128).transpose(0, 2, 1, 3).reshape(
+                            32, 2, 384
+                        ),
+                        w_out[layer].T.reshape(32, 2, 128),
+                    ],
+                    2,
+                )
+                for layer in range(2)
             ],
             2,
         )
-    )
-    lead = gather_early([lead[None, :, k * 128 : (k + 1) * 128] for k in range(4)])
-    lead, norm_gains = lax.optimization_barrier((lead, norm_gains))
-    lead = gather_late(lead)
-
-    later = jnp.concatenate(
-        [w_in[0], w_back[0].T, w_qkv[1].reshape(32, 768), w_out[1].T, w_in[1], w_back[1].T], 1
-    )
+    ).reshape(1, 64, 2, 4, 128)
+    lead = gather_early([lead[:, :, :, k].reshape(1, 64, 256) for k in range(4)])
+    later = jnp.concatenate([w_in[0], w_back[0].T, w_in[1], w_back[1].T], 1)
     later = lax.all_gather(later, "tensor", axis=0, tiled=True)
+    lead, norm_gains, later = lax.optimization_barrier((lead, norm_gains, later))
+    lead_one = [value[:, :, 128:] for value in lead]
+    lead = gather_late([value[:, :, :128] for value in lead])
+    lead, lead_one = lax.optimization_barrier((lead, lead_one))
+    near_one = [swap(value, *ORDERS[k][4]) for k, value in enumerate(lead_one)]
+    far_one = [swap(value, *ORDERS[k][5]) for k, value in enumerate(lead_one)]
 
     def everywhere(value):
         value = lax.all_gather(value, ("dp", "ctx"), axis=0, tiled=True)
         return value.reshape(16, 2, 4, 32, value.shape[1])
 
     feed_zero = everywhere(later[:, :2048])
-    attention_one = everywhere(later[:, 2048:3072])
-    feed_one = everywhere(later[:, 3072:])
-    attention_w = [
-        [Exchanged(k, lead[k], 128) for k in range(4)],
-        [Gathered(attention_one, 2 * k, 128, 1) for k in range(4)],
-    ]
+    feed_one = everywhere(later[:, 2048:])
+    attention_w = [[Exchanged(k, lead[k], 128) for k in range(4)]]
     feed_w = [
         [Gathered(value, base, 256, 2) for base in (0, 1, 4, 5)] for value in (feed_zero, feed_one)
     ]
@@ -669,8 +673,15 @@
         gathered = both(state.astype(LOW))
         qkv = project(order, gathered, attention_w[layer], bias[0], bias[1])
         qkv = trade(qkv.reshape(8, 2 * rows, 384)).reshape(16 * rows, 384)
+        if layer == 0:
+            qkv, near_one, far_one = lax.optimization_barrier((qkv, near_one, far_one))
+            last_one = [swap(value, *ORDERS[k][5]) for k, value in enumerate(near_one)]
         mixed, summary = attend(qkv, marks_t, marks)
         mixed = trade(mixed.reshape(8, 2 * rows, 128)).reshape(2, 4, 2 * rows, 128)
+        if layer == 0:
+            mixed, last_one = lax.optimization_barrier((mixed, last_one))
+            pieces = zip(lead_one, near_one, far_one, last_one)
+            attention_w.append([Exchanged(k, four, 128) for k, four in enumerate(pieces)])
         mixed, attended = mix(order, mixed, attention_w[layer][3])
         attended = own_sum(attended) + shift[layer, 2]
         first, unit_one, inv_one = normalize(state + attended, gains[layer, 0], shift[layer, 0])
@@ -697,31 +708,40 @@
         grad_feed, grad_upbias, grad_first = feed_back(
             order, spread_two, gathered_two, hidden, active, feed_w[layer]
         )
-        grad_feed = reduce_first(grad_feed, (0, 2))
+        grad_feed = reduce_first(grad_feed, range(4))
         grad_first = grad_two + own_sum(grad_first)
         grad_one, gain_one, shift_one = normalize_back(
             grad_first, unit_one, inv_one, gains[layer, 0]
         )
         spread_one = both(grad_one.astype(LOW))
+        if layer == 0:
+            spread_one, later = lax.optimization_barrier((spread_one, later))
         grad_mixed = trade(mix_back(order, spread_one, attention_w[layer][3]).reshape(8, 2 * rows, 128))
         grad_mixed = grad_mixed.reshape(16 * rows, 128)
+        if layer == 0:
+            grad_mixed, grad_feed = lax.optimization_barrier((grad_mixed, grad_feed))
+            tail = [jnp.concatenate([a, b], 2) for a, b in zip(grad_feed, later)]
+            tail = reduce_phase(reduce_phase(tail, range(4), 2), range(4), 3)
         low_packed, grad_pair = attend_back(qkv, grad_mixed, marks_t, marks, summary)
         grad_pair = grad_pair.reshape(2, 2, 64).sum(1)
         low_packed = trade(low_packed.reshape(8, 2 * rows, 384)).reshape(2, 4, 2 * rows, 384)
+        if layer:
+            low_packed, grad_feed = lax.optimization_barrier((low_packed, grad_feed))
+        else:
+            low_packed, tail = lax.optimization_barrier((low_packed, tail))
         grad_attention, grad_x = project_back(
             order, low_packed, gathered, spread_one, mixed, attention_w[layer],
-            PAIRED if layer else APART,
+            APART,
         )
         incoming = grad_one + own_sum(grad_x)
         if layer:
-            grad_attention = reduce_first(grad_attention, (0, 2))
-            later = reduce_rest(
-                [jnp.concatenate(pair, 2) for pair in zip(grad_feed, grad_attention)], (0, 2)
-            )
+            grad_attention = reduce_first(grad_attention, range(4))
+            later = [jnp.concatenate(pair, 2) for pair in zip(grad_feed, grad_attention)]
         else:
-            tail = reduce_rest(grad_feed, (0, 2))
-            grad_attention, later, tail = lax.optimization_barrier((grad_attention, later, tail))
-            lead = reduce_rest(reduce_first(grad_attention, range(4)), range(4))
+            lead = reduce_first(grad_attention, range(4))
+            lead = reduce_phase(reduce_phase(lead, range(4), 2), range(4), 3)
+            tail = [jnp.concatenate(pair, 2) for pair in zip(tail, lead)]
+            tail = reduce_phases(tail, range(4), 4)
         small[layer] = (
             jnp.stack([gain_one, gain_two]),
             jnp.stack(
@@ -741,10 +761,9 @@
             [jnp.where(core == 0, keep, new), jnp.where(core == 0, new, keep)], 1
         ).astype(FULL)
 
-    tail = own_rows([jnp.concatenate([a, b], 1) for a, b in zip(tail, later)])
-    lead = own_rows(lead)
-    attention = [lead, tail[..., 1024:].reshape(32, 2, 4, 128)]
-    feeds = [tail[..., i * 512 : (i + 1) * 512].reshape(32, 2, 4, 256) for i in range(2)]
+    tail = own_rows(tail)
+    attention = [tail[..., 640:], tail[..., 512:640]]
+    feeds = [tail[..., :256], tail[..., 256:512]]
     out_qkv = jnp.stack(
         [value[:, :, :3].transpose(0, 2, 1, 3).reshape(32, 3, 256) for value in attention]
     )

time: 779 us -> 689 us (0.88)
  waiting for transfers between devices: 297 us -> 178 us
  starting transfers between devices: 148 us -> 186 us
  blocking collectives: 42.7 us -> 29.6 us
  other arithmetic: 54.1 us -> 62.2 us
    all_gather x3 -> x2, waiting for transfers between devices: 76 us -> 20.6 us  [everywhere(): value = lax.all_gather(value, ('dp', 'ctx'), axis=0, tiled=True)]
    all_to_all x5 -> x6, waiting for transfers between devices: 49.1 us -> 14.2 us  [trade(): lax.all_to_all(value, ('ctx', 'tensor'), 0, 0, axis_index_groups=GROUPS,...]
    all_gather x1, waiting for transfers between devices: 27 us -> 0.02 us  [local(): later = lax.all_gather(later, 'tensor', axis=0, tiled=True)]
    ppermute x99 -> x114, starting transfers between devices: 111 us -> 132 us  [swap(): return lax.ppermute(value, ALL, exchange_perm(axis, mask))]
    all_to_all x5 -> x6, starting transfers between devices: 20.2 us -> 35.4 us  [trade(): lax.all_to_all(value, ('ctx', 'tensor'), 0, 0, axis_index_groups=GROUPS,...]
    all_to_all x3 -> x2, blocking collectives: 42.7 us -> 29.6 us  [trade(): lax.all_to_all(value, ('ctx', 'tensor'), 0, 0, axis_index_groups=GROUPS,...]
    convert_element_type x48 -> x56, other arithmetic: 24.1 us -> 29.4 us  [add_low(): return (left.astype(FULL) + right.astype(FULL)).astype(LOW)]
    ppermute x99 -> x114, waiting for transfers between devices: 132 us -> 130 us  [swap(): return lax.ppermute(value, ALL, exchange_perm(axis, mask))]
  transfers between devices with their start and end apart: 110 -> 125, of which waited for: 49 -> 52; matrix products, arithmetic and copies ran while one was open for 12% -> 15% of each run, Pallas kernels for 13% -> 12%
where the time goes in v4:
time: 689 us; the launch traced here: 677 us
  starting transfers between devices  186 us (27%)
  waiting for transfers between devices  178 us (26%)
  Pallas kernels  142 us (21%)
  other arithmetic  62.2 us (9%)
  local copies, waits for them, and re-layouts  50.9 us (7%)
  blocking collectives  29.6 us (4%)
  between operations  17 us (2%)
  matrix products  11.4 us (2%)
    pallas_call x16, Pallas kernels, call(): pl.pallas_call(body, grid_spec=pltpu.PrefetchScalarGridSpec(num_scalar_pr...  142 us
    ppermute x114, starting transfers between devices, swap(): return lax.ppermute(value, ALL, exchange_perm(axis, mask))  132 us
    ppermute x114, waiting for transfers between devices, swap(): return lax.ppermute(value, ALL, exchange_perm(axis, mask))  130 us
    all_to_all x6, starting transfers between devices, trade(): lax.all_to_all(value, ('ctx', 'tensor'), 0, 0, axis_index_groups=GROUPS,...  35.4 us
    all_to_all x2, blocking collectives, trade(): lax.all_to_all(value, ('ctx', 'tensor'), 0, 0, axis_index_groups=GROUPS,...  29.6 us
    convert_element_type x56, other arithmetic, add_low(): return (left.astype(FULL) + right.astype(FULL)).astype(LOW)  29.4 us
    all_gather x2, waiting for transfers between devices, everywhere(): value = lax.all_gather(value, ('dp', 'ctx'), axis=0, tiled=True)  20.6 us
    all_to_all x6, waiting for transfers between devices, trade(): lax.all_to_all(value, ('ctx', 'tensor'), 0, 0, axis_index_groups=GROUPS,...  14.2 us
  transfers between devices with their start and end apart: 125, of which 52 were waited for; matrix products, arithmetic and copies ran while one was open for 15% of the time, Pallas kernels for 12%

profile of v4, /device:TPU:1, one launch (start us, length us, event | category | flops | bytes accessed | tf_op | source)
XLA Modules:
  0.0 677.5 jit_solution(801612372822761068)
XLA Ops:
  24.6 3.6 collective-permute-start.7
  29.5 3.5 collective-permute-done.3
  55.0 10.7 %all-to-all-start = ((bf16[128,2,256]{2,1,0:T(2,128)(2,1)}), bf16[128,2,256]{2,1,0:T(2,128)(2,1)S(1)}, u32[]{:S(2)}, u32[]{:S(2)}) async-start(bf16[128,2,256]{2,1,0:T(2,128)(2,1)} %reshape.742), calls=%async_computation | async-start | bytes 262144 | tf_op jit(solution)/shard_map/all_to_all | solution.py:617
  66.5 9.1 %all-to-all-done = bf16[128,2,256]{2,1,0:T(2,128)(2,1)S(1)} async-done(((bf16[128,2,256]{2,1,0:T(2,128)(2,1)}), bf16[128,2,256]{2,1,0:T(2,128)(2,1)S(1)}, u32[]{:S(2)}, u32[]{:S(2)}) %all-to-all-start) | async-done | bytes 131104 | tf_op jit(solution)/shard_map/all_to_all | solution.py:617
  85.2 4.0 collective-permute-done.24
  103.0 6.3 collective-permute-done.29
  109.3 6.5 shard_map.186
  115.9 12.7 %all-to-all-start.1 = ((bf16[8,144,384]{2,1,0:T(8,128)(2,1)}), bf16[8,144,384]{2,1,0:T(8,128)(2,1)}, u32[]{:S(2)}, u32[]{:S(2)}) async-start(bf16[8,144,384]{2,1,0:T(8,128)(2,1)} %bitcast.331), calls=%async_computation.1 | async-start | bytes 1769472 | tf_op jit(solution)/shard_map/all_to_all | solution.py:552
  133.5 8.3 %collective-permute-done.30 = bf16[16,64,128]{2,1,0:T(8,128)(2,1)S(1)} collective-permute-done((bf16[16,64,128]{2,1,0:T(8,128)(2,1)S(1)}, bf16[16,64,128]{2,1,0:T(8,128)(2,1)S(1)}, u32[]{:S(2)}, u32[]{:S(2)}) %collective-permute-start.30) | collective-permute-done | bytes 262176 | tf_op jit(solution)/shard_map/ppermute | solution.py:41
  144.5 9.9 %collective-permute-done.31 = bf16[16,64,128]{2,1,0:T(8,128)(2,1)} collective-permute-done((bf16[16,64,128]{2,1,0:T(8,128)(2,1)S(1)}, bf16[16,64,128]{2,1,0:T(8,128)(2,1)}, u32[]{:S(2)}, u32[]{:S(2)}) %collective-permute-start.31) | collective-permute-done | bytes 262176 | tf_op jit(solution)/shard_map/ppermute | solution.py:41
  156.7 8.9 %collective-permute-done.34 = bf16[16,64,128]{2,1,0:T(8,128)(2,1)S(1)} collective-permute-done((bf16[16,64,128]{2,1,0:T(8,128)(2,1)S(1)}, bf16[16,64,128]{2,1,0:T(8,128)(2,1)S(1)}, u32[]{:S(2)}, u32[]{:S(2)}) %collective-permute-start.34) | collective-permute-done | bytes 262176 | tf_op jit(solution)/shard_map/ppermute | solution.py:41
  168.2 8.0 %shard_map.187 = (bf16[1152,128]{1,0:T(8,128)(2,1)}, f32[2,1152]{1,0:T(2,128)}) custom-call(bf16[1152,384]{1,0:T(8,128)(2,1)} %bitcast.54.query.keys.values, bf16[1152,384]{1,0:T(8,128)(2,1)} %bitcast.54.query.keys.values, bf16[1152,384]{1,0:T(8,128)(2,1)} %bitcast.54.query.keys.values, s32[1152,2]{1,0:T(8,128)} %copy.96.mark_keys, s32[2,1152]{1,0:T(2,128)} %copy-done.70), custom_call_target="tpu_custom_call" | custom-call | flops 1358954496 | bytes 2976768 | tf_op jit(solution)/shard_map/pallas_call | solution.py:250
  176.3 5.1 all-to-all-start.2
  182.9 4.9 all-to-all-done.2
  188.5 5.2 shard_map.188
  194.9 4.4 collective-permute-start.42
  205.0 9.2 %shard_map.189 = (f32[4,2,288,256]{3,2,1,0:T(8,128)}, bf16[4,2,288,256]{3,2,1,0:T(8,128)(2,1)}, f32[288,1024]{1,0:T(8,128)}) custom-call(s32[21]{0:T(128)} %stack.185.info, bf16[288,1024]{1,0:T(8,128)(2,1)} %pad_maximum_fusion.5.x, f32[4,2,256]{2,1,0:T(2,128)} %get-tuple-element.374.bias, bf16[16,2,4,32,2048]{4,3,2,1,0:T(8,128)(2,1)} %bitcast.315, ...), custom_call_target="tpu_custom_call" | custom-call | flops 2415919104 | bytes 72425472 | tf_op jit(solution)/shard_map/pallas_call | solution.py:250
  221.4 6.5 shard_map.190
  227.9 18.6 %all_to_all.55 = bf16[8,144,384]{2,1,0:T(8,128)(2,1)} all-to-all(bf16[8,144,384]{2,1,0:T(8,128)(2,1)} %bitcast.332), channel_id=1, replica_groups={{0,1,2,3,8,9,10,11},{4,5,6,7,12,13,14,15},{16,17,18,19,24,25,26,27},{20..., dimensions={0} | all-to-all | bytes 1769472 | tf_op jit(solution)/shard_map/all_to_all | solution.py:552
  246.5 7.9 %shard_map.191 = (bf16[1152,128]{1,0:T(8,128)(2,1)}, f32[2,1152]{1,0:T(2,128)}) custom-call(bf16[1152,384]{1,0:T(8,128)(2,1)} %bitcast.367, bf16[1152,384]{1,0:T(8,128)(2,1)} %bitcast.368, bf16[1152,384]{1,0:T(8,128)(2,1)} %bitcast.369, s32[1152,2]{1,0:T(8,128)} %copy.96.mark_keys, s32[2,1152]{1,0:T(2,128)} %copy-done.70), custom_call_target="tpu_custom_call" | custom-call | flops 1358954496 | bytes 2976768 | tf_op jit(solution)/shard_map/pallas_call | solution.py:250
  254.4 11.0 %all_to_all.56 = bf16[8,144,128]{2,1,0:T(8,128)(2,1)} all-to-all(bf16[8,144,128]{2,1,0:T(8,128)(2,1)} %bitcast.383), channel_id=1, replica_groups={{0,1,2,3,8,9,10,11},{4,5,6,7,12,13,14,15},{16,17,18,19,24,25,26,27},{20..., dimensions={0} | all-to-all | bytes 589824 | tf_op jit(solution)/shard_map/all_to_all | solution.py:552
  265.4 5.2 shard_map.192
  279.6 20.6 %all-gather.8.cloned.1.call-done = bf16[4096,2048]{1,0:T(8,128)(2,1)} async-done(((bf16[128,2048]{1,0:T(8,128)(2,1)}), bf16[4096,2048]{1,0:T(8,128)(2,1)}) %all-gather.8.cloned.1.call-update) | async-done | bytes 16777232 | tf_op jit(solution)/shard_map/all_gather | solution.py:603
  300.2 9.0 %shard_map.193 = (f32[4,2,288,256]{3,2,1,0:T(8,128)}, bf16[4,2,288,256]{3,2,1,0:T(8,128)(2,1)}, f32[288,1024]{1,0:T(8,128)}) custom-call(s32[21]{0:T(128)} %stack.185.info, bf16[288,1024]{1,0:T(8,128)(2,1)} %pad_maximum_fusion.7.x, f32[4,2,256]{2,1,0:T(2,128)} %get-tuple-element.373.bias, bf16[16,2,4,32,2048]{4,3,2,1,0:T(8,128)(2,1)} %bitcast.323, ...), custom_call_target="tpu_custom_call" | custom-call | flops 2415919104 | bytes 72425472 | tf_op jit(solution)/shard_map/pallas_call | solution.py:250
  317.1 13.9 %shard_map.194 = (bf16[2,2,2,2,2,64,256]{6,5,4,3,2,1,0:T(8,128)(2,1)}, bf16[2,2,2,2,2,64,256]{6,5,4,3,2,1,0:T(8,128)(2,1)}, bf16[2,2,2,2,2,64,256]{6,5,4,3,2,1,0...) custom-call(s32[21]{0:T(128)} %stack.185.info, ...), custom_call_target="tpu_custom_call" | custom-call | flops 4831838208 | bytes 81403904 | tf_op jit(solution)/shard_map/pallas_call | solution.py:250
  339.2 4.9 shard_map.195
  344.1 4.1 all-to-all-start.5
  351.2 9.3 %all-to-all-done.5 = bf16[8,144,128]{2,1,0:T(8,128)(2,1)S(1)} async-done(((bf16[8,144,128]{2,1,0:T(8,128)(2,1)}), bf16[8,144,128]{2,1,0:T(8,128)(2,1)S(1)}, u32[]{:S(2)}, u32[]{:S(2)}) %all-to-all-start.5) | async-done | bytes 294944 | tf_op jit(solution)/shard_map/all_to_all | solution.py:552
  361.2 11.8 %shard_map.196 = (bf16[1152,384]{1,0:T(8,128)(2,1)}, f32[2,128]{1,0:T(2,128)}) custom-call(bf16[1152,384]{1,0:T(8,128)(2,1)} %bitcast.370, bf16[1152,384]{1,0:T(8,128)(2,1)} %bitcast.371, bf16[1152,384]{1,0:T(8,128)(2,1)} %bitcast.372, bf16[1152,128]{1,0:T(8,128)(2,1)} %bitcast.382, s32[1152,2]{1,0:T(8,128)} %copy.96.mark_keys, s32[2,1152]{1,0:T(2,128)} %copy-done.70, ...), custom_call_target="tpu_custom_call" | custom-call | flops 3397386240 | bytes 3862528 | tf_op jit(solution)/shard_map/pallas_call | solution.py:250
  373.0 4.4 all-to-all-start.6
  392.4 8.6 %collective-permute-done.55 = bf16[16,64,256]{2,1,0:T(8,128)(2,1)S(1)} collective-permute-done((bf16[16,64,256]{2,1,0:T(8,128)(2,1)S(1)}, bf16[16,64,256]{2,1,0:T(8,128)(2,1)S(1)}, u32[]{:S(2)}, u32[]{:S(2)}) %collective-permute-start.55) | collective-permute-done | bytes 524320 | tf_op jit(solution)/shard_map/ppermute | solution.py:41
  403.9 11.4 %shard_map.197 = (bf16[2,2,2,2,2,64,128]{6,5,4,3,2,1,0:T(8,128)(2,1)}, bf16[2,2,2,2,2,64,128]{6,5,4,3,2,1,0:T(8,128)(2,1)}, bf16[2,2,2,2,2,64,128]{6,5,4,3,2,1,0...) custom-call(s32[21]{0:T(128)} %stack.185.info, ...), custom_call_target="tpu_custom_call" | custom-call | flops 2113929216 | bytes 10878976 | tf_op jit(solution)/shard_map/pallas_call | solution.py:250
  427.8 6.9 %collective-permute-done.64 = bf16[32,64,128]{2,1,0:T(8,128)(2,1)S(1)} collective-permute-done((bf16[32,64,128]{2,1,0:T(8,128)(2,1)}, bf16[32,64,128]{2,1,0:T(8,128)(2,1)S(1)}, u32[]{:S(2)}, u32[]{:S(2)}) %collective-permute-start.64) | collective-permute-done | bytes 524320 | tf_op jit(solution)/shard_map/ppermute | solution.py:41
  444.2 14.1 %shard_map.198 = (bf16[2,2,2,2,2,64,256]{6,5,4,3,2,1,0:T(8,128)(2,1)}, bf16[2,2,2,2,2,64,256]{6,5,4,3,2,1,0:T(8,128)(2,1)}, bf16[2,2,2,2,2,64,256]{6,5,4,3,2,1,0...) custom-call(s32[21]{0:T(128)} %stack.185.info, ...), custom_call_target="tpu_custom_call" | custom-call | flops 4831838208 | bytes 81403904 | tf_op jit(solution)/shard_map/pallas_call | solution.py:250
  482.1 5.0 shard_map.199
  487.1 4.6 all-to-all-start.7
  505.5 4.0 collective-permute-done.73
  517.7 11.9 %shard_map.200 = (bf16[1152,384]{1,0:T(8,128)(2,1)}, f32[2,128]{1,0:T(2,128)}) custom-call(bf16[1152,384]{1,0:T(8,128)(2,1)} %bitcast.54.query.keys.values, bf16[1152,384]{1,0:T(8,128)(2,1)} %bitcast.54.query.keys.values, bf16[1152,384]{1,0:T(8,128)(2,1)} %bitcast.54.query.keys.values, bf16[1152,128]{1,0:T(8,128)(2,1)} %bitcast.127.grad_mixed, ...), custom_call_target="tpu_custom_call" | custom-call | flops 3397386240 | bytes 3862528 | tf_op jit(solution)/shard_map/pallas_call | solution.py:250
  529.6 4.4 all-to-all-start.8
  545.5 5.3 collective-permute-done.80
  554.5 6.7 collective-permute-done.82
  574.1 11.3 %shard_map.201 = (bf16[2,2,2,2,2,64,128]{6,5,4,3,2,1,0:T(8,128)(2,1)}, bf16[2,2,2,2,2,64,128]{6,5,4,3,2,1,0:T(8,128)(2,1)}, bf16[2,2,2,2,2,64,128]{6,5,4,3,2,1,0...) custom-call(s32[21]{0:T(128)} %stack.185.info, ...), custom_call_target="tpu_custom_call" | custom-call | flops 2113929216 | bytes 10878976 | tf_op jit(solution)/shard_map/pallas_call | solution.py:250
  588.5 7.6 %all-to-all-start.9 = ((f32[128,1,512]{2,1,0:T(1,128)}), f32[128,1,512]{2,1,0:T(1,128)S(1)}, u32[]{:S(2)}, u32[]{:S(2)}) async-start(f32[128,1,512]{2,1,0:T(1,128)} %all_to_all.43), calls=%async_computation.9 | async-start | bytes 524288 | tf_op jit(solution)/shard_map/all_to_all | solution.py:788
  599.4 4.1 fusion.2
  603.5 3.7 all-to-all-done.9
  618.3 8.6 %collective-permute-done.95 = bf16[32,64,128]{2,1,0:T(8,128)(2,1)S(1)} collective-permute-done((bf16[32,64,128]{2,1,0:T(8,128)(2,1)}, bf16[32,64,128]{2,1,0:T(8,128)(2,1)S(1)}, u32[]{:S(2)}, u32[]{:S(2)}) %collective-permute-start.95) | collective-permute-done | bytes 524320 | tf_op jit(solution)/shard_map/ppermute | solution.py:41
  628.6 3.9 collective-permute-done.102
  655.5 7.1 %collective-permute-start.113 = (bf16[32,4,768]{2,1,0:T(4,128)(2,1)S(1)}, bf16[32,4,768]{2,1,0:T(4,128)(2,1)S(1)}, u32[]{:S(2)}, u32[]{:S(2)}) collective-permute-start(bf16[32,4,768]{2,1,0:T(4,128)(2,1)S(1)} %bitcast.398), channel_id=1, source_target_pairs={{0,4},{1,5},{2,6},{3,7},{4,0},{5,1},{6,2},{7,3},{8,12},{9,13},{10,... | collective-permute-start | bytes 589832 | tf_op jit(solution)/shard_map/ppermute | solution.py:41
  (740 shorter events, 283.4 us)
Async XLA Ops:
  7.2 36.4 %all-gather.4.cloned.1.call-start = ((), (), s32[]{:S(2)}) async-start(), calls=%async_computation.10 | async-start | bytes 1310720 | tf_op jit(solution)/shard_map/all_gather | solution.py:594
  11.5 193.5 %all-gather.6.cloned.1.call-start = ((), (), s32[]{:S(2)}) async-start(), calls=%async_computation.11 | async-start | bytes 17301504 | tf_op jit(solution)/shard_map/all_gather | solution.py:603
  46.2 254.0 %all-gather.8.cloned.1.call-start = ((), (), s32[]{:S(2)}) async-start(), calls=%async_computation.12 | async-start | bytes 17301504 | tf_op jit(solution)/shard_map/all_gather | solution.py:603
  47.5 32.4 %collective-permute-start.18 = (bf16[16,64,128]{2,1,0:T(8,128)(2,1)S(1)}, bf16[16,64,128]{2,1,0:T(8,128)(2,1)}, u32[]{:S(2)}, u32[]{:S(2)}) collective-permute-start(bf16[16,64,128]{2,1,0:T(8,128)(2,1)S(1)} %get-tuple-element.131), channel_id=1, source_target_pairs={{0,16},{1,17},{2,18},{3,19},{4,20},{5,21},{6,22},{7,23},{8,24},{9,... | collective-permute-start | bytes 786440 | tf_op jit(solution)/shard_map/ppermute | solution.py:41
  47.8 32.9 %collective-permute-start.19 = (bf16[16,64,128]{2,1,0:T(8,128)(2,1)S(1)}, bf16[16,64,128]{2,1,0:T(8,128)(2,1)}, u32[]{:S(2)}, u32[]{:S(2)}) collective-permute-start(bf16[16,64,128]{2,1,0:T(8,128)(2,1)S(1)} %get-tuple-element.131), channel_id=1, source_target_pairs={{0,8},{1,9},{2,10},{3,11},{4,12},{5,13},{6,14},{7,15},{8,0},{9,1},... | collective-permute-start | bytes 786440 | tf_op jit(solution)/shard_map/ppermute | solution.py:41
  49.8 31.4 %collective-permute-start.21 = (bf16[16,64,128]{2,1,0:T(8,128)(2,1)S(1)}, bf16[16,64,128]{2,1,0:T(8,128)(2,1)}, u32[]{:S(2)}, u32[]{:S(2)}) collective-permute-start(bf16[16,64,128]{2,1,0:T(8,128)(2,1)S(1)} %get-tuple-element.135), channel_id=1, source_target_pairs={{0,8},{1,9},{2,10},{3,11},{4,12},{5,13},{6,14},{7,15},{8,0},{9,1},... | collective-permute-start | bytes 786440 | tf_op jit(solution)/shard_map/ppermute | solution.py:41
  50.1 35.0 %collective-permute-start.22 = (bf16[16,64,128]{2,1,0:T(8,128)(2,1)S(1)}, bf16[16,64,128]{2,1,0:T(8,128)(2,1)}, u32[]{:S(2)}, u32[]{:S(2)}) collective-permute-start(bf16[16,64,128]{2,1,0:T(8,128)(2,1)S(1)} %get-tuple-element.135), channel_id=1, source_target_pairs={{0,48},{1,49},{2,50},{3,51},{4,52},{5,53},{6,54},{7,55},{8,56},{9,... | collective-permute-start | bytes 786440 | tf_op jit(solution)/shard_map/ppermute | solution.py:41
  55.0 20.6 %all-to-all-start = ((bf16[128,2,256]{2,1,0:T(2,128)(2,1)}), bf16[128,2,256]{2,1,0:T(2,128)(2,1)S(1)}, u32[]{:S(2)}, u32[]{:S(2)}) async-start(bf16[128,2,256]{2,1,0:T(2,128)(2,1)} %reshape.742), calls=%async_computation | async-start | bytes 262144 | tf_op jit(solution)/shard_map/all_to_all | solution.py:617
  79.2 16.3 %collective-permute-start.17 = (bf16[144,1024]{1,0:T(8,128)(2,1)S(1)}, bf16[144,1024]{1,0:T(8,128)(2,1)}, u32[]{:S(2)}, u32[]{:S(2)}) collective-permute-start(bf16[144,1024]{1,0:T(8,128)(2,1)S(1)} %slice.936), channel_id=1, source_target_pairs={{0,4},{1,5},{2,6},{3,7},{4,0},{5,1},{6,2},{7,3},{8,12},{9,13},{10,... | collective-permute-start | bytes 884744 | tf_op jit(solution)/shard_map/ppermute | solution.py:41
  115.9 49.7 %all-to-all-start.1 = ((bf16[8,144,384]{2,1,0:T(8,128)(2,1)}), bf16[8,144,384]{2,1,0:T(8,128)(2,1)}, u32[]{:S(2)}, u32[]{:S(2)}) async-start(bf16[8,144,384]{2,1,0:T(8,128)(2,1)} %bitcast.331), calls=%async_computation.1 | async-start | bytes 1769472 | tf_op jit(solution)/shard_map/all_to_all | solution.py:552
  128.7 25.7 %collective-permute-start.31 = (bf16[16,64,128]{2,1,0:T(8,128)(2,1)S(1)}, bf16[16,64,128]{2,1,0:T(8,128)(2,1)}, u32[]{:S(2)}, u32[]{:S(2)}) collective-permute-start(bf16[16,64,128]{2,1,0:T(8,128)(2,1)S(1)} %copy-done.44), channel_id=1, source_target_pairs={{0,8},{1,9},{2,10},{3,11},{4,12},{5,13},{6,14},{7,15},{8,0},{9,1},... | collective-permute-start | bytes 786440 | tf_op jit(solution)/shard_map/ppermute | solution.py:41
  130.7 24.6 %collective-permute-start.32 = (bf16[16,64,128]{2,1,0:T(8,128)(2,1)S(1)}, bf16[16,64,128]{2,1,0:T(8,128)(2,1)}, u32[]{:S(2)}, u32[]{:S(2)}) collective-permute-start(bf16[16,64,128]{2,1,0:T(8,128)(2,1)S(1)} %copy-done.45), channel_id=1, source_target_pairs={{0,48},{1,49},{2,50},{3,51},{4,52},{5,53},{6,54},{7,55},{8,56},{9,... | collective-permute-start | bytes 786440 | tf_op jit(solution)/shard_map/ppermute | solution.py:41
  130.7 34.9 %collective-permute-start.34 = (bf16[16,64,128]{2,1,0:T(8,128)(2,1)S(1)}, bf16[16,64,128]{2,1,0:T(8,128)(2,1)S(1)}, u32[]{:S(2)}, u32[]{:S(2)}) collective-permute-start(bf16[16,64,128]{2,1,0:T(8,128)(2,1)S(1)} %get-tuple-element.143), channel_id=1, source_target_pairs={{0,8},{1,9},{2,10},{3,11},{4,12},{5,13},{6,14},{7,15},{8,0},{9,1},... | collective-permute-start | bytes 786440 | tf_op jit(solution)/shard_map/ppermute | solution.py:41
  130.9 34.7 %collective-permute-start.35 = (bf16[16,64,128]{2,1,0:T(8,128)(2,1)S(1)}, bf16[16,64,128]{2,1,0:T(8,128)(2,1)}, u32[]{:S(2)}, u32[]{:S(2)}) collective-permute-start(bf16[16,64,128]{2,1,0:T(8,128)(2,1)S(1)} %copy-done.44), channel_id=1, source_target_pairs={{0,48},{1,49},{2,50},{3,51},{4,52},{5,53},{6,54},{7,55},{8,56},{9,... | collective-permute-start | bytes 786440 | tf_op jit(solution)/shard_map/ppermute | solution.py:41
  165.7 22.2 %collective-permute-start.38 = (bf16[16,64,128]{2,1,0:T(8,128)(2,1)S(1)}, bf16[16,64,128]{2,1,0:T(8,128)(2,1)S(1)}, u32[]{:S(2)}, u32[]{:S(2)}) collective-permute-start(bf16[16,64,128]{2,1,0:T(8,128)(2,1)S(1)} %collective-permute-done.30), channel_id=1, source_target_pairs={{0,8},{1,9},{2,10},{3,11},{4,12},{5,13},{6,14},{7,15},{8,0},{9,1},... | collective-permute-start | bytes 786440 | tf_op jit(solution)/shard_map/ppermute | solution.py:41
  165.7 22.1 %collective-permute-start.39 = (bf16[16,64,128]{2,1,0:T(8,128)(2,1)}, bf16[16,64,128]{2,1,0:T(8,128)(2,1)S(1)}, u32[]{:S(2)}, u32[]{:S(2)}) collective-permute-start(bf16[16,64,128]{2,1,0:T(8,128)(2,1)} %collective-permute-done.31), channel_id=1, source_target_pairs={{0,48},{1,49},{2,50},{3,51},{4,52},{5,53},{6,54},{7,55},{8,56},{9,... | collective-permute-start | bytes 786440 | tf_op jit(solution)/shard_map/ppermute | solution.py:41
  165.8 22.0 %collective-permute-start.40 = (bf16[16,64,128]{2,1,0:T(8,128)(2,1)}, bf16[16,64,128]{2,1,0:T(8,128)(2,1)}, u32[]{:S(2)}, u32[]{:S(2)}) collective-permute-start(bf16[16,64,128]{2,1,0:T(8,128)(2,1)} %collective-permute-done.32), channel_id=1, source_target_pairs={{0,72},{1,73},{2,74},{3,75},{4,76},{5,77},{6,78},{7,79},{8,64},{9,... | collective-permute-start | bytes 786440 | tf_op jit(solution)/shard_map/ppermute | solution.py:41
  167.8 20.0 %collective-permute-start.41 = (bf16[16,64,128]{2,1,0:T(8,128)(2,1)S(1)}, bf16[16,64,128]{2,1,0:T(8,128)(2,1)S(1)}, u32[]{:S(2)}, u32[]{:S(2)}) collective-permute-start(bf16[16,64,128]{2,1,0:T(8,128)(2,1)S(1)} %collective-permute-done.33), channel_id=1, source_target_pairs={{0,16},{1,17},{2,18},{3,19},{4,20},{5,21},{6,22},{7,23},{8,24},{9,... | collective-permute-start | bytes 786440 | tf_op jit(solution)/shard_map/ppermute | solution.py:41
  332.5 44.9 %collective-permute-start.52 = (bf16[32,64,256]{2,1,0:T(8,128)(2,1)}, bf16[32,64,256]{2,1,0:T(8,128)(2,1)}, u32[]{:S(2)}, u32[]{:S(2)}) collective-permute-start(bf16[32,64,256]{2,1,0:T(8,128)(2,1)} %bitcast.453), channel_id=1, source_target_pairs={{0,8},{1,9},{2,10},{3,11},{4,12},{5,13},{6,14},{7,15},{8,0},{9,1},... | collective-permute-start | bytes 3145736 | tf_op jit(solution)/shard_map/ppermute | solution.py:41
  336.0 43.2 %collective-permute-start.54 = (bf16[32,64,256]{2,1,0:T(8,128)(2,1)}, bf16[32,64,256]{2,1,0:T(8,128)(2,1)}, u32[]{:S(2)}, u32[]{:S(2)}) collective-permute-start(bf16[32,64,256]{2,1,0:T(8,128)(2,1)} %bitcast.113), channel_id=1, source_target_pairs={{0,48},{1,49},{2,50},{3,51},{4,52},{5,53},{6,54},{7,55},{8,56},{9,... | collective-permute-start | bytes 3145736 | tf_op jit(solution)/shard_map/ppermute | solution.py:41
  344.1 16.4 %all-to-all-start.5 = ((bf16[8,144,128]{2,1,0:T(8,128)(2,1)}), bf16[8,144,128]{2,1,0:T(8,128)(2,1)S(1)}, u32[]{:S(2)}, u32[]{:S(2)}) async-start(bf16[8,144,128]{2,1,0:T(8,128)(2,1)} %bitcast.341), calls=%async_computation.5 | async-start | bytes 589824 | tf_op jit(solution)/shard_map/all_to_all | solution.py:552
  348.2 35.1 %collective-permute-start.56 = (bf16[32,64,256]{2,1,0:T(8,128)(2,1)}, bf16[32,64,256]{2,1,0:T(8,128)(2,1)}, u32[]{:S(2)}, u32[]{:S(2)}) collective-permute-start(bf16[32,64,256]{2,1,0:T(8,128)(2,1)} %bitcast.452), channel_id=1, source_target_pairs={{0,72},{1,73},{2,74},{3,75},{4,76},{5,77},{6,78},{7,79},{8,64},{9,... | collective-permute-start | bytes 3145736 | tf_op jit(solution)/shard_map/ppermute | solution.py:41
  351.2 36.7 %collective-permute-start.58 = (bf16[32,64,256]{2,1,0:T(8,128)(2,1)}, bf16[32,64,256]{2,1,0:T(8,128)(2,1)}, u32[]{:S(2)}, u32[]{:S(2)}) collective-permute-start(bf16[32,64,256]{2,1,0:T(8,128)(2,1)} %bitcast.451), channel_id=1, source_target_pairs={{0,16},{1,17},{2,18},{3,19},{4,20},{5,21},{6,22},{7,23},{8,24},{9,... | collective-permute-start | bytes 3145736 | tf_op jit(solution)/shard_map/ppermute | solution.py:41
  373.0 30.9 %all-to-all-start.6 = ((bf16[8,144,384]{2,1,0:T(8,128)(2,1)}), bf16[8,144,384]{2,1,0:T(8,128)(2,1)}, u32[]{:S(2)}, u32[]{:S(2)}) async-start(bf16[8,144,384]{2,1,0:T(8,128)(2,1)} %bitcast.374), calls=%async_computation.6 | async-start | bytes 1769472 | tf_op jit(solution)/shard_map/all_to_all | solution.py:552
  381.9 19.1 %collective-permute-start.55 = (bf16[16,64,256]{2,1,0:T(8,128)(2,1)S(1)}, bf16[16,64,256]{2,1,0:T(8,128)(2,1)S(1)}, u32[]{:S(2)}, u32[]{:S(2)}) collective-permute-start(bf16[16,64,256]{2,1,0:T(8,128)(2,1)S(1)} %slice.728), channel_id=1, source_target_pairs={{0,8},{1,9},{2,10},{3,11},{4,12},{5,13},{6,14},{7,15},{8,0},{9,1},... | collective-permute-start | bytes 1572872 | tf_op jit(solution)/shard_map/ppermute | solution.py:41
  385.0 17.0 %collective-permute-start.57 = (bf16[16,64,256]{2,1,0:T(8,128)(2,1)S(1)}, bf16[16,64,256]{2,1,0:T(8,128)(2,1)S(1)}, u32[]{:S(2)}, u32[]{:S(2)}) collective-permute-start(bf16[16,64,256]{2,1,0:T(8,128)(2,1)S(1)} %slice.730), channel_id=1, source_target_pairs={{0,48},{1,49},{2,50},{3,51},{4,52},{5,53},{6,54},{7,55},{8,56},{9,... | collective-permute-start | bytes 1572872 | tf_op jit(solution)/shard_map/ppermute | solution.py:41
  422.3 15.8 %collective-permute-start.68 = (bf16[32,64,128]{2,1,0:T(8,128)(2,1)}, bf16[32,64,128]{2,1,0:T(8,128)(2,1)S(1)}, u32[]{:S(2)}, u32[]{:S(2)}) collective-permute-start(bf16[32,64,128]{2,1,0:T(8,128)(2,1)} %bitcast.455), channel_id=1, source_target_pairs={{0,72},{1,73},{2,74},{3,75},{4,76},{5,77},{6,78},{7,79},{8,64},{9,... | collective-permute-start | bytes 1572872 | tf_op jit(solution)/shard_map/ppermute | solution.py:41
  426.8 16.5 %collective-permute-start.61 = (bf16[144,1024]{1,0:T(8,128)(2,1)S(1)}, bf16[144,1024]{1,0:T(8,128)(2,1)S(1)}, u32[]{:S(2)}, u32[]{:S(2)}) collective-permute-start(bf16[144,1024]{1,0:T(8,128)(2,1)S(1)} %convert_element_type.663), channel_id=1, source_target_pairs={{0,4},{1,5},{2,6},{3,7},{4,0},{5,1},{6,2},{7,3},{8,12},{9,13},{10,... | collective-permute-start | bytes 884744 | tf_op jit(solution)/shard_map/ppermute | solution.py:41
  435.7 31.4 %collective-permute-start.65 = (bf16[16,64,128]{2,1,0:T(8,128)(2,1)}, bf16[16,64,128]{2,1,0:T(8,128)(2,1)S(1)}, u32[]{:S(2)}, u32[]{:S(2)}) collective-permute-start(bf16[16,64,128]{2,1,0:T(8,128)(2,1)} %slice.736), channel_id=1, source_target_pairs={{0,16},{1,17},{2,18},{3,19},{4,20},{5,21},{6,22},{7,23},{8,24},{9,... | collective-permute-start | bytes 786440 | tf_op jit(solution)/shard_map/ppermute | solution.py:41
  436.8 30.8 %collective-permute-start.67 = (bf16[16,64,128]{2,1,0:T(8,128)(2,1)}, bf16[16,64,128]{2,1,0:T(8,128)(2,1)}, u32[]{:S(2)}, u32[]{:S(2)}) collective-permute-start(bf16[16,64,128]{2,1,0:T(8,128)(2,1)} %slice.738), channel_id=1, source_target_pairs={{0,8},{1,9},{2,10},{3,11},{4,12},{5,13},{6,14},{7,15},{8,0},{9,1},... | collective-permute-start | bytes 786440 | tf_op jit(solution)/shard_map/ppermute | solution.py:41
  439.1 31.7 %collective-permute-start.69 = (bf16[16,64,128]{2,1,0:T(8,128)(2,1)}, bf16[16,64,128]{2,1,0:T(8,128)(2,1)}, u32[]{:S(2)}, u32[]{:S(2)}) collective-permute-start(bf16[16,64,128]{2,1,0:T(8,128)(2,1)} %slice.740), channel_id=1, source_target_pairs={{0,48},{1,49},{2,50},{3,51},{4,52},{5,53},{6,54},{7,55},{8,56},{9,... | collective-permute-start | bytes 786440 | tf_op jit(solution)/shard_map/ppermute | solution.py:41
  440.9 33.0 %collective-permute-start.71 = (bf16[16,64,128]{2,1,0:T(8,128)(2,1)}, bf16[16,64,128]{2,1,0:T(8,128)(2,1)}, u32[]{:S(2)}, u32[]{:S(2)}) collective-permute-start(bf16[16,64,128]{2,1,0:T(8,128)(2,1)} %slice.742), channel_id=1, source_target_pairs={{0,72},{1,73},{2,74},{3,75},{4,76},{5,77},{6,78},{7,79},{8,64},{9,... | collective-permute-start | bytes 786440 | tf_op jit(solution)/shard_map/ppermute | solution.py:41
  467.1 25.3 %collective-permute-start.72 = (bf16[32,64,256]{2,1,0:T(8,128)(2,1)}, bf16[32,64,256]{2,1,0:T(8,128)(2,1)}, u32[]{:S(2)}, u32[]{:S(2)}) collective-permute-start(bf16[32,64,256]{2,1,0:T(8,128)(2,1)} %bitcast.450), channel_id=1, source_target_pairs={{0,8},{1,9},{2,10},{3,11},{4,12},{5,13},{6,14},{7,15},{8,0},{9,1},... | collective-permute-start | bytes 3145736 | tf_op jit(solution)/shard_map/ppermute | solution.py:41
  467.7 27.8 %collective-permute-start.74 = (bf16[32,64,256]{2,1,0:T(8,128)(2,1)}, bf16[32,64,256]{2,1,0:T(8,128)(2,1)}, u32[]{:S(2)}, u32[]{:S(2)}) collective-permute-start(bf16[32,64,256]{2,1,0:T(8,128)(2,1)} %bitcast.131), channel_id=1, source_target_pairs={{0,48},{1,49},{2,50},{3,51},{4,52},{5,53},{6,54},{7,55},{8,56},{9,... | collective-permute-start | bytes 3145736 | tf_op jit(solution)/shard_map/ppermute | solution.py:41
  470.8 27.9 %collective-permute-start.76 = (bf16[32,64,256]{2,1,0:T(8,128)(2,1)}, bf16[32,64,256]{2,1,0:T(8,128)(2,1)}, u32[]{:S(2)}, u32[]{:S(2)}) collective-permute-start(bf16[32,64,256]{2,1,0:T(8,128)(2,1)} %bitcast.133), channel_id=1, source_target_pairs={{0,72},{1,73},{2,74},{3,75},{4,76},{5,77},{6,78},{7,79},{8,64},{9,... | collective-permute-start | bytes 3145736 | tf_op jit(solution)/shard_map/ppermute | solution.py:41
  474.0 28.2 %collective-permute-start.78 = (bf16[32,64,256]{2,1,0:T(8,128)(2,1)}, bf16[32,64,256]{2,1,0:T(8,128)(2,1)}, u32[]{:S(2)}, u32[]{:S(2)}) collective-permute-start(bf16[32,64,256]{2,1,0:T(8,128)(2,1)} %bitcast.135), channel_id=1, source_target_pairs={{0,16},{1,17},{2,18},{3,19},{4,20},{5,21},{6,22},{7,23},{8,24},{9,... | collective-permute-start | bytes 3145736 | tf_op jit(solution)/shard_map/ppermute | solution.py:41
  487.1 30.6 %all-to-all-start.7 = ((bf16[8,144,128]{2,1,0:T(8,128)(2,1)}), bf16[8,144,128]{2,1,0:T(8,128)(2,1)}, u32[]{:S(2)}, u32[]{:S(2)}) async-start(bf16[8,144,128]{2,1,0:T(8,128)(2,1)} %bitcast.340), calls=%async_computation.7 | async-start | bytes 589824 | tf_op jit(solution)/shard_map/all_to_all | solution.py:552
  529.6 44.6 %all-to-all-start.8 = ((bf16[8,144,384]{2,1,0:T(8,128)(2,1)}), bf16[8,144,384]{2,1,0:T(8,128)(2,1)}, u32[]{:S(2)}, u32[]{:S(2)}) async-start(bf16[8,144,384]{2,1,0:T(8,128)(2,1)} %bitcast.373), calls=%async_computation.8 | async-start | bytes 1769472 | tf_op jit(solution)/shard_map/all_to_all | solution.py:552
  535.1 15.7 %collective-permute-start.80 = (bf16[8,64,640]{2,1,0:T(8,128)(2,1)}, bf16[8,64,640]{2,1,0:T(8,128)(2,1)}, u32[]{:S(2)}, u32[]{:S(2)}) collective-permute-start(bf16[8,64,640]{2,1,0:T(8,128)(2,1)} %slice.752), channel_id=1, source_target_pairs={{0,72},{1,73},{2,74},{3,75},{4,76},{5,77},{6,78},{7,79},{8,64},{9,... | collective-permute-start | bytes 1966088 | tf_op jit(solution)/shard_map/ppermute | solution.py:41
  538.8 22.3 %collective-permute-start.82 = (bf16[8,64,640]{2,1,0:T(8,128)(2,1)}, bf16[8,64,640]{2,1,0:T(8,128)(2,1)}, u32[]{:S(2)}, u32[]{:S(2)}) collective-permute-start(bf16[8,64,640]{2,1,0:T(8,128)(2,1)} %slice.756), channel_id=1, source_target_pairs={{0,3},{1,2},{2,1},{3,0},{4,7},{5,6},{6,5},{7,4},{8,11},{9,10},{10,... | collective-permute-start | bytes 1966088 | tf_op jit(solution)/shard_map/ppermute | solution.py:41
  542.5 22.5 %collective-permute-start.84 = (bf16[8,64,640]{2,1,0:T(8,128)(2,1)}, bf16[8,64,640]{2,1,0:T(8,128)(2,1)}, u32[]{:S(2)}, u32[]{:S(2)}) collective-permute-start(bf16[8,64,640]{2,1,0:T(8,128)(2,1)} %slice.760), channel_id=1, source_target_pairs={{0,16},{1,17},{2,18},{3,19},{4,20},{5,21},{6,22},{7,23},{8,24},{9,... | collective-permute-start | bytes 1966088 | tf_op jit(solution)/shard_map/ppermute | solution.py:41
  545.2 21.1 %collective-permute-start.86 = (bf16[8,64,640]{2,1,0:T(8,128)(2,1)S(1)}, bf16[8,64,640]{2,1,0:T(8,128)(2,1)S(1)}, u32[]{:S(2)}, u32[]{:S(2)}) collective-permute-start(bf16[8,64,640]{2,1,0:T(8,128)(2,1)S(1)} %slice.764), channel_id=1, source_target_pairs={{0,1},{1,0},{2,3},{3,2},{4,5},{5,4},{6,7},{7,6},{8,9},{9,8},{10,11... | collective-permute-start | bytes 1966088 | tf_op jit(solution)/shard_map/ppermute | solution.py:41
  552.2 15.9 %collective-permute-start.81 = (bf16[4,64,640]{2,1,0:T(8,128)(2,1)S(1)}, bf16[4,64,640]{2,1,0:T(8,128)(2,1)S(1)}, u32[]{:S(2)}, u32[]{:S(2)}) collective-permute-start(bf16[4,64,640]{2,1,0:T(8,128)(2,1)S(1)} %slice.754), channel_id=1, source_target_pairs={{0,3},{1,2},{2,1},{3,0},{4,7},{5,6},{6,5},{7,4},{8,11},{9,10},{10,... | collective-permute-start | bytes 983048 | tf_op jit(solution)/shard_map/ppermute | solution.py:41
  585.5 27.6 %collective-permute-start.107 = (bf16[32,64,128]{2,1,0:T(8,128)(2,1)}, bf16[32,64,128]{2,1,0:T(8,128)(2,1)S(1)}, u32[]{:S(2)}, u32[]{:S(2)}) collective-permute-start(bf16[32,64,128]{2,1,0:T(8,128)(2,1)} %bitcast.461), channel_id=1, source_target_pairs={{0,16},{1,17},{2,18},{3,19},{4,20},{5,21},{6,22},{7,23},{8,24},{9,... | collective-permute-start | bytes 1572872 | tf_op jit(solution)/shard_map/ppermute | solution.py:41
  588.5 18.8 %all-to-all-start.9 = ((f32[128,1,512]{2,1,0:T(1,128)}), f32[128,1,512]{2,1,0:T(1,128)S(1)}, u32[]{:S(2)}, u32[]{:S(2)}) async-start(f32[128,1,512]{2,1,0:T(1,128)} %all_to_all.43), calls=%async_computation.9 | async-start | bytes 524288 | tf_op jit(solution)/shard_map/all_to_all | solution.py:788
  596.1 18.5 %collective-permute-start.101 = (bf16[32,64,128]{2,1,0:T(8,128)(2,1)}, bf16[32,64,128]{2,1,0:T(8,128)(2,1)}, u32[]{:S(2)}, u32[]{:S(2)}) collective-permute-start(bf16[32,64,128]{2,1,0:T(8,128)(2,1)} %bitcast.460), channel_id=1, source_target_pairs={{0,72},{1,73},{2,74},{3,75},{4,76},{5,77},{6,78},{7,79},{8,64},{9,... | collective-permute-start | bytes 1572872 | tf_op jit(solution)/shard_map/ppermute | solution.py:41
  611.5 51.1 %collective-permute-start.88 = (bf16[144,1024]{1,0:T(8,128)(2,1)S(1)}, bf16[144,1024]{1,0:T(8,128)(2,1)S(1)}, u32[]{:S(2)}, u32[]{:S(2)}) collective-permute-start(bf16[144,1024]{1,0:T(8,128)(2,1)S(1)} %slice.928), channel_id=1, source_target_pairs={{0,4},{1,5},{2,6},{3,7},{4,0},{5,1},{6,2},{7,3},{8,12},{9,13},{10,... | collective-permute-start | bytes 884744 | tf_op jit(solution)/shard_map/ppermute | solution.py:41
  615.8 16.7 %collective-permute-start.102 = (bf16[16,64,128]{2,1,0:T(8,128)(2,1)S(1)}, bf16[16,64,128]{2,1,0:T(8,128)(2,1)S(1)}, u32[]{:S(2)}, u32[]{:S(2)}) collective-permute-start(bf16[16,64,128]{2,1,0:T(8,128)(2,1)S(1)} %slice.789), channel_id=1, source_target_pairs={{0,48},{1,49},{2,50},{3,51},{4,52},{5,53},{6,54},{7,55},{8,56},{9,... | collective-permute-start | bytes 786440 | tf_op jit(solution)/shard_map/ppermute | solution.py:41
  (163 other events, 1606.1 us)
Sparse Core Ops, SparseCore 0:
  11.6 27.4 all-gather.3
  46.3 146.3 all-gather.5
  194.4 105.7 all-gather.7

commit v5 on v4

--- a/solution.py
+++ b/solution.py
@@ -60,8 +60,7 @@
 
 
 def reduce_first(pairs, orders):
-    parts = [add_low(kept, swap(sent, *ORDERS[k][5])) for k, (kept, sent) in zip(orders, pairs)]
-    return reduce_phase(parts, orders, 1)
+    return [add_low(kept, swap(sent, *ORDERS[k][5])) for k, (kept, sent) in zip(orders, pairs)]
 
 
 def reduce_phase(parts, orders, phase):
@@ -597,7 +596,6 @@
     lead = gather_late([value[:, :, :128] for value in lead])
     lead, lead_one = lax.optimization_barrier((lead, lead_one))
     near_one = [swap(value, *ORDERS[k][4]) for k, value in enumerate(lead_one)]
-    far_one = [swap(value, *ORDERS[k][5]) for k, value in enumerate(lead_one)]
 
     def everywhere(value):
         value = lax.all_gather(value, ("dp", "ctx"), axis=0, tiled=True)
@@ -674,18 +672,21 @@
         qkv = project(order, gathered, attention_w[layer], bias[0], bias[1])
         qkv = trade(qkv.reshape(8, 2 * rows, 384)).reshape(16 * rows, 384)
         if layer == 0:
-            qkv, near_one, far_one = lax.optimization_barrier((qkv, near_one, far_one))
+            qkv, near_one = lax.optimization_barrier((qkv, near_one))
+            far_one = [swap(value, *ORDERS[k][5]) for k, value in enumerate(lead_one)]
             last_one = [swap(value, *ORDERS[k][5]) for k, value in enumerate(near_one)]
         mixed, summary = attend(qkv, marks_t, marks)
         mixed = trade(mixed.reshape(8, 2 * rows, 128)).reshape(2, 4, 2 * rows, 128)
         if layer == 0:
-            mixed, last_one = lax.optimization_barrier((mixed, last_one))
-            pieces = zip(lead_one, near_one, far_one, last_one)
-            attention_w.append([Exchanged(k, four, 128) for k, four in enumerate(pieces)])
+            mixed, far_one = lax.optimization_barrier((mixed, far_one))
         mixed, attended = mix(order, mixed, attention_w[layer][3])
         attended = own_sum(attended) + shift[layer, 2]
         first, unit_one, inv_one = normalize(state + attended, gains[layer, 0], shift[layer, 0])
         gathered_two = both(first.astype(LOW))
+        if layer == 0:
+            gathered_two, last_one = lax.optimization_barrier((gathered_two, last_one))
+            pieces = zip(lead_one, near_one, far_one, last_one)
+            attention_w.append([Exchanged(k, four, 128) for k, four in enumerate(pieces)])
         hidden, active, down = feed(order, gathered_two, up[layer], feed_w[layer])
         down = own_sum(down)
         state, unit_two, inv_two = normalize(
@@ -698,6 +699,24 @@
     result = absolute(state)
 
     small = [None] * layers
+
+    def vector_sums():
+        vec = absolute(
+            jnp.concatenate([small[layer][0] for layer in range(layers)]
+                            + [small[layer][1] for layer in range(layers)])
+        )
+        vec = vec.reshape(12, 32, 32).transpose(1, 0, 2).reshape(32, 1, 384)
+        vec = jnp.broadcast_to(vec, (32, 4, 384))
+        pair = jnp.stack([small[layer][2] for layer in range(layers)])
+        head = me_x * 4 + core * 2 + z_lo
+        pair = jnp.where((jnp.arange(16) == head)[:, None], pair[:, :, None], 0.0)
+        pair = pair.reshape(layers, 2, 4, 4, 32, 2).transpose(4, 2, 0, 1, 3, 5).reshape(32, 4, 32)
+        up = take_absolute(jnp.stack([small[layer][3] for layer in range(layers)]), me_x, 1)
+        up = jnp.where((jnp.arange(2) == core)[:, None, None], up[:, :, None], 0.0)
+        up = up.reshape(layers, 4, 4, 32, 8).transpose(3, 1, 0, 2, 4).reshape(32, 4, 64)
+        vec = jnp.concatenate([vec, pair, up, jnp.zeros((32, 4, 32), FULL)], 2).reshape(128, 512)
+        return jnp.sum(lax.all_to_all(vec, ALL, 0, 0, tiled=True), axis=0)
+
     for layer in reversed(range(layers)):
         (gathered, qkv, summary, mixed, unit_one, inv_one, gathered_two, hidden, active,
          unit_two, inv_two) = saved[layer]
@@ -708,7 +727,8 @@
         grad_feed, grad_upbias, grad_first = feed_back(
             order, spread_two, gathered_two, hidden, active, feed_w[layer]
         )
-        grad_feed = reduce_first(grad_feed, range(4))
+        if layer == 0:
+            grad_feed = reduce_first(grad_feed, range(4))
         grad_first = grad_two + own_sum(grad_first)
         grad_one, gain_one, shift_one = normalize_back(
             grad_first, unit_one, inv_one, gains[layer, 0]
@@ -716,32 +736,18 @@
         spread_one = both(grad_one.astype(LOW))
         if layer == 0:
             spread_one, later = lax.optimization_barrier((spread_one, later))
+            later = reduce_phase(later, range(4), 1)
         grad_mixed = trade(mix_back(order, spread_one, attention_w[layer][3]).reshape(8, 2 * rows, 128))
         grad_mixed = grad_mixed.reshape(16 * rows, 128)
         if layer == 0:
-            grad_mixed, grad_feed = lax.optimization_barrier((grad_mixed, grad_feed))
+            grad_mixed, grad_feed, later = lax.optimization_barrier((grad_mixed, grad_feed, later))
+            grad_feed = reduce_phase(grad_feed, range(4), 1)
+        low_packed, grad_pair = attend_back(qkv, grad_mixed, marks_t, marks, summary)
+        grad_pair = grad_pair.reshape(2, 2, 64).sum(1)
+        if layer == 0:
+            low_packed, grad_feed = lax.optimization_barrier((low_packed, grad_feed))
             tail = [jnp.concatenate([a, b], 2) for a, b in zip(grad_feed, later)]
             tail = reduce_phase(reduce_phase(tail, range(4), 2), range(4), 3)
-        low_packed, grad_pair = attend_back(qkv, grad_mixed, marks_t, marks, summary)
-        grad_pair = grad_pair.reshape(2, 2, 64).sum(1)
-        low_packed = trade(low_packed.reshape(8, 2 * rows, 384)).reshape(2, 4, 2 * rows, 384)
-        if layer:
-            low_packed, grad_feed = lax.optimization_barrier((low_packed, grad_feed))
-        else:
-            low_packed, tail = lax.optimization_barrier((low_packed, tail))
-        grad_attention, grad_x = project_back(
-            order, low_packed, gathered, spread_one, mixed, attention_w[layer],
-            APART,
-        )
-        incoming = grad_one + own_sum(grad_x)
-        if layer:
-            grad_attention = reduce_first(grad_attention, range(4))
-            later = [jnp.concatenate(pair, 2) for pair in zip(grad_feed, grad_attention)]
-        else:
-            lead = reduce_first(grad_attention, range(4))
-            lead = reduce_phase(reduce_phase(lead, range(4), 2), range(4), 3)
-            tail = [jnp.concatenate(pair, 2) for pair in zip(tail, lead)]
-            tail = reduce_phases(tail, range(4), 4)
         small[layer] = (
             jnp.stack([gain_one, gain_two]),
             jnp.stack(
@@ -750,6 +756,25 @@
             grad_pair,
             grad_upbias,
         )
+        low_packed = trade(low_packed.reshape(8, 2 * rows, 384)).reshape(2, 4, 2 * rows, 384)
+        if layer == 0:
+            low_packed, tail, vec = lax.optimization_barrier((low_packed, tail, vector_sums()))
+        grad_attention, grad_x = project_back(
+            order, low_packed, gathered, spread_one, mixed, attention_w[layer],
+            APART,
+        )
+        incoming = grad_one + own_sum(grad_x)
+        if layer:
+            later = [
+                [jnp.concatenate(half, 2) for half in zip(*pairs)]
+                for pairs in zip(grad_feed, grad_attention)
+            ]
+            later = reduce_first(later, range(4))
+        else:
+            lead = reduce_phase(reduce_first(grad_attention, range(4)), range(4), 1)
+            lead = reduce_phase(reduce_phase(lead, range(4), 2), range(4), 3)
+            tail = [jnp.concatenate(pair, 2) for pair in zip(tail, lead)]
+            tail = reduce_phases(tail, range(4), 4)
     grad_stream = absolute(incoming)
 
     def own_rows(parts):
@@ -770,22 +795,6 @@
     out_o = jnp.stack([value[:, :, 3].reshape(32, 256).T for value in attention])
     out_up = jnp.stack([value[:, :, :2].reshape(32, 1024) for value in feeds])
     out_down = jnp.stack([value[:, :, 2:].reshape(32, 1024).T for value in feeds])
-
-    vec = absolute(
-        jnp.concatenate([small[layer][0] for layer in range(layers)]
-                        + [small[layer][1] for layer in range(layers)])
-    )
-    vec = vec.reshape(12, 32, 32).transpose(1, 0, 2).reshape(32, 1, 384)
-    vec = jnp.broadcast_to(vec, (32, 4, 384))
-    pair = jnp.stack([small[layer][2] for layer in range(layers)])
-    head = me_x * 4 + core * 2 + z_lo
-    pair = jnp.where((jnp.arange(16) == head)[:, None], pair[:, :, None], 0.0)
-    pair = pair.reshape(layers, 2, 4, 4, 32, 2).transpose(4, 2, 0, 1, 3, 5).reshape(32, 4, 32)
-    up = take_absolute(jnp.stack([small[layer][3] for layer in range(layers)]), me_x, 1)
-    up = jnp.where((jnp.arange(2) == core)[:, None, None], up[:, :, None], 0.0)
-    up = up.reshape(layers, 4, 4, 32, 8).transpose(3, 1, 0, 2, 4).reshape(32, 4, 64)
-    vec = jnp.concatenate([vec, pair, up, jnp.zeros((32, 4, 32), FULL)], 2).reshape(128, 512)
-    vec = jnp.sum(lax.all_to_all(vec, ALL, 0, 0, tiled=True), axis=0)
 
     return (
         result.reshape(stream.shape),

time: 689 us -> 706 us (1.025)
  blocking collectives: 29.6 us -> 58.1 us
  starting transfers between devices: 186 us -> 164 us
  other arithmetic: 62.2 us -> 76.6 us
    all_to_all x2 -> x4, blocking collectives: 29.6 us -> 58.1 us  [trade(): lax.all_to_all(value, ('ctx', 'tensor'), 0, 0, axis_index_groups=GROUPS,...]
    ppermute x114 -> x106, starting transfers between devices: 132 us -> 119 us  [swap(): return lax.ppermute(value, ALL, exchange_perm(axis, mask))]
    ppermute x114 -> x106, waiting for transfers between devices: 130 us -> 140 us  [swap(): return lax.ppermute(value, ALL, exchange_perm(axis, mask))]
    all_to_all x6 -> x4, waiting for transfers between devices: 14.2 us -> 4.82 us  [trade(): lax.all_to_all(value, ('ctx', 'tensor'), 0, 0, axis_index_groups=GROUPS,...]
    all_to_all x6 -> x4, starting transfers between devices: 35.4 us -> 26.3 us  [trade(): lax.all_to_all(value, ('ctx', 'tensor'), 0, 0, axis_index_groups=GROUPS,...]
    convert_element_type x56 -> x48, other arithmetic: 29.4 us -> 37.2 us  [add_low(): return (left.astype(FULL) + right.astype(FULL)).astype(LOW)]
  transfers between devices with their start and end apart: 125 -> 115, of which waited for: 52 -> 51; matrix products, arithmetic and copies ran while one was open for 15% -> 16% of each run, Pallas kernels for 12% -> 11%
where the time goes in v5:
time: 706 us; the launch traced here: 695 us
  waiting for transfers between devices  172 us (24%)
  starting transfers between devices  164 us (23%)
  Pallas kernels  142 us (20%)
  other arithmetic  76.6 us (11%)
  blocking collectives  58.1 us (8%)
  local copies, waits for them, and re-layouts  53.1 us (8%)
  between operations  16.8 us (2%)
  matrix products  11.7 us (2%)
    pallas_call x16, Pallas kernels, call(): pl.pallas_call(body, grid_spec=pltpu.PrefetchScalarGridSpec(num_scalar_pr...  142 us
    ppermute x106, waiting for transfers between devices, swap(): return lax.ppermute(value, ALL, exchange_perm(axis, mask))  140 us
    ppermute x106, starting transfers between devices, swap(): return lax.ppermute(value, ALL, exchange_perm(axis, mask))  119 us
    all_to_all x4, blocking collectives, trade(): lax.all_to_all(value, ('ctx', 'tensor'), 0, 0, axis_index_groups=GROUPS,...  58.1 us
    convert_element_type x48, other arithmetic, add_low(): return (left.astype(FULL) + right.astype(FULL)).astype(LOW)  37.2 us
    all_to_all x4, starting transfers between devices, trade(): lax.all_to_all(value, ('ctx', 'tensor'), 0, 0, axis_index_groups=GROUPS,...  26.3 us
    all_gather x2, waiting for transfers between devices, everywhere(): value = lax.all_gather(value, ('dp', 'ctx'), axis=0, tiled=True)  16.7 us
  transfers between devices with their start and end apart: 115, of which 51 were waited for; matrix products, arithmetic and copies ran while one was open for 16% of the time, Pallas kernels for 11%

profile of v5, /device:TPU:1, one launch (start us, length us, event | category | flops | bytes accessed | tf_op | source)
XLA Modules:
  0.0 694.6 jit_solution(7334441349222651449)
XLA Ops:
  25.5 3.6 collective-permute-start.7
  30.4 3.6 collective-permute-done.3
  56.1 10.4 %all-to-all-start = ((bf16[128,2,256]{2,1,0:T(2,128)(2,1)}), bf16[128,2,256]{2,1,0:T(2,128)(2,1)S(1)}, u32[]{:S(2)}, u32[]{:S(2)}) async-start(bf16[128,2,256]{2,1,0:T(2,128)(2,1)} %reshape.742), calls=%async_computation | async-start | bytes 262144 | tf_op jit(solution)/shard_map/all_to_all | solution.py:615
  67.3 9.1 %all-to-all-done = bf16[128,2,256]{2,1,0:T(2,128)(2,1)S(1)} async-done(((bf16[128,2,256]{2,1,0:T(2,128)(2,1)}), bf16[128,2,256]{2,1,0:T(2,128)(2,1)S(1)}, u32[]{:S(2)}, u32[]{:S(2)}) %all-to-all-start) | async-done | bytes 131104 | tf_op jit(solution)/shard_map/all_to_all | solution.py:615
  86.1 4.1 collective-permute-done.24
  92.5 3.4 collective-permute-done.27
  104.0 6.2 collective-permute-done.29
  110.2 6.5 shard_map.186
  116.7 12.7 %all-to-all-start.1 = ((bf16[8,144,384]{2,1,0:T(8,128)(2,1)}), bf16[8,144,384]{2,1,0:T(8,128)(2,1)S(1)}, u32[]{:S(2)}, u32[]{:S(2)}) async-start(bf16[8,144,384]{2,1,0:T(8,128)(2,1)} %bitcast.315), calls=%async_computation.1 | async-start | bytes 1769472 | tf_op jit(solution)/shard_map/all_to_all | solution.py:551
  134.3 8.0 %collective-permute-done.30 = bf16[16,64,128]{2,1,0:T(8,128)(2,1)S(1)} collective-permute-done((bf16[16,64,128]{2,1,0:T(8,128)(2,1)S(1)}, bf16[16,64,128]{2,1,0:T(8,128)(2,1)S(1)}, u32[]{:S(2)}, u32[]{:S(2)}) %collective-permute-start.30) | collective-permute-done | bytes 262176 | tf_op jit(solution)/shard_map/ppermute | solution.py:41
  142.3 12.1 %collective-permute-done.31 = bf16[16,64,128]{2,1,0:T(8,128)(2,1)} collective-permute-done((bf16[16,64,128]{2,1,0:T(8,128)(2,1)S(1)}, bf16[16,64,128]{2,1,0:T(8,128)(2,1)}, u32[]{:S(2)}, u32[]{:S(2)}) %collective-permute-start.31) | collective-permute-done | bytes 262176 | tf_op jit(solution)/shard_map/ppermute | solution.py:41
  156.8 7.9 %shard_map.187 = (bf16[1152,128]{1,0:T(8,128)(2,1)}, f32[2,1152]{1,0:T(2,128)}) custom-call(bf16[1152,384]{1,0:T(8,128)(2,1)} %bitcast.357, bf16[1152,384]{1,0:T(8,128)(2,1)} %bitcast.358, bf16[1152,384]{1,0:T(8,128)(2,1)} %bitcast.359, s32[1152,2]{1,0:T(8,128)} %copy.96.mark_keys, s32[2,1152]{1,0:T(2,128)} %copy-done.65), custom_call_target="tpu_custom_call" | custom-call | flops 1358954496 | bytes 2976768 | tf_op jit(solution)/shard_map/pallas_call | solution.py:249
  164.7 5.2 all-to-all-start.2
  171.5 4.8 all-to-all-done.2
  177.1 5.2 shard_map.188
  199.4 5.1 collective-permute-done.43
  204.5 9.3 %shard_map.189 = (f32[4,2,288,256]{3,2,1,0:T(8,128)}, bf16[4,2,288,256]{3,2,1,0:T(8,128)(2,1)}, f32[288,1024]{1,0:T(8,128)}) custom-call(s32[21]{0:T(128)} %stack.185.info, bf16[288,1024]{1,0:T(8,128)(2,1)} %pad_maximum_fusion.5.x, f32[4,2,256]{2,1,0:T(2,128)} %get-tuple-element.386.bias, bf16[16,2,4,32,2048]{4,3,2,1,0:T(8,128)(2,1)} %bitcast.299, ...), custom_call_target="tpu_custom_call" | custom-call | flops 2415919104 | bytes 72425472 | tf_op jit(solution)/shard_map/pallas_call | solution.py:249
  222.7 6.5 shard_map.190
  229.2 18.6 %all_to_all.55 = bf16[8,144,384]{2,1,0:T(8,128)(2,1)} all-to-all(bf16[8,144,384]{2,1,0:T(8,128)(2,1)} %bitcast.316), channel_id=1, replica_groups={{0,1,2,3,8,9,10,11},{4,5,6,7,12,13,14,15},{16,17,18,19,24,25,26,27},{20..., dimensions={0} | all-to-all | bytes 1769472 | tf_op jit(solution)/shard_map/all_to_all | solution.py:551
  247.8 7.9 %shard_map.191 = (bf16[1152,128]{1,0:T(8,128)(2,1)}, f32[2,1152]{1,0:T(2,128)}) custom-call(bf16[1152,384]{1,0:T(8,128)(2,1)} %bitcast.364, bf16[1152,384]{1,0:T(8,128)(2,1)} %bitcast.365, bf16[1152,384]{1,0:T(8,128)(2,1)} %bitcast.366, s32[1152,2]{1,0:T(8,128)} %copy.96.mark_keys, s32[2,1152]{1,0:T(2,128)} %copy-done.65), custom_call_target="tpu_custom_call" | custom-call | flops 1358954496 | bytes 2976768 | tf_op jit(solution)/shard_map/pallas_call | solution.py:249
  255.7 10.9 %all_to_all.56 = bf16[8,144,128]{2,1,0:T(8,128)(2,1)} all-to-all(bf16[8,144,128]{2,1,0:T(8,128)(2,1)} %bitcast.388), channel_id=1, replica_groups={{0,1,2,3,8,9,10,11},{4,5,6,7,12,13,14,15},{16,17,18,19,24,25,26,27},{20..., dimensions={0} | all-to-all | bytes 589824 | tf_op jit(solution)/shard_map/all_to_all | solution.py:551
  266.6 5.2 shard_map.192
  280.8 16.7 %all-gather.8.cloned.1.call-done = bf16[4096,2048]{1,0:T(8,128)(2,1)} async-done(((bf16[128,2048]{1,0:T(8,128)(2,1)}), bf16[4096,2048]{1,0:T(8,128)(2,1)}) %all-gather.8.cloned.1.call-update) | async-done | bytes 16777232 | tf_op jit(solution)/shard_map/all_gather | solution.py:601
  297.4 9.1 %shard_map.193 = (f32[4,2,288,256]{3,2,1,0:T(8,128)}, bf16[4,2,288,256]{3,2,1,0:T(8,128)(2,1)}, f32[288,1024]{1,0:T(8,128)}) custom-call(s32[21]{0:T(128)} %stack.185.info, bf16[288,1024]{1,0:T(8,128)(2,1)} %pad_maximum_fusion.7.x, f32[4,2,256]{2,1,0:T(2,128)} %get-tuple-element.385.bias, bf16[16,2,4,32,2048]{4,3,2,1,0:T(8,128)(2,1)} %bitcast.307, ...), custom_call_target="tpu_custom_call" | custom-call | flops 2415919104 | bytes 72425472 | tf_op jit(solution)/shard_map/pallas_call | solution.py:249
  315.6 13.9 %shard_map.194 = (bf16[2,2,2,2,2,64,256]{6,5,4,3,2,1,0:T(8,128)(2,1)}, bf16[2,2,2,2,2,64,256]{6,5,4,3,2,1,0:T(8,128)(2,1)}, bf16[2,2,2,2,2,64,256]{6,5,4,3,2,1,0...) custom-call(s32[21]{0:T(128)} %stack.185.info, ...), custom_call_target="tpu_custom_call" | custom-call | flops 4831838208 | bytes 81403904 | tf_op jit(solution)/shard_map/pallas_call | solution.py:249
  337.7 4.9 shard_map.195
  342.7 11.8 %all_to_all.57 = bf16[8,144,128]{2,1,0:T(8,128)(2,1)} all-to-all(bf16[8,144,128]{2,1,0:T(8,128)(2,1)} %bitcast.325), channel_id=1, replica_groups={{0,1,2,3,8,9,10,11},{4,5,6,7,12,13,14,15},{16,17,18,19,24,25,26,27},{20..., dimensions={0} | all-to-all | bytes 589824 | tf_op jit(solution)/shard_map/all_to_all | solution.py:551
  354.5 11.8 %shard_map.196 = (bf16[1152,384]{1,0:T(8,128)(2,1)}, f32[2,128]{1,0:T(2,128)}) custom-call(bf16[1152,384]{1,0:T(8,128)(2,1)} %bitcast.367, bf16[1152,384]{1,0:T(8,128)(2,1)} %bitcast.368, bf16[1152,384]{1,0:T(8,128)(2,1)} %bitcast.369, bf16[1152,128]{1,0:T(8,128)(2,1)} %bitcast.387, s32[1152,2]{1,0:T(8,128)} %copy.96.mark_keys, s32[2,1152]{1,0:T(2,128)} %copy-done.65, ...), custom_call_target="tpu_custom_call" | custom-call | flops 3397386240 | bytes 3862528 | tf_op jit(solution)/shard_map/pallas_call | solution.py:249
  366.3 16.8 %all_to_all.58 = bf16[8,144,384]{2,1,0:T(8,128)(2,1)} all-to-all(bf16[8,144,384]{2,1,0:T(8,128)(2,1)} %bitcast.371), channel_id=1, replica_groups={{0,1,2,3,8,9,10,11},{4,5,6,7,12,13,14,15},{16,17,18,19,24,25,26,27},{20..., dimensions={0} | all-to-all | bytes 1769472 | tf_op jit(solution)/shard_map/all_to_all | solution.py:551
  383.0 11.4 %shard_map.197 = (bf16[2,2,2,2,2,64,128]{6,5,4,3,2,1,0:T(8,128)(2,1)}, bf16[2,2,2,2,2,64,128]{6,5,4,3,2,1,0:T(8,128)(2,1)}, bf16[2,2,2,2,2,64,128]{6,5,4,3,2,1,0...) custom-call(s32[21]{0:T(128)} %stack.185.info, ...), custom_call_target="tpu_custom_call" | custom-call | flops 2113929216 | bytes 10878976 | tf_op jit(solution)/shard_map/pallas_call | solution.py:249
  415.5 14.1 %shard_map.198 = (bf16[2,2,2,2,2,64,256]{6,5,4,3,2,1,0:T(8,128)(2,1)}, bf16[2,2,2,2,2,64,256]{6,5,4,3,2,1,0:T(8,128)(2,1)}, bf16[2,2,2,2,2,64,256]{6,5,4,3,2,1,0...) custom-call(s32[21]{0:T(128)} %stack.185.info, ...), custom_call_target="tpu_custom_call" | custom-call | flops 4831838208 | bytes 81403904 | tf_op jit(solution)/shard_map/pallas_call | solution.py:249
  455.2 14.8 %collective-permute-done.59 = bf16[32,64,384]{2,1,0:T(8,128)(2,1)} collective-permute-done((bf16[32,64,384]{2,1,0:T(8,128)(2,1)}, bf16[32,64,384]{2,1,0:T(8,128)(2,1)}, u32[]{:S(2)}, u32[]{:S(2)}) %collective-permute-start.59) | collective-permute-done | bytes 1572896 | tf_op jit(solution)/shard_map/ppermute | solution.py:41
  473.3 4.9 shard_map.199
  478.2 4.1 all-to-all-start.7
  497.5 11.7 %collective-permute-done.64 = bf16[16,64,384]{2,1,0:T(8,128)(2,1)S(1)} collective-permute-done((bf16[16,64,384]{2,1,0:T(8,128)(2,1)S(1)}, bf16[16,64,384]{2,1,0:T(8,128)(2,1)S(1)}, u32[]{:S(2)}, u32[]{:S(2)}) %collective-permute-start.64) | collective-permute-done | bytes 786464 | tf_op jit(solution)/shard_map/ppermute | solution.py:41
  515.7 11.8 %shard_map.200 = (bf16[1152,384]{1,0:T(8,128)(2,1)}, f32[2,128]{1,0:T(2,128)}) custom-call(bf16[1152,384]{1,0:T(8,128)(2,1)} %bitcast.360, bf16[1152,384]{1,0:T(8,128)(2,1)} %bitcast.361, bf16[1152,384]{1,0:T(8,128)(2,1)} %bitcast.362, bf16[1152,128]{1,0:T(8,128)(2,1)} %bitcast.127.grad_mixed, s32[1152,2]{1,0:T(8,128)} %copy.96.mark_keys, ...), custom_call_target="tpu_custom_call" | custom-call | flops 3397386240 | bytes 3862528 | tf_op jit(solution)/shard_map/pallas_call | solution.py:249
  530.1 8.6 %all-to-all-start.9 = ((f32[128,1,512]{2,1,0:T(1,128)}), f32[128,1,512]{2,1,0:T(1,128)S(1)}, u32[]{:S(2)}, u32[]{:S(2)}) async-start(f32[128,1,512]{2,1,0:T(1,128)} %all_to_all.43), calls=%async_computation.9 | async-start | bytes 524288 | tf_op jit(solution)/shard_map/all_to_all | solution.py:718
  545.1 3.4 collective-permute-start.71
  553.4 3.6 collective-permute-done.70
  561.7 4.4 all-to-all-start.8
  566.4 3.4 collective-permute-start.72
  574.0 8.7 %collective-permute-done.72 = bf16[8,64,640]{2,1,0:T(8,128)(2,1)S(1)} collective-permute-done((bf16[8,64,640]{2,1,0:T(8,128)(2,1)S(1)}, bf16[8,64,640]{2,1,0:T(8,128)(2,1)S(1)}, u32[]{:S(2)}, u32[]{:S(2)}) %collective-permute-start.72) | collective-permute-done | bytes 655392 | tf_op jit(solution)/shard_map/ppermute | solution.py:41
  585.4 7.8 %collective-permute-done.74 = bf16[8,64,640]{2,1,0:T(8,128)(2,1)S(1)} collective-permute-done((bf16[8,64,640]{2,1,0:T(8,128)(2,1)S(1)}, bf16[8,64,640]{2,1,0:T(8,128)(2,1)S(1)}, u32[]{:S(2)}, u32[]{:S(2)}) %collective-permute-start.74) | collective-permute-done | bytes 655392 | tf_op jit(solution)/shard_map/ppermute | solution.py:41
  604.7 11.4 %shard_map.201 = (bf16[2,2,2,2,2,64,128]{6,5,4,3,2,1,0:T(8,128)(2,1)}, bf16[2,2,2,2,2,64,128]{6,5,4,3,2,1,0:T(8,128)(2,1)}, bf16[2,2,2,2,2,64,128]{6,5,4,3,2,1,0...) custom-call(s32[21]{0:T(128)} %stack.185.info, ...), custom_call_target="tpu_custom_call" | custom-call | flops 2113929216 | bytes 10878976 | tf_op jit(solution)/shard_map/pallas_call | solution.py:249
  617.6 3.3 fusion.2
  636.6 4.7 collective-permute-done.87
  672.4 6.5 collective-permute-start.105
  678.8 4.3 fusion
  (730 shorter events, 283.7 us)
Async XLA Ops:
  7.2 37.3 %all-gather.4.cloned.1.call-start = ((), (), s32[]{:S(2)}) async-start(), calls=%async_computation.10 | async-start | bytes 1310720 | tf_op jit(solution)/shard_map/all_gather | solution.py:593
  12.3 192.2 %all-gather.6.cloned.1.call-start = ((), (), s32[]{:S(2)}) async-start(), calls=%async_computation.11 | async-start | bytes 17301504 | tf_op jit(solution)/shard_map/all_gather | solution.py:601
  47.1 250.3 %all-gather.8.cloned.1.call-start = ((), (), s32[]{:S(2)}) async-start(), calls=%async_computation.12 | async-start | bytes 17301504 | tf_op jit(solution)/shard_map/all_gather | solution.py:601
  48.5 32.4 %collective-permute-start.18 = (bf16[16,64,128]{2,1,0:T(8,128)(2,1)S(1)}, bf16[16,64,128]{2,1,0:T(8,128)(2,1)}, u32[]{:S(2)}, u32[]{:S(2)}) collective-permute-start(bf16[16,64,128]{2,1,0:T(8,128)(2,1)S(1)} %get-tuple-element.137), channel_id=1, source_target_pairs={{0,16},{1,17},{2,18},{3,19},{4,20},{5,21},{6,22},{7,23},{8,24},{9,... | collective-permute-start | bytes 786440 | tf_op jit(solution)/shard_map/ppermute | solution.py:41
  49.6 32.0 %collective-permute-start.19 = (bf16[16,64,128]{2,1,0:T(8,128)(2,1)S(1)}, bf16[16,64,128]{2,1,0:T(8,128)(2,1)}, u32[]{:S(2)}, u32[]{:S(2)}) collective-permute-start(bf16[16,64,128]{2,1,0:T(8,128)(2,1)S(1)} %get-tuple-element.137), channel_id=1, source_target_pairs={{0,8},{1,9},{2,10},{3,11},{4,12},{5,13},{6,14},{7,15},{8,0},{9,1},... | collective-permute-start | bytes 786440 | tf_op jit(solution)/shard_map/ppermute | solution.py:41
  50.8 31.3 %collective-permute-start.21 = (bf16[16,64,128]{2,1,0:T(8,128)(2,1)S(1)}, bf16[16,64,128]{2,1,0:T(8,128)(2,1)}, u32[]{:S(2)}, u32[]{:S(2)}) collective-permute-start(bf16[16,64,128]{2,1,0:T(8,128)(2,1)S(1)} %get-tuple-element.141), channel_id=1, source_target_pairs={{0,8},{1,9},{2,10},{3,11},{4,12},{5,13},{6,14},{7,15},{8,0},{9,1},... | collective-permute-start | bytes 786440 | tf_op jit(solution)/shard_map/ppermute | solution.py:41
  52.0 34.0 %collective-permute-start.22 = (bf16[16,64,128]{2,1,0:T(8,128)(2,1)S(1)}, bf16[16,64,128]{2,1,0:T(8,128)(2,1)}, u32[]{:S(2)}, u32[]{:S(2)}) collective-permute-start(bf16[16,64,128]{2,1,0:T(8,128)(2,1)S(1)} %get-tuple-element.141), channel_id=1, source_target_pairs={{0,48},{1,49},{2,50},{3,51},{4,52},{5,53},{6,54},{7,55},{8,56},{9,... | collective-permute-start | bytes 786440 | tf_op jit(solution)/shard_map/ppermute | solution.py:41
  56.1 20.4 %all-to-all-start = ((bf16[128,2,256]{2,1,0:T(2,128)(2,1)}), bf16[128,2,256]{2,1,0:T(2,128)(2,1)S(1)}, u32[]{:S(2)}, u32[]{:S(2)}) async-start(bf16[128,2,256]{2,1,0:T(2,128)(2,1)} %reshape.742), calls=%async_computation | async-start | bytes 262144 | tf_op jit(solution)/shard_map/all_to_all | solution.py:615
  80.2 16.2 %collective-permute-start.17 = (bf16[144,1024]{1,0:T(8,128)(2,1)S(1)}, bf16[144,1024]{1,0:T(8,128)(2,1)}, u32[]{:S(2)}, u32[]{:S(2)}) collective-permute-start(bf16[144,1024]{1,0:T(8,128)(2,1)S(1)} %slice.876), channel_id=1, source_target_pairs={{0,4},{1,5},{2,6},{3,7},{4,0},{5,1},{6,2},{7,3},{8,12},{9,13},{10,... | collective-permute-start | bytes 884744 | tf_op jit(solution)/shard_map/ppermute | solution.py:41
  82.1 13.8 %collective-permute-start.27 = (bf16[16,64,128]{2,1,0:T(8,128)(2,1)S(1)}, bf16[16,64,128]{2,1,0:T(8,128)(2,1)S(1)}, u32[]{:S(2)}, u32[]{:S(2)}) collective-permute-start(bf16[16,64,128]{2,1,0:T(8,128)(2,1)S(1)} %get-tuple-element.156), channel_id=1, source_target_pairs={{0,72},{1,73},{2,74},{3,75},{4,76},{5,77},{6,78},{7,79},{8,64},{9,... | collective-permute-start | bytes 786440 | tf_op jit(solution)/shard_map/ppermute | solution.py:41
  86.0 14.1 %collective-permute-start.28 = (bf16[16,64,128]{2,1,0:T(8,128)(2,1)S(1)}, bf16[16,64,128]{2,1,0:T(8,128)(2,1)S(1)}, u32[]{:S(2)}, u32[]{:S(2)}) collective-permute-start(bf16[16,64,128]{2,1,0:T(8,128)(2,1)S(1)} %get-tuple-element.156), channel_id=1, source_target_pairs={{0,16},{1,17},{2,18},{3,19},{4,20},{5,21},{6,22},{7,23},{8,24},{9,... | collective-permute-start | bytes 786440 | tf_op jit(solution)/shard_map/ppermute | solution.py:41
  96.4 13.8 %collective-permute-start.29 = (bf16[16,64,128]{2,1,0:T(8,128)(2,1)S(1)}, bf16[16,64,128]{2,1,0:T(8,128)(2,1)S(1)}, u32[]{:S(2)}, u32[]{:S(2)}) collective-permute-start(bf16[16,64,128]{2,1,0:T(8,128)(2,1)S(1)} %collective-permute-done.27), channel_id=1, source_target_pairs={{0,16},{1,17},{2,18},{3,19},{4,20},{5,21},{6,22},{7,23},{8,24},{9,... | collective-permute-start | bytes 786440 | tf_op jit(solution)/shard_map/ppermute | solution.py:41
  116.7 39.2 %all-to-all-start.1 = ((bf16[8,144,384]{2,1,0:T(8,128)(2,1)}), bf16[8,144,384]{2,1,0:T(8,128)(2,1)S(1)}, u32[]{:S(2)}, u32[]{:S(2)}) async-start(bf16[8,144,384]{2,1,0:T(8,128)(2,1)} %bitcast.315), calls=%async_computation.1 | async-start | bytes 1769472 | tf_op jit(solution)/shard_map/all_to_all | solution.py:551
  129.5 25.0 %collective-permute-start.31 = (bf16[16,64,128]{2,1,0:T(8,128)(2,1)S(1)}, bf16[16,64,128]{2,1,0:T(8,128)(2,1)}, u32[]{:S(2)}, u32[]{:S(2)}) collective-permute-start(bf16[16,64,128]{2,1,0:T(8,128)(2,1)S(1)} %copy-done.34), channel_id=1, source_target_pairs={{0,8},{1,9},{2,10},{3,11},{4,12},{5,13},{6,14},{7,15},{8,0},{9,1},... | collective-permute-start | bytes 786440 | tf_op jit(solution)/shard_map/ppermute | solution.py:41
  131.0 24.8 %collective-permute-start.32 = (bf16[16,64,128]{2,1,0:T(8,128)(2,1)}, bf16[16,64,128]{2,1,0:T(8,128)(2,1)}, u32[]{:S(2)}, u32[]{:S(2)}) collective-permute-start(bf16[16,64,128]{2,1,0:T(8,128)(2,1)} %get-tuple-element.151), channel_id=1, source_target_pairs={{0,48},{1,49},{2,50},{3,51},{4,52},{5,53},{6,54},{7,55},{8,56},{9,... | collective-permute-start | bytes 786440 | tf_op jit(solution)/shard_map/ppermute | solution.py:41
  131.0 24.9 %collective-permute-start.33 = (bf16[16,64,128]{2,1,0:T(8,128)(2,1)S(1)}, bf16[16,64,128]{2,1,0:T(8,128)(2,1)S(1)}, u32[]{:S(2)}, u32[]{:S(2)}) collective-permute-start(bf16[16,64,128]{2,1,0:T(8,128)(2,1)S(1)} %get-tuple-element.152), channel_id=1, source_target_pairs={{0,72},{1,73},{2,74},{3,75},{4,76},{5,77},{6,78},{7,79},{8,64},{9,... | collective-permute-start | bytes 786440 | tf_op jit(solution)/shard_map/ppermute | solution.py:41
  133.6 37.9 %collective-permute-start.34 = (bf16[16,64,128]{2,1,0:T(8,128)(2,1)S(1)}, bf16[16,64,128]{2,1,0:T(8,128)(2,1)}, u32[]{:S(2)}, u32[]{:S(2)}) collective-permute-start(bf16[16,64,128]{2,1,0:T(8,128)(2,1)S(1)} %get-tuple-element.149), channel_id=1, source_target_pairs={{0,8},{1,9},{2,10},{3,11},{4,12},{5,13},{6,14},{7,15},{8,0},{9,1},... | collective-permute-start | bytes 786440 | tf_op jit(solution)/shard_map/ppermute | solution.py:41
  142.3 29.2 %collective-permute-start.35 = (bf16[16,64,128]{2,1,0:T(8,128)(2,1)S(1)}, bf16[16,64,128]{2,1,0:T(8,128)(2,1)}, u32[]{:S(2)}, u32[]{:S(2)}) collective-permute-start(bf16[16,64,128]{2,1,0:T(8,128)(2,1)S(1)} %copy-done.34), channel_id=1, source_target_pairs={{0,48},{1,49},{2,50},{3,51},{4,52},{5,53},{6,54},{7,55},{8,56},{9,... | collective-permute-start | bytes 786440 | tf_op jit(solution)/shard_map/ppermute | solution.py:41
  154.4 17.1 %collective-permute-start.36 = (bf16[16,64,128]{2,1,0:T(8,128)(2,1)}, bf16[16,64,128]{2,1,0:T(8,128)(2,1)}, u32[]{:S(2)}, u32[]{:S(2)}) collective-permute-start(bf16[16,64,128]{2,1,0:T(8,128)(2,1)} %get-tuple-element.151), channel_id=1, source_target_pairs={{0,72},{1,73},{2,74},{3,75},{4,76},{5,77},{6,78},{7,79},{8,64},{9,... | collective-permute-start | bytes 786440 | tf_op jit(solution)/shard_map/ppermute | solution.py:41
  155.8 15.8 %collective-permute-start.37 = (bf16[16,64,128]{2,1,0:T(8,128)(2,1)S(1)}, bf16[16,64,128]{2,1,0:T(8,128)(2,1)S(1)}, u32[]{:S(2)}, u32[]{:S(2)}) collective-permute-start(bf16[16,64,128]{2,1,0:T(8,128)(2,1)S(1)} %get-tuple-element.152), channel_id=1, source_target_pairs={{0,16},{1,17},{2,18},{3,19},{4,20},{5,21},{6,22},{7,23},{8,24},{9,... | collective-permute-start | bytes 786440 | tf_op jit(solution)/shard_map/ppermute | solution.py:41
  404.0 38.0 %collective-permute-start.56 = (bf16[32,64,384]{2,1,0:T(8,128)(2,1)}, bf16[32,64,384]{2,1,0:T(8,128)(2,1)}, u32[]{:S(2)}, u32[]{:S(2)}) collective-permute-start(bf16[32,64,384]{2,1,0:T(8,128)(2,1)} %pad_maximum_fusion), channel_id=1, source_target_pairs={{0,8},{1,9},{2,10},{3,11},{4,12},{5,13},{6,14},{7,15},{8,0},{9,1},... | collective-permute-start | bytes 4718600 | tf_op jit(solution)/shard_map/ppermute | solution.py:41
  409.3 37.2 %collective-permute-start.57 = (bf16[32,64,384]{2,1,0:T(8,128)(2,1)}, bf16[32,64,384]{2,1,0:T(8,128)(2,1)}, u32[]{:S(2)}, u32[]{:S(2)}) collective-permute-start(bf16[32,64,384]{2,1,0:T(8,128)(2,1)} %pad_maximum_fusion.1), channel_id=1, source_target_pairs={{0,48},{1,49},{2,50},{3,51},{4,52},{5,53},{6,54},{7,55},{8,56},{9,... | collective-permute-start | bytes 4718600 | tf_op jit(solution)/shard_map/ppermute | solution.py:41
  412.7 39.0 %collective-permute-start.58 = (bf16[32,64,384]{2,1,0:T(8,128)(2,1)}, bf16[32,64,384]{2,1,0:T(8,128)(2,1)}, u32[]{:S(2)}, u32[]{:S(2)}) collective-permute-start(bf16[32,64,384]{2,1,0:T(8,128)(2,1)} %pad_maximum_fusion.2), channel_id=1, source_target_pairs={{0,72},{1,73},{2,74},{3,75},{4,76},{5,77},{6,78},{7,79},{8,64},{9,... | collective-permute-start | bytes 4718600 | tf_op jit(solution)/shard_map/ppermute | solution.py:41
  433.7 36.3 %collective-permute-start.59 = (bf16[32,64,384]{2,1,0:T(8,128)(2,1)}, bf16[32,64,384]{2,1,0:T(8,128)(2,1)}, u32[]{:S(2)}, u32[]{:S(2)}) collective-permute-start(bf16[32,64,384]{2,1,0:T(8,128)(2,1)} %pad_maximum_fusion.3), channel_id=1, source_target_pairs={{0,16},{1,17},{2,18},{3,19},{4,20},{5,21},{6,22},{7,23},{8,24},{9,... | collective-permute-start | bytes 4718600 | tf_op jit(solution)/shard_map/ppermute | solution.py:41
  440.9 43.8 %collective-permute-start.60 = (bf16[32,64,256]{2,1,0:T(8,128)(2,1)}, bf16[32,64,256]{2,1,0:T(8,128)(2,1)S(1)}, u32[]{:S(2)}, u32[]{:S(2)}) collective-permute-start(bf16[32,64,256]{2,1,0:T(8,128)(2,1)} %bitcast.456), channel_id=1, source_target_pairs={{0,8},{1,9},{2,10},{3,11},{4,12},{5,13},{6,14},{7,15},{8,0},{9,1},... | collective-permute-start | bytes 3145736 | tf_op jit(solution)/shard_map/ppermute | solution.py:41
  441.9 46.0 %collective-permute-start.61 = (bf16[32,64,256]{2,1,0:T(8,128)(2,1)}, bf16[32,64,256]{2,1,0:T(8,128)(2,1)}, u32[]{:S(2)}, u32[]{:S(2)}) collective-permute-start(bf16[32,64,256]{2,1,0:T(8,128)(2,1)} %bitcast.455), channel_id=1, source_target_pairs={{0,48},{1,49},{2,50},{3,51},{4,52},{5,53},{6,54},{7,55},{8,56},{9,... | collective-permute-start | bytes 3145736 | tf_op jit(solution)/shard_map/ppermute | solution.py:41
  446.5 44.9 %collective-permute-start.62 = (bf16[32,64,256]{2,1,0:T(8,128)(2,1)}, bf16[32,64,256]{2,1,0:T(8,128)(2,1)}, u32[]{:S(2)}, u32[]{:S(2)}) collective-permute-start(bf16[32,64,256]{2,1,0:T(8,128)(2,1)} %bitcast.133), channel_id=1, source_target_pairs={{0,72},{1,73},{2,74},{3,75},{4,76},{5,77},{6,78},{7,79},{8,64},{9,... | collective-permute-start | bytes 3145736 | tf_op jit(solution)/shard_map/ppermute | solution.py:41
  451.7 43.2 %collective-permute-start.63 = (bf16[32,64,256]{2,1,0:T(8,128)(2,1)}, bf16[32,64,256]{2,1,0:T(8,128)(2,1)}, u32[]{:S(2)}, u32[]{:S(2)}) collective-permute-start(bf16[32,64,256]{2,1,0:T(8,128)(2,1)} %bitcast.135), channel_id=1, source_target_pairs={{0,16},{1,17},{2,18},{3,19},{4,20},{5,21},{6,22},{7,23},{8,24},{9,... | collective-permute-start | bytes 3145736 | tf_op jit(solution)/shard_map/ppermute | solution.py:41
  478.2 35.6 %all-to-all-start.7 = ((bf16[8,144,128]{2,1,0:T(8,128)(2,1)}), bf16[8,144,128]{2,1,0:T(8,128)(2,1)}, u32[]{:S(2)}, u32[]{:S(2)}) async-start(bf16[8,144,128]{2,1,0:T(8,128)(2,1)} %bitcast.324), calls=%async_computation.7 | async-start | bytes 589824 | tf_op jit(solution)/shard_map/all_to_all | solution.py:551
  482.4 26.8 %collective-permute-start.64 = (bf16[16,64,384]{2,1,0:T(8,128)(2,1)S(1)}, bf16[16,64,384]{2,1,0:T(8,128)(2,1)S(1)}, u32[]{:S(2)}, u32[]{:S(2)}) collective-permute-start(bf16[16,64,384]{2,1,0:T(8,128)(2,1)S(1)} %slice.573), channel_id=1, source_target_pairs={{0,16},{1,17},{2,18},{3,19},{4,20},{5,21},{6,22},{7,23},{8,24},{9,... | collective-permute-start | bytes 2359304 | tf_op jit(solution)/shard_map/ppermute | solution.py:41
  484.8 25.6 %collective-permute-start.65 = (bf16[16,64,384]{2,1,0:T(8,128)(2,1)S(1)}, bf16[16,64,384]{2,1,0:T(8,128)(2,1)S(1)}, u32[]{:S(2)}, u32[]{:S(2)}) collective-permute-start(bf16[16,64,384]{2,1,0:T(8,128)(2,1)S(1)} %slice.575), channel_id=1, source_target_pairs={{0,8},{1,9},{2,10},{3,11},{4,12},{5,13},{6,14},{7,15},{8,0},{9,1},... | collective-permute-start | bytes 2359304 | tf_op jit(solution)/shard_map/ppermute | solution.py:41
  487.9 23.6 %collective-permute-start.66 = (bf16[16,64,384]{2,1,0:T(8,128)(2,1)S(1)}, bf16[16,64,384]{2,1,0:T(8,128)(2,1)S(1)}, u32[]{:S(2)}, u32[]{:S(2)}) collective-permute-start(bf16[16,64,384]{2,1,0:T(8,128)(2,1)S(1)} %slice.577), channel_id=1, source_target_pairs={{0,48},{1,49},{2,50},{3,51},{4,52},{5,53},{6,54},{7,55},{8,56},{9,... | collective-permute-start | bytes 2359304 | tf_op jit(solution)/shard_map/ppermute | solution.py:41
  491.4 21.3 %collective-permute-start.67 = (bf16[16,64,384]{2,1,0:T(8,128)(2,1)S(1)}, bf16[16,64,384]{2,1,0:T(8,128)(2,1)S(1)}, u32[]{:S(2)}, u32[]{:S(2)}) collective-permute-start(bf16[16,64,384]{2,1,0:T(8,128)(2,1)S(1)} %slice.579), channel_id=1, source_target_pairs={{0,72},{1,73},{2,74},{3,75},{4,76},{5,77},{6,78},{7,79},{8,64},{9,... | collective-permute-start | bytes 2359304 | tf_op jit(solution)/shard_map/ppermute | solution.py:41
  514.7 35.3 %collective-permute-start.68 = (bf16[16,64,256]{2,1,0:T(8,128)(2,1)}, bf16[16,64,256]{2,1,0:T(8,128)(2,1)}, u32[]{:S(2)}, u32[]{:S(2)}) collective-permute-start(bf16[16,64,256]{2,1,0:T(8,128)(2,1)} %slice.581), channel_id=1, source_target_pairs={{0,16},{1,17},{2,18},{3,19},{4,20},{5,21},{6,22},{7,23},{8,24},{9,... | collective-permute-start | bytes 1572872 | tf_op jit(solution)/shard_map/ppermute | solution.py:41
  515.7 36.4 %collective-permute-start.69 = (bf16[16,64,256]{2,1,0:T(8,128)(2,1)}, bf16[16,64,256]{2,1,0:T(8,128)(2,1)}, u32[]{:S(2)}, u32[]{:S(2)}) collective-permute-start(bf16[16,64,256]{2,1,0:T(8,128)(2,1)} %slice.583), channel_id=1, source_target_pairs={{0,8},{1,9},{2,10},{3,11},{4,12},{5,13},{6,14},{7,15},{8,0},{9,1},... | collective-permute-start | bytes 1572872 | tf_op jit(solution)/shard_map/ppermute | solution.py:41
  530.1 19.7 %all-to-all-start.9 = ((f32[128,1,512]{2,1,0:T(1,128)}), f32[128,1,512]{2,1,0:T(1,128)S(1)}, u32[]{:S(2)}, u32[]{:S(2)}) async-start(f32[128,1,512]{2,1,0:T(1,128)} %all_to_all.43), calls=%async_computation.9 | async-start | bytes 524288 | tf_op jit(solution)/shard_map/all_to_all | solution.py:718
  540.6 16.4 %collective-permute-start.70 = (bf16[16,64,256]{2,1,0:T(8,128)(2,1)}, bf16[16,64,256]{2,1,0:T(8,128)(2,1)}, u32[]{:S(2)}, u32[]{:S(2)}) collective-permute-start(bf16[16,64,256]{2,1,0:T(8,128)(2,1)} %slice.585), channel_id=1, source_target_pairs={{0,48},{1,49},{2,50},{3,51},{4,52},{5,53},{6,54},{7,55},{8,56},{9,... | collective-permute-start | bytes 1572872 | tf_op jit(solution)/shard_map/ppermute | solution.py:41
  545.1 15.4 %collective-permute-start.71 = (bf16[16,64,256]{2,1,0:T(8,128)(2,1)}, bf16[16,64,256]{2,1,0:T(8,128)(2,1)}, u32[]{:S(2)}, u32[]{:S(2)}) collective-permute-start(bf16[16,64,256]{2,1,0:T(8,128)(2,1)} %slice.587), channel_id=1, source_target_pairs={{0,72},{1,73},{2,74},{3,75},{4,76},{5,77},{6,78},{7,79},{8,64},{9,... | collective-permute-start | bytes 1572872 | tf_op jit(solution)/shard_map/ppermute | solution.py:41
  561.7 43.0 %all-to-all-start.8 = ((bf16[8,144,384]{2,1,0:T(8,128)(2,1)}), bf16[8,144,384]{2,1,0:T(8,128)(2,1)}, u32[]{:S(2)}, u32[]{:S(2)}) async-start(bf16[8,144,384]{2,1,0:T(8,128)(2,1)} %bitcast.363), calls=%async_computation.8 | async-start | bytes 1769472 | tf_op jit(solution)/shard_map/all_to_all | solution.py:551
  566.4 16.4 %collective-permute-start.72 = (bf16[8,64,640]{2,1,0:T(8,128)(2,1)S(1)}, bf16[8,64,640]{2,1,0:T(8,128)(2,1)S(1)}, u32[]{:S(2)}, u32[]{:S(2)}) collective-permute-start(bf16[8,64,640]{2,1,0:T(8,128)(2,1)S(1)} %slice.696), channel_id=1, source_target_pairs={{0,72},{1,73},{2,74},{3,75},{4,76},{5,77},{6,78},{7,79},{8,64},{9,... | collective-permute-start | bytes 1966088 | tf_op jit(solution)/shard_map/ppermute | solution.py:41
  570.0 23.1 %collective-permute-start.74 = (bf16[8,64,640]{2,1,0:T(8,128)(2,1)S(1)}, bf16[8,64,640]{2,1,0:T(8,128)(2,1)S(1)}, u32[]{:S(2)}, u32[]{:S(2)}) collective-permute-start(bf16[8,64,640]{2,1,0:T(8,128)(2,1)S(1)} %slice.700), channel_id=1, source_target_pairs={{0,3},{1,2},{2,1},{3,0},{4,7},{5,6},{6,5},{7,4},{8,11},{9,10},{10,... | collective-permute-start | bytes 1966088 | tf_op jit(solution)/shard_map/ppermute | solution.py:41
  572.8 23.8 %collective-permute-start.76 = (bf16[8,64,640]{2,1,0:T(8,128)(2,1)S(1)}, bf16[8,64,640]{2,1,0:T(8,128)(2,1)S(1)}, u32[]{:S(2)}, u32[]{:S(2)}) collective-permute-start(bf16[8,64,640]{2,1,0:T(8,128)(2,1)S(1)} %slice.704), channel_id=1, source_target_pairs={{0,16},{1,17},{2,18},{3,19},{4,20},{5,21},{6,22},{7,23},{8,24},{9,... | collective-permute-start | bytes 1966088 | tf_op jit(solution)/shard_map/ppermute | solution.py:41
  573.9 22.9 %collective-permute-start.78 = (bf16[8,64,640]{2,1,0:T(8,128)(2,1)S(1)}, bf16[8,64,640]{2,1,0:T(8,128)(2,1)S(1)}, u32[]{:S(2)}, u32[]{:S(2)}) collective-permute-start(bf16[8,64,640]{2,1,0:T(8,128)(2,1)S(1)} %slice.708), channel_id=1, source_target_pairs={{0,1},{1,0},{2,3},{3,2},{4,5},{5,4},{6,7},{7,6},{8,9},{9,8},{10,11... | collective-permute-start | bytes 1966088 | tf_op jit(solution)/shard_map/ppermute | solution.py:41
  582.9 17.2 %collective-permute-start.73 = (bf16[4,64,640]{2,1,0:T(8,128)(2,1)S(1)}, bf16[4,64,640]{2,1,0:T(8,128)(2,1)S(1)}, u32[]{:S(2)}, u32[]{:S(2)}) collective-permute-start(bf16[4,64,640]{2,1,0:T(8,128)(2,1)S(1)} %slice.698), channel_id=1, source_target_pairs={{0,3},{1,2},{2,1},{3,0},{4,7},{5,6},{6,5},{7,4},{8,11},{9,10},{10,... | collective-permute-start | bytes 983048 | tf_op jit(solution)/shard_map/ppermute | solution.py:41
  616.3 17.1 %collective-permute-start.93 = (bf16[32,64,128]{2,1,0:T(8,128)(2,1)}, bf16[32,64,128]{2,1,0:T(8,128)(2,1)S(1)}, u32[]{:S(2)}, u32[]{:S(2)}) collective-permute-start(bf16[32,64,128]{2,1,0:T(8,128)(2,1)} %bitcast.457), channel_id=1, source_target_pairs={{0,72},{1,73},{2,74},{3,75},{4,76},{5,77},{6,78},{7,79},{8,64},{9,... | collective-permute-start | bytes 1572872 | tf_op jit(solution)/shard_map/ppermute | solution.py:41
  622.9 55.9 %collective-permute-start.80 = (bf16[144,1024]{1,0:T(8,128)(2,1)}, bf16[144,1024]{1,0:T(8,128)(2,1)}, u32[]{:S(2)}, u32[]{:S(2)}) collective-permute-start(bf16[144,1024]{1,0:T(8,128)(2,1)} %slice.868), channel_id=1, source_target_pairs={{0,4},{1,5},{2,6},{3,7},{4,0},{5,1},{6,2},{7,3},{8,12},{9,13},{10,... | collective-permute-start | bytes 884744 | tf_op jit(solution)/shard_map/ppermute | solution.py:41
  626.2 15.1 %collective-permute-start.87 = (bf16[32,64,128]{2,1,0:T(8,128)(2,1)}, bf16[32,64,128]{2,1,0:T(8,128)(2,1)}, u32[]{:S(2)}, u32[]{:S(2)}) collective-permute-start(bf16[32,64,128]{2,1,0:T(8,128)(2,1)} %bitcast.160), channel_id=1, source_target_pairs={{0,48},{1,49},{2,50},{3,51},{4,52},{5,53},{6,54},{7,55},{8,56},{9,... | collective-permute-start | bytes 1572872 | tf_op jit(solution)/shard_map/ppermute | solution.py:41
  626.3 16.3 %collective-permute-start.81 = (bf16[32,64,128]{2,1,0:T(8,128)(2,1)}, bf16[32,64,128]{2,1,0:T(8,128)(2,1)S(1)}, u32[]{:S(2)}, u32[]{:S(2)}) collective-permute-start(bf16[32,64,128]{2,1,0:T(8,128)(2,1)} %bitcast.157), channel_id=1, source_target_pairs={{0,8},{1,9},{2,10},{3,11},{4,12},{5,13},{6,14},{7,15},{8,0},{9,1},... | collective-permute-start | bytes 1572872 | tf_op jit(solution)/shard_map/ppermute | solution.py:41
  (163 other events, 1497.3 us)
Sparse Core Ops, SparseCore 0:
  12.4 27.3 all-gather.3
  47.3 141.5 all-gather.5
  190.6 106.8 all-gather.7

commit v6 on v4

--- a/solution.py
+++ b/solution.py
@@ -739,6 +739,8 @@
             later = [jnp.concatenate(pair, 2) for pair in zip(grad_feed, grad_attention)]
         else:
             lead = reduce_first(grad_attention, range(4))
+            lead, small_zero = lax.optimization_barrier((lead, (gain_one, gain_two)))
+            gain_one, gain_two = small_zero
             lead = reduce_phase(reduce_phase(lead, range(4), 2), range(4), 3)
             tail = [jnp.concatenate(pair, 2) for pair in zip(tail, lead)]
             tail = reduce_phases(tail, range(4), 4)

time: 689 us -> 696 us (1.010)
    ppermute x114, waiting for transfers between devices: 130 us -> 138 us  [swap(): return lax.ppermute(value, ALL, exchange_perm(axis, mask))]
  transfers between devices with their start and end apart: 125 -> 125, of which waited for: 52 -> 50; matrix products, arithmetic and copies ran while one was open for 15% -> 14% of each run, Pallas kernels for 12% -> 12%
where the time goes in v6:
time: 696 us; the launch traced here: 685 us
  starting transfers between devices  192 us (28%)
  waiting for transfers between devices  182 us (26%)
  Pallas kernels  141 us (20%)
  other arithmetic  60.9 us (9%)
  local copies, waits for them, and re-layouts  51.1 us (7%)
  blocking collectives  29.6 us (4%)
  between operations  17 us (2%)
  matrix products  10.5 us (2%)
    pallas_call x16, Pallas kernels, call(): pl.pallas_call(body, grid_spec=pltpu.PrefetchScalarGridSpec(num_scalar_pr...  141 us
    ppermute x114, waiting for transfers between devices, swap(): return lax.ppermute(value, ALL, exchange_perm(axis, mask))  138 us
    ppermute x114, starting transfers between devices, swap(): return lax.ppermute(value, ALL, exchange_perm(axis, mask))  136 us
    all_to_all x6, starting transfers between devices, trade(): lax.all_to_all(value, ('ctx', 'tensor'), 0, 0, axis_index_groups=GROUPS,...  36.8 us
    all_to_all x2, blocking collectives, trade(): lax.all_to_all(value, ('ctx', 'tensor'), 0, 0, axis_index_groups=GROUPS,...  29.6 us
    convert_element_type x56, other arithmetic, add_low(): return (left.astype(FULL) + right.astype(FULL)).astype(LOW)  26.9 us
    all_gather x2, waiting for transfers between devices, everywhere(): value = lax.all_gather(value, ('dp', 'ctx'), axis=0, tiled=True)  21.8 us
  transfers between devices with their start and end apart: 125, of which 50 were waited for; matrix products, arithmetic and copies ran while one was open for 14% of the time, Pallas kernels for 12%

profile of v6, /device:TPU:1, one launch (start us, length us, event | category | flops | bytes accessed | tf_op | source)
XLA Modules:
  0.0 684.6 jit_solution(12493054355690463777)
XLA Ops:
  24.6 3.6 collective-permute-start.7
  54.9 10.7 %all-to-all-start = ((bf16[128,2,256]{2,1,0:T(2,128)(2,1)}), bf16[128,2,256]{2,1,0:T(2,128)(2,1)S(1)}, u32[]{:S(2)}, u32[]{:S(2)}) async-start(bf16[128,2,256]{2,1,0:T(2,128)(2,1)} %reshape.742), calls=%async_computation | async-start | bytes 262144 | tf_op jit(solution)/shard_map/all_to_all | solution.py:617
  66.5 9.1 %all-to-all-done = bf16[128,2,256]{2,1,0:T(2,128)(2,1)S(1)} async-done(((bf16[128,2,256]{2,1,0:T(2,128)(2,1)}), bf16[128,2,256]{2,1,0:T(2,128)(2,1)S(1)}, u32[]{:S(2)}, u32[]{:S(2)}) %all-to-all-start) | async-done | bytes 131104 | tf_op jit(solution)/shard_map/all_to_all | solution.py:617
  84.2 3.9 collective-permute-done.24
  90.5 3.6 collective-permute-done.27
  102.2 6.0 collective-permute-done.29
  108.2 6.4 shard_map.186
  114.7 12.7 %all-to-all-start.1 = ((bf16[8,144,384]{2,1,0:T(8,128)(2,1)}), bf16[8,144,384]{2,1,0:T(8,128)(2,1)}, u32[]{:S(2)}, u32[]{:S(2)}) async-start(bf16[8,144,384]{2,1,0:T(8,128)(2,1)} %bitcast.331), calls=%async_computation.1 | async-start | bytes 1769472 | tf_op jit(solution)/shard_map/all_to_all | solution.py:552
  132.5 7.6 %collective-permute-done.30 = bf16[16,64,128]{2,1,0:T(8,128)(2,1)S(1)} collective-permute-done((bf16[16,64,128]{2,1,0:T(8,128)(2,1)S(1)}, bf16[16,64,128]{2,1,0:T(8,128)(2,1)S(1)}, u32[]{:S(2)}, u32[]{:S(2)}) %collective-permute-start.30) | collective-permute-done | bytes 262176 | tf_op jit(solution)/shard_map/ppermute | solution.py:41
  143.3 9.9 %collective-permute-done.31 = bf16[16,64,128]{2,1,0:T(8,128)(2,1)} collective-permute-done((bf16[16,64,128]{2,1,0:T(8,128)(2,1)S(1)}, bf16[16,64,128]{2,1,0:T(8,128)(2,1)}, u32[]{:S(2)}, u32[]{:S(2)}) %collective-permute-start.31) | collective-permute-done | bytes 262176 | tf_op jit(solution)/shard_map/ppermute | solution.py:41
  155.6 8.8 %collective-permute-done.34 = bf16[16,64,128]{2,1,0:T(8,128)(2,1)S(1)} collective-permute-done((bf16[16,64,128]{2,1,0:T(8,128)(2,1)S(1)}, bf16[16,64,128]{2,1,0:T(8,128)(2,1)S(1)}, u32[]{:S(2)}, u32[]{:S(2)}) %collective-permute-start.34) | collective-permute-done | bytes 262176 | tf_op jit(solution)/shard_map/ppermute | solution.py:41
  167.1 7.9 %shard_map.187 = (bf16[1152,128]{1,0:T(8,128)(2,1)}, f32[2,1152]{1,0:T(2,128)}) custom-call(bf16[1152,384]{1,0:T(8,128)(2,1)} %bitcast.54.query.keys.values, bf16[1152,384]{1,0:T(8,128)(2,1)} %bitcast.54.query.keys.values, bf16[1152,384]{1,0:T(8,128)(2,1)} %bitcast.54.query.keys.values, s32[1152,2]{1,0:T(8,128)} %copy.96.mark_keys, s32[2,1152]{1,0:T(2,128)} %copy-done.57), custom_call_target="tpu_custom_call" | custom-call | flops 1358954496 | bytes 2976768 | tf_op jit(solution)/shard_map/pallas_call | solution.py:250
  175.0 5.0 all-to-all-start.2
  181.5 4.9 all-to-all-done.2
  187.1 5.2 shard_map.188
  193.4 5.1 collective-permute-start.42
  203.9 9.2 %shard_map.189 = (f32[4,2,288,256]{3,2,1,0:T(8,128)}, bf16[4,2,288,256]{3,2,1,0:T(8,128)(2,1)}, f32[288,1024]{1,0:T(8,128)}) custom-call(s32[21]{0:T(128)} %stack.185.info, bf16[288,1024]{1,0:T(8,128)(2,1)} %pad_maximum_fusion.5.x, f32[4,2,256]{2,1,0:T(2,128)} %get-tuple-element.386.bias, bf16[16,2,4,32,2048]{4,3,2,1,0:T(8,128)(2,1)} %bitcast.315, ...), custom_call_target="tpu_custom_call" | custom-call | flops 2415919104 | bytes 72425472 | tf_op jit(solution)/shard_map/pallas_call | solution.py:250
  220.4 6.5 shard_map.190
  226.8 18.6 %all_to_all.55 = bf16[8,144,384]{2,1,0:T(8,128)(2,1)} all-to-all(bf16[8,144,384]{2,1,0:T(8,128)(2,1)} %bitcast.332), channel_id=1, replica_groups={{0,1,2,3,8,9,10,11},{4,5,6,7,12,13,14,15},{16,17,18,19,24,25,26,27},{20..., dimensions={0} | all-to-all | bytes 1769472 | tf_op jit(solution)/shard_map/all_to_all | solution.py:552
  245.5 7.9 %shard_map.191 = (bf16[1152,128]{1,0:T(8,128)(2,1)}, f32[2,1152]{1,0:T(2,128)}) custom-call(bf16[1152,384]{1,0:T(8,128)(2,1)} %bitcast.367, bf16[1152,384]{1,0:T(8,128)(2,1)} %bitcast.368, bf16[1152,384]{1,0:T(8,128)(2,1)} %bitcast.369, s32[1152,2]{1,0:T(8,128)} %copy.96.mark_keys, s32[2,1152]{1,0:T(2,128)} %copy-done.57), custom_call_target="tpu_custom_call" | custom-call | flops 1358954496 | bytes 2976768 | tf_op jit(solution)/shard_map/pallas_call | solution.py:250
  253.3 10.9 %all_to_all.56 = bf16[8,144,128]{2,1,0:T(8,128)(2,1)} all-to-all(bf16[8,144,128]{2,1,0:T(8,128)(2,1)} %bitcast.383), channel_id=1, replica_groups={{0,1,2,3,8,9,10,11},{4,5,6,7,12,13,14,15},{16,17,18,19,24,25,26,27},{20..., dimensions={0} | all-to-all | bytes 589824 | tf_op jit(solution)/shard_map/all_to_all | solution.py:552
  264.3 5.2 shard_map.192
  278.5 21.8 %all-gather.8.cloned.1.call-done = bf16[4096,2048]{1,0:T(8,128)(2,1)} async-done(((bf16[128,2048]{1,0:T(8,128)(2,1)}), bf16[4096,2048]{1,0:T(8,128)(2,1)}) %all-gather.8.cloned.1.call-update) | async-done | bytes 16777232 | tf_op jit(solution)/shard_map/all_gather | solution.py:603
  300.3 9.1 %shard_map.193 = (f32[4,2,288,256]{3,2,1,0:T(8,128)}, bf16[4,2,288,256]{3,2,1,0:T(8,128)(2,1)}, f32[288,1024]{1,0:T(8,128)}) custom-call(s32[21]{0:T(128)} %stack.185.info, bf16[288,1024]{1,0:T(8,128)(2,1)} %pad_maximum_fusion.7.x, f32[4,2,256]{2,1,0:T(2,128)} %get-tuple-element.385.bias, bf16[16,2,4,32,2048]{4,3,2,1,0:T(8,128)(2,1)} %bitcast.323, ...), custom_call_target="tpu_custom_call" | custom-call | flops 2415919104 | bytes 72425472 | tf_op jit(solution)/shard_map/pallas_call | solution.py:250
  318.3 13.9 %shard_map.194 = (bf16[2,2,2,2,2,64,256]{6,5,4,3,2,1,0:T(8,128)(2,1)}, bf16[2,2,2,2,2,64,256]{6,5,4,3,2,1,0:T(8,128)(2,1)}, bf16[2,2,2,2,2,64,256]{6,5,4,3,2,1,0...) custom-call(s32[21]{0:T(128)} %stack.185.info, ...), custom_call_target="tpu_custom_call" | custom-call | flops 4831838208 | bytes 81403904 | tf_op jit(solution)/shard_map/pallas_call | solution.py:250
  341.5 4.9 shard_map.195
  346.4 4.1 all-to-all-start.5
  353.5 8.1 %all-to-all-done.5 = bf16[8,144,128]{2,1,0:T(8,128)(2,1)S(1)} async-done(((bf16[8,144,128]{2,1,0:T(8,128)(2,1)}), bf16[8,144,128]{2,1,0:T(8,128)(2,1)S(1)}, u32[]{:S(2)}, u32[]{:S(2)}) %all-to-all-start.5) | async-done | bytes 294944 | tf_op jit(solution)/shard_map/all_to_all | solution.py:552
  362.3 11.8 %shard_map.196 = (bf16[1152,384]{1,0:T(8,128)(2,1)}, f32[2,128]{1,0:T(2,128)}) custom-call(bf16[1152,384]{1,0:T(8,128)(2,1)} %bitcast.370, bf16[1152,384]{1,0:T(8,128)(2,1)} %bitcast.371, bf16[1152,384]{1,0:T(8,128)(2,1)} %bitcast.372, bf16[1152,128]{1,0:T(8,128)(2,1)} %bitcast.381, s32[1152,2]{1,0:T(8,128)} %copy.96.mark_keys, s32[2,1152]{1,0:T(2,128)} %copy-done.57, ...), custom_call_target="tpu_custom_call" | custom-call | flops 3397386240 | bytes 3862528 | tf_op jit(solution)/shard_map/pallas_call | solution.py:250
  374.1 4.4 all-to-all-start.6
  393.3 8.8 %collective-permute-done.55 = bf16[16,64,256]{2,1,0:T(8,128)(2,1)S(1)} collective-permute-done((bf16[16,64,256]{2,1,0:T(8,128)(2,1)S(1)}, bf16[16,64,256]{2,1,0:T(8,128)(2,1)S(1)}, u32[]{:S(2)}, u32[]{:S(2)}) %collective-permute-start.55) | collective-permute-done | bytes 524320 | tf_op jit(solution)/shard_map/ppermute | solution.py:41
  405.0 11.3 %shard_map.197 = (bf16[2,2,2,2,2,64,128]{6,5,4,3,2,1,0:T(8,128)(2,1)}, bf16[2,2,2,2,2,64,128]{6,5,4,3,2,1,0:T(8,128)(2,1)}, bf16[2,2,2,2,2,64,128]{6,5,4,3,2,1,0...) custom-call(s32[21]{0:T(128)} %stack.185.info, ...), custom_call_target="tpu_custom_call" | custom-call | flops 2113929216 | bytes 10878976 | tf_op jit(solution)/shard_map/pallas_call | solution.py:250
  432.2 5.6 collective-permute-done.64
  448.5 14.1 %shard_map.198 = (bf16[2,2,2,2,2,64,256]{6,5,4,3,2,1,0:T(8,128)(2,1)}, bf16[2,2,2,2,2,64,256]{6,5,4,3,2,1,0:T(8,128)(2,1)}, bf16[2,2,2,2,2,64,256]{6,5,4,3,2,1,0...) custom-call(s32[21]{0:T(128)} %stack.185.info, ...), custom_call_target="tpu_custom_call" | custom-call | flops 4831838208 | bytes 81403904 | tf_op jit(solution)/shard_map/pallas_call | solution.py:250
  479.3 4.9 shard_map.199
  484.3 4.7 all-to-all-start.7
  489.0 3.7 collective-permute-done.72
  518.7 11.8 %shard_map.200 = (bf16[1152,384]{1,0:T(8,128)(2,1)}, f32[2,128]{1,0:T(2,128)}) custom-call(bf16[1152,384]{1,0:T(8,128)(2,1)} %bitcast.54.query.keys.values, bf16[1152,384]{1,0:T(8,128)(2,1)} %bitcast.54.query.keys.values, bf16[1152,384]{1,0:T(8,128)(2,1)} %bitcast.54.query.keys.values, bf16[1152,128]{1,0:T(8,128)(2,1)} %bitcast.127.grad_mixed, ...), custom_call_target="tpu_custom_call" | custom-call | flops 3397386240 | bytes 3862528 | tf_op jit(solution)/shard_map/pallas_call | solution.py:250
  530.5 6.0 all-to-all-start.8
  543.2 9.3 %collective-permute-done.80 = bf16[8,64,640]{2,1,0:T(8,128)(2,1)S(1)} collective-permute-done((bf16[8,64,640]{2,1,0:T(8,128)(2,1)S(1)}, bf16[8,64,640]{2,1,0:T(8,128)(2,1)S(1)}, u32[]{:S(2)}, u32[]{:S(2)}) %collective-permute-start.80) | collective-permute-done | bytes 655392 | tf_op jit(solution)/shard_map/ppermute | solution.py:41
  555.3 8.0 %collective-permute-done.82 = bf16[8,64,640]{2,1,0:T(8,128)(2,1)S(1)} collective-permute-done((bf16[8,64,640]{2,1,0:T(8,128)(2,1)S(1)}, bf16[8,64,640]{2,1,0:T(8,128)(2,1)S(1)}, u32[]{:S(2)}, u32[]{:S(2)}) %collective-permute-start.82) | collective-permute-done | bytes 655392 | tf_op jit(solution)/shard_map/ppermute | solution.py:41
  566.5 3.7 collective-permute-done.81
  572.5 11.4 %shard_map.201 = (bf16[2,2,2,2,2,64,128]{6,5,4,3,2,1,0:T(8,128)(2,1)}, bf16[2,2,2,2,2,64,128]{6,5,4,3,2,1,0:T(8,128)(2,1)}, bf16[2,2,2,2,2,64,128]{6,5,4,3,2,1,0...) custom-call(s32[21]{0:T(128)} %stack.185.info, ...), custom_call_target="tpu_custom_call" | custom-call | flops 2113929216 | bytes 10878976 | tf_op jit(solution)/shard_map/pallas_call | solution.py:250
  589.4 5.8 collective-permute-start.88
  600.1 10.1 %collective-permute-done.93 = bf16[32,64,128]{2,1,0:T(8,128)(2,1)S(1)} collective-permute-done((bf16[32,64,128]{2,1,0:T(8,128)(2,1)}, bf16[32,64,128]{2,1,0:T(8,128)(2,1)S(1)}, u32[]{:S(2)}, u32[]{:S(2)}) %collective-permute-start.93) | collective-permute-done | bytes 524320 | tf_op jit(solution)/shard_map/ppermute | solution.py:41
  630.5 8.1 %all-to-all-start.9 = ((f32[128,1,512]{2,1,0:T(1,128)}), f32[128,1,512]{2,1,0:T(1,128)S(1)}, u32[]{:S(2)}, u32[]{:S(2)}) async-start(f32[128,1,512]{2,1,0:T(1,128)} %all_to_all.43), calls=%async_computation.9 | async-start | bytes 524288 | tf_op jit(solution)/shard_map/all_to_all | solution.py:790
  651.0 4.2 collective-permute-done.111
  665.8 4.3 fusion.1
  (734 shorter events, 285.2 us)
Async XLA Ops:
  7.2 36.4 %all-gather.4.cloned.1.call-start = ((), (), s32[]{:S(2)}) async-start(), calls=%async_computation.10 | async-start | bytes 1310720 | tf_op jit(solution)/shard_map/all_gather | solution.py:594
  11.5 192.4 %all-gather.6.cloned.1.call-start = ((), (), s32[]{:S(2)}) async-start(), calls=%async_computation.11 | async-start | bytes 17301504 | tf_op jit(solution)/shard_map/all_gather | solution.py:603
  46.1 254.1 %all-gather.8.cloned.1.call-start = ((), (), s32[]{:S(2)}) async-start(), calls=%async_computation.12 | async-start | bytes 17301504 | tf_op jit(solution)/shard_map/all_gather | solution.py:603
  47.5 31.3 %collective-permute-start.18 = (bf16[16,64,128]{2,1,0:T(8,128)(2,1)S(1)}, bf16[16,64,128]{2,1,0:T(8,128)(2,1)}, u32[]{:S(2)}, u32[]{:S(2)}) collective-permute-start(bf16[16,64,128]{2,1,0:T(8,128)(2,1)S(1)} %get-tuple-element.137), channel_id=1, source_target_pairs={{0,16},{1,17},{2,18},{3,19},{4,20},{5,21},{6,22},{7,23},{8,24},{9,... | collective-permute-start | bytes 786440 | tf_op jit(solution)/shard_map/ppermute | solution.py:41
  47.8 31.9 %collective-permute-start.19 = (bf16[16,64,128]{2,1,0:T(8,128)(2,1)S(1)}, bf16[16,64,128]{2,1,0:T(8,128)(2,1)}, u32[]{:S(2)}, u32[]{:S(2)}) collective-permute-start(bf16[16,64,128]{2,1,0:T(8,128)(2,1)S(1)} %get-tuple-element.137), channel_id=1, source_target_pairs={{0,8},{1,9},{2,10},{3,11},{4,12},{5,13},{6,14},{7,15},{8,0},{9,1},... | collective-permute-start | bytes 786440 | tf_op jit(solution)/shard_map/ppermute | solution.py:41
  49.8 30.4 %collective-permute-start.21 = (bf16[16,64,128]{2,1,0:T(8,128)(2,1)S(1)}, bf16[16,64,128]{2,1,0:T(8,128)(2,1)}, u32[]{:S(2)}, u32[]{:S(2)}) collective-permute-start(bf16[16,64,128]{2,1,0:T(8,128)(2,1)S(1)} %get-tuple-element.141), channel_id=1, source_target_pairs={{0,8},{1,9},{2,10},{3,11},{4,12},{5,13},{6,14},{7,15},{8,0},{9,1},... | collective-permute-start | bytes 786440 | tf_op jit(solution)/shard_map/ppermute | solution.py:41
  50.1 34.0 %collective-permute-start.22 = (bf16[16,64,128]{2,1,0:T(8,128)(2,1)S(1)}, bf16[16,64,128]{2,1,0:T(8,128)(2,1)}, u32[]{:S(2)}, u32[]{:S(2)}) collective-permute-start(bf16[16,64,128]{2,1,0:T(8,128)(2,1)S(1)} %get-tuple-element.141), channel_id=1, source_target_pairs={{0,48},{1,49},{2,50},{3,51},{4,52},{5,53},{6,54},{7,55},{8,56},{9,... | collective-permute-start | bytes 786440 | tf_op jit(solution)/shard_map/ppermute | solution.py:41
  54.9 20.6 %all-to-all-start = ((bf16[128,2,256]{2,1,0:T(2,128)(2,1)}), bf16[128,2,256]{2,1,0:T(2,128)(2,1)S(1)}, u32[]{:S(2)}, u32[]{:S(2)}) async-start(bf16[128,2,256]{2,1,0:T(2,128)(2,1)} %reshape.742), calls=%async_computation | async-start | bytes 262144 | tf_op jit(solution)/shard_map/all_to_all | solution.py:617
  78.2 16.3 %collective-permute-start.17 = (bf16[144,1024]{1,0:T(8,128)(2,1)S(1)}, bf16[144,1024]{1,0:T(8,128)(2,1)}, u32[]{:S(2)}, u32[]{:S(2)}) collective-permute-start(bf16[144,1024]{1,0:T(8,128)(2,1)S(1)} %slice.928), channel_id=1, source_target_pairs={{0,4},{1,5},{2,6},{3,7},{4,0},{5,1},{6,2},{7,3},{8,12},{9,13},{10,... | collective-permute-start | bytes 884744 | tf_op jit(solution)/shard_map/ppermute | solution.py:41
  114.7 49.7 %all-to-all-start.1 = ((bf16[8,144,384]{2,1,0:T(8,128)(2,1)}), bf16[8,144,384]{2,1,0:T(8,128)(2,1)}, u32[]{:S(2)}, u32[]{:S(2)}) async-start(bf16[8,144,384]{2,1,0:T(8,128)(2,1)} %bitcast.331), calls=%async_computation.1 | async-start | bytes 1769472 | tf_op jit(solution)/shard_map/all_to_all | solution.py:552
  127.4 25.8 %collective-permute-start.31 = (bf16[16,64,128]{2,1,0:T(8,128)(2,1)S(1)}, bf16[16,64,128]{2,1,0:T(8,128)(2,1)}, u32[]{:S(2)}, u32[]{:S(2)}) collective-permute-start(bf16[16,64,128]{2,1,0:T(8,128)(2,1)S(1)} %copy-done.31), channel_id=1, source_target_pairs={{0,8},{1,9},{2,10},{3,11},{4,12},{5,13},{6,14},{7,15},{8,0},{9,1},... | collective-permute-start | bytes 786440 | tf_op jit(solution)/shard_map/ppermute | solution.py:41
  129.7 24.5 %collective-permute-start.32 = (bf16[16,64,128]{2,1,0:T(8,128)(2,1)S(1)}, bf16[16,64,128]{2,1,0:T(8,128)(2,1)}, u32[]{:S(2)}, u32[]{:S(2)}) collective-permute-start(bf16[16,64,128]{2,1,0:T(8,128)(2,1)S(1)} %copy-done.32), channel_id=1, source_target_pairs={{0,48},{1,49},{2,50},{3,51},{4,52},{5,53},{6,54},{7,55},{8,56},{9,... | collective-permute-start | bytes 786440 | tf_op jit(solution)/shard_map/ppermute | solution.py:41
  129.7 34.7 %collective-permute-start.34 = (bf16[16,64,128]{2,1,0:T(8,128)(2,1)S(1)}, bf16[16,64,128]{2,1,0:T(8,128)(2,1)S(1)}, u32[]{:S(2)}, u32[]{:S(2)}) collective-permute-start(bf16[16,64,128]{2,1,0:T(8,128)(2,1)S(1)} %get-tuple-element.149), channel_id=1, source_target_pairs={{0,8},{1,9},{2,10},{3,11},{4,12},{5,13},{6,14},{7,15},{8,0},{9,1},... | collective-permute-start | bytes 786440 | tf_op jit(solution)/shard_map/ppermute | solution.py:41
  129.9 34.5 %collective-permute-start.35 = (bf16[16,64,128]{2,1,0:T(8,128)(2,1)S(1)}, bf16[16,64,128]{2,1,0:T(8,128)(2,1)}, u32[]{:S(2)}, u32[]{:S(2)}) collective-permute-start(bf16[16,64,128]{2,1,0:T(8,128)(2,1)S(1)} %copy-done.31), channel_id=1, source_target_pairs={{0,48},{1,49},{2,50},{3,51},{4,52},{5,53},{6,54},{7,55},{8,56},{9,... | collective-permute-start | bytes 786440 | tf_op jit(solution)/shard_map/ppermute | solution.py:41
  164.4 22.0 %collective-permute-start.38 = (bf16[16,64,128]{2,1,0:T(8,128)(2,1)S(1)}, bf16[16,64,128]{2,1,0:T(8,128)(2,1)S(1)}, u32[]{:S(2)}, u32[]{:S(2)}) collective-permute-start(bf16[16,64,128]{2,1,0:T(8,128)(2,1)S(1)} %collective-permute-done.30), channel_id=1, source_target_pairs={{0,8},{1,9},{2,10},{3,11},{4,12},{5,13},{6,14},{7,15},{8,0},{9,1},... | collective-permute-start | bytes 786440 | tf_op jit(solution)/shard_map/ppermute | solution.py:41
  164.5 21.9 %collective-permute-start.39 = (bf16[16,64,128]{2,1,0:T(8,128)(2,1)}, bf16[16,64,128]{2,1,0:T(8,128)(2,1)S(1)}, u32[]{:S(2)}, u32[]{:S(2)}) collective-permute-start(bf16[16,64,128]{2,1,0:T(8,128)(2,1)} %collective-permute-done.31), channel_id=1, source_target_pairs={{0,48},{1,49},{2,50},{3,51},{4,52},{5,53},{6,54},{7,55},{8,56},{9,... | collective-permute-start | bytes 786440 | tf_op jit(solution)/shard_map/ppermute | solution.py:41
  164.6 21.8 %collective-permute-start.40 = (bf16[16,64,128]{2,1,0:T(8,128)(2,1)}, bf16[16,64,128]{2,1,0:T(8,128)(2,1)}, u32[]{:S(2)}, u32[]{:S(2)}) collective-permute-start(bf16[16,64,128]{2,1,0:T(8,128)(2,1)} %collective-permute-done.32), channel_id=1, source_target_pairs={{0,72},{1,73},{2,74},{3,75},{4,76},{5,77},{6,78},{7,79},{8,64},{9,... | collective-permute-start | bytes 786440 | tf_op jit(solution)/shard_map/ppermute | solution.py:41
  166.6 19.8 %collective-permute-start.41 = (bf16[16,64,128]{2,1,0:T(8,128)(2,1)S(1)}, bf16[16,64,128]{2,1,0:T(8,128)(2,1)S(1)}, u32[]{:S(2)}, u32[]{:S(2)}) collective-permute-start(bf16[16,64,128]{2,1,0:T(8,128)(2,1)S(1)} %collective-permute-done.33), channel_id=1, source_target_pairs={{0,16},{1,17},{2,18},{3,19},{4,20},{5,21},{6,22},{7,23},{8,24},{9,... | collective-permute-start | bytes 786440 | tf_op jit(solution)/shard_map/ppermute | solution.py:41
  333.6 44.8 %collective-permute-start.52 = (bf16[32,64,256]{2,1,0:T(8,128)(2,1)}, bf16[32,64,256]{2,1,0:T(8,128)(2,1)}, u32[]{:S(2)}, u32[]{:S(2)}) collective-permute-start(bf16[32,64,256]{2,1,0:T(8,128)(2,1)} %bitcast.454), channel_id=1, source_target_pairs={{0,8},{1,9},{2,10},{3,11},{4,12},{5,13},{6,14},{7,15},{8,0},{9,1},... | collective-permute-start | bytes 3145736 | tf_op jit(solution)/shard_map/ppermute | solution.py:41
  338.2 42.0 %collective-permute-start.54 = (bf16[32,64,256]{2,1,0:T(8,128)(2,1)}, bf16[32,64,256]{2,1,0:T(8,128)(2,1)}, u32[]{:S(2)}, u32[]{:S(2)}) collective-permute-start(bf16[32,64,256]{2,1,0:T(8,128)(2,1)} %bitcast.113), channel_id=1, source_target_pairs={{0,48},{1,49},{2,50},{3,51},{4,52},{5,53},{6,54},{7,55},{8,56},{9,... | collective-permute-start | bytes 3145736 | tf_op jit(solution)/shard_map/ppermute | solution.py:41
  350.5 33.9 %collective-permute-start.56 = (bf16[32,64,256]{2,1,0:T(8,128)(2,1)}, bf16[32,64,256]{2,1,0:T(8,128)(2,1)}, u32[]{:S(2)}, u32[]{:S(2)}) collective-permute-start(bf16[32,64,256]{2,1,0:T(8,128)(2,1)} %bitcast.453), channel_id=1, source_target_pairs={{0,72},{1,73},{2,74},{3,75},{4,76},{5,77},{6,78},{7,79},{8,64},{9,... | collective-permute-start | bytes 3145736 | tf_op jit(solution)/shard_map/ppermute | solution.py:41
  353.5 35.3 %collective-permute-start.58 = (bf16[32,64,256]{2,1,0:T(8,128)(2,1)}, bf16[32,64,256]{2,1,0:T(8,128)(2,1)}, u32[]{:S(2)}, u32[]{:S(2)}) collective-permute-start(bf16[32,64,256]{2,1,0:T(8,128)(2,1)} %bitcast.452), channel_id=1, source_target_pairs={{0,16},{1,17},{2,18},{3,19},{4,20},{5,21},{6,22},{7,23},{8,24},{9,... | collective-permute-start | bytes 3145736 | tf_op jit(solution)/shard_map/ppermute | solution.py:41
  374.1 30.9 %all-to-all-start.6 = ((bf16[8,144,384]{2,1,0:T(8,128)(2,1)}), bf16[8,144,384]{2,1,0:T(8,128)(2,1)}, u32[]{:S(2)}, u32[]{:S(2)}) async-start(bf16[8,144,384]{2,1,0:T(8,128)(2,1)} %bitcast.374), calls=%async_computation.6 | async-start | bytes 1769472 | tf_op jit(solution)/shard_map/all_to_all | solution.py:552
  383.0 19.1 %collective-permute-start.55 = (bf16[16,64,256]{2,1,0:T(8,128)(2,1)S(1)}, bf16[16,64,256]{2,1,0:T(8,128)(2,1)S(1)}, u32[]{:S(2)}, u32[]{:S(2)}) collective-permute-start(bf16[16,64,256]{2,1,0:T(8,128)(2,1)S(1)} %slice.728), channel_id=1, source_target_pairs={{0,8},{1,9},{2,10},{3,11},{4,12},{5,13},{6,14},{7,15},{8,0},{9,1},... | collective-permute-start | bytes 1572872 | tf_op jit(solution)/shard_map/ppermute | solution.py:41
  386.1 16.9 %collective-permute-start.57 = (bf16[16,64,256]{2,1,0:T(8,128)(2,1)S(1)}, bf16[16,64,256]{2,1,0:T(8,128)(2,1)S(1)}, u32[]{:S(2)}, u32[]{:S(2)}) collective-permute-start(bf16[16,64,256]{2,1,0:T(8,128)(2,1)S(1)} %slice.730), channel_id=1, source_target_pairs={{0,48},{1,49},{2,50},{3,51},{4,52},{5,53},{6,54},{7,55},{8,56},{9,... | collective-permute-start | bytes 1572872 | tf_op jit(solution)/shard_map/ppermute | solution.py:41
  431.2 16.5 %collective-permute-start.61 = (bf16[144,1024]{1,0:T(8,128)(2,1)S(1)}, bf16[144,1024]{1,0:T(8,128)(2,1)S(1)}, u32[]{:S(2)}, u32[]{:S(2)}) collective-permute-start(bf16[144,1024]{1,0:T(8,128)(2,1)S(1)} %convert_element_type.663), channel_id=1, source_target_pairs={{0,4},{1,5},{2,6},{3,7},{4,0},{5,1},{6,2},{7,3},{8,12},{9,13},{10,... | collective-permute-start | bytes 884744 | tf_op jit(solution)/shard_map/ppermute | solution.py:41
  438.7 28.9 %collective-permute-start.65 = (bf16[16,64,128]{2,1,0:T(8,128)(2,1)}, bf16[16,64,128]{2,1,0:T(8,128)(2,1)S(1)}, u32[]{:S(2)}, u32[]{:S(2)}) collective-permute-start(bf16[16,64,128]{2,1,0:T(8,128)(2,1)} %slice.736), channel_id=1, source_target_pairs={{0,16},{1,17},{2,18},{3,19},{4,20},{5,21},{6,22},{7,23},{8,24},{9,... | collective-permute-start | bytes 786440 | tf_op jit(solution)/shard_map/ppermute | solution.py:41
  440.0 27.8 %collective-permute-start.67 = (bf16[16,64,128]{2,1,0:T(8,128)(2,1)}, bf16[16,64,128]{2,1,0:T(8,128)(2,1)}, u32[]{:S(2)}, u32[]{:S(2)}) collective-permute-start(bf16[16,64,128]{2,1,0:T(8,128)(2,1)} %slice.738), channel_id=1, source_target_pairs={{0,8},{1,9},{2,10},{3,11},{4,12},{5,13},{6,14},{7,15},{8,0},{9,1},... | collective-permute-start | bytes 786440 | tf_op jit(solution)/shard_map/ppermute | solution.py:41
  442.1 28.6 %collective-permute-start.69 = (bf16[16,64,128]{2,1,0:T(8,128)(2,1)}, bf16[16,64,128]{2,1,0:T(8,128)(2,1)}, u32[]{:S(2)}, u32[]{:S(2)}) collective-permute-start(bf16[16,64,128]{2,1,0:T(8,128)(2,1)} %slice.740), channel_id=1, source_target_pairs={{0,48},{1,49},{2,50},{3,51},{4,52},{5,53},{6,54},{7,55},{8,56},{9,... | collective-permute-start | bytes 786440 | tf_op jit(solution)/shard_map/ppermute | solution.py:41
  444.9 27.2 %collective-permute-start.71 = (bf16[16,64,128]{2,1,0:T(8,128)(2,1)}, bf16[16,64,128]{2,1,0:T(8,128)(2,1)}, u32[]{:S(2)}, u32[]{:S(2)}) collective-permute-start(bf16[16,64,128]{2,1,0:T(8,128)(2,1)} %slice.742), channel_id=1, source_target_pairs={{0,72},{1,73},{2,74},{3,75},{4,76},{5,77},{6,78},{7,79},{8,64},{9,... | collective-permute-start | bytes 786440 | tf_op jit(solution)/shard_map/ppermute | solution.py:41
  467.7 25.1 %collective-permute-start.72 = (bf16[32,64,256]{2,1,0:T(8,128)(2,1)}, bf16[32,64,256]{2,1,0:T(8,128)(2,1)}, u32[]{:S(2)}, u32[]{:S(2)}) collective-permute-start(bf16[32,64,256]{2,1,0:T(8,128)(2,1)} %bitcast.451), channel_id=1, source_target_pairs={{0,8},{1,9},{2,10},{3,11},{4,12},{5,13},{6,14},{7,15},{8,0},{9,1},... | collective-permute-start | bytes 3145736 | tf_op jit(solution)/shard_map/ppermute | solution.py:41
  467.8 27.1 %collective-permute-start.74 = (bf16[32,64,256]{2,1,0:T(8,128)(2,1)}, bf16[32,64,256]{2,1,0:T(8,128)(2,1)}, u32[]{:S(2)}, u32[]{:S(2)}) collective-permute-start(bf16[32,64,256]{2,1,0:T(8,128)(2,1)} %bitcast.450), channel_id=1, source_target_pairs={{0,48},{1,49},{2,50},{3,51},{4,52},{5,53},{6,54},{7,55},{8,56},{9,... | collective-permute-start | bytes 3145736 | tf_op jit(solution)/shard_map/ppermute | solution.py:41
  470.7 27.0 %collective-permute-start.76 = (bf16[32,64,256]{2,1,0:T(8,128)(2,1)}, bf16[32,64,256]{2,1,0:T(8,128)(2,1)}, u32[]{:S(2)}, u32[]{:S(2)}) collective-permute-start(bf16[32,64,256]{2,1,0:T(8,128)(2,1)} %bitcast.133), channel_id=1, source_target_pairs={{0,72},{1,73},{2,74},{3,75},{4,76},{5,77},{6,78},{7,79},{8,64},{9,... | collective-permute-start | bytes 3145736 | tf_op jit(solution)/shard_map/ppermute | solution.py:41
  472.1 30.6 %collective-permute-start.78 = (bf16[32,64,256]{2,1,0:T(8,128)(2,1)}, bf16[32,64,256]{2,1,0:T(8,128)(2,1)}, u32[]{:S(2)}, u32[]{:S(2)}) collective-permute-start(bf16[32,64,256]{2,1,0:T(8,128)(2,1)} %bitcast.135), channel_id=1, source_target_pairs={{0,16},{1,17},{2,18},{3,19},{4,20},{5,21},{6,22},{7,23},{8,24},{9,... | collective-permute-start | bytes 3145736 | tf_op jit(solution)/shard_map/ppermute | solution.py:41
  484.3 34.4 %all-to-all-start.7 = ((bf16[8,144,128]{2,1,0:T(8,128)(2,1)}), bf16[8,144,128]{2,1,0:T(8,128)(2,1)}, u32[]{:S(2)}, u32[]{:S(2)}) async-start(bf16[8,144,128]{2,1,0:T(8,128)(2,1)} %bitcast.340), calls=%async_computation.7 | async-start | bytes 589824 | tf_op jit(solution)/shard_map/all_to_all | solution.py:552
  530.5 42.1 %all-to-all-start.8 = ((bf16[8,144,384]{2,1,0:T(8,128)(2,1)}), bf16[8,144,384]{2,1,0:T(8,128)(2,1)}, u32[]{:S(2)}, u32[]{:S(2)}) async-start(bf16[8,144,384]{2,1,0:T(8,128)(2,1)} %bitcast.373), calls=%async_computation.8 | async-start | bytes 1769472 | tf_op jit(solution)/shard_map/all_to_all | solution.py:552
  539.3 23.9 %collective-permute-start.82 = (bf16[8,64,640]{2,1,0:T(8,128)(2,1)S(1)}, bf16[8,64,640]{2,1,0:T(8,128)(2,1)S(1)}, u32[]{:S(2)}, u32[]{:S(2)}) collective-permute-start(bf16[8,64,640]{2,1,0:T(8,128)(2,1)S(1)} %slice.756), channel_id=1, source_target_pairs={{0,3},{1,2},{2,1},{3,0},{4,7},{5,6},{6,5},{7,4},{8,11},{9,10},{10,... | collective-permute-start | bytes 1966088 | tf_op jit(solution)/shard_map/ppermute | solution.py:41
  542.1 22.4 %collective-permute-start.84 = (bf16[8,64,640]{2,1,0:T(8,128)(2,1)S(1)}, bf16[8,64,640]{2,1,0:T(8,128)(2,1)S(1)}, u32[]{:S(2)}, u32[]{:S(2)}) collective-permute-start(bf16[8,64,640]{2,1,0:T(8,128)(2,1)S(1)} %slice.760), channel_id=1, source_target_pairs={{0,16},{1,17},{2,18},{3,19},{4,20},{5,21},{6,22},{7,23},{8,24},{9,... | collective-permute-start | bytes 1966088 | tf_op jit(solution)/shard_map/ppermute | solution.py:41
  543.1 21.6 %collective-permute-start.86 = (bf16[8,64,640]{2,1,0:T(8,128)(2,1)S(1)}, bf16[8,64,640]{2,1,0:T(8,128)(2,1)S(1)}, u32[]{:S(2)}, u32[]{:S(2)}) collective-permute-start(bf16[8,64,640]{2,1,0:T(8,128)(2,1)S(1)} %slice.764), channel_id=1, source_target_pairs={{0,1},{1,0},{2,3},{3,2},{4,5},{5,4},{6,7},{7,6},{8,9},{9,8},{10,11... | collective-permute-start | bytes 1966088 | tf_op jit(solution)/shard_map/ppermute | solution.py:41
  552.8 17.5 %collective-permute-start.81 = (bf16[4,64,640]{2,1,0:T(8,128)(2,1)S(1)}, bf16[4,64,640]{2,1,0:T(8,128)(2,1)S(1)}, u32[]{:S(2)}, u32[]{:S(2)}) collective-permute-start(bf16[4,64,640]{2,1,0:T(8,128)(2,1)S(1)} %slice.754), channel_id=1, source_target_pairs={{0,3},{1,2},{2,1},{3,0},{4,7},{5,6},{6,5},{7,4},{8,11},{9,10},{10,... | collective-permute-start | bytes 983048 | tf_op jit(solution)/shard_map/ppermute | solution.py:41
  589.4 76.3 %collective-permute-start.88 = (bf16[144,1024]{1,0:T(8,128)(2,1)}, bf16[144,1024]{1,0:T(8,128)(2,1)}, u32[]{:S(2)}, u32[]{:S(2)}) collective-permute-start(bf16[144,1024]{1,0:T(8,128)(2,1)} %slice.920), channel_id=1, source_target_pairs={{0,4},{1,5},{2,6},{3,7},{4,0},{5,1},{6,2},{7,3},{8,12},{9,13},{10,... | collective-permute-start | bytes 884744 | tf_op jit(solution)/shard_map/ppermute | solution.py:41
  597.8 18.8 %collective-permute-start.90 = (bf16[16,64,128]{2,1,0:T(8,128)(2,1)S(1)}, bf16[16,64,128]{2,1,0:T(8,128)(2,1)S(1)}, u32[]{:S(2)}, u32[]{:S(2)}) collective-permute-start(bf16[16,64,128]{2,1,0:T(8,128)(2,1)S(1)} %slice.769), channel_id=1, source_target_pairs={{0,16},{1,17},{2,18},{3,19},{4,20},{5,21},{6,22},{7,23},{8,24},{9,... | collective-permute-start | bytes 786440 | tf_op jit(solution)/shard_map/ppermute | solution.py:41
  599.6 17.1 %collective-permute-start.92 = (bf16[16,64,128]{2,1,0:T(8,128)(2,1)S(1)}, bf16[16,64,128]{2,1,0:T(8,128)(2,1)S(1)}, u32[]{:S(2)}, u32[]{:S(2)}) collective-permute-start(bf16[16,64,128]{2,1,0:T(8,128)(2,1)S(1)} %slice.771), channel_id=1, source_target_pairs={{0,8},{1,9},{2,10},{3,11},{4,12},{5,13},{6,14},{7,15},{8,0},{9,1},... | collective-permute-start | bytes 786440 | tf_op jit(solution)/shard_map/ppermute | solution.py:41
  621.1 17.5 %collective-permute-start.109 = (bf16[8,64,128]{2,1,0:T(8,128)(2,1)}, bf16[8,64,128]{2,1,0:T(8,128)(2,1)S(1)}, u32[]{:S(2)}, u32[]{:S(2)}) collective-permute-start(bf16[8,64,128]{2,1,0:T(8,128)(2,1)} %slice.671), channel_id=1, source_target_pairs={{0,1},{1,0},{2,3},{3,2},{4,5},{5,4},{6,7},{7,6},{8,9},{9,8},{10,11... | collective-permute-start | bytes 393224 | tf_op jit(solution)/shard_map/ppermute | solution.py:41
  621.7 19.7 %collective-permute-start.105 = (bf16[8,64,128]{2,1,0:T(8,128)(2,1)}, bf16[8,64,128]{2,1,0:T(8,128)(2,1)S(1)}, u32[]{:S(2)}, u32[]{:S(2)}) collective-permute-start(bf16[8,64,128]{2,1,0:T(8,128)(2,1)} %slice.663), channel_id=1, source_target_pairs={{0,16},{1,17},{2,18},{3,19},{4,20},{5,21},{6,22},{7,23},{8,24},{9,... | collective-permute-start | bytes 393224 | tf_op jit(solution)/shard_map/ppermute | solution.py:41
  622.4 20.4 %collective-permute-start.101 = (bf16[8,64,128]{2,1,0:T(8,128)(2,1)}, bf16[8,64,128]{2,1,0:T(8,128)(2,1)S(1)}, u32[]{:S(2)}, u32[]{:S(2)}) collective-permute-start(bf16[8,64,128]{2,1,0:T(8,128)(2,1)} %slice.655), channel_id=1, source_target_pairs={{0,3},{1,2},{2,1},{3,0},{4,7},{5,6},{6,5},{7,4},{8,11},{9,10},{10,... | collective-permute-start | bytes 393224 | tf_op jit(solution)/shard_map/ppermute | solution.py:41
  624.5 21.6 %collective-permute-start.97 = (bf16[8,64,128]{2,1,0:T(8,128)(2,1)}, bf16[8,64,128]{2,1,0:T(8,128)(2,1)S(1)}, u32[]{:S(2)}, u32[]{:S(2)}) collective-permute-start(bf16[8,64,128]{2,1,0:T(8,128)(2,1)} %slice.647), channel_id=1, source_target_pairs={{0,72},{1,73},{2,74},{3,75},{4,76},{5,77},{6,78},{7,79},{8,64},{9,... | collective-permute-start | bytes 393224 | tf_op jit(solution)/shard_map/ppermute | solution.py:41
  630.5 39.5 %all-to-all-start.9 = ((f32[128,1,512]{2,1,0:T(1,128)}), f32[128,1,512]{2,1,0:T(1,128)S(1)}, u32[]{:S(2)}, u32[]{:S(2)}) async-start(f32[128,1,512]{2,1,0:T(1,128)} %all_to_all.43), calls=%async_computation.9 | async-start | bytes 524288 | tf_op jit(solution)/shard_map/all_to_all | solution.py:790
  (160 other events, 1989.0 us)
Sparse Core Ops, SparseCore 0:
  11.6 27.4 all-gather.3
  46.2 147.0 all-gather.5
  195.0 105.1 all-gather.7
